TPU v7x, 32 devices: a whole 2x2x4 slice. The times are simulated.
32 devices in a mesh: req: 8 (over z, y), tp: 4 (over x, core).
Axes of the slice: x: 2, y: 2, z: 4, core: 2. Of those that a mesh axis runs over, the one named last changes fastest.
Arguments:
- hidden_in: bfloat16 [2048, 1024], P('req'), may hold values from -42 to 42
- prompt_kv: bfloat16 [2, 64, 512, 1024], P(None, 'req', None, 'tp'), may hold values from -9 to 9
- tail_kv: bfloat16 [2, 2048, 64, 1024], P(None, 'req', None, 'tp'), may hold values from -9 to 9
- group_of: int32 [2048], P('req'), may hold values from 0 to 7
- prompt_len: int32 [64], P('req'), may hold values from 64 to 512, as said below
- tail_len: int32 [2048], P('req'), may hold values from 0 to 63, as said below
- bucket_of: int32 [577], replicated, may hold values from 0 to 31, never falling along the last dimension, each value on 1 to 38 neighbouring positions
- bias_table: float32 [32, 16], P(None, 'tp'), may hold values from -6 to 302
- attn_gain: float32 [1024], replicated, may hold values from 0.1 to 1.9
- w_query: bfloat16 [1024, 1024], P(None, 'tp'), may hold values from -0.1875 to 0.1875
- w_key: bfloat16 [1024, 1024], P(None, 'tp'), may hold values from -0.1875 to 0.1875
- w_value: bfloat16 [1024, 1024], P(None, 'tp'), may hold values from -0.1875 to 0.1875
- w_out: bfloat16 [1024, 1024], P('tp'), may hold values from -0.75 to 0.75
- ffn_gain: float32 [1024], replicated, may hold values from 0.1 to 1.9
- router_weight: bfloat16 [1024, 8], replicated, may hold values from -0.1875 to 0.1875
- expert_ids: int32 [2048, 2], P('req'), may hold values from 0 to 7, all different within a row; in each aligned block of 256 rows (0 to 255, 256 to 511, ...) at most 80 rows name the same one
- w_gate: bfloat16 [8, 1024, 2816], P('req', None, 'tp'), may hold values from -0.1875 to 0.1875
- w_up: bfloat16 [8, 1024, 2816], P('req', None, 'tp'), may hold values from -0.1875 to 0.1875
- w_down: bfloat16 [8, 2816, 1024], P('req', 'tp'), may hold values from -0.109375 to 0.109375
- new_slot: int32 [2048], replicated, may hold values from 0 to 2047, as said below
Outputs:
- out_hidden: bfloat16 [2048, 1024], P('req')
- new_tail_kv: bfloat16 [2, 2048, 64, 1024], P(None, 'req', None, 'tp')
Inputs may be any that keep to these rules, and one draw needn't show every extreme that they name: `expert_ids`: in each replica's aligned block of 256 tokens no expert is named by more than 80 of them, a bound that some block reaches. `new_slot`: A permutation. Exactly 4 requests of each replica are movers; all movers of one replica go to one replica (possibly itself), each taking a slot that a mover of that replica leaves; every other request keeps its slot. `prompt_len`: each replica has a group of 512 rows. `tail_len`: each replica has a request of 63 own rows and one of none.
All inputs are finite; a program needn't handle non-finite values.
Results may differ from a plain program's by a relative error of at most 0.013.
Values may be sent and summed in bfloat16 or wider, within the bound.
No kernel may reach another device: no remote copies, remote signals or barrier semaphores. Data moves between devices by JAX's collectives and lax.ppermute only.
A program may use at most 128 MiB of HBM per device.

v0:
```python
import functools
import jax
import jax.numpy as jnp
from jax import lax
from jax.experimental import pallas as pl
from jax.experimental.pallas import tpu as pltpu

HD = 64
EPS = 1e-06
F32 = jnp.float32
BF16 = jnp.bfloat16
NT = (((1,), (1,)), ((), ()))
LANES = 128
CHUNK = 16
TILE = 64


def attention_kernel(
    group_sm, plen_sm, tlen_sm, group_row, bucket_rev, bias_rows,
    hidden_hbm, gain_ref, wq_hbm, wk_hbm, wv_hbm, prompt_hbm, tail_hbm,
    head_ref, tail_out,
    hidden_v, wq_v, wk_v, wv_v, pk_v, pv_v, kbuf, vbuf,
    q_v, knew_v, vnew_v, table, bias_p, bias_t, s_t, o_v,
    w_sem, p_sem, in_sem, out_sem,
):
    rows = hidden_v.shape[0]
    groups, prompt_rows, cols = pv_v.shape
    tail_rows = kbuf.shape[1]
    heads = cols // HD
    per8 = 8 // heads
    width_t = per8 * tail_rows
    span_end = bias_p.shape[1] + tail_rows
    tile_rows = TILE * heads
    chunks = rows // CHUNK

    def weight_copies():
        return [
            pltpu.make_async_copy(hidden_hbm, hidden_v, w_sem.at[0]),
            pltpu.make_async_copy(wq_hbm, wq_v, w_sem.at[1]),
            pltpu.make_async_copy(wk_hbm, wk_v, w_sem.at[2]),
            pltpu.make_async_copy(wv_hbm, wv_v, w_sem.at[3]),
        ]

    def prompt_copies():
        return [
            pltpu.make_async_copy(
                prompt_hbm.at[0, g], pk_v.at[:, pl.ds(g * cols, cols)], p_sem.at[g]
            )
            for g in range(groups)
        ]

    def value_copy():
        return pltpu.make_async_copy(prompt_hbm.at[1], pv_v, p_sem.at[groups])

    def chunk_in(c):
        at = pl.ds(c * CHUNK, CHUNK)
        return [
            pltpu.make_async_copy(tail_hbm.at[0, at], kbuf.at[at], in_sem.at[0, c]),
            pltpu.make_async_copy(tail_hbm.at[1, at], vbuf.at[at], in_sem.at[1, c]),
        ]

    def chunk_out(c):
        at = pl.ds(c * CHUNK, CHUNK)
        return [
            pltpu.make_async_copy(kbuf.at[at], tail_out.at[0, at], out_sem.at[0, c]),
            pltpu.make_async_copy(vbuf.at[at], tail_out.at[1, at], out_sem.at[1, c]),
        ]

    for copy in weight_copies() + prompt_copies() + [value_copy()]:
        copy.start()
    for c in range(chunks):
        for copy in chunk_in(c):
            copy.start()

    buckets = bias_rows.shape[1]
    ids = bucket_rev[...]
    found = jnp.zeros(table.shape, F32)
    for k in range(buckets):
        found = jnp.where(ids == k, bias_rows[:, k : k + 1], found)
    table[...] = found

    for copy in weight_copies():
        copy.wait()
    v = hidden_v[...].astype(F32)
    normed = (
        v * lax.rsqrt(jnp.mean(v * v, axis=-1, keepdims=True) + EPS) * gain_ref[...]
    ).astype(BF16)
    query = jnp.dot(normed, wq_v[...], preferred_element_type=F32).astype(BF16)
    q_v[...] = query * jnp.asarray(HD ** (-0.5), BF16)
    knew_v[...] = jnp.dot(normed, wk_v[...], preferred_element_type=F32).astype(BF16).astype(F32)
    vnew_v[...] = jnp.dot(normed, wv_v[...], preferred_element_type=F32).astype(BF16).astype(F32)

    lane = lax.broadcasted_iota(jnp.int32, (8, LANES), 1)
    sub = lax.broadcasted_iota(jnp.int32, (8, LANES), 0)
    row16 = lax.broadcasted_iota(jnp.int32, (16, cols), 0)
    minus = jnp.float32(-jnp.inf)

    def build_bias(tile):
        def step(i, carry):
            base = tile * TILE + i * per8
            out_p = [jnp.full((8, LANES), minus) for _ in range(prompt_rows // LANES)]
            out_t = [jnp.full((8, LANES), minus) for _ in range(width_t // LANES)]
            for j in range(per8):
                r = base + j
                length = tlen_sm[r]
                plen = plen_sm[group_sm[r]]
                start = span_end - plen - length
                block = start // LANES
                off = start - block * LANES
                mine = (sub >= j * heads) & (sub < (j + 1) * heads)
                window = table[:, pl.ds(pl.multiple_of(block * LANES, LANES), prompt_rows + LANES)]
                turn = jnp.where(off == 0, 0, LANES - off)
                turned = [
                    pltpu.roll(window[:, k * LANES : (k + 1) * LANES], turn, 1)
                    for k in range(prompt_rows // LANES + 1)
                ]
                for k in range(prompt_rows // LANES):
                    here = jnp.where(lane < LANES - off, turned[k], turned[k + 1])
                    out_p[k] = jnp.where(mine & (lane + k * LANES < plen), here, out_p[k])
                place = j * tail_rows
                k = place // LANES
                place = place - k * LANES
                own = table[:, prompt_rows : prompt_rows + LANES]
                shift = place - (tail_rows - length)
                shift = jnp.where(shift < 0, shift + LANES, shift)
                own = pltpu.roll(own, shift, 1)
                live = mine & (lane >= place) & (lane <= place + length)
                out_t[k] = jnp.where(live, own, out_t[k])
            at = pl.ds(pl.multiple_of(i * 8, 8), 8)
            for k in range(prompt_rows // LANES):
                bias_p[at, k * LANES : (k + 1) * LANES] = out_p[k]
            for k in range(width_t // LANES):
                bias_t[at, k * LANES : (k + 1) * LANES] = out_t[k]
            return carry

        lax.fori_loop(0, TILE // per8, step, 0, unroll=4)

    def insert(c):
        def step(i, carry):
            r = c * CHUNK + i
            length = tlen_sm[r]
            first = pl.multiple_of(length // 16 * 16, 16)
            hit = row16 == length - first
            for new, buf in ((knew_v, kbuf), (vnew_v, vbuf)):
                fresh = jnp.broadcast_to(new[pl.ds(r, 1), :], (16, cols))
                old = buf[r, pl.ds(first, 16), :].astype(F32)
                buf[r, pl.ds(first, 16), :] = jnp.where(hit, fresh, old).astype(BF16)
            return carry

        lax.fori_loop(0, CHUNK, step, 0, unroll=4)

    rr = lax.broadcasted_iota(jnp.int32, (tile_rows, rows), 0) // heads
    rc = lax.broadcasted_iota(jnp.int32, (tile_rows, rows), 1)
    hrow = lax.broadcasted_iota(jnp.int32, (tile_rows, cols), 0) % heads
    hcol = lax.broadcasted_iota(jnp.int32, (tile_rows, cols), 1) // HD
    own_head = hrow == hcol
    group_hot = (
        lax.broadcasted_iota(jnp.int32, (groups, rows), 0) == group_row[...]
    ).astype(BF16)
    first_head = lax.broadcasted_iota(jnp.int32, (TILE, LANES), 1) < HD
    per16 = 16 // heads

    def do_tile(tile, carry):
        build_bias(tile)
        spread = (rr + tile * TILE == rc).astype(BF16)
        member = lax.dot_general(
            spread, group_hot, NT, preferred_element_type=F32
        )
        qrep = jnp.dot(spread, q_v[...], preferred_element_type=F32)
        qbd = jnp.where(own_head, qrep, 0.0).astype(BF16)

        @pl.when(tile == 0)
        def _():
            for copy in prompt_copies():
                copy.wait()

        spread_q = jnp.concatenate(
            [jnp.where(member[:, g : g + 1] > 0.5, qbd, jnp.zeros_like(qbd)) for g in range(groups)],
            axis=1,
        )
        s_p = (
            lax.dot_general(spread_q, pk_v[...], NT, preferred_element_type=F32) + bias_p[...]
        )
        for n in range(TILE // CHUNK):
            c = tile * (TILE // CHUNK) + n
            for copy in chunk_in(c):
                copy.wait()
            insert(c)
            for copy in chunk_out(c):
                copy.start()
            for i in range(CHUNK // per16):
                at = n * CHUNK * heads + i * 16
                keys = kbuf[pl.ds(c * CHUNK + i * per16, per16)].reshape(per16 * tail_rows, cols)
                got = lax.dot_general(qbd[at : at + 16], keys, NT, preferred_element_type=F32)
                s_t[at : at + 8, :] = got[:8, :width_t]
                s_t[at + 8 : at + 16, :] = got[8:, width_t:]
        tail_s = s_t[...] + bias_t[...]
        top = jnp.maximum(
            jnp.max(s_p, axis=1, keepdims=True), jnp.max(tail_s, axis=1, keepdims=True)
        )
        pe = jnp.exp(s_p - top)
        te = jnp.exp(tail_s - top)
        total = jnp.sum(pe, axis=1, keepdims=True) + jnp.sum(te, axis=1, keepdims=True)
        part = 1.0 / total
        pw = (pe * part).astype(BF16)
        tw = te * part

        @pl.when(tile == 0)
        def _():
            value_copy().wait()

        spread_p = jnp.concatenate(
            [jnp.where(member[:, g : g + 1] > 0.5, pw, jnp.zeros_like(pw)) for g in range(groups)],
            axis=1,
        )
        o_p = jnp.dot(
            spread_p, pv_v[...].reshape(groups * prompt_rows, cols), preferred_element_type=F32
        )
        none = jnp.zeros((8, width_t), F32)
        for i in range(TILE // per16):
            at = i * 16
            upper = jnp.concatenate([tw[at : at + 8], none], axis=1)
            lower = jnp.concatenate([none, tw[at + 8 : at + 16]], axis=1)
            both = jnp.concatenate([upper, lower], axis=0).astype(BF16)
            vals = vbuf[pl.ds(tile * TILE + i * per16, per16)].reshape(per16 * tail_rows, cols)
            o_t = jnp.dot(both, vals, preferred_element_type=F32) + o_p[at : at + 16]
            for b in range(cols // LANES):
                o_v[b, at : at + 16, :] = o_t[:, b * LANES : (b + 1) * LANES]
        for b in range(cols // LANES):
            low = o_v[b, pl.ds(2 * b, TILE, stride=heads), :]
            high = o_v[b, pl.ds(2 * b + 1, TILE, stride=heads), :]
            head_ref[
                pl.ds(pl.multiple_of(tile * TILE, TILE), TILE), b * LANES : (b + 1) * LANES
            ] = jnp.where(first_head, low, high).astype(BF16)
        return carry

    lax.fori_loop(0, rows // TILE, do_tile, 0)
    for c in range(chunks):
        for copy in chunk_out(c):
            copy.wait()


def attention(
    hidden_in, prompt_kv, tail_kv, group_of, prompt_len, tail_len, bucket_of, bias_table,
    attn_gain, w_query, w_key, w_value,
):
    rows, width = hidden_in.shape
    cols = w_query.shape[1]
    heads = cols // HD
    groups, prompt_rows = prompt_kv.shape[1:3]
    tail_rows = tail_kv.shape[2]
    span = bucket_of.shape[0]
    table_width = 2 * prompt_rows + LANES
    bucket_rev = jnp.pad(bucket_of[::-1], (0, table_width - span))[None, :]
    bias_rows = jnp.tile(bias_table.T, (8 // heads, 1))
    per8 = 8 // heads
    tile_rows = TILE * heads
    vm = pl.BlockSpec(memory_space=pltpu.VMEM)
    sm = pl.BlockSpec(memory_space=pltpu.SMEM)
    hbm = pl.BlockSpec(memory_space=pl.ANY)
    chunks = rows // CHUNK
    return pl.pallas_call(
        attention_kernel,
        out_shape=(
            jax.ShapeDtypeStruct((rows, cols), BF16),
            jax.ShapeDtypeStruct(tail_kv.shape, BF16),
        ),
        in_specs=[sm, sm, sm, vm, vm, vm, hbm, vm, hbm, hbm, hbm, hbm, hbm],
        out_specs=(vm, hbm),
        scratch_shapes=[
            pltpu.VMEM((rows, width), BF16),
            pltpu.VMEM((width, cols), BF16),
            pltpu.VMEM((width, cols), BF16),
            pltpu.VMEM((width, cols), BF16),
            pltpu.VMEM((prompt_rows, groups * cols), BF16),
            pltpu.VMEM((groups, prompt_rows, cols), BF16),
            pltpu.VMEM((rows, tail_rows, cols), BF16),
            pltpu.VMEM((rows, tail_rows, cols), BF16),
            pltpu.VMEM((rows, cols), BF16),
            pltpu.VMEM((rows, cols), F32),
            pltpu.VMEM((rows, cols), F32),
            pltpu.VMEM((8, table_width), F32),
            pltpu.VMEM((tile_rows, prompt_rows), F32),
            pltpu.VMEM((tile_rows, per8 * tail_rows), F32),
            pltpu.VMEM((tile_rows, per8 * tail_rows), F32),
            pltpu.VMEM((cols // LANES, tile_rows, LANES), F32),
            pltpu.SemaphoreType.DMA((4,)),
            pltpu.SemaphoreType.DMA((groups + 1,)),
            pltpu.SemaphoreType.DMA((2, chunks)),
            pltpu.SemaphoreType.DMA((2, chunks)),
        ],
        compiler_params=pltpu.CompilerParams(vmem_limit_bytes=48 * 1024 * 1024),
        cost_estimate=pl.CostEstimate(flops=8_000_000_000, bytes_accessed=45_000_000, transcendentals=700_000),
        name="attention",
    )(
        group_of, prompt_len, tail_len, group_of[None, :], bucket_rev, bias_rows,
        hidden_in, attn_gain[None, :], w_query, w_key, w_value, prompt_kv, tail_kv,
    )
TOP = 2
MIG = 4
EXTRA = 16
TN = (((0,), (0,)), ((), ()))


def iota(shape, dim):
    return lax.broadcasted_iota(jnp.int32, shape, dim)


def block_rows(cap):
    return cap + EXTRA


def plan_kernel(cap, slots_ref, ids_ref, place_ref, wide_ref, kron_ref, plan_ref, slot_s):
    replicas, rows = slots_ref.shape
    experts = slot_s.shape[0]
    size = place_ref.shape[0] // replicas
    me = lax.axis_index("req")
    ns = slots_ref[...]
    at_sub = iota((replicas, rows), 0)
    at_lane = iota((replicas, rows), 1)
    moved = ns != at_sub * rows + at_lane
    tri = (iota((rows, rows), 0) < iota((rows, rows), 1)).astype(BF16)
    rank = jnp.dot(moved.astype(F32).astype(BF16), tri, preferred_element_type=F32).astype(jnp.int32)
    going_to = ns // rows
    mine = at_sub == me

    def own(values):
        return jnp.sum(jnp.where(mine, values, 0), axis=0, keepdims=True)

    moved_me = own(moved.astype(jnp.int32))
    rank_me = own(rank)
    to_me = own(going_to)
    ids = ids_ref[...]
    pick = (iota((8, TOP), 0) == iota((8, TOP), 1)).astype(BF16)
    ids_rows = lax.dot_general(
        pick, ids.astype(F32).astype(BF16), NT, preferred_element_type=F32
    ).astype(jnp.int32)
    at_e = iota((experts, rows), 0)
    hit = (ids_rows[0:1] == at_e) | (ids_rows[1:2] == at_e)
    normal = (hit & (moved_me == 0)).astype(F32).astype(BF16)
    slot = jnp.dot(normal, tri, preferred_element_type=F32).astype(jnp.int32)
    slot_s[...] = jnp.where(hit, jnp.where(moved_me > 0, cap + rank_me, slot), -1)
    at_row = iota((size, rows), 0)
    for k in range(replicas):
        e = me ^ k
        block = pl.ds(k * size, size)
        row = slot_s[pl.ds(e, 1), :]
        leaving = jnp.where((moved_me > 0) & (to_me == e), cap + rank_me, -100)
        place_ref[block, 0:rows] = (at_row == row).astype(F32).astype(BF16)
        place_ref[block, rows : 2 * rows] = (at_row == leaving + MIG).astype(F32).astype(BF16)
        place_ref[block, 2 * rows :] = (at_row == leaving + 2 * MIG).astype(F32).astype(BF16)
    lane = iota(wide_ref.shape, 1)
    idf = ids.astype(F32)
    wide_ref[...] = jnp.where(
        lane == 0, idf[:, 0:1], jnp.where(lane == 1, idf[:, 1:2], 0.0)
    ).astype(BF16)
    dest = jnp.max(jnp.where(moved, going_to, -1), axis=1, keepdims=True)
    dest = jnp.where(dest < 0, iota((replicas, 1), 0), dest)
    hot = (dest == iota((replicas, replicas), 1)).astype(F32).astype(BF16)
    span = replicas * EXTRA
    mixed_row = (iota((span, replicas), 0) // EXTRA) ^ me
    a = (mixed_row == iota((span, replicas), 1)).astype(F32).astype(BF16)
    by_source = lax.dot_general(a, hot, NT, preferred_element_type=F32).astype(BF16)
    pairs = lax.dot_general(by_source, a, NT, preferred_element_type=F32)
    same = iota((span, span), 0) % EXTRA == iota((span, span), 1) % EXTRA
    kron_ref[...] = jnp.where(same, pairs, 0.0).astype(BF16)
    sub1 = iota((replicas, 1), 0)

    def source_of(who):
        return jnp.sum(jnp.where(dest == who, sub1, 0), axis=0, keepdims=True)

    bits = replicas.bit_length() - 1

    def held(diff):
        found = jnp.zeros_like(diff)
        for i in range(bits - 1):
            found = found + (((diff >> (bits - 1 - i)) & 1) << i)
        return found

    diff = source_of(me) ^ me
    final = jnp.where((diff & 1) == 1, 1 << (bits - 1), held(diff))
    send = held(source_of(me ^ 1) ^ (me ^ 1))
    lane8 = iota((8, LANES), 1)
    plan = jnp.where(lane8 == 0, final, jnp.where(lane8 == 1, send, -1))
    lane1 = iota((1, rows), 1)
    for m in range(MIG):
        is_m = (moved_me > 0) & (rank_me == m)
        mover = jnp.sum(jnp.where(is_m, lane1, 0), axis=1, keepdims=True)
        plan = jnp.where(lane8 == 8 + m, mover, plan)
        come = moved & (going_to == me) & (rank == m)
        to = jnp.sum(jnp.where(come, ns - me * rows + 1, 0), axis=1, keepdims=True)
        to = jnp.sum(to, axis=0, keepdims=True) - 1
        plan = jnp.where(lane8 == 16 + m, to, plan)
    plan_ref[...] = plan


def make_plan(slots, expert_ids, experts, cap, half):
    replicas, rows = slots.shape
    size = block_rows(cap)
    vm = pl.BlockSpec(memory_space=pltpu.VMEM)
    span = replicas * EXTRA
    return pl.pallas_call(
        functools.partial(plan_kernel, cap),
        out_shape=(
            jax.ShapeDtypeStruct((replicas * size, 3 * rows), BF16),
            jax.ShapeDtypeStruct((rows, half), BF16),
            jax.ShapeDtypeStruct((span, span), BF16),
            jax.ShapeDtypeStruct((8, LANES), jnp.int32),
        ),
        in_specs=[vm, vm],
        out_specs=(vm, vm, vm, vm),
        scratch_shapes=[pltpu.VMEM((experts, rows), jnp.int32)],
        cost_estimate=pl.CostEstimate(flops=20_000_000, bytes_accessed=4_000_000, transcendentals=0),
        name="plan",
    )(slots, expert_ids)


def norm(values, gain):
    v = values.astype(F32)
    return (v * lax.rsqrt(jnp.mean(v * v, axis=-1, keepdims=True) + EPS) * gain).astype(BF16)


def dispatch_kernel(pieces, replicas, *refs):
    heads_hbm = refs[:pieces]
    wout_hbm = refs[pieces : 2 * pieces]
    hidden_ref, gain_ref, place_ref, wide_ref = refs[2 * pieces : 2 * pieces + 4]
    refs = refs[2 * pieces + 4 :]
    resid_ref = refs[0]
    outs = refs[1 : 1 + replicas]
    head_v, wout_v, stack, sem = refs[1 + replicas :]
    tp = lax.axis_index("tp")
    core = tp & 1
    rows, width = hidden_ref.shape
    cols = width // pieces
    half = width // 2

    def copies():
        made = []
        for k in range(pieces):
            at = pl.ds(pl.multiple_of((tp ^ k) * cols, cols), cols)
            made.append(pltpu.make_async_copy(wout_hbm[k], wout_v.at[at], sem.at[0, k]))
            made.append(pltpu.make_async_copy(heads_hbm[k], head_v.at[:, at], sem.at[1, k]))
        return made

    for copy in copies():
        copy.start()
    for copy in copies():
        copy.wait()
    attn = jnp.dot(head_v[...], wout_v[...], preferred_element_type=F32)
    resid = (hidden_ref[...].astype(F32) + attn).astype(BF16)
    resid_ref[...] = resid
    normed = norm(resid, gain_ref[...])
    first = core == 0
    stack[0:rows, :] = jnp.where(first, normed[:, :half], normed[:, half:])
    stack[rows : 2 * rows, :] = jnp.where(first, resid[:, :half], resid[:, half:])
    stack[2 * rows :, :] = wide_ref[...]
    size = place_ref.shape[0] // replicas
    for k in range(replicas):
        outs[k][...] = jnp.dot(
            place_ref[k * size : (k + 1) * size], stack[...], preferred_element_type=F32
        ).astype(BF16)


def dispatch(heads, wouts, hidden, gain, place, wide, replicas):
    rows, width = hidden.shape
    pieces = len(heads)
    half = width // 2
    size = place.shape[0] // replicas
    vm = pl.BlockSpec(memory_space=pltpu.VMEM)
    hbm = pl.BlockSpec(memory_space=pl.ANY)
    return pl.pallas_call(
        functools.partial(dispatch_kernel, pieces, replicas),
        out_shape=(jax.ShapeDtypeStruct((rows, width), BF16),)
        + tuple(jax.ShapeDtypeStruct((size, half), BF16) for _ in range(replicas)),
        in_specs=[hbm] * (2 * pieces) + [vm] * 4,
        out_specs=(vm,) * (1 + replicas),
        scratch_shapes=[
            pltpu.VMEM((rows, width), BF16),
            pltpu.VMEM((width, width), BF16),
            pltpu.VMEM((3 * rows, half), BF16),
            pltpu.SemaphoreType.DMA((2, pieces)),
        ],
        compiler_params=pltpu.CompilerParams(vmem_limit_bytes=32 * 1024 * 1024),
        cost_estimate=pl.CostEstimate(flops=1_200_000_000, bytes_accessed=6_000_000, transcendentals=0),
        name="dispatch",
    )(*heads, *wouts, hidden, gain[None, :], place, wide)


def expert_kernel(replicas, *refs):
    own = refs[:replicas]
    pair = refs[replicas : 2 * replicas]
    wg_hbm, wu_hbm, wd_hbm, keep_ref, give_ref, x_own, x_pair, wg, wu, wd, sem, xsem = refs[2 * replicas :]
    core = lax.axis_index("tp") & 1
    size, half = own[0].shape

    def weight_copies():
        return [
            pltpu.make_async_copy(wg_hbm.at[0], wg, sem.at[0]),
            pltpu.make_async_copy(wu_hbm.at[0], wu, sem.at[1]),
            pltpu.make_async_copy(wd_hbm.at[0], wd, sem.at[2]),
        ]

    def block_copies():
        made = []
        for k in range(replicas):
            at = pl.ds(k * size, size)
            made.append(pltpu.make_async_copy(own[k], x_own.at[at], xsem.at[0, k]))
            made.append(pltpu.make_async_copy(pair[k], x_pair.at[at], xsem.at[1, k]))
        return made

    for copy in weight_copies() + block_copies():
        copy.start()
    for copy in block_copies() + weight_copies():
        copy.wait()
    here = pl.ds(pl.multiple_of(core * half, half), half)
    there = pl.ds(pl.multiple_of((1 - core) * half, half), half)
    total = replicas * size
    step = 256 if total % 256 == 0 else size

    def tile(i, carry):
        at = pl.ds(pl.multiple_of(i * step, step), step)
        a, b = x_own[at, :], x_pair[at, :]
        gate = jnp.dot(a, wg[here, :], preferred_element_type=F32) + jnp.dot(
            b, wg[there, :], preferred_element_type=F32
        )
        up = jnp.dot(a, wu[here, :], preferred_element_type=F32) + jnp.dot(
            b, wu[there, :], preferred_element_type=F32
        )
        act = (jax.nn.gelu(gate, approximate=True) * up).astype(BF16)
        give_ref[at, :] = jnp.dot(act, wd[:, there], preferred_element_type=F32).astype(BF16)
        keep_ref[at, :] = jnp.dot(act, wd[:, here], preferred_element_type=F32).astype(BF16)
        return carry

    lax.fori_loop(0, total // step, tile, 0)


def expert(own, pair, w_gate, w_up, w_down):
    replicas = len(own)
    size, half = own[0].shape
    _, width, hidden = w_gate.shape
    total = replicas * size
    vm = pl.BlockSpec(memory_space=pltpu.VMEM)
    hbm = pl.BlockSpec(memory_space=pl.ANY)
    shape = jax.ShapeDtypeStruct((total, half), BF16)
    return pl.pallas_call(
        functools.partial(expert_kernel, replicas),
        out_shape=(shape, shape),
        in_specs=[hbm] * (2 * replicas + 3),
        out_specs=(vm, vm),
        scratch_shapes=[
            pltpu.VMEM((total, half), BF16),
            pltpu.VMEM((total, half), BF16),
            pltpu.VMEM((width, hidden), BF16),
            pltpu.VMEM((width, hidden), BF16),
            pltpu.VMEM((hidden, width), BF16),
            pltpu.SemaphoreType.DMA((3,)),
            pltpu.SemaphoreType.DMA((2, replicas)),
        ],
        compiler_params=pltpu.CompilerParams(vmem_limit_bytes=32 * 1024 * 1024),
        cost_estimate=pl.CostEstimate(flops=3_400_000_000, bytes_accessed=8_000_000, transcendentals=600_000),
        name="expert",
    )(*own, *pair, w_gate, w_up, w_down)


def give_back_kernel(cap, keep_ref, got_ref, kron_ref, *refs):
    replicas = len(refs) - 1
    outs, rows_v = refs[:replicas], refs[replicas]
    size = outs[0].shape[0]
    for k in range(replicas):
        at = slice(k * size, (k + 1) * size)
        both = keep_ref[at, :].astype(F32) + got_ref[at, :].astype(F32)
        outs[k][...] = both.astype(BF16)
        rows_v[k * EXTRA : (k + 1) * EXTRA, :] = both[size - EXTRA :].astype(BF16)
    moved = jnp.dot(kron_ref[...], rows_v[...], preferred_element_type=F32)
    first = iota((EXTRA, 1), 0) >= cap - (size - EXTRA)
    for k in range(replicas):
        at = slice(k * EXTRA, (k + 1) * EXTRA)
        outs[k][size - EXTRA :, :] = jnp.where(
            first, moved[at], rows_v[at, :].astype(F32)
        ).astype(BF16)


def give_back(keep, got, kron, cap, replicas):
    total, half = keep.shape
    size = total // replicas
    vm = pl.BlockSpec(memory_space=pltpu.VMEM)
    return pl.pallas_call(
        functools.partial(give_back_kernel, cap),
        out_shape=tuple(jax.ShapeDtypeStruct((size, half), BF16) for _ in range(replicas)),
        in_specs=[vm] * 3,
        out_specs=(vm,) * replicas,
        scratch_shapes=[pltpu.VMEM((replicas * EXTRA, half), BF16)],
        compiler_params=pltpu.CompilerParams(vmem_limit_bytes=32 * 1024 * 1024),
        cost_estimate=pl.CostEstimate(flops=30_000_000, bytes_accessed=2_500_000, transcendentals=0),
        name="give_back",
    )(keep, got, kron)


def gates_kernel(cap, replicas, *refs):
    own = refs[:replicas]
    pair = refs[replicas : 2 * replicas]
    (resid_ref, slots_ref, ids_ref, gain_ref, router_ref, first_ref, second_ref, gate_ref, new_ref) = refs[
        2 * replicas :
    ]
    me = lax.axis_index("req")
    core = lax.axis_index("tp") & 1
    rows, width = resid_ref.shape
    half = width // 2
    size = own[0].shape[0]
    low = size - EXTRA
    skip = cap - low
    ns = slots_ref[...]
    count = ns.shape[0]
    at_sub = iota((count, rows), 0)
    moved = ns != at_sub * rows + iota((count, rows), 1)
    before = (iota((rows, rows), 0) < iota((rows, rows), 1)).astype(BF16)
    movedf = moved.astype(F32)
    rank = jnp.dot(movedf.astype(BF16), before, preferred_element_type=F32)
    coming = moved & (ns // rows == me)
    slot_to = jnp.sum(jnp.where(coming, ns - me * rows + 1, 0), axis=0, keepdims=True) - 1
    rank_in = jnp.sum(jnp.where(coming, rank, 0.0), axis=0, keepdims=True).astype(jnp.int32)
    landing = (iota((rows, rows), 0) == slot_to).astype(F32).astype(BF16)
    at16 = iota((EXTRA, rows), 0)

    def taken(offset):
        hot = (at16 == rank_in + (skip + offset)) & (slot_to >= 0)
        return lax.dot_general(landing, hot.astype(F32).astype(BF16), NT, preferred_element_type=F32)

    take_resid = taken(MIG)
    take_ids = taken(2 * MIG)
    vacated = jnp.sum(take_resid, axis=1, keepdims=True) > 0.5
    in_own = own[0][low:, :].astype(F32)
    in_pair = pair[0][low:, :].astype(F32)
    for k in range(1, replicas):
        in_own = in_own + own[k][low:, :].astype(F32)
        in_pair = in_pair + pair[k][low:, :].astype(F32)
    in_own, in_pair = in_own.astype(BF16), in_pair.astype(BF16)
    first_core = core == 0
    in_low = jnp.where(first_core, in_own, in_pair)
    in_high = jnp.where(first_core, in_pair, in_own)
    picked = take_resid.astype(BF16)
    resid = resid_ref[...]
    new_low = jnp.where(
        vacated, jnp.dot(picked, in_low, preferred_element_type=F32), resid[:, :half].astype(F32)
    ).astype(BF16)
    new_high = jnp.where(
        vacated, jnp.dot(picked, in_high, preferred_element_type=F32), resid[:, half:].astype(F32)
    ).astype(BF16)
    new_ref[...] = jnp.where(first_core, new_low, new_high)
    normed = norm(jnp.concatenate([new_low, new_high], axis=1), gain_ref[...])
    logits = jnp.dot(normed, router_ref[...], preferred_element_type=F32)
    experts = logits.shape[1]
    ids_in = jnp.dot(take_ids.astype(BF16), in_low[:, :LANES], preferred_element_type=F32)
    ids = ids_ref[...].astype(F32)
    id1 = jnp.where(vacated, ids_in[:, 0:1], ids[:, 0:1]).astype(jnp.int32)
    id2 = jnp.where(vacated, ids_in[:, 1:2], ids[:, 1:2]).astype(jnp.int32)
    at_e = iota((rows, experts), 1)
    hit1, hit2 = id1 == at_e, id2 == at_e
    picked1 = jnp.sum(jnp.where(hit1, logits, 0.0), axis=1, keepdims=True)
    picked2 = jnp.sum(jnp.where(hit2, logits, 0.0), axis=1, keepdims=True)
    gate = jax.nn.sigmoid(picked1 - picked2)
    gate_ref[...] = jnp.broadcast_to(gate, gate_ref.shape)
    mine = at_sub == me
    moved_me = jnp.sum(jnp.where(mine, movedf, 0.0), axis=0, keepdims=True)
    eye = (iota((rows, rows), 0) == iota((rows, rows), 1)).astype(BF16)
    moved_col = lax.dot_general(
        eye, jnp.broadcast_to(moved_me, (8, rows)).astype(BF16), NT, preferred_element_type=F32
    )[:, 0:1]
    old1 = ids_ref[:, 0:1] == at_e
    old2 = ids_ref[:, 1:2] == at_e
    normal = ((old1 | old2) & (moved_col < 0.5)).astype(F32).astype(BF16)
    after = (iota((rows, rows), 0) > iota((rows, rows), 1)).astype(BF16)
    slot = jnp.dot(after, normal, preferred_element_type=F32)
    slot1 = jnp.sum(jnp.where(hit1, slot, 0.0), axis=1, keepdims=True)
    slot2 = jnp.sum(jnp.where(hit2, slot, 0.0), axis=1, keepdims=True)
    in_rank = jnp.sum(
        jnp.where(take_resid > 0.5, iota((rows, EXTRA), 1), 0), axis=1, keepdims=True
    ) - (skip + MIG)
    slot1 = jnp.where(vacated, cap + in_rank, slot1.astype(jnp.int32))
    slot2 = jnp.where(vacated, cap + in_rank, slot2.astype(jnp.int32))
    lane = iota((rows, replicas * size), 1)
    first_ref[...] = (lane == (id1 ^ me) * size + slot1).astype(F32).astype(BF16)
    second_ref[...] = (lane == (id2 ^ me) * size + slot2).astype(F32).astype(BF16)


def make_gates(own, pair, resid, slots, ids, gain, router, cap):
    replicas = len(own)
    size, half = own[0].shape
    rows, width = resid.shape
    vm = pl.BlockSpec(memory_space=pltpu.VMEM)
    hot = jax.ShapeDtypeStruct((rows, replicas * size), BF16)
    return pl.pallas_call(
        functools.partial(gates_kernel, cap, replicas),
        out_shape=(
            hot,
            hot,
            jax.ShapeDtypeStruct((rows, LANES), F32),
            jax.ShapeDtypeStruct((rows, half), BF16),
        ),
        in_specs=[vm] * (2 * replicas + 5),
        out_specs=(vm,) * 4,
        compiler_params=pltpu.CompilerParams(vmem_limit_bytes=32 * 1024 * 1024),
        cost_estimate=pl.CostEstimate(flops=200_000_000, bytes_accessed=6_000_000, transcendentals=0),
        name="gates",
    )(*own, *pair, resid, slots, ids, gain[None, :], router)


def combine_kernel(replicas, *refs):
    blocks = refs[:replicas]
    first_ref, second_ref, gate_ref, out_ref, all_v = refs[replicas:]
    size = blocks[0].shape[0]
    for k in range(replicas):
        all_v[k * size : (k + 1) * size, :] = blocks[k][...]
    gate = gate_ref[:, 0:1]
    one = jnp.dot(first_ref[...], all_v[...], preferred_element_type=F32)
    two = jnp.dot(second_ref[...], all_v[...], preferred_element_type=F32)
    out_ref[...] = (gate * one + (1.0 - gate) * two).astype(BF16)


def combine(blocks, first, second, gate):
    replicas = len(blocks)
    size, half = blocks[0].shape
    rows = first.shape[0]
    vm = pl.BlockSpec(memory_space=pltpu.VMEM)
    return pl.pallas_call(
        functools.partial(combine_kernel, replicas),
        out_shape=jax.ShapeDtypeStruct((rows, half), BF16),
        in_specs=[vm] * (replicas + 3),
        out_specs=vm,
        scratch_shapes=[pltpu.VMEM((replicas * size, half), BF16)],
        compiler_params=pltpu.CompilerParams(vmem_limit_bytes=32 * 1024 * 1024),
        cost_estimate=pl.CostEstimate(flops=400_000_000, bytes_accessed=2_500_000, transcendentals=0),
        name="combine",
    )(*blocks, first, second, gate)


def pack_kernel(plan_ref, tail_hbm, out_hbm, sem):
    tail_rows = tail_hbm.shape[2]

    def copies():
        made = []
        for m in range(MIG):
            r = jnp.maximum(plan_ref[0, 8 + m], 0)
            for side in range(2):
                made.append(
                    pltpu.make_async_copy(
                        tail_hbm.at[side, r], out_hbm.at[2 * m + side], sem.at[2 * m + side]
                    )
                )
        return made

    for copy in copies():
        copy.start()
    for copy in copies():
        copy.wait()


def pack(plan, tail_new):
    _, _, tail_rows, cols = tail_new.shape
    hbm = pl.BlockSpec(memory_space=pl.ANY)
    return pl.pallas_call(
        pack_kernel,
        out_shape=jax.ShapeDtypeStruct((2 * MIG, tail_rows, cols), BF16),
        in_specs=[pl.BlockSpec(memory_space=pltpu.SMEM), hbm],
        out_specs=hbm,
        scratch_shapes=[pltpu.SemaphoreType.DMA((2 * MIG,))],
        cost_estimate=pl.CostEstimate(flops=0, bytes_accessed=500_000, transcendentals=0),
        name="pack",
    )(plan, tail_new)


def choose_kernel(plan_ref, *refs):
    choices = refs[:-2]
    out_hbm, sem = refs[-2:]
    index = plan_ref[0, 1]
    for i, choice in enumerate(choices):
        @pl.when(index == i)
        def _():
            copy = pltpu.make_async_copy(choice, out_hbm, sem)
            copy.start()
            copy.wait()


def choose(plan, held):
    hbm = pl.BlockSpec(memory_space=pl.ANY)
    return pl.pallas_call(
        choose_kernel,
        out_shape=jax.ShapeDtypeStruct(held[0].shape, BF16),
        in_specs=[pl.BlockSpec(memory_space=pltpu.SMEM)] + [hbm] * len(held),
        out_specs=hbm,
        scratch_shapes=[pltpu.SemaphoreType.DMA],
        cost_estimate=pl.CostEstimate(flops=0, bytes_accessed=500_000, transcendentals=0),
        name="choose",
    )(plan, *held)


def patch_kernel(plan_ref, *refs):
    choices = refs[:-3]
    out_hbm, sem = refs[-2:]
    index = plan_ref[0, 0]
    for i, choice in enumerate(choices):
        @pl.when(index == i)
        def _():
            for m in range(MIG):
                to = plan_ref[0, 16 + m]

                @pl.when(to >= 0)
                def _():
                    made = [
                        pltpu.make_async_copy(
                            choice.at[2 * m + side], out_hbm.at[side, to], sem.at[side]
                        )
                        for side in range(2)
                    ]
                    for copy in made:
                        copy.start()
                    for copy in made:
                        copy.wait()


def patch(plan, held, tail_new):
    hbm = pl.BlockSpec(memory_space=pl.ANY)
    return pl.pallas_call(
        patch_kernel,
        out_shape=jax.ShapeDtypeStruct(tail_new.shape, BF16),
        in_specs=[pl.BlockSpec(memory_space=pltpu.SMEM)] + [hbm] * (len(held) + 1),
        out_specs=hbm,
        scratch_shapes=[pltpu.SemaphoreType.DMA((2,))],
        input_output_aliases={len(held) + 1: 0},
        cost_estimate=pl.CostEstimate(flops=0, bytes_accessed=500_000, transcendentals=0),
        name="patch",
    )(plan, *held, tail_new)


def body(
    hidden_in, prompt_kv, tail_kv, group_of, prompt_len, tail_len, bucket_of, bias_table,
    attn_gain, w_query, w_key, w_value, w_out, ffn_gain, router_weight, expert_ids,
    w_gate, w_up, w_down, new_slot,
):
    rows, width = hidden_in.shape
    replicas = lax.axis_size("req")
    pieces = lax.axis_size("tp")
    experts = router_weight.shape[1]
    cap = -(-(5 * rows * TOP // (4 * experts)) // 16) * 16
    half = width // 2

    def across(axis, size, k):
        return lambda v: lax.ppermute(v, axis, [(i, i ^ k) for i in range(size)])

    def over_req(k):
        return across("req", replicas, k)

    def over_tp(k):
        return across("tp", pieces, k)

    wouts = [w_out] + [over_tp(k)(w_out) for k in range(1, pieces)]
    head_out, tail_new = attention(
        hidden_in, prompt_kv, tail_kv, group_of, prompt_len, tail_len, bucket_of, bias_table,
        attn_gain, w_query, w_key, w_value,
    )
    heads = [head_out] + [over_tp(k)(head_out) for k in range(1, pieces)]
    slots = new_slot.reshape(replicas, rows)
    place, wide, kron, plan = make_plan(slots, expert_ids, experts, cap, half)
    held = [pack(plan, tail_new)]
    bits = replicas.bit_length() - 1
    for i in range(bits - 1):
        held = held + [over_req(1 << (bits - 1 - i))(p) for p in held]
    held.append(over_req(1)(choose(plan, held)))
    new_tail_kv = patch(plan, held, tail_new)

    resid, *blocks = dispatch(heads, wouts, hidden_in, ffn_gain, place, wide, replicas)
    own = [blocks[0]] + [over_req(k)(blocks[k]) for k in range(1, replicas)]
    pair = [over_tp(1)(b) for b in own]
    keep, give = expert(own, pair, w_gate, w_up, w_down)
    back = give_back(keep, over_tp(1)(give), kron, cap, replicas)
    first, second, gate, resid_new = make_gates(
        own, pair, resid, slots, expert_ids, ffn_gain, router_weight, cap
    )
    result = [back[0]] + [over_req(k)(back[k]) for k in range(1, replicas)]
    mixed = combine(result, first, second, gate)
    k = 2
    while k < pieces:
        other = over_tp(k)(mixed)
        mixed = mixed.astype(F32) + other.astype(F32)
        k *= 2
        if k < pieces:
            mixed = mixed.astype(BF16)
    out_half = (resid_new.astype(F32) + mixed.astype(F32)).astype(BF16)
    out_other = over_tp(1)(out_half)
    core = lax.axis_index("tp") & 1
    out_hidden = jnp.where(
        core == 0,
        jnp.concatenate([out_half, out_other], axis=1),
        jnp.concatenate([out_other, out_half], axis=1),
    )
    return (out_hidden, new_tail_kv)


def solution(mesh):
    from jax.sharding import PartitionSpec as P

    return jax.shard_map(
        body,
        mesh=mesh,
        in_specs=(
            P("req", None), P(None, "req", None, "tp"), P(None, "req", None, "tp"),
            P("req"), P("req"), P("req"), P(), P(None, "tp"), P(),
            P(None, "tp"), P(None, "tp"), P(None, "tp"), P("tp", None), P(), P(),
            P("req", None), P("req", None, "tp"), P("req", None, "tp"), P("req", "tp", None), P(),
        ),
        out_specs=(P("req", None), P(None, "req", None, "tp")),
        check_vma=False,
    )
```

profile of v0, /device:TPU:0, one launch (start us, length us, event | category | flops | bytes accessed | tf_op | source)
XLA Modules:
  0.0 185.3 jit_solution(2563552138087941952)
XLA Ops:
  0.6 0.5 collective-permute-start.3
  1.1 2.6 %collective-permute-start.4 = (bf16[256,1024]{1,0:T(8,128)(2,1)}, bf16[256,1024]{1,0:T(8,128)(2,1)S(1)}, u32[]{:S(2)}, u32[]{:S(2)}) collective-permute-start(bf16[256,1024]{1,0:T(8,128)(2,1)} %refs_4_.1), channel_id=1, source_target_pairs={{0,2},{1,3},{2,0},{3,1},{4,6},{5,7},{6,4},{7,5},{8,10},{9,11},{10,... | collective-permute-start | bytes 1572872 | tf_op jit(solution)/shard_map/ppermute | solution.py:848
  3.8 0.8 reverse
  4.6 0.7 tile.4
  5.3 1.0 copy-done.6
  6.4 1.0 copy-done.23
  7.4 1.0 copy-done.24
  8.5 1.0 copy-done.25
  9.5 0.7 copy-done.26
  10.2 0.7 copy-done.27
  10.9 0.7 copy-done.28
  11.5 0.7 copy-done.29
  12.2 32.5 %attention.1 = (bf16[256,256]{1,0:T(8,128)(2,1)S(1)}, bf16[2,256,64,256]{3,2,1,0:T(8,128)(2,1)}) custom-call(s32[256]{0:T(256)S(1)} %copy-done.27, s32[8]{0:T(128)S(1)} %copy-done.29, s32[256]{0:T(256)S(1)} %copy-done.28, s32[1,256]{1,0:T(1,128)S(1)} %bitcast.10, s32[1,1152]{1,0:T(1,128)S(1)} %broadcast_in_dim.14.bucket_rev, f32[8,32]{1,0:T(8,128)S(1)} %bitcast.8, ...), custom_call_target="tpu_custom_call" | custom-call | flops 8000000000 | bytes 45000000 | tf_op jit(solution)/shard_map/attention/pallas_call | solution.py:262
  44.9 1.9 %collective-permute-start.1 = (bf16[256,256]{1,0:T(8,128)(2,1)S(1)}, bf16[256,256]{1,0:T(8,128)(2,1)S(1)}, u32[]{:S(2)}, u32[]{:S(2)}) collective-permute-start(bf16[256,256]{1,0:T(8,128)(2,1)S(1)} %get-tuple-element.31.refs_0_), channel_id=1, source_target_pairs={{0,2},{1,3},{2,0},{3,1},{4,6},{5,7},{6,4},{7,5},{8,10},{9,11},{10,... | collective-permute-start | bytes 393224 | tf_op jit(solution)/shard_map/ppermute | solution.py:848
  46.9 0.9 collective-permute-start.2
  47.8 0.8 copy.23.ids_ref.refs_18_
  48.6 0.6 reshape.11.slots_ref.refs_17_
  49.2 2.6 %plan.1 = (bf16[768,768]{1,0:T(8,128)(2,1)}, bf16[256,512]{1,0:T(8,128)(2,1)}, bf16[128,128]{1,0:T(8,128)(2,1)}, s32[8,128]{1,0:T(8,128)}) custom-call(s32[8,256]{1,0:T(8,128)} %reshape.11.slots_ref.refs_17_, s32[256,2]{1,0:T(8,128)} %copy.23.ids_ref.refs_18_), custom_call_target="tpu_custom_call" | custom-call | flops 20000000 | bytes 4000000 | tf_op jit(solution)/shard_map/plan/pallas_call | solution.py:402
  51.8 1.1 collective-permute-done.2.refs_3_
  53.0 1.3 copy-done.1
  54.3 0.9 copy-done.9
  55.2 2.3 %dispatch.1 = (bf16[256,1024]{1,0:T(8,128)(2,1)S(1)}, bf16[96,512]{1,0:T(8,128)(2,1)S(1)}, bf16[96,512]{1,0:T(8,128)(2,1)S(1)}, bf16[96,512]{1,0:T(8,128)(2,1)S(...) custom-call(bf16[256,256]{1,0:T(8,128)(2,1)S(1)} %get-tuple-element., ...), custom_call_target="tpu_custom_call" | custom-call | flops 1200000000 | bytes 6000000 | tf_op jit(solution)/shard_map/dispatch/pallas_call | solution.py:471
  57.6 0.8 copy-done.4
  58.4 1.5 collective-permute-start.6
  59.9 1.6 collective-permute-start.7
  61.9 2.6 %collective-permute-start.9 = (bf16[96,512]{1,0:T(8,128)(2,1)S(1)}, bf16[96,512]{1,0:T(8,128)(2,1)}, u32[]{:S(2)}, u32[]{:S(2)}) collective-permute-start(bf16[96,512]{1,0:T(8,128)(2,1)S(1)} %get-tuple-element.38), channel_id=1, source_target_pairs={{0,16},{4,20},{8,24},{12,28},{16,0},{20,4},{24,8},{28,12},{1,17},{... | collective-permute-start | bytes 294920 | tf_op jit(solution)/shard_map/ppermute | solution.py:848
  64.5 1.3 collective-permute-start.10
  65.8 3.6 %collective-permute-start.11 = (bf16[96,512]{1,0:T(8,128)(2,1)S(1)}, bf16[96,512]{1,0:T(8,128)(2,1)}, u32[]{:S(2)}, u32[]{:S(2)}) collective-permute-start(bf16[96,512]{1,0:T(8,128)(2,1)S(1)} %get-tuple-element.40), channel_id=1, source_target_pairs={{0,24},{4,28},{8,16},{12,20},{16,8},{20,12},{24,0},{28,4},{1,25},{... | collective-permute-start | bytes 294920 | tf_op jit(solution)/shard_map/ppermute | solution.py:848
  70.0 0.5 collective-permute-start.14
  70.5 9.2 %collective-permute-done.10.refs_5_ = bf16[96,512]{1,0:T(8,128)(2,1)} collective-permute-done((bf16[96,512]{1,0:T(8,128)(2,1)S(1)}, bf16[96,512]{1,0:T(8,128)(2,1)}, u32[]{:S(2)}, u32[]{:S(2)}) %collective-permute-start.10) | collective-permute-done | bytes 98336 | tf_op jit(solution)/shard_map/ppermute | solution.py:848
  79.7 0.5 collective-permute-start.16
  80.3 0.6 copy-done.10
  81.4 0.6 copy-done.13
  82.1 0.6 copy-done.16
  83.2 1.7 copy.26.refs_16_
  84.9 1.7 copy.27.refs_17_
  86.6 0.9 copy-done.11
  87.5 0.9 copy-done.14
  88.4 0.9 copy-done.17
  89.3 1.4 copy-done.22
  90.7 7.8 %expert.1 = (bf16[768,512]{1,0:T(8,128)(2,1)S(1)}, bf16[768,512]{1,0:T(8,128)(2,1)}) custom-call(bf16[96,512]{1,0:T(8,128)(2,1)S(1)} %get-tuple-element.34.refs_0_, bf16[96,512]{1,0:T(8,128)(2,1)S(1)} %collective-permute-done.6.refs_1_, bf16[96,512]{1,0:T(8,128)(2,1)S(1)} %collective-permute-done.7.refs_2_, ...), custom_call_target="tpu_custom_call" | custom-call | flops 3400000000 | bytes 8000000 | tf_op jit(solution)/shard_map/expert/pallas_call | solution.py:545
  98.5 0.9 copy-done.2
  99.5 10.0 %pack.1.refs_0_ = bf16[8,64,256]{2,1,0:T(8,128)(2,1)} custom-call(s32[8,128]{1,0:T(8,128)} %get-tuple-element.58.plan_ref, bf16[2,256,64,256]{3,2,1,0:T(8,128)(2,1)} %get-tuple-element.59.tail_hbm.refs_5_), custom_call_target="tpu_custom_call" | custom-call | bytes 500000 | tf_op jit(solution)/shard_map/pack/pallas_call | solution.py:761
  109.5 5.5 %collective-permute-start.31 = (bf16[8,64,256]{2,1,0:T(8,128)(2,1)}, bf16[8,64,256]{2,1,0:T(8,128)(2,1)S(1)}, u32[]{:S(2)}, u32[]{:S(2)}) collective-permute-start(bf16[8,64,256]{2,1,0:T(8,128)(2,1)} %pack.1.refs_0_), channel_id=1, source_target_pairs={{0,16},{4,20},{8,24},{12,28},{16,0},{20,4},{24,8},{28,12},{1,17},{... | collective-permute-start | bytes 786440 | tf_op jit(solution)/shard_map/ppermute | solution.py:848
  115.1 1.0 give_back.1
  116.1 0.6 collective-permute-start.22
  116.7 2.9 %collective-permute-start.24 = (bf16[96,512]{1,0:T(8,128)(2,1)}, bf16[96,512]{1,0:T(8,128)(2,1)S(1)}, u32[]{:S(2)}, u32[]{:S(2)}) collective-permute-start(bf16[96,512]{1,0:T(8,128)(2,1)} %get-tuple-element.50), channel_id=1, source_target_pairs={{0,12},{4,8},{8,4},{12,0},{16,28},{20,24},{24,20},{28,16},{1,13},{... | collective-permute-start | bytes 294920 | tf_op jit(solution)/shard_map/ppermute | solution.py:848
  119.6 12.7 %collective-permute-done.31.refs_1_ = bf16[8,64,256]{2,1,0:T(8,128)(2,1)S(1)} collective-permute-done((bf16[8,64,256]{2,1,0:T(8,128)(2,1)}, bf16[8,64,256]{2,1,0:T(8,128)(2,1)S(1)}, u32[]{:S(2)}, u32[]{:S(2)}) %collective-permute-start.31) | collective-permute-done | bytes 262176 | tf_op jit(solution)/shard_map/ppermute | solution.py:848
  132.4 0.6 copy-done.31
  133.0 3.5 %collective-permute-start.28 = (bf16[96,512]{1,0:T(8,128)(2,1)}, bf16[96,512]{1,0:T(8,128)(2,1)S(1)}, u32[]{:S(2)}, u32[]{:S(2)}) collective-permute-start(bf16[96,512]{1,0:T(8,128)(2,1)} %get-tuple-element.54), channel_id=1, source_target_pairs={{0,28},{4,24},{8,20},{12,16},{16,12},{20,8},{24,4},{28,0},{1,29},{... | collective-permute-start | bytes 294920 | tf_op jit(solution)/shard_map/ppermute | solution.py:848
  136.8 2.8 %gates.1 = (bf16[256,768]{1,0:T(8,128)(2,1)S(1)}, bf16[256,768]{1,0:T(8,128)(2,1)S(1)}, f32[256,128]{1,0:T(8,128)S(1)}, bf16[256,512]{1,0:T(8,128)(2,1)S(1)}) custom-call(bf16[96,512]{1,0:T(8,128)(2,1)S(1)} %get-tuple-element.34.refs_0_, bf16[96,512]{1,0:T(8,128)(2,1)S(1)} %collective-permute-done.6.refs_1_, ...), custom_call_target="tpu_custom_call" | custom-call | flops 200000000 | bytes 6000000 | tf_op jit(solution)/shard_map/gates/pallas_call | solution.py:692
  139.9 1.8 collective-permute-start.33
  141.7 1.4 collective-permute-done.26.refs_5_
  143.2 0.6 combine.1
  143.7 1.6 collective-permute-start.29
  145.3 3.6 %collective-permute-done.32.refs_2_ = bf16[8,64,256]{2,1,0:T(8,128)(2,1)S(1)} collective-permute-done((bf16[8,64,256]{2,1,0:T(8,128)(2,1)S(1)}, bf16[8,64,256]{2,1,0:T(8,128)(2,1)S(1)}, u32[]{:S(2)}, u32[]{:S(2)}) %collective-permute-start.32) | collective-permute-done | bytes 262176 | tf_op jit(solution)/shard_map/ppermute | solution.py:848
  148.9 3.4 %collective-permute-done.33.refs_3_ = bf16[8,64,256]{2,1,0:T(8,128)(2,1)S(1)} collective-permute-done((bf16[8,64,256]{2,1,0:T(8,128)(2,1)S(1)}, bf16[8,64,256]{2,1,0:T(8,128)(2,1)S(1)}, u32[]{:S(2)}, u32[]{:S(2)}) %collective-permute-start.33) | collective-permute-done | bytes 262176 | tf_op jit(solution)/shard_map/ppermute | solution.py:848
  152.4 0.7 copy-done.34
  153.1 9.8 %choose.1 = bf16[8,64,256]{2,1,0:T(8,128)(2,1)} custom-call(s32[8,128]{1,0:T(8,128)} %get-tuple-element.58.plan_ref, bf16[8,64,256]{2,1,0:T(8,128)(2,1)} %pack.1.refs_0_, bf16[8,64,256]{2,1,0:T(8,128)(2,1)} %copy-done.31, bf16[8,64,256]{2,1,0:T(8,128)(2,1)} %copy-done.33, bf16[8,64,256]{2,1,0:T(8,128)(2,1)} %copy-done.34), custom_call_target="tpu_custom_call" | custom-call | bytes 500000 | tf_op jit(solution)/shard_map/choose/pallas_call | solution.py:786
  162.9 2.1 %collective-permute-start.34 = (bf16[8,64,256]{2,1,0:T(8,128)(2,1)}, bf16[8,64,256]{2,1,0:T(8,128)(2,1)S(1)}, u32[]{:S(2)}, u32[]{:S(2)}) collective-permute-start(bf16[8,64,256]{2,1,0:T(8,128)(2,1)} %choose.1), channel_id=1, source_target_pairs={{0,4},{4,0},{8,12},{12,8},{16,20},{20,16},{24,28},{28,24},{1,5},{5... | collective-permute-start | bytes 786440 | tf_op jit(solution)/shard_map/ppermute | solution.py:848
  165.2 5.3 %collective-permute-done.34.refs_4_ = bf16[8,64,256]{2,1,0:T(8,128)(2,1)S(1)} collective-permute-done((bf16[8,64,256]{2,1,0:T(8,128)(2,1)}, bf16[8,64,256]{2,1,0:T(8,128)(2,1)S(1)}, u32[]{:S(2)}, u32[]{:S(2)}) %collective-permute-start.34) | collective-permute-done | bytes 262176 | tf_op jit(solution)/shard_map/ppermute | solution.py:848
  170.5 0.7 copy-done.35
  171.2 13.1 %patch.1 = bf16[2,256,64,256]{3,2,1,0:T(8,128)(2,1)} custom-call(s32[8,128]{1,0:T(8,128)} %get-tuple-element.58.plan_ref, bf16[8,64,256]{2,1,0:T(8,128)(2,1)} %pack.1.refs_0_, bf16[8,64,256]{2,1,0:T(8,128)(2,1)} %copy-done.31, bf16[8,64,256]{2,1,0:T(8,128)(2,1)} %copy-done.33, bf16[8,64,256]{2,1,0:T(8,128)(2,1)} %copy-done.34, ...), custom_call_target="tpu_custom_call", output_to_operand_aliasing={{}: (6, {})} | custom-call | bytes 500000 | tf_op jit(solution)/shard_map/patch/pallas_call | solution.py:823
  184.3 0.9 maximum_select_fusion
  (106 shorter events, 3.4 us)
Async XLA Ops:
  0.6 52.3 %collective-permute-start.3 = (bf16[256,1024]{1,0:T(8,128)(2,1)}, bf16[256,1024]{1,0:T(8,128)(2,1)S(1)}, u32[]{:S(2)}, u32[]{:S(2)}) collective-permute-start(bf16[256,1024]{1,0:T(8,128)(2,1)} %refs_4_.1), channel_id=1, source_target_pairs={{0,1},{1,0},{2,3},{3,2},{4,5},{5,4},{6,7},{7,6},{8,9},{9,8},{10,11... | collective-permute-start | bytes 1572872 | tf_op jit(solution)/shard_map/ppermute | solution.py:848
  1.1 51.8 %collective-permute-start.4 = (bf16[256,1024]{1,0:T(8,128)(2,1)}, bf16[256,1024]{1,0:T(8,128)(2,1)S(1)}, u32[]{:S(2)}, u32[]{:S(2)}) collective-permute-start(bf16[256,1024]{1,0:T(8,128)(2,1)} %refs_4_.1), channel_id=1, source_target_pairs={{0,2},{1,3},{2,0},{3,1},{4,6},{5,7},{6,4},{7,5},{8,10},{9,11},{10,... | collective-permute-start | bytes 1572872 | tf_op jit(solution)/shard_map/ppermute | solution.py:848
  3.7 49.3 %collective-permute-start.5 = (bf16[256,1024]{1,0:T(8,128)(2,1)}, bf16[256,1024]{1,0:T(8,128)(2,1)S(1)}, u32[]{:S(2)}, u32[]{:S(2)}) collective-permute-start(bf16[256,1024]{1,0:T(8,128)(2,1)} %refs_4_.1), channel_id=1, source_target_pairs={{0,3},{1,2},{2,1},{3,0},{4,7},{5,6},{6,5},{7,4},{8,11},{9,10},{10,... | collective-permute-start | bytes 1572872 | tf_op jit(solution)/shard_map/ppermute | solution.py:848
  5.3 1.0 copy-start.6
  6.4 1.0 copy-start.23
  7.4 1.0 copy-start.24
  8.4 1.0 copy-start.25
  12.2 35.6 %copy-start.38 = (s32[256,2]{0,1:T(2,128)S(1)}, s32[256,2]{0,1:T(2,128)}, u32[]{:S(2)}) copy-start(s32[256,2]{0,1:T(2,128)} %param.35) | copy-start | bytes 6148
  12.2 36.4 %copy-start.37 = (s32[2048]{0:T(1024)S(1)}, s32[2048]{0:T(1024)}, u32[]{:S(2)}) copy-start(s32[2048]{0:T(1024)} %param.39) | copy-start | bytes 24580
  12.2 40.8 %copy-start.7 = (bf16[256,1024]{1,0:T(8,128)(2,1)S(1)}, bf16[256,1024]{1,0:T(8,128)(2,1)}, u32[]{:S(2)}) copy-start(bf16[256,1024]{1,0:T(8,128)(2,1)} %refs_8_.1) | copy-start | bytes 1572868
  12.2 40.8 %copy-start.8 = (bf16[256,1024]{1,0:T(8,128)(2,1)S(1)}, bf16[256,1024]{1,0:T(8,128)(2,1)}, u32[]{:S(2)}) copy-start(bf16[256,1024]{1,0:T(8,128)(2,1)} %refs_4_.1) | copy-start | bytes 1572868
  12.2 40.8 %copy-start.21 = (f32[1024]{0:T(1024)S(1)}, f32[1024]{0:T(1024)}, u32[]{:S(2)}) copy-start(f32[1024]{0:T(1024)} %param.33) | copy-start | bytes 12292
  44.7 2.1 %collective-permute-start = (bf16[256,256]{1,0:T(8,128)(2,1)S(1)}, bf16[256,256]{1,0:T(8,128)(2,1)S(1)}, u32[]{:S(2)}, u32[]{:S(2)}) collective-permute-start(bf16[256,256]{1,0:T(8,128)(2,1)S(1)} %get-tuple-element.31.refs_0_), channel_id=1, source_target_pairs={{0,1},{1,0},{2,3},{3,2},{4,5},{5,4},{6,7},{7,6},{8,9},{9,8},{10,11... | collective-permute-start | bytes 393224 | tf_op jit(solution)/shard_map/ppermute | solution.py:848
  44.9 6.9 %collective-permute-start.1 = (bf16[256,256]{1,0:T(8,128)(2,1)S(1)}, bf16[256,256]{1,0:T(8,128)(2,1)S(1)}, u32[]{:S(2)}, u32[]{:S(2)}) collective-permute-start(bf16[256,256]{1,0:T(8,128)(2,1)S(1)} %get-tuple-element.31.refs_0_), channel_id=1, source_target_pairs={{0,2},{1,3},{2,0},{3,1},{4,6},{5,7},{6,4},{7,5},{8,10},{9,11},{10,... | collective-permute-start | bytes 393224 | tf_op jit(solution)/shard_map/ppermute | solution.py:848
  46.9 6.1 %collective-permute-start.2 = (bf16[256,256]{1,0:T(8,128)(2,1)S(1)}, bf16[256,256]{1,0:T(8,128)(2,1)S(1)}, u32[]{:S(2)}, u32[]{:S(2)}) collective-permute-start(bf16[256,256]{1,0:T(8,128)(2,1)S(1)} %get-tuple-element.31.refs_0_), channel_id=1, source_target_pairs={{0,3},{1,2},{2,1},{3,0},{4,7},{5,6},{6,5},{7,4},{8,11},{9,10},{10,... | collective-permute-start | bytes 393224 | tf_op jit(solution)/shard_map/ppermute | solution.py:848
  53.0 1.3 copy-start.1
  54.3 0.9 copy-start.9
  57.6 0.8 copy-start.4
  58.4 7.4 %collective-permute-start.6 = (bf16[96,512]{1,0:T(8,128)(2,1)S(1)}, bf16[96,512]{1,0:T(8,128)(2,1)S(1)}, u32[]{:S(2)}, u32[]{:S(2)}) collective-permute-start(bf16[96,512]{1,0:T(8,128)(2,1)S(1)} %get-tuple-element.35), channel_id=1, source_target_pairs={{0,4},{4,0},{8,12},{12,8},{16,20},{20,16},{24,28},{28,24},{1,5},{5... | collective-permute-start | bytes 294920 | tf_op jit(solution)/shard_map/ppermute | solution.py:848
  59.9 9.5 %collective-permute-start.7 = (bf16[96,512]{1,0:T(8,128)(2,1)S(1)}, bf16[96,512]{1,0:T(8,128)(2,1)S(1)}, u32[]{:S(2)}, u32[]{:S(2)}) collective-permute-start(bf16[96,512]{1,0:T(8,128)(2,1)S(1)} %get-tuple-element.36), channel_id=1, source_target_pairs={{0,8},{4,12},{8,0},{12,4},{16,24},{20,28},{24,16},{28,20},{1,9},{5... | collective-permute-start | bytes 294920 | tf_op jit(solution)/shard_map/ppermute | solution.py:848
  61.5 8.5 %collective-permute-start.8 = (bf16[96,512]{1,0:T(8,128)(2,1)S(1)}, bf16[96,512]{1,0:T(8,128)(2,1)S(1)}, u32[]{:S(2)}, u32[]{:S(2)}) collective-permute-start(bf16[96,512]{1,0:T(8,128)(2,1)S(1)} %get-tuple-element.37), channel_id=1, source_target_pairs={{0,12},{4,8},{8,4},{12,0},{16,28},{20,24},{24,20},{28,16},{1,13},{... | collective-permute-start | bytes 294920 | tf_op jit(solution)/shard_map/ppermute | solution.py:848
  61.9 8.1 %collective-permute-start.9 = (bf16[96,512]{1,0:T(8,128)(2,1)S(1)}, bf16[96,512]{1,0:T(8,128)(2,1)}, u32[]{:S(2)}, u32[]{:S(2)}) collective-permute-start(bf16[96,512]{1,0:T(8,128)(2,1)S(1)} %get-tuple-element.38), channel_id=1, source_target_pairs={{0,16},{4,20},{8,24},{12,28},{16,0},{20,4},{24,8},{28,12},{1,17},{... | collective-permute-start | bytes 294920 | tf_op jit(solution)/shard_map/ppermute | solution.py:848
  64.5 15.3 %collective-permute-start.10 = (bf16[96,512]{1,0:T(8,128)(2,1)S(1)}, bf16[96,512]{1,0:T(8,128)(2,1)}, u32[]{:S(2)}, u32[]{:S(2)}) collective-permute-start(bf16[96,512]{1,0:T(8,128)(2,1)S(1)} %get-tuple-element.39), channel_id=1, source_target_pairs={{0,20},{4,16},{8,28},{12,24},{16,4},{20,0},{24,12},{28,8},{1,21},{... | collective-permute-start | bytes 294920 | tf_op jit(solution)/shard_map/ppermute | solution.py:848
  65.8 14.0 %collective-permute-start.11 = (bf16[96,512]{1,0:T(8,128)(2,1)S(1)}, bf16[96,512]{1,0:T(8,128)(2,1)}, u32[]{:S(2)}, u32[]{:S(2)}) collective-permute-start(bf16[96,512]{1,0:T(8,128)(2,1)S(1)} %get-tuple-element.40), channel_id=1, source_target_pairs={{0,24},{4,28},{8,16},{12,20},{16,8},{20,12},{24,0},{28,4},{1,25},{... | collective-permute-start | bytes 294920 | tf_op jit(solution)/shard_map/ppermute | solution.py:848
  69.4 10.9 %collective-permute-start.12 = (bf16[96,512]{1,0:T(8,128)(2,1)S(1)}, bf16[96,512]{1,0:T(8,128)(2,1)}, u32[]{:S(2)}, u32[]{:S(2)}) collective-permute-start(bf16[96,512]{1,0:T(8,128)(2,1)S(1)} %get-tuple-element.41), channel_id=1, source_target_pairs={{0,28},{4,24},{8,20},{12,16},{16,12},{20,8},{24,4},{28,0},{1,29},{... | collective-permute-start | bytes 294920 | tf_op jit(solution)/shard_map/ppermute | solution.py:848
  70.0 10.3 %collective-permute-start.13 = (bf16[96,512]{1,0:T(8,128)(2,1)S(1)}, bf16[96,512]{1,0:T(8,128)(2,1)S(1)}, u32[]{:S(2)}, u32[]{:S(2)}) collective-permute-start(bf16[96,512]{1,0:T(8,128)(2,1)S(1)} %get-tuple-element.34.refs_0_), channel_id=1, source_target_pairs={{0,1},{1,0},{2,3},{3,2},{4,5},{5,4},{6,7},{7,6},{8,9},{9,8},{10,11... | collective-permute-start | bytes 294920 | tf_op jit(solution)/shard_map/ppermute | solution.py:848
  70.0 11.4 %collective-permute-start.14 = (bf16[96,512]{1,0:T(8,128)(2,1)S(1)}, bf16[96,512]{1,0:T(8,128)(2,1)S(1)}, u32[]{:S(2)}, u32[]{:S(2)}) collective-permute-start(bf16[96,512]{1,0:T(8,128)(2,1)S(1)} %collective-permute-done.6.refs_1_), channel_id=1, source_target_pairs={{0,1},{1,0},{2,3},{3,2},{4,5},{5,4},{6,7},{7,6},{8,9},{9,8},{10,11... | collective-permute-start | bytes 294920 | tf_op jit(solution)/shard_map/ppermute | solution.py:848
  79.7 2.4 %collective-permute-start.15 = (bf16[96,512]{1,0:T(8,128)(2,1)S(1)}, bf16[96,512]{1,0:T(8,128)(2,1)S(1)}, u32[]{:S(2)}, u32[]{:S(2)}) collective-permute-start(bf16[96,512]{1,0:T(8,128)(2,1)S(1)} %collective-permute-done.7.refs_2_), channel_id=1, source_target_pairs={{0,1},{1,0},{2,3},{3,2},{4,5},{5,4},{6,7},{7,6},{8,9},{9,8},{10,11... | collective-permute-start | bytes 294920 | tf_op jit(solution)/shard_map/ppermute | solution.py:848
  79.7 6.8 %collective-permute-start.16 = (bf16[96,512]{1,0:T(8,128)(2,1)S(1)}, bf16[96,512]{1,0:T(8,128)(2,1)}, u32[]{:S(2)}, u32[]{:S(2)}) collective-permute-start(bf16[96,512]{1,0:T(8,128)(2,1)S(1)} %collective-permute-done.8.refs_3_), channel_id=1, source_target_pairs={{0,1},{1,0},{2,3},{3,2},{4,5},{5,4},{6,7},{7,6},{8,9},{9,8},{10,11... | collective-permute-start | bytes 294920 | tf_op jit(solution)/shard_map/ppermute | solution.py:848
  80.2 6.3 %collective-permute-start.17 = (bf16[96,512]{1,0:T(8,128)(2,1)}, bf16[96,512]{1,0:T(8,128)(2,1)}, u32[]{:S(2)}, u32[]{:S(2)}) collective-permute-start(bf16[96,512]{1,0:T(8,128)(2,1)} %collective-permute-done.9.refs_4_), channel_id=1, source_target_pairs={{0,1},{1,0},{2,3},{3,2},{4,5},{5,4},{6,7},{7,6},{8,9},{9,8},{10,11... | collective-permute-start | bytes 294920 | tf_op jit(solution)/shard_map/ppermute | solution.py:848
  81.0 5.6 %collective-permute-start.18 = (bf16[96,512]{1,0:T(8,128)(2,1)}, bf16[96,512]{1,0:T(8,128)(2,1)}, u32[]{:S(2)}, u32[]{:S(2)}) collective-permute-start(bf16[96,512]{1,0:T(8,128)(2,1)} %collective-permute-done.10.refs_5_), channel_id=1, source_target_pairs={{0,1},{1,0},{2,3},{3,2},{4,5},{5,4},{6,7},{7,6},{8,9},{9,8},{10,11... | collective-permute-start | bytes 294920 | tf_op jit(solution)/shard_map/ppermute | solution.py:848
  82.0 4.6 %collective-permute-start.19 = (bf16[96,512]{1,0:T(8,128)(2,1)}, bf16[96,512]{1,0:T(8,128)(2,1)}, u32[]{:S(2)}, u32[]{:S(2)}) collective-permute-start(bf16[96,512]{1,0:T(8,128)(2,1)} %collective-permute-done.11.refs_6_), channel_id=1, source_target_pairs={{0,1},{1,0},{2,3},{3,2},{4,5},{5,4},{6,7},{7,6},{8,9},{9,8},{10,11... | collective-permute-start | bytes 294920 | tf_op jit(solution)/shard_map/ppermute | solution.py:848
  82.7 3.9 %collective-permute-start.20 = (bf16[96,512]{1,0:T(8,128)(2,1)}, bf16[96,512]{1,0:T(8,128)(2,1)}, u32[]{:S(2)}, u32[]{:S(2)}) collective-permute-start(bf16[96,512]{1,0:T(8,128)(2,1)} %collective-permute-done.12.refs_7_), channel_id=1, source_target_pairs={{0,1},{1,0},{2,3},{3,2},{4,5},{5,4},{6,7},{7,6},{8,9},{9,8},{10,11... | collective-permute-start | bytes 294920 | tf_op jit(solution)/shard_map/ppermute | solution.py:848
  86.6 0.9 copy-start.11
  87.5 0.9 copy-start.14
  88.4 0.9 copy-start.17
  89.3 1.4 copy-start.22
  98.5 0.9 copy-start.2
  99.4 15.6 %collective-permute-start.21 = (bf16[768,512]{1,0:T(8,128)(2,1)}, bf16[768,512]{1,0:T(8,128)(2,1)S(1)}, u32[]{:S(2)}, u32[]{:S(2)}) collective-permute-start(bf16[768,512]{1,0:T(8,128)(2,1)} %get-tuple-element.45), channel_id=1, source_target_pairs={{0,1},{1,0},{2,3},{3,2},{4,5},{5,4},{6,7},{7,6},{8,9},{9,8},{10,11... | collective-permute-start | bytes 2359304 | tf_op jit(solution)/shard_map/ppermute | solution.py:848
  99.5 15.6 %copy-start.3 = (bf16[768,512]{1,0:T(8,128)(2,1)S(1)}, bf16[768,512]{1,0:T(8,128)(2,1)}, u32[]{:S(2)}) copy-start(bf16[768,512]{1,0:T(8,128)(2,1)} %copy-done.2) | copy-start | bytes 2359300
  99.5 15.6 %copy-start.20 = (bf16[128,128]{1,0:T(8,128)(2,1)S(1)}, bf16[128,128]{1,0:T(8,128)(2,1)}, u32[]{:S(2)}) copy-start(bf16[128,128]{1,0:T(8,128)(2,1)} %get-tuple-element.46.kron_ref) | copy-start | bytes 98308
  109.4 27.1 %copy-start.36 = (bf16[1024,8]{0,1:T(8,128)(2,1)S(1)}, bf16[1024,8]{0,1:T(8,128)(2,1)}, u32[]{:S(2)}) copy-start(bf16[1024,8]{0,1:T(8,128)(2,1)} %param.34) | copy-start | bytes 49156
  109.5 27.3 %copy-start = (s32[256,2]{1,0:T(8,128)S(1)}, s32[256,2]{1,0:T(8,128)}, u32[]{:S(2)}) copy-start(s32[256,2]{1,0:T(8,128)} %copy.23.ids_ref.refs_18_) | copy-start | bytes 6148
  109.5 27.3 %copy-start.5 = (bf16[256,1024]{1,0:T(8,128)(2,1)S(1)}, bf16[256,1024]{1,0:T(8,128)(2,1)}, u32[]{:S(2)}) copy-start(bf16[256,1024]{1,0:T(8,128)(2,1)} %copy-done.4) | copy-start | bytes 1572868
  109.5 27.3 %copy-start.12 = (bf16[96,512]{1,0:T(8,128)(2,1)S(1)}, bf16[96,512]{1,0:T(8,128)(2,1)}, u32[]{:S(2)}) copy-start(bf16[96,512]{1,0:T(8,128)(2,1)} %copy-done.10) | copy-start | bytes 294916
  109.5 27.3 %copy-start.15 = (bf16[96,512]{1,0:T(8,128)(2,1)S(1)}, bf16[96,512]{1,0:T(8,128)(2,1)}, u32[]{:S(2)}) copy-start(bf16[96,512]{1,0:T(8,128)(2,1)} %copy-done.13) | copy-start | bytes 294916
  109.5 27.3 %copy-start.18 = (bf16[96,512]{1,0:T(8,128)(2,1)S(1)}, bf16[96,512]{1,0:T(8,128)(2,1)}, u32[]{:S(2)}) copy-start(bf16[96,512]{1,0:T(8,128)(2,1)} %copy-done.16) | copy-start | bytes 294916
  109.5 27.3 %copy-start.19 = (s32[8,256]{1,0:T(8,128)S(1)}, s32[8,256]{1,0:T(8,128)}, u32[]{:S(2)}) copy-start(s32[8,256]{1,0:T(8,128)} %reshape.11.slots_ref.refs_17_) | copy-start | bytes 24580
  109.5 22.8 %collective-permute-start.31 = (bf16[8,64,256]{2,1,0:T(8,128)(2,1)}, bf16[8,64,256]{2,1,0:T(8,128)(2,1)S(1)}, u32[]{:S(2)}, u32[]{:S(2)}) collective-permute-start(bf16[8,64,256]{2,1,0:T(8,128)(2,1)} %pack.1.refs_0_), channel_id=1, source_target_pairs={{0,16},{4,20},{8,24},{12,28},{16,0},{20,4},{24,8},{28,12},{1,17},{... | collective-permute-start | bytes 786440 | tf_op jit(solution)/shard_map/ppermute | solution.py:848
  116.1 23.5 %copy-start.30 = (bf16[8,64,256]{2,1,0:T(8,128)(2,1)S(1)}, bf16[8,64,256]{2,1,0:T(8,128)(2,1)}, u32[]{:S(2)}) copy-start(bf16[8,64,256]{2,1,0:T(8,128)(2,1)} %pack.1.refs_0_) | copy-start | bytes 786436
  116.1 16.2 %collective-permute-start.22 = (bf16[96,512]{1,0:T(8,128)(2,1)S(1)}, bf16[96,512]{1,0:T(8,128)(2,1)S(1)}, u32[]{:S(2)}, u32[]{:S(2)}) collective-permute-start(bf16[96,512]{1,0:T(8,128)(2,1)S(1)} %get-tuple-element.48), channel_id=1, source_target_pairs={{0,4},{4,0},{8,12},{12,8},{16,20},{20,16},{24,28},{28,24},{1,5},{5... | collective-permute-start | bytes 294920 | tf_op jit(solution)/shard_map/ppermute | solution.py:848
  116.7 15.7 %collective-permute-start.23 = (bf16[96,512]{1,0:T(8,128)(2,1)S(1)}, bf16[96,512]{1,0:T(8,128)(2,1)S(1)}, u32[]{:S(2)}, u32[]{:S(2)}) collective-permute-start(bf16[96,512]{1,0:T(8,128)(2,1)S(1)} %get-tuple-element.49), channel_id=1, source_target_pairs={{0,8},{4,12},{8,0},{12,4},{16,24},{20,28},{24,16},{28,20},{1,9},{5... | collective-permute-start | bytes 294920 | tf_op jit(solution)/shard_map/ppermute | solution.py:848
  116.7 22.9 %collective-permute-start.24 = (bf16[96,512]{1,0:T(8,128)(2,1)}, bf16[96,512]{1,0:T(8,128)(2,1)S(1)}, u32[]{:S(2)}, u32[]{:S(2)}) collective-permute-start(bf16[96,512]{1,0:T(8,128)(2,1)} %get-tuple-element.50), channel_id=1, source_target_pairs={{0,12},{4,8},{8,4},{12,0},{16,28},{20,24},{24,20},{28,16},{1,13},{... | collective-permute-start | bytes 294920 | tf_op jit(solution)/shard_map/ppermute | solution.py:848
  119.6 20.3 %collective-permute-start.25 = (bf16[96,512]{1,0:T(8,128)(2,1)}, bf16[96,512]{1,0:T(8,128)(2,1)S(1)}, u32[]{:S(2)}, u32[]{:S(2)}) collective-permute-start(bf16[96,512]{1,0:T(8,128)(2,1)} %get-tuple-element.51), channel_id=1, source_target_pairs={{0,16},{4,20},{8,24},{12,28},{16,0},{20,4},{24,8},{28,12},{1,17},{... | collective-permute-start | bytes 294920 | tf_op jit(solution)/shard_map/ppermute | solution.py:848
  132.3 10.9 %collective-permute-start.26 = (bf16[96,512]{1,0:T(8,128)(2,1)}, bf16[96,512]{1,0:T(8,128)(2,1)S(1)}, u32[]{:S(2)}, u32[]{:S(2)}) collective-permute-start(bf16[96,512]{1,0:T(8,128)(2,1)} %get-tuple-element.52), channel_id=1, source_target_pairs={{0,20},{4,16},{8,28},{12,24},{16,4},{20,0},{24,12},{28,8},{1,21},{... | collective-permute-start | bytes 294920 | tf_op jit(solution)/shard_map/ppermute | solution.py:848
  132.3 10.9 %collective-permute-start.27 = (bf16[96,512]{1,0:T(8,128)(2,1)}, bf16[96,512]{1,0:T(8,128)(2,1)S(1)}, u32[]{:S(2)}, u32[]{:S(2)}) collective-permute-start(bf16[96,512]{1,0:T(8,128)(2,1)} %get-tuple-element.53), channel_id=1, source_target_pairs={{0,24},{4,28},{8,16},{12,20},{16,8},{20,12},{24,0},{28,4},{1,25},{... | collective-permute-start | bytes 294920 | tf_op jit(solution)/shard_map/ppermute | solution.py:848
  133.0 10.2 %collective-permute-start.28 = (bf16[96,512]{1,0:T(8,128)(2,1)}, bf16[96,512]{1,0:T(8,128)(2,1)S(1)}, u32[]{:S(2)}, u32[]{:S(2)}) collective-permute-start(bf16[96,512]{1,0:T(8,128)(2,1)} %get-tuple-element.54), channel_id=1, source_target_pairs={{0,28},{4,24},{8,20},{12,16},{16,12},{20,8},{24,4},{28,0},{1,29},{... | collective-permute-start | bytes 294920 | tf_op jit(solution)/shard_map/ppermute | solution.py:848
  136.5 3.4 %copy-start.32 = (bf16[8,64,256]{2,1,0:T(8,128)(2,1)S(1)}, bf16[8,64,256]{2,1,0:T(8,128)(2,1)}, u32[]{:S(2)}) copy-start(bf16[8,64,256]{2,1,0:T(8,128)(2,1)} %copy-done.31) | copy-start | bytes 786436
  139.6 9.3 %collective-permute-start.32 = (bf16[8,64,256]{2,1,0:T(8,128)(2,1)S(1)}, bf16[8,64,256]{2,1,0:T(8,128)(2,1)S(1)}, u32[]{:S(2)}, u32[]{:S(2)}) collective-permute-start(bf16[8,64,256]{2,1,0:T(8,128)(2,1)S(1)} %copy-done.30), channel_id=1, source_target_pairs={{0,8},{4,12},{8,0},{12,4},{16,24},{20,28},{24,16},{28,20},{1,9},{5... | collective-permute-start | bytes 786440 | tf_op jit(solution)/shard_map/ppermute | solution.py:848
  139.9 12.4 %collective-permute-start.33 = (bf16[8,64,256]{2,1,0:T(8,128)(2,1)S(1)}, bf16[8,64,256]{2,1,0:T(8,128)(2,1)S(1)}, u32[]{:S(2)}, u32[]{:S(2)}) collective-permute-start(bf16[8,64,256]{2,1,0:T(8,128)(2,1)S(1)} %copy-done.32), channel_id=1, source_target_pairs={{0,8},{4,12},{8,0},{12,4},{16,24},{20,28},{24,16},{28,20},{1,9},{5... | collective-permute-start | bytes 786440 | tf_op jit(solution)/shard_map/ppermute | solution.py:848
  143.7 21.2 %collective-permute-start.29 = (bf16[256,512]{1,0:T(8,128)(2,1)S(1)}, bf16[256,512]{1,0:T(8,128)(2,1)S(1)}, u32[]{:S(2)}, u32[]{:S(2)}) collective-permute-start(bf16[256,512]{1,0:T(8,128)(2,1)S(1)} %combine.1), channel_id=1, source_target_pairs={{0,2},{1,3},{2,0},{3,1},{4,6},{5,7},{6,4},{7,5},{8,10},{9,11},{10,... | collective-permute-start | bytes 786440 | tf_op jit(solution)/shard_map/ppermute | solution.py:848
  148.9 3.4 %copy-start.33 = (bf16[8,64,256]{2,1,0:T(8,128)(2,1)}, bf16[8,64,256]{2,1,0:T(8,128)(2,1)S(1)}, u32[]{:S(2)}) copy-start(bf16[8,64,256]{2,1,0:T(8,128)(2,1)S(1)} %collective-permute-done.32.refs_2_) | copy-start | bytes 786436
  162.9 7.6 %collective-permute-start.34 = (bf16[8,64,256]{2,1,0:T(8,128)(2,1)}, bf16[8,64,256]{2,1,0:T(8,128)(2,1)S(1)}, u32[]{:S(2)}, u32[]{:S(2)}) collective-permute-start(bf16[8,64,256]{2,1,0:T(8,128)(2,1)} %choose.1), channel_id=1, source_target_pairs={{0,4},{4,0},{8,12},{12,8},{16,20},{20,16},{24,28},{28,24},{1,5},{5... | collective-permute-start | bytes 786440 | tf_op jit(solution)/shard_map/ppermute | solution.py:848
  165.1 19.2 %collective-permute-start.30 = (bf16[256,512]{1,0:T(8,128)(2,1)S(1)}, bf16[256,512]{1,0:T(8,128)(2,1)S(1)}, u32[]{:S(2)}, u32[]{:S(2)}) collective-permute-start(bf16[256,512]{1,0:T(8,128)(2,1)S(1)} %add_convert_fusion), channel_id=1, source_target_pairs={{0,1},{1,0},{2,3},{3,2},{4,5},{5,4},{6,7},{7,6},{8,9},{9,8},{10,11... | collective-permute-start | bytes 786440 | tf_op jit(solution)/shard_map/ppermute | solution.py:848
  (10 other events, 6.7 us)
where the time goes:
time: 186 us; the launch traced here: 185 us
  Pallas kernels  82.6 us (44%)
  starting transfers between devices  38 us (20%)
  waiting for transfers between devices  37.3 us (20%)
  local copies, waits for them, and re-layouts  25.3 us (14%)
    ppermute x35, starting transfers between devices, across(): return lambda v: lax.ppermute(v, axis, [(i, i ^ k) for i in range(size)])  38 us
    ppermute x35, waiting for transfers between devices, across(): return lambda v: lax.ppermute(v, axis, [(i, i ^ k) for i in range(size)])  37.3 us
    pallas_call x1, Pallas kernels, attention(): pl.pallas_call(attention_kernel, out_shape=(jax.ShapeDtypeStruct((rows, c...  32.5 us
    unnamed x84, local copies, waits for them, and re-layouts  24 us
    pallas_call x1, Pallas kernels, patch(): pl.pallas_call(patch_kernel, out_shape=jax.ShapeDtypeStruct(tail_new.shap...  13.1 us
    pallas_call x1, Pallas kernels, pack(): pl.pallas_call(pack_kernel, out_shape=jax.ShapeDtypeStruct((2 * MIG, tail...  9.97 us
    pallas_call x1, Pallas kernels, choose(): pl.pallas_call(choose_kernel, out_shape=jax.ShapeDtypeStruct(held[0].shap...  9.78 us
    pallas_call x1, Pallas kernels, expert(): pl.pallas_call(functools.partial(expert_kernel, replicas), out_shape=(sha...  7.83 us
  transfers between devices with their start and end apart: 35, of which 8 were waited for; matrix products, arithmetic and copies ran while one was open for 4% of the time, Pallas kernels for 39%

commit v1 on v0

v1 whole, which is shorter than its diff:
```python
import functools
import jax
import jax.numpy as jnp
from jax import lax
from jax.experimental import pallas as pl
from jax.experimental.pallas import tpu as pltpu
from jax.sharding import PartitionSpec as P

HD = 64
EPS = 1e-06
F32 = jnp.float32
BF16 = jnp.bfloat16
NT = (((1,), (1,)), ((), ()))
LANES = 128
TILE = 64
TOP = 2
MIG = 4
EXTRA = 16
VMEM_BYTES = 60 * 1024 * 1024


def iota(shape, dim):
    return lax.broadcasted_iota(jnp.int32, shape, dim)


def onehot(hit):
    return hit.astype(F32).astype(BF16)


def attention_kernel(
    group_hbm, plen_hbm, tlen_hbm, group_row_hbm, bucket_hbm, bias_hbm, gain_hbm,
    hidden_hbm, wq_hbm, wk_hbm, wv_hbm, prompt_hbm, tail_hbm, slots_hbm,
    head_ref, tail_out, packet_out,
    group_sm, plen_sm, tlen_sm, perm_sm, slots_sm, mover_sm, group_row, bucket_row, bias_rows, gain_v, perm_v,
    hidden_v, wq_v, wk_v, wv_v, pk_v, pv_v, kbuf, vbuf,
    q_v, knew_v, vnew_v, table, s_p, s_t, w_p, o_v, sorted_v, qbd_v,
    small_sem, w_sem, p_sem, in_sem, out_sem, perm_sem, packet_sem,
):
    rows, width = hidden_v.shape
    groups, prompt_rows, cols = pv_v.shape
    tail_rows = kbuf.shape[1]
    heads = cols // HD
    per8 = 8 // heads
    per16 = 16 // heads
    width_t = per8 * tail_rows
    span_end = prompt_rows + tail_rows
    tile_rows = TILE * heads
    tiles = rows // TILE

    small = [
        pltpu.make_async_copy(src, dst, small_sem.at[i])
        for i, (src, dst) in enumerate(
            (
                (group_hbm, group_sm), (plen_hbm, plen_sm), (tlen_hbm, tlen_sm),
                (group_row_hbm, group_row), (bucket_hbm, bucket_row),
                (bias_hbm, bias_rows), (gain_hbm, gain_v), (slots_hbm, slots_sm),
            )
        )
    ]
    weights = [
        pltpu.make_async_copy(src, dst, w_sem.at[i])
        for i, (src, dst) in enumerate(
            ((hidden_hbm, hidden_v), (wq_hbm, wq_v), (wk_hbm, wk_v), (wv_hbm, wv_v))
        )
    ]
    prompts = [
        pltpu.make_async_copy(prompt_hbm.at[0], pk_v, p_sem.at[0]),
        pltpu.make_async_copy(prompt_hbm.at[1], pv_v, p_sem.at[1]),
    ]

    def tile_in(t):
        at = pl.ds(t * TILE, TILE)
        return [
            pltpu.make_async_copy(tail_hbm.at[0, at], kbuf.at[at], in_sem.at[0, t]),
            pltpu.make_async_copy(tail_hbm.at[1, at], vbuf.at[at], in_sem.at[1, t]),
        ]

    def tile_out(t):
        at = pl.ds(t * TILE, TILE)
        return [
            pltpu.make_async_copy(kbuf.at[at], tail_out.at[0, at], out_sem.at[0, t]),
            pltpu.make_async_copy(vbuf.at[at], tail_out.at[1, at], out_sem.at[1, t]),
        ]

    for copy in small + weights + prompts[:1]:
        copy.start()
    for copy in small:
        copy.wait()

    eye = onehot(iota((rows, rows), 0) == iota((rows, rows), 1))
    g_row = group_row[...]
    g_col = lax.dot_general(
        eye, jnp.broadcast_to(g_row.astype(F32), (8, rows)).astype(BF16), NT,
        preferred_element_type=F32,
    )[:, 0:1].astype(jnp.int32)
    key_row = g_row * rows + iota((1, rows), 1)
    key_col = g_col * rows + iota((rows, 1), 0)
    rank_row = jnp.sum((key_col < key_row).astype(jnp.int32), axis=0, keepdims=True)
    rank_col = jnp.sum((key_row < key_col).astype(jnp.int32), axis=1, keepdims=True)
    perm_row = jnp.sum(
        jnp.where(rank_col == iota((rows, rows), 1), iota((rows, rows), 0), 0), axis=0, keepdims=True
    )
    perm_v[...] = jnp.broadcast_to(perm_row, perm_v.shape)
    perm_copy = pltpu.make_async_copy(perm_v, perm_sm, perm_sem)
    perm_copy.start()

    span = bucket_row.shape[1]
    buckets = bias_rows.shape[1]
    below = (bucket_row[...] < iota((buckets, span), 0)).astype(jnp.int32)
    starts = jnp.sum(below, axis=1, keepdims=True)
    bias = jnp.concatenate([bias_rows[...]] * per8, axis=0)
    distance = span_end - iota(table.shape, 1)
    found = jnp.broadcast_to(bias[:, 0:1], table.shape)
    for k in range(1, buckets):
        found = jnp.where(distance >= starts[k : k + 1, 0:1], bias[:, k : k + 1], found)
    table[...] = found

    base = lax.axis_index("req") * rows
    for m in range(MIG + 1):
        mover_sm[m] = 0

    def look(i, count):
        away = slots_sm[base + i] != base + i

        @pl.when(away)
        def _():
            mover_sm[jnp.minimum(count, MIG)] = i

        return count + away.astype(jnp.int32)

    lax.fori_loop(0, rows, look, 0, unroll=16)
    for copy in weights:
        copy.wait()
    for t in range(tiles):
        for copy in tile_in(t):
            copy.start()
    prompts[1].start()
    v = hidden_v[...].astype(F32)
    normed = (
        v * lax.rsqrt(jnp.mean(v * v, axis=-1, keepdims=True) + EPS) * gain_v[...]
    ).astype(BF16)
    query = jnp.dot(normed, wq_v[...], preferred_element_type=F32).astype(BF16)
    q_v[...] = query * jnp.asarray(HD ** (-0.5), BF16)
    key_new = jnp.dot(normed, wk_v[...], preferred_element_type=F32).astype(BF16)
    value_new = jnp.dot(normed, wv_v[...], preferred_element_type=F32).astype(BF16)
    knew_v[...] = key_new.astype(F32)
    vnew_v[...] = value_new.astype(F32)
    perm_copy.wait()

    lane = iota((8, LANES), 1)
    sub = iota((8, LANES), 0)
    row16 = iota((16, cols), 0)
    minus = jnp.float32(-jnp.inf)
    pieces = prompt_rows // LANES

    def build_bias(tile):
        def step(i, carry):
            base = tile * TILE + i * per8
            out_p = [jnp.full((8, LANES), minus) for _ in range(pieces)]
            out_t = [jnp.full((8, LANES), minus) for _ in range(width_t // LANES)]
            for j in range(per8):
                r = perm_sm[0, base + j]
                length = tlen_sm[r]
                plen = plen_sm[group_sm[r]]
                start = span_end - plen - length
                block = start // LANES
                off = start - block * LANES
                mine = (sub >= j * heads) & (sub < (j + 1) * heads)
                window = table[:, pl.ds(pl.multiple_of(block * LANES, LANES), prompt_rows + LANES)]
                turn = jnp.where(off == 0, 0, LANES - off)
                turned = [
                    pltpu.roll(window[:, k * LANES : (k + 1) * LANES], turn, 1)
                    for k in range(pieces + 1)
                ]
                for k in range(pieces):
                    here = jnp.where(lane < LANES - off, turned[k], turned[k + 1])
                    out_p[k] = jnp.where(mine & (lane < plen - k * LANES), here, out_p[k])
                place = j * tail_rows
                k = place // LANES
                place = place - k * LANES
                own = table[:, prompt_rows : prompt_rows + LANES]
                shift = place - (tail_rows - length)
                shift = jnp.where(shift < 0, shift + LANES, shift)
                own = pltpu.roll(own, shift, 1)
                live = mine & (lane >= place) & (lane <= place + length)
                out_t[k] = jnp.where(live, own, out_t[k])
            at = pl.ds(pl.multiple_of(tile * tile_rows + i * 8, 8), 8)
            for k in range(pieces):
                s_p[at, k * LANES : (k + 1) * LANES] = out_p[k]
            for k in range(width_t // LANES):
                s_t[at, k * LANES : (k + 1) * LANES] = out_t[k]
            return carry

        lax.fori_loop(0, TILE // per8, step, 0, unroll=8)

    def insert(t):
        def step(i, carry):
            r = t * TILE + i
            length = tlen_sm[r]
            first = pl.multiple_of(length // 16 * 16, 16)
            hit = row16 == length - first
            for new, buf in ((knew_v, kbuf), (vnew_v, vbuf)):
                fresh = jnp.broadcast_to(new[pl.ds(r, 1), :], (16, cols))
                old = buf[r, pl.ds(first, 16), :].astype(F32)
                buf[r, pl.ds(first, 16), :] = jnp.where(hit, fresh, old).astype(BF16)
            return carry

        lax.fori_loop(0, TILE, step, 0, unroll=8)

    own_head = iota((tile_rows, cols), 0) % heads == iota((tile_rows, cols), 1) // HD
    spread_row = iota((tile_rows, rows), 0) // heads
    first_head = iota((TILE, LANES), 1) < HD

    def spread_of(tile):
        return onehot(rank_row == spread_row + tile * TILE)

    def member_of(tile):
        group8 = jnp.broadcast_to(g_row.astype(F32), (8, rows)).astype(BF16)
        return lax.dot_general(
            spread_of(tile), group8, NT, preferred_element_type=F32
        )[:, 0:1].astype(jnp.int32)

    def group_range(tile):
        low = group_sm[perm_sm[0, tile * TILE]]
        high = group_sm[perm_sm[0, tile * TILE + TILE - 1]]
        return low, high + 1

    def scores(tile, carry):
        build_bias(tile)
        at = pl.ds(pl.multiple_of(tile * tile_rows, tile_rows), tile_rows)
        qrep = jnp.dot(spread_of(tile), q_v[...], preferred_element_type=F32)
        qbd = jnp.where(own_head, qrep, 0.0)
        qbd_v[at, :] = qbd.astype(BF16)
        member = member_of(tile)

        @pl.when(tile == 0)
        def _():
            prompts[0].wait()

        def one_group(g, carry):
            part = jnp.where(member == g, qbd, 0.0).astype(BF16)
            s_p[at, :] += lax.dot_general(part, pk_v[g], NT, preferred_element_type=F32)
            return carry

        low, high = group_range(tile)
        lax.fori_loop(low, high, one_group, 0)
        for copy in tile_in(tile):
            copy.wait()
        insert(tile)
        for copy in tile_out(tile):
            copy.start()
        return carry

    lax.fori_loop(0, tiles, scores, 0)
    packet = [
        pltpu.make_async_copy(
            buf.at[mover_sm[m]], packet_out.at[2 * m + side], packet_sem.at[2 * m + side]
        )
        for m in range(MIG)
        for side, buf in enumerate((kbuf, vbuf))
    ]
    for copy in packet:
        copy.start()
    prompts[1].wait()

    def gathered(buf, first):
        return jnp.concatenate([buf[perm_sm[0, first + j]] for j in range(per16)], axis=0)

    def values(tile, carry):
        base = pl.multiple_of(tile * tile_rows, tile_rows)
        at = pl.ds(base, tile_rows)
        for i in range(TILE // per16):
            keys = gathered(kbuf, tile * TILE + i * per16)
            here = pl.ds(pl.multiple_of(base + i * 16, 16), 16)
            got = lax.dot_general(qbd_v[here, :], keys, NT, preferred_element_type=F32)
            upper = pl.ds(pl.multiple_of(base + i * 16, 8), 8)
            lower = pl.ds(pl.multiple_of(base + i * 16 + 8, 8), 8)
            s_t[upper, :] += got[:8, :width_t]
            s_t[lower, :] += got[8:, width_t:]
        prompt_s = s_p[at, :]
        tail_s = s_t[at, :]
        top = jnp.maximum(
            jnp.max(prompt_s, axis=1, keepdims=True), jnp.max(tail_s, axis=1, keepdims=True)
        )
        pe = jnp.exp(prompt_s - top)
        te = jnp.exp(tail_s - top)
        total = jnp.sum(pe, axis=1, keepdims=True) + jnp.sum(te, axis=1, keepdims=True)
        part = 1.0 / total
        w_p[...] = (pe * part).astype(BF16)
        tw = te * part
        none = jnp.zeros((8, width_t), F32)
        for i in range(TILE // per16):
            row = i * 16
            upper = jnp.concatenate([tw[row : row + 8], none], axis=1)
            lower = jnp.concatenate([none, tw[row + 8 : row + 16]], axis=1)
            both = jnp.concatenate([upper, lower], axis=0).astype(BF16)
            vals = gathered(vbuf, tile * TILE + i * per16)
            o_t = jnp.dot(both, vals, preferred_element_type=F32)
            for b in range(cols // LANES):
                o_v[b, row : row + 16, :] = o_t[:, b * LANES : (b + 1) * LANES]
        member = member_of(tile)

        def one_group(g, carry):
            w = jnp.where(member == g, w_p[...].astype(F32), 0.0).astype(BF16)
            o_p = jnp.dot(w, pv_v[g], preferred_element_type=F32)
            for b in range(cols // LANES):
                o_v[b] += o_p[:, b * LANES : (b + 1) * LANES]
            return carry

        low, high = group_range(tile)
        lax.fori_loop(low, high, one_group, 0)
        to = pl.ds(pl.multiple_of(tile * TILE, TILE), TILE)
        for b in range(cols // LANES):
            even = o_v[b, pl.ds(2 * b, TILE, stride=heads), :]
            odd = o_v[b, pl.ds(2 * b + 1, TILE, stride=heads), :]
            sorted_v[to, b * LANES : (b + 1) * LANES] = jnp.where(first_head, even, odd).astype(BF16)
        return carry

    lax.fori_loop(0, tiles, values, 0)
    unsort = onehot(rank_col == iota((rows, rows), 1))
    head_ref[...] = jnp.dot(unsort, sorted_v[...], preferred_element_type=F32).astype(BF16)
    for copy in packet:
        copy.wait()
    for t in range(tiles):
        for copy in tile_out(t):
            copy.wait()


def attention(
    hidden_in, prompt_kv, tail_kv, group_of, prompt_len, tail_len, bucket_of, bias_table,
    attn_gain, w_query, w_key, w_value, new_slot,
):
    rows, width = hidden_in.shape
    cols = w_query.shape[1]
    heads = cols // HD
    groups, prompt_rows = prompt_kv.shape[1:3]
    tail_rows = tail_kv.shape[2]
    span = bucket_of.shape[0]
    buckets = bias_table.shape[0]
    table_width = 2 * prompt_rows + LANES
    width_t = 8 // heads * tail_rows
    tiles = rows // TILE
    vm = pl.BlockSpec(memory_space=pltpu.VMEM)
    hbm = pl.BlockSpec(memory_space=pl.ANY)
    return pl.pallas_call(
        attention_kernel,
        out_shape=(
            jax.ShapeDtypeStruct((rows, cols), BF16),
            jax.ShapeDtypeStruct(tail_kv.shape, BF16),
            jax.ShapeDtypeStruct((2 * MIG, tail_rows, cols), BF16),
        ),
        in_specs=[hbm] * 14,
        out_specs=(vm, hbm, hbm),
        scratch_shapes=[
            pltpu.SMEM((rows,), jnp.int32),
            pltpu.SMEM((groups,), jnp.int32),
            pltpu.SMEM((rows,), jnp.int32),
            pltpu.SMEM((8, rows), jnp.int32),
            pltpu.SMEM(new_slot.shape, jnp.int32),
            pltpu.SMEM((MIG + 1,), jnp.int32),
            pltpu.VMEM((1, rows), jnp.int32),
            pltpu.VMEM((1, span), jnp.int32),
            pltpu.VMEM((heads, buckets), F32),
            pltpu.VMEM((1, width), F32),
            pltpu.VMEM((8, rows), jnp.int32),
            pltpu.VMEM((rows, width), BF16),
            pltpu.VMEM((width, cols), BF16),
            pltpu.VMEM((width, cols), BF16),
            pltpu.VMEM((width, cols), BF16),
            pltpu.VMEM((groups, prompt_rows, cols), BF16),
            pltpu.VMEM((groups, prompt_rows, cols), BF16),
            pltpu.VMEM((rows, tail_rows, cols), BF16),
            pltpu.VMEM((rows, tail_rows, cols), BF16),
            pltpu.VMEM((rows, cols), BF16),
            pltpu.VMEM((rows, cols), F32),
            pltpu.VMEM((rows, cols), F32),
            pltpu.VMEM((8, table_width), F32),
            pltpu.VMEM((rows * heads, prompt_rows), F32),
            pltpu.VMEM((rows * heads, width_t), F32),
            pltpu.VMEM((TILE * heads, prompt_rows), BF16),
            pltpu.VMEM((cols // LANES, TILE * heads, LANES), F32),
            pltpu.VMEM((rows, cols), BF16),
            pltpu.VMEM((rows * heads, cols), BF16),
            pltpu.SemaphoreType.DMA((8,)),
            pltpu.SemaphoreType.DMA((4,)),
            pltpu.SemaphoreType.DMA((2,)),
            pltpu.SemaphoreType.DMA((2, tiles)),
            pltpu.SemaphoreType.DMA((2, tiles)),
            pltpu.SemaphoreType.DMA,
            pltpu.SemaphoreType.DMA((2 * MIG,)),
        ],
        compiler_params=pltpu.CompilerParams(vmem_limit_bytes=VMEM_BYTES),
        cost_estimate=pl.CostEstimate(flops=8_000_000_000, bytes_accessed=45_000_000, transcendentals=700_000),
        name="attention",
    )(
        group_of, prompt_len, tail_len, group_of[None, :], bucket_of[None, :], bias_table.T,
        attn_gain[None, :], hidden_in, w_query, w_key, w_value, prompt_kv, tail_kv, new_slot,
    )


def block_rows(cap):
    return cap + EXTRA


def plan_kernel(cap, slots_ref, ids_ref, *refs):
    place_ref, extra_ref, wide_ref, kron_ref, plan_ref, slot_s = refs[-6:]
    replicas, rows = slots_ref.shape
    experts = slot_s.shape[0]
    size = place_ref.shape[0] // replicas
    me = lax.axis_index("req")
    ns = slots_ref[...]
    at_sub = iota((replicas, rows), 0)
    at_lane = iota((replicas, rows), 1)
    moved = ns != at_sub * rows + at_lane
    tri = (iota((rows, rows), 0) < iota((rows, rows), 1)).astype(BF16)
    rank = jnp.dot(moved.astype(F32).astype(BF16), tri, preferred_element_type=F32).astype(jnp.int32)
    going_to = ns // rows
    mine = at_sub == me

    def own(values):
        return jnp.sum(jnp.where(mine, values, 0), axis=0, keepdims=True)

    moved_me = own(moved.astype(jnp.int32))
    rank_me = own(rank)
    to_me = own(going_to)
    ids_rows = ids_ref[...]
    at_e = iota((experts, rows), 0)
    hit = (ids_rows[0:1] == at_e) | (ids_rows[1:2] == at_e)
    normal = (hit & (moved_me == 0)).astype(F32).astype(BF16)
    slot = jnp.dot(normal, tri, preferred_element_type=F32).astype(jnp.int32)
    slot_s[...] = jnp.where(hit, jnp.where(moved_me > 0, cap + rank_me, slot), -1)
    at_row = iota((size, rows), 0)
    at_extra = iota((EXTRA, rows), 0)
    for k in range(replicas):
        e = me ^ k
        block = pl.ds(k * size, size)
        row = slot_s[pl.ds(e, 1), :]
        leaving = jnp.where((moved_me > 0) & (to_me == e), rank_me, -100)
        place_ref[block, :] = onehot(at_row == row)
        more = pl.ds(k * EXTRA, EXTRA)
        extra_ref[more, 0:rows] = onehot(at_extra == leaving + MIG)
        extra_ref[more, rows:] = onehot(at_extra == leaving + 2 * MIG)
    lane = iota(wide_ref.shape, 1)
    eye = onehot(iota((rows, rows), 0) == iota((rows, rows), 1))
    facts = jnp.concatenate([ids_rows, jnp.zeros((6, rows), jnp.int32)], axis=0)
    columns = lax.dot_general(
        eye, facts.astype(F32).astype(BF16), NT, preferred_element_type=F32
    )
    wide_ref[...] = jnp.where(
        lane == 0, columns[:, 0:1], jnp.where(lane == 1, columns[:, 1:2], 0.0)
    ).astype(BF16)
    dest = jnp.max(jnp.where(moved, going_to, -1), axis=1, keepdims=True)
    dest = jnp.where(dest < 0, iota((replicas, 1), 0), dest)
    hot = (dest == iota((replicas, replicas), 1)).astype(F32).astype(BF16)
    span = replicas * EXTRA
    mixed_row = (iota((span, replicas), 0) // EXTRA) ^ me
    a = (mixed_row == iota((span, replicas), 1)).astype(F32).astype(BF16)
    by_source = lax.dot_general(a, hot, NT, preferred_element_type=F32).astype(BF16)
    pairs = lax.dot_general(by_source, a, NT, preferred_element_type=F32)
    same = iota((span, span), 0) % EXTRA == iota((span, span), 1) % EXTRA
    kron_ref[...] = jnp.where(same, pairs, 0.0).astype(BF16)
    sub1 = iota((replicas, 1), 0)

    def source_of(who):
        return jnp.sum(jnp.where(dest == who, sub1, 0), axis=0, keepdims=True)

    bits = replicas.bit_length() - 1

    def held(diff):
        found = jnp.zeros_like(diff)
        for i in range(bits - 1):
            found = found + (((diff >> (bits - 1 - i)) & 1) << i)
        return found

    diff = source_of(me) ^ me
    final = jnp.where((diff & 1) == 1, 1 << (bits - 1), held(diff))
    send = held(source_of(me ^ 1) ^ (me ^ 1))
    lane8 = iota((8, LANES), 1)
    plan = jnp.where(lane8 == 0, final, jnp.where(lane8 == 1, send, -1))
    lane1 = iota((1, rows), 1)
    for m in range(MIG):
        is_m = (moved_me > 0) & (rank_me == m)
        mover = jnp.sum(jnp.where(is_m, lane1, 0), axis=1, keepdims=True)
        plan = jnp.where(lane8 == 8 + m, mover, plan)
        come = moved & (going_to == me) & (rank == m)
        to = jnp.sum(jnp.where(come, ns - me * rows + 1, 0), axis=1, keepdims=True)
        to = jnp.sum(to, axis=0, keepdims=True) - 1
        plan = jnp.where(lane8 == 16 + m, to, plan)
    plan_ref[...] = plan


def make_plan(slots, expert_ids, experts, cap, after):
    replicas, rows = slots.shape
    size = block_rows(cap)
    vm = pl.BlockSpec(memory_space=pltpu.VMEM)
    span = replicas * EXTRA
    return pl.pallas_call(
        functools.partial(plan_kernel, cap),
        out_shape=(
            jax.ShapeDtypeStruct((replicas * size, rows), BF16),
            jax.ShapeDtypeStruct((replicas * EXTRA, 2 * rows), BF16),
            jax.ShapeDtypeStruct((rows, LANES), BF16),
            jax.ShapeDtypeStruct((span, span), BF16),
            jax.ShapeDtypeStruct((8, LANES), jnp.int32),
        ),
        in_specs=[vm, vm] + [pl.BlockSpec(memory_space=pl.ANY)] * len(after),
        out_specs=(vm,) * 5,
        scratch_shapes=[pltpu.VMEM((experts, rows), jnp.int32)],
        compiler_params=pltpu.CompilerParams(vmem_limit_bytes=VMEM_BYTES),
        cost_estimate=pl.CostEstimate(flops=0, bytes_accessed=0, transcendentals=0),
        name="plan",
    )(slots, expert_ids.T, *after)


def load(sem, *pairs):
    made = [pltpu.make_async_copy(src, dst, sem.at[i]) for i, (src, dst) in enumerate(pairs)]
    for copy in made:
        copy.start()
    for copy in made:
        copy.wait()


def norm(values, gain):
    v = values.astype(F32)
    return (v * lax.rsqrt(jnp.mean(v * v, axis=-1, keepdims=True) + EPS) * gain).astype(BF16)


def dispatch_kernel(pieces, replicas, *refs):
    heads_hbm = refs[:pieces]
    wout_hbm = refs[pieces : 2 * pieces]
    hidden_hbm, gain_ref, place_hbm, extra_hbm, wide_hbm = refs[2 * pieces : 2 * pieces + 5]
    refs = refs[2 * pieces + 6 :]
    resid_ref = refs[0]
    outs = refs[1 : 1 + replicas]
    head_v, wout_v, stack, hidden_ref, place_ref, extra_ref, wide_ref, sem, more = refs[1 + replicas :]
    tp = lax.axis_index("tp")
    core = tp & 1
    rows, width = hidden_ref.shape
    cols = width // pieces
    half = width // 2

    def copies():
        made = []
        for k in range(pieces):
            at = pl.ds(pl.multiple_of((tp ^ k) * cols, cols), cols)
            made.append(pltpu.make_async_copy(wout_hbm[k], wout_v.at[at], sem.at[0, k]))
            made.append(pltpu.make_async_copy(heads_hbm[k], head_v.at[:, at], sem.at[1, k]))
        made.append(pltpu.make_async_copy(hidden_hbm, hidden_ref, more.at[0]))
        return made

    late = [
        pltpu.make_async_copy(place_hbm, place_ref, more.at[1]),
        pltpu.make_async_copy(extra_hbm, extra_ref, more.at[2]),
        pltpu.make_async_copy(wide_hbm, wide_ref, more.at[3]),
    ]

    for copy in copies() + late:
        copy.start()
    for copy in copies():
        copy.wait()
    attn = jnp.dot(head_v[...], wout_v[...], preferred_element_type=F32)
    resid = (hidden_ref[...].astype(F32) + attn).astype(BF16)
    resid_ref[...] = resid
    normed = norm(resid, gain_ref[...])
    first = core == 0
    stack[0:rows, :] = jnp.where(first, normed[:, :half], normed[:, half:])
    stack[rows : 2 * rows, :] = jnp.where(first, resid[:, :half], resid[:, half:])
    for copy in late:
        copy.wait()
    size = place_ref.shape[0] // replicas
    extra = jnp.dot(extra_ref[:, 0:rows], stack[rows:, :], preferred_element_type=F32)
    names = jnp.dot(extra_ref[:, rows:], wide_ref[...], preferred_element_type=F32)
    for k in range(replicas):
        block = jnp.dot(
            place_ref[k * size : (k + 1) * size], stack[0:rows, :], preferred_element_type=F32
        )
        more_k = slice(k * EXTRA, (k + 1) * EXTRA)
        outs[k][0 : size - EXTRA, :] = block[: size - EXTRA].astype(BF16)
        tail = block[size - EXTRA :] + extra[more_k]
        outs[k][size - EXTRA :, 0:LANES] = (tail[:, :LANES] + names[more_k]).astype(BF16)
        outs[k][size - EXTRA :, LANES:] = tail[:, LANES:].astype(BF16)


def dispatch(heads, wouts, hidden, gain, place, extra, wide, after, replicas):
    rows, width = hidden.shape
    pieces = len(heads)
    half = width // 2
    size = place.shape[0] // replicas
    vm = pl.BlockSpec(memory_space=pltpu.VMEM)
    hbm = pl.BlockSpec(memory_space=pl.ANY)
    return pl.pallas_call(
        functools.partial(dispatch_kernel, pieces, replicas),
        out_shape=(jax.ShapeDtypeStruct((rows, width), BF16),)
        + tuple(jax.ShapeDtypeStruct((size, half), BF16) for _ in range(replicas)),
        in_specs=[hbm] * (2 * pieces) + [hbm, vm, hbm, hbm, hbm, hbm],
        out_specs=(vm,) * (1 + replicas),
        scratch_shapes=[
            pltpu.VMEM((rows, width), BF16),
            pltpu.VMEM((width, width), BF16),
            pltpu.VMEM((2 * rows, half), BF16),
            pltpu.VMEM((rows, width), BF16),
            pltpu.VMEM(place.shape, BF16),
            pltpu.VMEM(extra.shape, BF16),
            pltpu.VMEM(wide.shape, BF16),
            pltpu.SemaphoreType.DMA((2, pieces)),
            pltpu.SemaphoreType.DMA((4,)),
        ],
        compiler_params=pltpu.CompilerParams(vmem_limit_bytes=VMEM_BYTES),
        cost_estimate=pl.CostEstimate(flops=1_200_000_000, bytes_accessed=6_000_000, transcendentals=0),
        name="dispatch",
    )(*heads, *wouts, hidden, gain[None, :], place, extra, wide, after)


def expert_kernel(replicas, *refs):
    own = refs[:replicas]
    pair = refs[replicas : 2 * replicas]
    wg_hbm, wu_hbm, wd_hbm, keep_ref, give_ref, x_own, x_pair, wg, wu, wd, sem, xsem = refs[2 * replicas :]
    core = lax.axis_index("tp") & 1
    size, half = own[0].shape

    def weight_copies():
        return [
            pltpu.make_async_copy(wg_hbm.at[0], wg, sem.at[0]),
            pltpu.make_async_copy(wu_hbm.at[0], wu, sem.at[1]),
            pltpu.make_async_copy(wd_hbm.at[0], wd, sem.at[2]),
        ]

    def block_copies():
        made = []
        for k in range(replicas):
            at = pl.ds(k * size, size)
            made.append(pltpu.make_async_copy(own[k], x_own.at[at], xsem.at[0, k]))
            made.append(pltpu.make_async_copy(pair[k], x_pair.at[at], xsem.at[1, k]))
        return made

    for copy in weight_copies() + block_copies():
        copy.start()
    for copy in block_copies() + weight_copies():
        copy.wait()
    here = pl.ds(pl.multiple_of(core * half, half), half)
    there = pl.ds(pl.multiple_of((1 - core) * half, half), half)
    total = replicas * size
    step = 256 if total % 256 == 0 else size

    def tile(i, carry):
        at = pl.ds(pl.multiple_of(i * step, step), step)
        a, b = x_own[at, :], x_pair[at, :]
        gate = lax.dot_general(a, wg[:, here], NT, preferred_element_type=F32) + lax.dot_general(
            b, wg[:, there], NT, preferred_element_type=F32
        )
        up = lax.dot_general(a, wu[:, here], NT, preferred_element_type=F32) + lax.dot_general(
            b, wu[:, there], NT, preferred_element_type=F32
        )
        act = (jax.nn.gelu(gate, approximate=True) * up).astype(BF16)
        give_ref[at, :] = jnp.dot(act, wd[:, there], preferred_element_type=F32).astype(BF16)
        keep_ref[at, :] = jnp.dot(act, wd[:, here], preferred_element_type=F32).astype(BF16)
        return carry

    lax.fori_loop(0, total // step, tile, 0)


def expert(own, pair, w_gate, w_up, w_down):
    replicas = len(own)
    size, half = own[0].shape
    _, width, hidden = w_gate.shape
    total = replicas * size
    vm = pl.BlockSpec(memory_space=pltpu.VMEM)
    hbm = pl.BlockSpec(memory_space=pl.ANY)
    shape = jax.ShapeDtypeStruct((total, half), BF16)
    return pl.pallas_call(
        functools.partial(expert_kernel, replicas),
        out_shape=(shape, shape),
        in_specs=[hbm] * (2 * replicas + 3),
        out_specs=(vm, vm),
        scratch_shapes=[
            pltpu.VMEM((total, half), BF16),
            pltpu.VMEM((total, half), BF16),
            pltpu.VMEM((hidden, width), BF16),
            pltpu.VMEM((hidden, width), BF16),
            pltpu.VMEM((hidden, width), BF16),
            pltpu.SemaphoreType.DMA((3,)),
            pltpu.SemaphoreType.DMA((2, replicas)),
        ],
        compiler_params=pltpu.CompilerParams(vmem_limit_bytes=VMEM_BYTES),
        cost_estimate=pl.CostEstimate(flops=3_400_000_000, bytes_accessed=8_000_000, transcendentals=600_000),
        name="expert",
    )(*own, *pair, jnp.swapaxes(w_gate, 1, 2), jnp.swapaxes(w_up, 1, 2), w_down)


def give_back_kernel(cap, keep_hbm, got_hbm, kron_hbm, *refs):
    replicas = len(refs) - 5
    outs = refs[:replicas]
    rows_v, keep_ref, got_ref, kron_ref, sem = refs[replicas:]
    load(sem, (keep_hbm, keep_ref), (got_hbm, got_ref), (kron_hbm, kron_ref))
    size = outs[0].shape[0]
    for k in range(replicas):
        at = slice(k * size, (k + 1) * size)
        both = keep_ref[at, :].astype(F32) + got_ref[at, :].astype(F32)
        outs[k][...] = both.astype(BF16)
        rows_v[k * EXTRA : (k + 1) * EXTRA, :] = both[size - EXTRA :].astype(BF16)
    moved = jnp.dot(kron_ref[...], rows_v[...], preferred_element_type=F32)
    first = iota((EXTRA, 1), 0) >= cap - (size - EXTRA)
    for k in range(replicas):
        at = slice(k * EXTRA, (k + 1) * EXTRA)
        outs[k][size - EXTRA :, :] = jnp.where(
            first, moved[at], rows_v[at, :].astype(F32)
        ).astype(BF16)


def give_back(keep, got, kron, cap, replicas):
    total, half = keep.shape
    size = total // replicas
    vm = pl.BlockSpec(memory_space=pltpu.VMEM)
    hbm = pl.BlockSpec(memory_space=pl.ANY)
    return pl.pallas_call(
        functools.partial(give_back_kernel, cap),
        out_shape=tuple(jax.ShapeDtypeStruct((size, half), BF16) for _ in range(replicas)),
        in_specs=[hbm] * 3,
        out_specs=(vm,) * replicas,
        scratch_shapes=[
            pltpu.VMEM((replicas * EXTRA, half), BF16),
            pltpu.VMEM((total, half), BF16),
            pltpu.VMEM((total, half), BF16),
            pltpu.VMEM(kron.shape, BF16),
            pltpu.SemaphoreType.DMA((3,)),
        ],
        compiler_params=pltpu.CompilerParams(vmem_limit_bytes=VMEM_BYTES),
        cost_estimate=pl.CostEstimate(flops=30_000_000, bytes_accessed=2_500_000, transcendentals=0),
        name="give_back",
    )(keep, got, kron)


def gates_kernel(cap, replicas, *refs):
    own = refs[:replicas]
    pair = refs[replicas : 2 * replicas]
    (after_hbm, resid_hbm, slots_ref, ids_ref, gain_ref, router_ref) = refs[
        2 * replicas : 2 * replicas + 6
    ]
    (first_ref, second_ref, gate_ref, new_ref, resid_ref, own_v, pair_v, sem) = refs[2 * replicas + 6 :]
    me = lax.axis_index("req")
    core = lax.axis_index("tp") & 1
    rows, width = resid_ref.shape
    half = width // 2
    size = own[0].shape[0]
    low = pl.ds(size - EXTRA, EXTRA)
    skip = 0
    load(
        sem,
        (resid_hbm, resid_ref),
        *[(own[k].at[low], own_v.at[k]) for k in range(replicas)],
        *[(pair[k].at[low], pair_v.at[k]) for k in range(replicas)],
    )
    ns = slots_ref[...]
    count = ns.shape[0]
    at_sub = iota((count, rows), 0)
    moved = ns != at_sub * rows + iota((count, rows), 1)
    before = (iota((rows, rows), 0) < iota((rows, rows), 1)).astype(BF16)
    movedf = moved.astype(F32)
    rank = jnp.dot(movedf.astype(BF16), before, preferred_element_type=F32)
    coming = moved & (ns // rows == me)
    slot_to = jnp.sum(jnp.where(coming, ns - me * rows + 1, 0), axis=0, keepdims=True) - 1
    rank_in = jnp.sum(jnp.where(coming, rank, 0.0), axis=0, keepdims=True).astype(jnp.int32)
    landing = (iota((rows, rows), 0) == slot_to).astype(F32).astype(BF16)
    at16 = iota((EXTRA, rows), 0)

    def taken(offset):
        hot = (at16 == rank_in + (skip + offset)) & (slot_to >= 0)
        return lax.dot_general(landing, hot.astype(F32).astype(BF16), NT, preferred_element_type=F32)

    take_resid = taken(MIG)
    take_ids = taken(2 * MIG)
    vacated = jnp.sum(take_resid, axis=1, keepdims=True) > 0.5
    in_own = own_v[0].astype(F32)
    in_pair = pair_v[0].astype(F32)
    for k in range(1, replicas):
        in_own = in_own + own_v[k].astype(F32)
        in_pair = in_pair + pair_v[k].astype(F32)
    in_own, in_pair = in_own.astype(BF16), in_pair.astype(BF16)
    first_core = core == 0
    in_low = jnp.where(first_core, in_own, in_pair)
    in_high = jnp.where(first_core, in_pair, in_own)
    picked = take_resid.astype(BF16)
    resid = resid_ref[...]
    new_low = jnp.where(
        vacated, jnp.dot(picked, in_low, preferred_element_type=F32), resid[:, :half].astype(F32)
    ).astype(BF16)
    new_high = jnp.where(
        vacated, jnp.dot(picked, in_high, preferred_element_type=F32), resid[:, half:].astype(F32)
    ).astype(BF16)
    new_ref[...] = jnp.where(first_core, new_low, new_high)
    normed = norm(jnp.concatenate([new_low, new_high], axis=1), gain_ref[...])
    logits = lax.dot_general(normed, router_ref[...], NT, preferred_element_type=F32)
    experts = logits.shape[1]
    ids_in = jnp.dot(take_ids.astype(BF16), in_low[:, :LANES], preferred_element_type=F32)
    eye = onehot(iota((rows, rows), 0) == iota((rows, rows), 1))
    mine = at_sub == me
    moved_me = jnp.sum(jnp.where(mine, movedf, 0.0), axis=0, keepdims=True)
    facts = jnp.concatenate(
        [ids_ref[...].astype(F32), moved_me, jnp.zeros((5, rows), F32)], axis=0
    ).astype(BF16)
    ids = lax.dot_general(eye, facts, NT, preferred_element_type=F32)
    moved_col = ids[:, 2:3]
    id1 = jnp.where(vacated, ids_in[:, 0:1], ids[:, 0:1]).astype(jnp.int32)
    id2 = jnp.where(vacated, ids_in[:, 1:2], ids[:, 1:2]).astype(jnp.int32)
    at_e = iota((rows, experts), 1)
    hit1, hit2 = id1 == at_e, id2 == at_e
    picked1 = jnp.sum(jnp.where(hit1, logits, 0.0), axis=1, keepdims=True)
    picked2 = jnp.sum(jnp.where(hit2, logits, 0.0), axis=1, keepdims=True)
    gate = jax.nn.sigmoid(picked1 - picked2)
    gate_ref[...] = jnp.broadcast_to(gate, gate_ref.shape)
    old1 = ids[:, 0:1].astype(jnp.int32) == at_e
    old2 = ids[:, 1:2].astype(jnp.int32) == at_e
    normal = ((old1 | old2) & (moved_col < 0.5)).astype(F32).astype(BF16)
    after = (iota((rows, rows), 0) > iota((rows, rows), 1)).astype(BF16)
    slot = jnp.dot(after, normal, preferred_element_type=F32)
    slot1 = jnp.sum(jnp.where(hit1, slot, 0.0), axis=1, keepdims=True)
    slot2 = jnp.sum(jnp.where(hit2, slot, 0.0), axis=1, keepdims=True)
    in_rank = jnp.sum(
        jnp.where(take_resid > 0.5, iota((rows, EXTRA), 1), 0), axis=1, keepdims=True
    ) - (skip + MIG)
    slot1 = jnp.where(vacated, cap + in_rank, slot1.astype(jnp.int32))
    slot2 = jnp.where(vacated, cap + in_rank, slot2.astype(jnp.int32))
    lane = iota((rows, replicas * size), 1)
    first_ref[...] = (lane == (id1 ^ me) * size + slot1).astype(F32).astype(BF16)
    second_ref[...] = (lane == (id2 ^ me) * size + slot2).astype(F32).astype(BF16)


def make_gates(own, pair, after, resid, slots, ids, gain, router, cap):
    replicas = len(own)
    size, half = own[0].shape
    rows, width = resid.shape
    vm = pl.BlockSpec(memory_space=pltpu.VMEM)
    hbm = pl.BlockSpec(memory_space=pl.ANY)
    hot = jax.ShapeDtypeStruct((rows, replicas * size), BF16)
    return pl.pallas_call(
        functools.partial(gates_kernel, cap, replicas),
        out_shape=(
            hot,
            hot,
            jax.ShapeDtypeStruct((rows, LANES), F32),
            jax.ShapeDtypeStruct((rows, half), BF16),
        ),
        in_specs=[hbm] * (2 * replicas + 2) + [vm] * 4,
        out_specs=(vm,) * 4,
        scratch_shapes=[
            pltpu.VMEM((rows, width), BF16),
            pltpu.VMEM((replicas, EXTRA, half), BF16),
            pltpu.VMEM((replicas, EXTRA, half), BF16),
            pltpu.SemaphoreType.DMA((2 * replicas + 1,)),
        ],
        compiler_params=pltpu.CompilerParams(vmem_limit_bytes=VMEM_BYTES),
        cost_estimate=pl.CostEstimate(flops=200_000_000, bytes_accessed=6_000_000, transcendentals=0),
        name="gates",
    )(*own, *pair, after, resid, slots, ids.T, gain[None, :], router.T)


def combine_kernel(replicas, *refs):
    blocks = refs[:replicas]
    first_hbm, second_hbm, gate_hbm, out_ref, all_v, first_ref, second_ref, gate_ref, sem = refs[
        replicas:
    ]
    size = blocks[0].shape[0]
    load(
        sem,
        (first_hbm, first_ref),
        (second_hbm, second_ref),
        (gate_hbm, gate_ref),
        *[(blocks[k], all_v.at[pl.ds(k * size, size)]) for k in range(replicas)],
    )
    gate = gate_ref[:, 0:1]
    one = jnp.dot(first_ref[...], all_v[...], preferred_element_type=F32)
    two = jnp.dot(second_ref[...], all_v[...], preferred_element_type=F32)
    out_ref[...] = (gate * one + (1.0 - gate) * two).astype(BF16)


def combine(blocks, first, second, gate):
    replicas = len(blocks)
    size, half = blocks[0].shape
    rows = first.shape[0]
    vm = pl.BlockSpec(memory_space=pltpu.VMEM)
    hbm = pl.BlockSpec(memory_space=pl.ANY)
    return pl.pallas_call(
        functools.partial(combine_kernel, replicas),
        out_shape=jax.ShapeDtypeStruct((rows, half), BF16),
        in_specs=[hbm] * (replicas + 3),
        out_specs=vm,
        scratch_shapes=[
            pltpu.VMEM((replicas * size, half), BF16),
            pltpu.VMEM(first.shape, BF16),
            pltpu.VMEM(second.shape, BF16),
            pltpu.VMEM(gate.shape, F32),
            pltpu.SemaphoreType.DMA((replicas + 3,)),
        ],
        compiler_params=pltpu.CompilerParams(vmem_limit_bytes=VMEM_BYTES),
        cost_estimate=pl.CostEstimate(flops=400_000_000, bytes_accessed=2_500_000, transcendentals=0),
        name="combine",
    )(*blocks, first, second, gate)


def choose_kernel(plan_hbm, *refs):
    choices = refs[:-5]
    out_ref, plan_sm, sem, plan_sem = refs[-4:]
    load(plan_sem, (plan_hbm, plan_sm))
    index = plan_sm[0, 1]
    for i, choice in enumerate(choices):
        @pl.when(index == i)
        def _():
            load(sem, (choice, out_ref))


def choose(plan, held, after):
    hbm = pl.BlockSpec(memory_space=pl.ANY)
    return pl.pallas_call(
        choose_kernel,
        out_shape=jax.ShapeDtypeStruct(held[0].shape, BF16),
        in_specs=[hbm] * (2 + len(held)),
        out_specs=pl.BlockSpec(memory_space=pltpu.VMEM),
        scratch_shapes=[
            pltpu.SMEM(plan.shape, jnp.int32),
            pltpu.SemaphoreType.DMA((1,)),
            pltpu.SemaphoreType.DMA((1,)),
        ],
        compiler_params=pltpu.CompilerParams(vmem_limit_bytes=VMEM_BYTES),
        cost_estimate=pl.CostEstimate(flops=0, bytes_accessed=0, transcendentals=0),
        name="choose",
    )(plan, *held, after)


def patch_kernel(count, plan_hbm, *refs):
    choices = refs[:count]
    after_hbm, tail_hbm, out_hbm, plan_sm, slabs, sem, slab_sem, out_sem = refs[count:]
    load(sem, (plan_hbm, plan_sm))
    index = plan_sm[0, 0]
    for i, choice in enumerate(choices):
        @pl.when(index == i)
        def _():
            load(slab_sem, (choice, slabs))

    def moves(m):
        to = plan_sm[0, 16 + m]
        return to, [
            pltpu.make_async_copy(
                slabs.at[2 * m + side], out_hbm.at[side, to], out_sem.at[2 * m + side]
            )
            for side in range(2)
        ]

    for m in range(MIG):
        to, copies = moves(m)

        @pl.when(to >= 0)
        def _():
            for copy in copies:
                copy.start()
    for m in range(MIG):
        to, copies = moves(m)

        @pl.when(to >= 0)
        def _():
            for copy in copies:
                copy.wait()


def patch(plan, held, after, tail_new):
    hbm = pl.BlockSpec(memory_space=pl.ANY)
    count = len(held)
    return pl.pallas_call(
        functools.partial(patch_kernel, count),
        out_shape=jax.ShapeDtypeStruct(tail_new.shape, BF16),
        in_specs=[hbm] * (3 + count),
        out_specs=hbm,
        scratch_shapes=[
            pltpu.SMEM(plan.shape, jnp.int32),
            pltpu.VMEM(held[0].shape, BF16),
            pltpu.SemaphoreType.DMA((1,)),
            pltpu.SemaphoreType.DMA((1,)),
            pltpu.SemaphoreType.DMA((2 * MIG,)),
        ],
        input_output_aliases={2 + count: 0},
        compiler_params=pltpu.CompilerParams(vmem_limit_bytes=VMEM_BYTES),
        cost_estimate=pl.CostEstimate(flops=0, bytes_accessed=0, transcendentals=0),
        name="patch",
    )(plan, *held, after, tail_new)


def body(
    hidden_in, prompt_kv, tail_kv, group_of, prompt_len, tail_len, bucket_of, bias_table,
    attn_gain, w_query, w_key, w_value, w_out, ffn_gain, router_weight, expert_ids,
    w_gate, w_up, w_down, new_slot,
):
    rows, width = hidden_in.shape
    replicas = lax.axis_size("req")
    pieces = lax.axis_size("tp")
    experts = router_weight.shape[1]
    cap = -(-(5 * rows * TOP // (4 * experts)) // 16) * 16
    half = width // 2

    def across(axis, size, k):
        return lambda v: lax.ppermute(v, axis, [(i, i ^ k) for i in range(size)])

    def over_req(k):
        return across("req", replicas, k)

    def over_tp(k):
        return across("tp", pieces, k)

    wouts = [w_out] + [over_tp(k)(w_out) for k in range(1, pieces)]
    head_out, tail_new, packet = attention(
        hidden_in, prompt_kv, tail_kv, group_of, prompt_len, tail_len, bucket_of, bias_table,
        attn_gain, w_query, w_key, w_value, new_slot,
    )
    heads = [head_out] + [over_tp(k)(head_out) for k in range(1, pieces)]
    slots = new_slot.reshape(replicas, rows)
    place, extra, wide, kron, plan = make_plan(
        slots, expert_ids, experts, cap, [head_out] + wouts[1:]
    )
    bits = replicas.bit_length() - 1
    held = [packet, over_req(1 << (bits - 1))(packet)]
    resid, *blocks = dispatch(
        heads, wouts, hidden_in, ffn_gain, place, extra, wide, held[1], replicas
    )
    own = [blocks[0]] + [over_req(k)(blocks[k]) for k in range(1, replicas)]
    pair = [over_tp(1)(b) for b in own]
    keep, give = expert(own, pair, w_gate, w_up, w_down)
    back = give_back(keep, over_tp(1)(give), kron, cap, replicas)
    for i in range(1, bits - 1):
        held = held + [over_req(1 << (bits - 1 - i))(p) for p in held]
    last = choose(plan, held, back[0])
    held.append(over_req(1)(last))
    first, second, gate, resid_new = make_gates(
        own, pair, last, resid, slots, expert_ids, ffn_gain, router_weight, cap
    )
    result = [back[0]] + [over_req(k)(back[k]) for k in range(1, replicas)]
    mixed = combine(result, first, second, gate)
    new_tail_kv = patch(plan, held, mixed, tail_new)
    k = 2
    while k < pieces:
        other = over_tp(k)(mixed)
        mixed = mixed.astype(F32) + other.astype(F32)
        k *= 2
        if k < pieces:
            mixed = mixed.astype(BF16)
    out_half = (resid_new.astype(F32) + mixed.astype(F32)).astype(BF16)
    out_other = over_tp(1)(out_half)
    core = lax.axis_index("tp") & 1
    out_hidden = jnp.where(
        core == 0,
        jnp.concatenate([out_half, out_other], axis=1),
        jnp.concatenate([out_other, out_half], axis=1),
    )
    return (out_hidden, new_tail_kv)


def solution(mesh):
    return jax.shard_map(
        body,
        mesh=mesh,
        in_specs=(
            P("req", None), P(None, "req", None, "tp"), P(None, "req", None, "tp"),
            P("req"), P("req"), P("req"), P(), P(None, "tp"), P(),
            P(None, "tp"), P(None, "tp"), P(None, "tp"), P("tp", None), P(), P(),
            P("req", None), P("req", None, "tp"), P("req", None, "tp"), P("req", "tp", None), P(),
        ),
        out_specs=(P("req", None), P(None, "req", None, "tp")),
        check_vma=False,
    )
```

time: 186 us -> 134 us (0.72)
  the two profiles are of different devices: /device:TPU:0 before, /device:TPU:11 now
where the time goes in v1:
time: 134 us
  Pallas kernels  52.2 us (39%)
  starting transfers between devices  44.5 us (33%)
  waiting for transfers between devices  28.1 us (21%)
  local copies, waits for them, and re-layouts  6.19 us (5%)
  other arithmetic  2.07 us (2%)
    ppermute x35, starting transfers between devices, across(): return lambda v: lax.ppermute(v, axis, [(i, i ^ k) for i in range(size)])  44.5 us
    ppermute x35, waiting for transfers between devices, across(): return lambda v: lax.ppermute(v, axis, [(i, i ^ k) for i in range(size)])  28.1 us
    pallas_call x1, Pallas kernels, attention(): pl.pallas_call(attention_kernel, out_shape=(jax.ShapeDtypeStruct((rows, c...  22.7 us
    pallas_call x1, Pallas kernels, expert(): pl.pallas_call(functools.partial(expert_kernel, replicas), out_shape=(sha...  8.31 us
    pallas_call x1, Pallas kernels, dispatch(): pl.pallas_call(functools.partial(dispatch_kernel, pieces, replicas), out_...  4.95 us
    pallas_call x1, Pallas kernels, make_gates(): pl.pallas_call(functools.partial(gates_kernel, cap, replicas), out_shape=...  4.41 us
    unnamed x74, local copies, waits for them, and re-layouts  4.32 us
    pallas_call x1, Pallas kernels, combine(): pl.pallas_call(functools.partial(combine_kernel, replicas), out_shape=jax...  2.75 us
  transfers between devices with their start and end apart: 35, of which 17 were waited for; matrix products, arithmetic and copies ran while one was open for 2% of the time, Pallas kernels for 27%

profile of v1, /device:TPU:11, one launch (start us, length us, event | category | flops | bytes accessed | tf_op | source)
XLA Modules:
  0.0 133.9 jit_solution(8597025761104706048)
XLA Ops:
  0.6 0.7 collective-permute-start.3
  1.4 0.3 collective-permute-start.4
  1.6 1.4 %collective-permute-start.5 = (bf16[256,1024]{1,0:T(8,128)(2,1)}, bf16[256,1024]{1,0:T(8,128)(2,1)S(1)}, u32[]{:S(2)}, u32[]{:S(2)}) collective-permute-start(bf16[256,1024]{1,0:T(8,128)(2,1)} %refs_4_.1), channel_id=1, source_target_pairs={{0,3},{1,2},{2,1},{3,0},{4,7},{5,6},{6,5},{7,4},{8,11},{9,10},{10,... | collective-permute-start | bytes 1572872 | tf_op jit(solution)/shard_map/ppermute | solution.py:999
  3.1 1.3 broadcast_in_dim.14.bucket_hbm
  4.4 22.7 %attention.1 = (bf16[256,256]{1,0:T(8,128)(2,1)}, bf16[2,256,64,256]{3,2,1,0:T(8,128)(2,1)}, bf16[8,64,256]{2,1,0:T(8,128)(2,1)}) custom-call(s32[256]{0:T(256)} %group_hbm.1, s32[8]{0:T(128)} %plen_hbm.1, s32[256]{0:T(256)} %tlen_hbm.1, s32[1,256]{1,0:T(1,128)} %bitcast.17, s32[1,577]{1,0:T(1,128)} %broadcast_in_dim.14.bucket_hbm, f32[4,32]{1,0:T(4,128)} %bitcast.16, ...), custom_call_target="tpu_custom_call" | custom-call | flops 8000000000 | bytes 45000000 | tf_op jit(solution)/shard_map/attention/pallas_call | solution.py:345
  27.1 2.4 %collective-permute-start.6 = (bf16[8,64,256]{2,1,0:T(8,128)(2,1)}, bf16[8,64,256]{2,1,0:T(8,128)(2,1)S(1)}, u32[]{:S(2)}, u32[]{:S(2)}) collective-permute-start(bf16[8,64,256]{2,1,0:T(8,128)(2,1)} %get-tuple-element.37.refs_0_), channel_id=1, source_target_pairs={{0,16},{4,20},{8,24},{12,28},{16,0},{20,4},{24,8},{28,12},{1,17},{... | collective-permute-start | bytes 786440 | tf_op jit(solution)/shard_map/ppermute | solution.py:999
  29.4 0.4 collective-permute-start
  29.9 0.2 collective-permute-start.1
  30.1 1.5 %collective-permute-start.2 = (bf16[256,256]{1,0:T(8,128)(2,1)}, bf16[256,256]{1,0:T(8,128)(2,1)S(1)}, u32[]{:S(2)}, u32[]{:S(2)}) collective-permute-start(bf16[256,256]{1,0:T(8,128)(2,1)} %get-tuple-element.33.refs_0_), channel_id=1, source_target_pairs={{0,3},{1,2},{2,1},{3,0},{4,7},{5,6},{6,5},{7,4},{8,11},{9,10},{10,... | collective-permute-start | bytes 393224 | tf_op jit(solution)/shard_map/ppermute | solution.py:999
  31.6 0.6 reshape.7.slots_ref.refs_18_
  32.2 0.8 copy-done.9
  33.0 1.8 %plan.1 = (bf16[768,256]{1,0:T(8,128)(2,1)}, bf16[128,512]{1,0:T(8,128)(2,1)}, bf16[256,128]{1,0:T(8,128)(2,1)}, bf16[128,128]{1,0:T(8,128)(2,1)}, s32[8,128]{1,0:T(8,128)}) custom-call(s32[8,256]{1,0:T(8,128)} %reshape.7.slots_ref.refs_18_, s32[2,256]{1,0:T(2,128)} %bitcast.9, bf16[256,256]{1,0:T(8,128)(2,1)} %get-tuple-element.33.refs_0_, ...), custom_call_target="tpu_custom_call" | custom-call | tf_op jit(solution)/shard_map/plan/pallas_call | solution.py:497
  34.8 0.3 collective-permute-done.1.refs_2_
  35.2 3.0 %collective-permute-done.2.refs_3_ = bf16[256,256]{1,0:T(8,128)(2,1)S(1)} collective-permute-done((bf16[256,256]{1,0:T(8,128)(2,1)}, bf16[256,256]{1,0:T(8,128)(2,1)S(1)}, u32[]{:S(2)}, u32[]{:S(2)}) %collective-permute-start.2) | collective-permute-done | bytes 131104 | tf_op jit(solution)/shard_map/ppermute | solution.py:999
  38.1 2.6 %collective-permute-done.6.refs_13_.refs_1_ = bf16[8,64,256]{2,1,0:T(8,128)(2,1)S(1)} collective-permute-done((bf16[8,64,256]{2,1,0:T(8,128)(2,1)}, bf16[8,64,256]{2,1,0:T(8,128)(2,1)S(1)}, u32[]{:S(2)}, u32[]{:S(2)}) %collective-permute-start.6) | collective-permute-done | bytes 262176 | tf_op jit(solution)/shard_map/ppermute | solution.py:999
  40.8 0.7 copy-done.1
  41.5 4.9 %dispatch.1 = (bf16[256,1024]{1,0:T(8,128)(2,1)}, bf16[96,512]{1,0:T(8,128)(2,1)}, bf16[96,512]{1,0:T(8,128)(2,1)}, bf16[96,512]{1,0:T(8,128)(2,1)}, bf16[96,512...) custom-call(bf16[256,256]{1,0:T(8,128)(2,1)} %get-tuple-element.33.r, ...), custom_call_target="tpu_custom_call" | custom-call | flops 1200000000 | bytes 6000000 | tf_op jit(solution)/shard_map/dispatch/pallas_call | solution.py:591
  46.4 1.8 %collective-permute-start.7 = (bf16[96,512]{1,0:T(8,128)(2,1)}, bf16[96,512]{1,0:T(8,128)(2,1)S(1)}, u32[]{:S(2)}, u32[]{:S(2)}) collective-permute-start(bf16[96,512]{1,0:T(8,128)(2,1)} %get-tuple-element.39), channel_id=1, source_target_pairs={{0,4},{4,0},{8,12},{12,8},{16,20},{20,16},{24,28},{28,24},{1,5},{5... | collective-permute-start | bytes 294920 | tf_op jit(solution)/shard_map/ppermute | solution.py:999
  48.3 0.5 collective-permute-start.8
  48.7 0.8 collective-permute-start.9
  49.5 3.0 %collective-permute-start.10 = (bf16[96,512]{1,0:T(8,128)(2,1)}, bf16[96,512]{1,0:T(8,128)(2,1)S(1)}, u32[]{:S(2)}, u32[]{:S(2)}) collective-permute-start(bf16[96,512]{1,0:T(8,128)(2,1)} %get-tuple-element.42), channel_id=1, source_target_pairs={{0,16},{4,20},{8,24},{12,28},{16,0},{20,4},{24,8},{28,12},{1,17},{... | collective-permute-start | bytes 294920 | tf_op jit(solution)/shard_map/ppermute | solution.py:999
  52.5 1.1 collective-permute-start.11
  53.6 1.2 collective-permute-start.12
  54.8 0.4 collective-permute-start.13
  55.2 2.1 %collective-permute-start.14 = (bf16[96,512]{1,0:T(8,128)(2,1)}, bf16[96,512]{1,0:T(8,128)(2,1)S(1)}, u32[]{:S(2)}, u32[]{:S(2)}) collective-permute-start(bf16[96,512]{1,0:T(8,128)(2,1)} %get-tuple-element.38.refs_0_), channel_id=1, source_target_pairs={{0,1},{1,0},{2,3},{3,2},{4,5},{5,4},{6,7},{7,6},{8,9},{9,8},{10,11... | collective-permute-start | bytes 294920 | tf_op jit(solution)/shard_map/ppermute | solution.py:999
  57.3 0.9 collective-permute-done.10.refs_4_
  58.2 6.9 %collective-permute-start.15 = (bf16[96,512]{1,0:T(8,128)(2,1)S(1)}, bf16[96,512]{1,0:T(8,128)(2,1)S(1)}, u32[]{:S(2)}, u32[]{:S(2)}) collective-permute-start(bf16[96,512]{1,0:T(8,128)(2,1)S(1)} %collective-permute-done.7.refs_1_), channel_id=1, source_target_pairs={{0,1},{1,0},{2,3},{3,2},{4,5},{5,4},{6,7},{7,6},{8,9},{9,8},{10,11... | collective-permute-start | bytes 294920 | tf_op jit(solution)/shard_map/ppermute | solution.py:999
  65.2 2.0 %collective-permute-start.16 = (bf16[96,512]{1,0:T(8,128)(2,1)S(1)}, bf16[96,512]{1,0:T(8,128)(2,1)S(1)}, u32[]{:S(2)}, u32[]{:S(2)}) collective-permute-start(bf16[96,512]{1,0:T(8,128)(2,1)S(1)} %collective-permute-done.8.refs_2_), channel_id=1, source_target_pairs={{0,1},{1,0},{2,3},{3,2},{4,5},{5,4},{6,7},{7,6},{8,9},{9,8},{10,11... | collective-permute-start | bytes 294920 | tf_op jit(solution)/shard_map/ppermute | solution.py:999
  67.2 0.7 collective-permute-done.12.refs_6_
  67.9 2.2 %collective-permute-start.17 = (bf16[96,512]{1,0:T(8,128)(2,1)S(1)}, bf16[96,512]{1,0:T(8,128)(2,1)S(1)}, u32[]{:S(2)}, u32[]{:S(2)}) collective-permute-start(bf16[96,512]{1,0:T(8,128)(2,1)S(1)} %collective-permute-done.9.refs_3_), channel_id=1, source_target_pairs={{0,1},{1,0},{2,3},{3,2},{4,5},{5,4},{6,7},{7,6},{8,9},{9,8},{10,11... | collective-permute-start | bytes 294920 | tf_op jit(solution)/shard_map/ppermute | solution.py:999
  70.1 0.9 collective-permute-done.13.refs_7_
  71.0 1.2 collective-permute-start.18
  72.3 0.4 collective-permute-start.20
  72.8 0.3 collective-permute-done.18.refs_12_
  73.2 0.4 collective-permute-done.19.refs_13_
  73.7 0.4 collective-permute-done.21.refs_15_
  74.2 0.2 copy-done.24
  74.3 0.3 copy-done.25
  74.7 8.3 %expert.1 = (bf16[768,512]{1,0:T(8,128)(2,1)}, bf16[768,512]{1,0:T(8,128)(2,1)}) custom-call(bf16[96,512]{1,0:T(8,128)(2,1)} %get-tuple-element.38.refs_0_, bf16[96,512]{1,0:T(8,128)(2,1)} %copy-done.11, bf16[96,512]{1,0:T(8,128)(2,1)} %copy-done.12, bf16[96,512]{1,0:T(8,128)(2,1)} %copy-done.13, bf16[96,512]{1,0:T(8,128)(2,1)} %copy-done.14, ...), custom_call_target="tpu_custom_call" | custom-call | flops 3400000000 | bytes 8000000 | tf_op jit(solution)/shard_map/expert/pallas_call | solution.py:670
  83.0 0.2 collective-permute-start.24
  83.3 1.5 %collective-permute-start.23 = (bf16[8,64,256]{2,1,0:T(8,128)(2,1)S(1)}, bf16[8,64,256]{2,1,0:T(8,128)(2,1)S(1)}, u32[]{:S(2)}, u32[]{:S(2)}) collective-permute-start(bf16[8,64,256]{2,1,0:T(8,128)(2,1)S(1)} %copy-done.2), channel_id=1, source_target_pairs={{0,8},{4,12},{8,0},{12,4},{16,24},{20,28},{24,16},{28,20},{1,9},{5... | collective-permute-start | bytes 786440 | tf_op jit(solution)/shard_map/ppermute | solution.py:999
  84.7 0.8 collective-permute-done.24.got_hbm
  85.6 0.9 copy-done.6
  86.5 2.4 %give_back.1 = (bf16[96,512]{1,0:T(8,128)(2,1)}, bf16[96,512]{1,0:T(8,128)(2,1)}, bf16[96,512]{1,0:T(8,128)(2,1)}, bf16[96,512]{1,0:T(8,128)(2,1)}, bf16[96,512]...) custom-call(bf16[768,512]{1,0:T(8,128)(2,1)} %get-tuple-element.47.keep_hbm, ...), custom_call_target="tpu_custom_call" | custom-call | flops 30000000 | bytes 2500000 | tf_op jit(solution)/shard_map/give_back/pallas_call | solution.py:715
  88.9 0.4 collective-permute-start.25
  89.3 2.3 %collective-permute-start.27 = (bf16[96,512]{1,0:T(8,128)(2,1)}, bf16[96,512]{1,0:T(8,128)(2,1)S(1)}, u32[]{:S(2)}, u32[]{:S(2)}) collective-permute-start(bf16[96,512]{1,0:T(8,128)(2,1)} %get-tuple-element.55), channel_id=1, source_target_pairs={{0,12},{4,8},{8,4},{12,0},{16,28},{20,24},{24,20},{28,16},{1,13},{... | collective-permute-start | bytes 294920 | tf_op jit(solution)/shard_map/ppermute | solution.py:999
  91.6 1.1 collective-permute-start.28
  92.7 3.8 %collective-permute-done.23.refs_3_ = bf16[8,64,256]{2,1,0:T(8,128)(2,1)S(1)} collective-permute-done((bf16[8,64,256]{2,1,0:T(8,128)(2,1)S(1)}, bf16[8,64,256]{2,1,0:T(8,128)(2,1)S(1)}, u32[]{:S(2)}, u32[]{:S(2)}) %collective-permute-start.23) | collective-permute-done | bytes 262176 | tf_op jit(solution)/shard_map/ppermute | solution.py:999
  96.5 3.5 %collective-permute-start.29 = (bf16[96,512]{1,0:T(8,128)(2,1)}, bf16[96,512]{1,0:T(8,128)(2,1)S(1)}, u32[]{:S(2)}, u32[]{:S(2)}) collective-permute-start(bf16[96,512]{1,0:T(8,128)(2,1)} %get-tuple-element.57), channel_id=1, source_target_pairs={{0,20},{4,16},{8,28},{12,24},{16,4},{20,0},{24,12},{28,8},{1,21},{... | collective-permute-start | bytes 294920 | tf_op jit(solution)/shard_map/ppermute | solution.py:999
  100.1 2.3 %collective-permute-start.31 = (bf16[96,512]{1,0:T(8,128)(2,1)}, bf16[96,512]{1,0:T(8,128)(2,1)S(1)}, u32[]{:S(2)}, u32[]{:S(2)}) collective-permute-start(bf16[96,512]{1,0:T(8,128)(2,1)} %get-tuple-element.59), channel_id=1, source_target_pairs={{0,28},{4,24},{8,20},{12,16},{16,12},{20,8},{24,4},{28,0},{1,29},{... | collective-permute-start | bytes 294920 | tf_op jit(solution)/shard_map/ppermute | solution.py:999
  102.4 2.4 %choose.1.refs_16_ = bf16[8,64,256]{2,1,0:T(8,128)(2,1)} custom-call(s32[8,128]{1,0:T(8,128)} %get-tuple-element.46.plan_hbm, bf16[8,64,256]{2,1,0:T(8,128)(2,1)} %get-tuple-element.37.refs_0_, bf16[8,64,256]{2,1,0:T(8,128)(2,1)} %copy-done.1, bf16[8,64,256]{2,1,0:T(8,128)(2,1)} %copy-done.3, bf16[8,64,256]{2,1,0:T(8,128)(2,1)} %copy-done.4, ...), custom_call_target="tpu_custom_call" | custom-call | tf_op jit(solution)/shard_map/choose/pallas_call | solution.py:913
  104.8 4.4 %gates.1 = (bf16[256,768]{1,0:T(8,128)(2,1)}, bf16[256,768]{1,0:T(8,128)(2,1)}, f32[256,128]{1,0:T(8,128)}, bf16[256,512]{1,0:T(8,128)(2,1)}) custom-call(bf16[96,512]{1,0:T(8,128)(2,1)} %get-tuple-element.38.refs_0_, bf16[96,512]{1,0:T(8,128)(2,1)} %copy-done.11, bf16[96,512]{1,0:T(8,128)(2,1)} %copy-done.12, bf16[96,512]{1,0:T(8,128)(2,1)} %copy-done.13, ...), custom_call_target="tpu_custom_call" | custom-call | flops 200000000 | bytes 6000000 | tf_op jit(solution)/shard_map/gates/pallas_call | solution.py:835
  109.3 1.2 collective-permute-done.29.refs_5_
  110.5 2.3 %collective-permute-done.30.refs_6_ = bf16[96,512]{1,0:T(8,128)(2,1)S(1)} collective-permute-done((bf16[96,512]{1,0:T(8,128)(2,1)}, bf16[96,512]{1,0:T(8,128)(2,1)S(1)}, u32[]{:S(2)}, u32[]{:S(2)}) %collective-permute-start.30) | collective-permute-done | bytes 98336 | tf_op jit(solution)/shard_map/ppermute | solution.py:999
  112.8 3.4 %collective-permute-done.31.refs_7_ = bf16[96,512]{1,0:T(8,128)(2,1)S(1)} collective-permute-done((bf16[96,512]{1,0:T(8,128)(2,1)}, bf16[96,512]{1,0:T(8,128)(2,1)S(1)}, u32[]{:S(2)}, u32[]{:S(2)}) %collective-permute-start.31) | collective-permute-done | bytes 98336 | tf_op jit(solution)/shard_map/ppermute | solution.py:999
  116.3 0.6 copy-done.32
  116.9 2.7 %combine.1.refs_5_ = bf16[256,512]{1,0:T(8,128)(2,1)} custom-call(bf16[96,512]{1,0:T(8,128)(2,1)} %get-tuple-element.50.refs_4_.refs_0_, bf16[96,512]{1,0:T(8,128)(2,1)} %copy-done.26, bf16[96,512]{1,0:T(8,128)(2,1)} %copy-done.27, bf16[96,512]{1,0:T(8,128)(2,1)} %copy-done.28, bf16[96,512]{1,0:T(8,128)(2,1)} %copy-done.29, bf16[96,512]{1,0:T(8,128)(2,1)} %copy-done.30, ...), custom_call_target="tpu_custom_call" | custom-call | flops 400000000 | bytes 2500000 | tf_op jit(solution)/shard_map/combine/pallas_call | solution.py:882
  119.6 0.3 collective-permute-start.32
  119.9 6.8 %collective-permute-done.32 = bf16[256,512]{1,0:T(8,128)(2,1)S(1)} collective-permute-done((bf16[256,512]{1,0:T(8,128)(2,1)}, bf16[256,512]{1,0:T(8,128)(2,1)S(1)}, u32[]{:S(2)}, u32[]{:S(2)}) %collective-permute-start.32) | collective-permute-done | bytes 262176 | tf_op jit(solution)/shard_map/ppermute | solution.py:999
  126.7 1.1 add_convert_fusion
  127.8 2.0 %collective-permute-start.33 = (bf16[256,512]{1,0:T(8,128)(2,1)S(1)}, bf16[256,512]{1,0:T(8,128)(2,1)S(1)}, u32[]{:S(2)}, u32[]{:S(2)}) collective-permute-start(bf16[256,512]{1,0:T(8,128)(2,1)S(1)} %add_convert_fusion), channel_id=1, source_target_pairs={{0,1},{1,0},{2,3},{3,2},{4,5},{5,4},{6,7},{7,6},{8,9},{9,8},{10,11... | collective-permute-start | bytes 786440 | tf_op jit(solution)/shard_map/ppermute | solution.py:999
  129.8 0.7 copy-done.10
  130.5 2.5 %patch.1 = bf16[2,256,64,256]{3,2,1,0:T(8,128)(2,1)} custom-call(s32[8,128]{1,0:T(8,128)} %get-tuple-element.46.plan_hbm, bf16[8,64,256]{2,1,0:T(8,128)(2,1)} %get-tuple-element.37.refs_0_, bf16[8,64,256]{2,1,0:T(8,128)(2,1)} %copy-done.1, bf16[8,64,256]{2,1,0:T(8,128)(2,1)} %copy-done.3, ...), custom_call_target="tpu_custom_call", output_to_operand_aliasing={{}: (7, {})} | custom-call | tf_op jit(solution)/shard_map/patch/pallas_call | solution.py:967
  133.0 0.9 maximum_select_fusion
  (93 shorter events, 0.7 us)
Async XLA Ops:
  0.6 29.3 %collective-permute-start.3 = (bf16[256,1024]{1,0:T(8,128)(2,1)}, bf16[256,1024]{1,0:T(8,128)(2,1)S(1)}, u32[]{:S(2)}, u32[]{:S(2)}) collective-permute-start(bf16[256,1024]{1,0:T(8,128)(2,1)} %refs_4_.1), channel_id=1, source_target_pairs={{0,1},{1,0},{2,3},{3,2},{4,5},{5,4},{6,7},{7,6},{8,9},{9,8},{10,11... | collective-permute-start | bytes 1572872 | tf_op jit(solution)/shard_map/ppermute | solution.py:999
  1.4 28.8 %collective-permute-start.4 = (bf16[256,1024]{1,0:T(8,128)(2,1)}, bf16[256,1024]{1,0:T(8,128)(2,1)S(1)}, u32[]{:S(2)}, u32[]{:S(2)}) collective-permute-start(bf16[256,1024]{1,0:T(8,128)(2,1)} %refs_4_.1), channel_id=1, source_target_pairs={{0,2},{1,3},{2,0},{3,1},{4,6},{5,7},{6,4},{7,5},{8,10},{9,11},{10,... | collective-permute-start | bytes 1572872 | tf_op jit(solution)/shard_map/ppermute | solution.py:999
  1.6 30.6 %collective-permute-start.5 = (bf16[256,1024]{1,0:T(8,128)(2,1)}, bf16[256,1024]{1,0:T(8,128)(2,1)S(1)}, u32[]{:S(2)}, u32[]{:S(2)}) collective-permute-start(bf16[256,1024]{1,0:T(8,128)(2,1)} %refs_4_.1), channel_id=1, source_target_pairs={{0,3},{1,2},{2,1},{3,0},{4,7},{5,6},{6,5},{7,4},{8,11},{9,10},{10,... | collective-permute-start | bytes 1572872 | tf_op jit(solution)/shard_map/ppermute | solution.py:999
  4.3 27.2 %copy-start.33 = (s32[2048]{0:T(1024)S(1)}, s32[2048]{0:T(1024)}, u32[]{:S(2)}) copy-start(s32[2048]{0:T(1024)} %slots_hbm.1) | copy-start | bytes 24580
  27.1 13.7 %collective-permute-start.6 = (bf16[8,64,256]{2,1,0:T(8,128)(2,1)}, bf16[8,64,256]{2,1,0:T(8,128)(2,1)S(1)}, u32[]{:S(2)}, u32[]{:S(2)}) collective-permute-start(bf16[8,64,256]{2,1,0:T(8,128)(2,1)} %get-tuple-element.37.refs_0_), channel_id=1, source_target_pairs={{0,16},{4,20},{8,24},{12,28},{16,0},{20,4},{24,8},{28,12},{1,17},{... | collective-permute-start | bytes 786440 | tf_op jit(solution)/shard_map/ppermute | solution.py:999
  29.4 5.4 %collective-permute-start = (bf16[256,256]{1,0:T(8,128)(2,1)}, bf16[256,256]{1,0:T(8,128)(2,1)S(1)}, u32[]{:S(2)}, u32[]{:S(2)}) collective-permute-start(bf16[256,256]{1,0:T(8,128)(2,1)} %get-tuple-element.33.refs_0_), channel_id=1, source_target_pairs={{0,1},{1,0},{2,3},{3,2},{4,5},{5,4},{6,7},{7,6},{8,9},{9,8},{10,11... | collective-permute-start | bytes 393224 | tf_op jit(solution)/shard_map/ppermute | solution.py:999
  29.9 2.3 %copy-start.7 = (bf16[256,1024]{1,0:T(8,128)(2,1)}, bf16[256,1024]{1,0:T(8,128)(2,1)S(1)}, u32[]{:S(2)}) copy-start(bf16[256,1024]{1,0:T(8,128)(2,1)S(1)} %collective-permute-done.3.refs_1_.refs_5_) | copy-start | bytes 1572868
  29.9 5.3 %collective-permute-start.1 = (bf16[256,256]{1,0:T(8,128)(2,1)}, bf16[256,256]{1,0:T(8,128)(2,1)S(1)}, u32[]{:S(2)}, u32[]{:S(2)}) collective-permute-start(bf16[256,256]{1,0:T(8,128)(2,1)} %get-tuple-element.33.refs_0_), channel_id=1, source_target_pairs={{0,2},{1,3},{2,0},{3,1},{4,6},{5,7},{6,4},{7,5},{8,10},{9,11},{10,... | collective-permute-start | bytes 393224 | tf_op jit(solution)/shard_map/ppermute | solution.py:999
  30.1 2.1 %copy-start.8 = (bf16[256,1024]{1,0:T(8,128)(2,1)}, bf16[256,1024]{1,0:T(8,128)(2,1)S(1)}, u32[]{:S(2)}) copy-start(bf16[256,1024]{1,0:T(8,128)(2,1)S(1)} %collective-permute-done.4.refs_2_.refs_6_) | copy-start | bytes 1572868
  30.1 8.0 %collective-permute-start.2 = (bf16[256,256]{1,0:T(8,128)(2,1)}, bf16[256,256]{1,0:T(8,128)(2,1)S(1)}, u32[]{:S(2)}, u32[]{:S(2)}) collective-permute-start(bf16[256,256]{1,0:T(8,128)(2,1)} %get-tuple-element.33.refs_0_), channel_id=1, source_target_pairs={{0,3},{1,2},{2,1},{3,0},{4,7},{5,6},{6,5},{7,4},{8,11},{9,10},{10,... | collective-permute-start | bytes 393224 | tf_op jit(solution)/shard_map/ppermute | solution.py:999
  34.8 6.0 %copy-start.34 = (bf16[256,256]{1,0:T(8,128)(2,1)}, bf16[256,256]{1,0:T(8,128)(2,1)S(1)}, u32[]{:S(2)}) copy-start(bf16[256,256]{1,0:T(8,128)(2,1)S(1)} %collective-permute-done.refs_1_) | copy-start | bytes 393220
  35.1 5.6 %copy-start.35 = (bf16[256,256]{1,0:T(8,128)(2,1)}, bf16[256,256]{1,0:T(8,128)(2,1)S(1)}, u32[]{:S(2)}) copy-start(bf16[256,256]{1,0:T(8,128)(2,1)S(1)} %collective-permute-done.1.refs_2_) | copy-start | bytes 393220
  38.1 2.7 %copy-start.36 = (bf16[256,256]{1,0:T(8,128)(2,1)}, bf16[256,256]{1,0:T(8,128)(2,1)S(1)}, u32[]{:S(2)}) copy-start(bf16[256,256]{1,0:T(8,128)(2,1)S(1)} %collective-permute-done.2.refs_3_) | copy-start | bytes 393220
  46.4 7.2 %collective-permute-start.7 = (bf16[96,512]{1,0:T(8,128)(2,1)}, bf16[96,512]{1,0:T(8,128)(2,1)S(1)}, u32[]{:S(2)}, u32[]{:S(2)}) collective-permute-start(bf16[96,512]{1,0:T(8,128)(2,1)} %get-tuple-element.39), channel_id=1, source_target_pairs={{0,4},{4,0},{8,12},{12,8},{16,20},{20,16},{24,28},{28,24},{1,5},{5... | collective-permute-start | bytes 294920 | tf_op jit(solution)/shard_map/ppermute | solution.py:999
  48.3 6.6 %collective-permute-start.8 = (bf16[96,512]{1,0:T(8,128)(2,1)}, bf16[96,512]{1,0:T(8,128)(2,1)S(1)}, u32[]{:S(2)}, u32[]{:S(2)}) collective-permute-start(bf16[96,512]{1,0:T(8,128)(2,1)} %get-tuple-element.40), channel_id=1, source_target_pairs={{0,8},{4,12},{8,0},{12,4},{16,24},{20,28},{24,16},{28,20},{1,9},{5... | collective-permute-start | bytes 294920 | tf_op jit(solution)/shard_map/ppermute | solution.py:999
  48.7 6.4 %collective-permute-start.9 = (bf16[96,512]{1,0:T(8,128)(2,1)}, bf16[96,512]{1,0:T(8,128)(2,1)S(1)}, u32[]{:S(2)}, u32[]{:S(2)}) collective-permute-start(bf16[96,512]{1,0:T(8,128)(2,1)} %get-tuple-element.41), channel_id=1, source_target_pairs={{0,12},{4,8},{8,4},{12,0},{16,28},{20,24},{24,20},{28,16},{1,13},{... | collective-permute-start | bytes 294920 | tf_op jit(solution)/shard_map/ppermute | solution.py:999
  49.5 8.7 %collective-permute-start.10 = (bf16[96,512]{1,0:T(8,128)(2,1)}, bf16[96,512]{1,0:T(8,128)(2,1)S(1)}, u32[]{:S(2)}, u32[]{:S(2)}) collective-permute-start(bf16[96,512]{1,0:T(8,128)(2,1)} %get-tuple-element.42), channel_id=1, source_target_pairs={{0,16},{4,20},{8,24},{12,28},{16,0},{20,4},{24,8},{28,12},{1,17},{... | collective-permute-start | bytes 294920 | tf_op jit(solution)/shard_map/ppermute | solution.py:999
  52.5 12.7 %collective-permute-start.11 = (bf16[96,512]{1,0:T(8,128)(2,1)}, bf16[96,512]{1,0:T(8,128)(2,1)S(1)}, u32[]{:S(2)}, u32[]{:S(2)}) collective-permute-start(bf16[96,512]{1,0:T(8,128)(2,1)} %get-tuple-element.43), channel_id=1, source_target_pairs={{0,20},{4,16},{8,28},{12,24},{16,4},{20,0},{24,12},{28,8},{1,21},{... | collective-permute-start | bytes 294920 | tf_op jit(solution)/shard_map/ppermute | solution.py:999
  53.6 20.4 %copy-start.11 = (bf16[96,512]{1,0:T(8,128)(2,1)}, bf16[96,512]{1,0:T(8,128)(2,1)S(1)}, u32[]{:S(2)}) copy-start(bf16[96,512]{1,0:T(8,128)(2,1)S(1)} %collective-permute-done.7.refs_1_) | copy-start | bytes 294916
  53.6 14.3 %collective-permute-start.12 = (bf16[96,512]{1,0:T(8,128)(2,1)}, bf16[96,512]{1,0:T(8,128)(2,1)S(1)}, u32[]{:S(2)}, u32[]{:S(2)}) collective-permute-start(bf16[96,512]{1,0:T(8,128)(2,1)} %get-tuple-element.44), channel_id=1, source_target_pairs={{0,24},{4,28},{8,16},{12,20},{16,8},{20,12},{24,0},{28,4},{1,25},{... | collective-permute-start | bytes 294920 | tf_op jit(solution)/shard_map/ppermute | solution.py:999
  54.8 19.2 %copy-start.12 = (bf16[96,512]{1,0:T(8,128)(2,1)}, bf16[96,512]{1,0:T(8,128)(2,1)S(1)}, u32[]{:S(2)}) copy-start(bf16[96,512]{1,0:T(8,128)(2,1)S(1)} %collective-permute-done.8.refs_2_) | copy-start | bytes 294916
  54.8 16.2 %collective-permute-start.13 = (bf16[96,512]{1,0:T(8,128)(2,1)}, bf16[96,512]{1,0:T(8,128)(2,1)S(1)}, u32[]{:S(2)}, u32[]{:S(2)}) collective-permute-start(bf16[96,512]{1,0:T(8,128)(2,1)} %get-tuple-element.45), channel_id=1, source_target_pairs={{0,28},{4,24},{8,20},{12,16},{16,12},{20,8},{24,4},{28,0},{1,29},{... | collective-permute-start | bytes 294920 | tf_op jit(solution)/shard_map/ppermute | solution.py:999
  55.2 18.9 %copy-start.13 = (bf16[96,512]{1,0:T(8,128)(2,1)}, bf16[96,512]{1,0:T(8,128)(2,1)S(1)}, u32[]{:S(2)}) copy-start(bf16[96,512]{1,0:T(8,128)(2,1)S(1)} %collective-permute-done.9.refs_3_) | copy-start | bytes 294916
  55.2 17.0 %collective-permute-start.14 = (bf16[96,512]{1,0:T(8,128)(2,1)}, bf16[96,512]{1,0:T(8,128)(2,1)S(1)}, u32[]{:S(2)}, u32[]{:S(2)}) collective-permute-start(bf16[96,512]{1,0:T(8,128)(2,1)} %get-tuple-element.38.refs_0_), channel_id=1, source_target_pairs={{0,1},{1,0},{2,3},{3,2},{4,5},{5,4},{6,7},{7,6},{8,9},{9,8},{10,11... | collective-permute-start | bytes 294920 | tf_op jit(solution)/shard_map/ppermute | solution.py:999
  58.2 15.9 %copy-start.14 = (bf16[96,512]{1,0:T(8,128)(2,1)}, bf16[96,512]{1,0:T(8,128)(2,1)S(1)}, u32[]{:S(2)}) copy-start(bf16[96,512]{1,0:T(8,128)(2,1)S(1)} %collective-permute-done.10.refs_4_) | copy-start | bytes 294916
  58.2 14.1 %collective-permute-start.15 = (bf16[96,512]{1,0:T(8,128)(2,1)S(1)}, bf16[96,512]{1,0:T(8,128)(2,1)S(1)}, u32[]{:S(2)}, u32[]{:S(2)}) collective-permute-start(bf16[96,512]{1,0:T(8,128)(2,1)S(1)} %collective-permute-done.7.refs_1_), channel_id=1, source_target_pairs={{0,1},{1,0},{2,3},{3,2},{4,5},{5,4},{6,7},{7,6},{8,9},{9,8},{10,11... | collective-permute-start | bytes 294920 | tf_op jit(solution)/shard_map/ppermute | solution.py:999
  65.2 8.9 %copy-start.15 = (bf16[96,512]{1,0:T(8,128)(2,1)}, bf16[96,512]{1,0:T(8,128)(2,1)S(1)}, u32[]{:S(2)}) copy-start(bf16[96,512]{1,0:T(8,128)(2,1)S(1)} %collective-permute-done.11.refs_5_) | copy-start | bytes 294916
  65.2 7.5 %collective-permute-start.16 = (bf16[96,512]{1,0:T(8,128)(2,1)S(1)}, bf16[96,512]{1,0:T(8,128)(2,1)S(1)}, u32[]{:S(2)}, u32[]{:S(2)}) collective-permute-start(bf16[96,512]{1,0:T(8,128)(2,1)S(1)} %collective-permute-done.8.refs_2_), channel_id=1, source_target_pairs={{0,1},{1,0},{2,3},{3,2},{4,5},{5,4},{6,7},{7,6},{8,9},{9,8},{10,11... | collective-permute-start | bytes 294920 | tf_op jit(solution)/shard_map/ppermute | solution.py:999
  67.9 6.2 %copy-start.16 = (bf16[96,512]{1,0:T(8,128)(2,1)}, bf16[96,512]{1,0:T(8,128)(2,1)S(1)}, u32[]{:S(2)}) copy-start(bf16[96,512]{1,0:T(8,128)(2,1)S(1)} %collective-permute-done.12.refs_6_) | copy-start | bytes 294916
  67.9 4.9 %collective-permute-start.17 = (bf16[96,512]{1,0:T(8,128)(2,1)S(1)}, bf16[96,512]{1,0:T(8,128)(2,1)S(1)}, u32[]{:S(2)}, u32[]{:S(2)}) collective-permute-start(bf16[96,512]{1,0:T(8,128)(2,1)S(1)} %collective-permute-done.9.refs_3_), channel_id=1, source_target_pairs={{0,1},{1,0},{2,3},{3,2},{4,5},{5,4},{6,7},{7,6},{8,9},{9,8},{10,11... | collective-permute-start | bytes 294920 | tf_op jit(solution)/shard_map/ppermute | solution.py:999
  71.0 3.1 %copy-start.17 = (bf16[96,512]{1,0:T(8,128)(2,1)}, bf16[96,512]{1,0:T(8,128)(2,1)S(1)}, u32[]{:S(2)}) copy-start(bf16[96,512]{1,0:T(8,128)(2,1)S(1)} %collective-permute-done.13.refs_7_) | copy-start | bytes 294916
  71.0 2.2 %collective-permute-start.18 = (bf16[96,512]{1,0:T(8,128)(2,1)S(1)}, bf16[96,512]{1,0:T(8,128)(2,1)S(1)}, u32[]{:S(2)}, u32[]{:S(2)}) collective-permute-start(bf16[96,512]{1,0:T(8,128)(2,1)S(1)} %collective-permute-done.10.refs_4_), channel_id=1, source_target_pairs={{0,1},{1,0},{2,3},{3,2},{4,5},{5,4},{6,7},{7,6},{8,9},{9,8},{10,11... | collective-permute-start | bytes 294920 | tf_op jit(solution)/shard_map/ppermute | solution.py:999
  72.2 1.9 %copy-start.18 = (bf16[96,512]{1,0:T(8,128)(2,1)}, bf16[96,512]{1,0:T(8,128)(2,1)S(1)}, u32[]{:S(2)}) copy-start(bf16[96,512]{1,0:T(8,128)(2,1)S(1)} %collective-permute-done.14.refs_8_) | copy-start | bytes 294916
  72.2 1.3 collective-permute-start.19
  72.3 1.8 %copy-start.19 = (bf16[96,512]{1,0:T(8,128)(2,1)}, bf16[96,512]{1,0:T(8,128)(2,1)S(1)}, u32[]{:S(2)}) copy-start(bf16[96,512]{1,0:T(8,128)(2,1)S(1)} %collective-permute-done.15.refs_9_) | copy-start | bytes 294916
  72.3 1.4 %collective-permute-start.20 = (bf16[96,512]{1,0:T(8,128)(2,1)S(1)}, bf16[96,512]{1,0:T(8,128)(2,1)S(1)}, u32[]{:S(2)}, u32[]{:S(2)}) collective-permute-start(bf16[96,512]{1,0:T(8,128)(2,1)S(1)} %collective-permute-done.12.refs_6_), channel_id=1, source_target_pairs={{0,1},{1,0},{2,3},{3,2},{4,5},{5,4},{6,7},{7,6},{8,9},{9,8},{10,11... | collective-permute-start | bytes 294920 | tf_op jit(solution)/shard_map/ppermute | solution.py:999
  72.7 1.4 %copy-start.20 = (bf16[96,512]{1,0:T(8,128)(2,1)}, bf16[96,512]{1,0:T(8,128)(2,1)S(1)}, u32[]{:S(2)}) copy-start(bf16[96,512]{1,0:T(8,128)(2,1)S(1)} %collective-permute-done.16.refs_10_) | copy-start | bytes 294916
  72.7 1.3 collective-permute-start.21
  72.8 1.3 copy-start.21
  73.2 1.0 copy-start.22
  74.7 8.6 %copy-start = (bf16[8,64,256]{2,1,0:T(8,128)(2,1)S(1)}, bf16[8,64,256]{2,1,0:T(8,128)(2,1)}, u32[]{:S(2)}) copy-start(bf16[8,64,256]{2,1,0:T(8,128)(2,1)} %get-tuple-element.37.refs_0_) | copy-start | bytes 786436
  74.7 8.6 %copy-start.2 = (bf16[8,64,256]{2,1,0:T(8,128)(2,1)S(1)}, bf16[8,64,256]{2,1,0:T(8,128)(2,1)}, u32[]{:S(2)}) copy-start(bf16[8,64,256]{2,1,0:T(8,128)(2,1)} %copy-done.1) | copy-start | bytes 786436
  83.0 2.6 %collective-permute-start.24 = (bf16[768,512]{1,0:T(8,128)(2,1)}, bf16[768,512]{1,0:T(8,128)(2,1)S(1)}, u32[]{:S(2)}, u32[]{:S(2)}) collective-permute-start(bf16[768,512]{1,0:T(8,128)(2,1)} %get-tuple-element.48), channel_id=1, source_target_pairs={{0,1},{1,0},{2,3},{3,2},{4,5},{5,4},{6,7},{7,6},{8,9},{9,8},{10,11... | collective-permute-start | bytes 2359304 | tf_op jit(solution)/shard_map/ppermute | solution.py:999
  83.2 8.4 %collective-permute-start.22 = (bf16[8,64,256]{2,1,0:T(8,128)(2,1)S(1)}, bf16[8,64,256]{2,1,0:T(8,128)(2,1)S(1)}, u32[]{:S(2)}, u32[]{:S(2)}) collective-permute-start(bf16[8,64,256]{2,1,0:T(8,128)(2,1)S(1)} %copy-done), channel_id=1, source_target_pairs={{0,8},{4,12},{8,0},{12,4},{16,24},{20,28},{24,16},{28,20},{1,9},{5... | collective-permute-start | bytes 786440 | tf_op jit(solution)/shard_map/ppermute | solution.py:999
  83.3 13.3 %collective-permute-start.23 = (bf16[8,64,256]{2,1,0:T(8,128)(2,1)S(1)}, bf16[8,64,256]{2,1,0:T(8,128)(2,1)S(1)}, u32[]{:S(2)}, u32[]{:S(2)}) collective-permute-start(bf16[8,64,256]{2,1,0:T(8,128)(2,1)S(1)} %copy-done.2), channel_id=1, source_target_pairs={{0,8},{4,12},{8,0},{12,4},{16,24},{20,28},{24,16},{28,20},{1,9},{5... | collective-permute-start | bytes 786440 | tf_op jit(solution)/shard_map/ppermute | solution.py:999
  88.9 11.1 %collective-permute-start.25 = (bf16[96,512]{1,0:T(8,128)(2,1)}, bf16[96,512]{1,0:T(8,128)(2,1)S(1)}, u32[]{:S(2)}, u32[]{:S(2)}) collective-permute-start(bf16[96,512]{1,0:T(8,128)(2,1)} %get-tuple-element.53), channel_id=1, source_target_pairs={{0,4},{4,0},{8,12},{12,8},{16,20},{20,16},{24,28},{28,24},{1,5},{5... | collective-permute-start | bytes 294920 | tf_op jit(solution)/shard_map/ppermute | solution.py:999
  89.3 10.8 %collective-permute-start.26 = (bf16[96,512]{1,0:T(8,128)(2,1)}, bf16[96,512]{1,0:T(8,128)(2,1)S(1)}, u32[]{:S(2)}, u32[]{:S(2)}) collective-permute-start(bf16[96,512]{1,0:T(8,128)(2,1)} %get-tuple-element.54), channel_id=1, source_target_pairs={{0,8},{4,12},{8,0},{12,4},{16,24},{20,28},{24,16},{28,20},{1,9},{5... | collective-permute-start | bytes 294920 | tf_op jit(solution)/shard_map/ppermute | solution.py:999
  89.3 20.0 %collective-permute-start.27 = (bf16[96,512]{1,0:T(8,128)(2,1)}, bf16[96,512]{1,0:T(8,128)(2,1)S(1)}, u32[]{:S(2)}, u32[]{:S(2)}) collective-permute-start(bf16[96,512]{1,0:T(8,128)(2,1)} %get-tuple-element.55), channel_id=1, source_target_pairs={{0,12},{4,8},{8,4},{12,0},{16,28},{20,24},{24,20},{28,16},{1,13},{... | collective-permute-start | bytes 294920 | tf_op jit(solution)/shard_map/ppermute | solution.py:999
  91.6 10.8 %copy-start.3 = (bf16[8,64,256]{2,1,0:T(8,128)(2,1)}, bf16[8,64,256]{2,1,0:T(8,128)(2,1)S(1)}, u32[]{:S(2)}) copy-start(bf16[8,64,256]{2,1,0:T(8,128)(2,1)S(1)} %collective-permute-done.22.refs_2_) | copy-start | bytes 786436
  91.6 17.6 %collective-permute-start.28 = (bf16[96,512]{1,0:T(8,128)(2,1)}, bf16[96,512]{1,0:T(8,128)(2,1)S(1)}, u32[]{:S(2)}, u32[]{:S(2)}) collective-permute-start(bf16[96,512]{1,0:T(8,128)(2,1)} %get-tuple-element.56), channel_id=1, source_target_pairs={{0,16},{4,20},{8,24},{12,28},{16,0},{20,4},{24,8},{28,12},{1,17},{... | collective-permute-start | bytes 294920 | tf_op jit(solution)/shard_map/ppermute | solution.py:999
  96.5 5.9 %copy-start.4 = (bf16[8,64,256]{2,1,0:T(8,128)(2,1)}, bf16[8,64,256]{2,1,0:T(8,128)(2,1)S(1)}, u32[]{:S(2)}) copy-start(bf16[8,64,256]{2,1,0:T(8,128)(2,1)S(1)} %collective-permute-done.23.refs_3_) | copy-start | bytes 786436
  96.5 14.0 %collective-permute-start.29 = (bf16[96,512]{1,0:T(8,128)(2,1)}, bf16[96,512]{1,0:T(8,128)(2,1)S(1)}, u32[]{:S(2)}, u32[]{:S(2)}) collective-permute-start(bf16[96,512]{1,0:T(8,128)(2,1)} %get-tuple-element.57), channel_id=1, source_target_pairs={{0,20},{4,16},{8,28},{12,24},{16,4},{20,0},{24,12},{28,8},{1,21},{... | collective-permute-start | bytes 294920 | tf_op jit(solution)/shard_map/ppermute | solution.py:999
  100.0 16.2 %copy-start.26 = (bf16[96,512]{1,0:T(8,128)(2,1)}, bf16[96,512]{1,0:T(8,128)(2,1)S(1)}, u32[]{:S(2)}) copy-start(bf16[96,512]{1,0:T(8,128)(2,1)S(1)} %collective-permute-done.25.refs_1_) | copy-start | bytes 294916
  100.0 12.8 %collective-permute-start.30 = (bf16[96,512]{1,0:T(8,128)(2,1)}, bf16[96,512]{1,0:T(8,128)(2,1)S(1)}, u32[]{:S(2)}, u32[]{:S(2)}) collective-permute-start(bf16[96,512]{1,0:T(8,128)(2,1)} %get-tuple-element.58), channel_id=1, source_target_pairs={{0,24},{4,28},{8,16},{12,20},{16,8},{20,12},{24,0},{28,4},{1,25},{... | collective-permute-start | bytes 294920 | tf_op jit(solution)/shard_map/ppermute | solution.py:999
  100.1 16.2 %copy-start.27 = (bf16[96,512]{1,0:T(8,128)(2,1)}, bf16[96,512]{1,0:T(8,128)(2,1)S(1)}, u32[]{:S(2)}) copy-start(bf16[96,512]{1,0:T(8,128)(2,1)S(1)} %collective-permute-done.26.refs_2_) | copy-start | bytes 294916
  100.1 16.1 %collective-permute-start.31 = (bf16[96,512]{1,0:T(8,128)(2,1)}, bf16[96,512]{1,0:T(8,128)(2,1)S(1)}, u32[]{:S(2)}, u32[]{:S(2)}) collective-permute-start(bf16[96,512]{1,0:T(8,128)(2,1)} %get-tuple-element.59), channel_id=1, source_target_pairs={{0,28},{4,24},{8,20},{12,16},{16,12},{20,8},{24,4},{28,0},{1,29},{... | collective-permute-start | bytes 294920 | tf_op jit(solution)/shard_map/ppermute | solution.py:999
  104.8 15.1 %copy-start.5 = (bf16[8,64,256]{2,1,0:T(8,128)(2,1)S(1)}, bf16[8,64,256]{2,1,0:T(8,128)(2,1)}, u32[]{:S(2)}) copy-start(bf16[8,64,256]{2,1,0:T(8,128)(2,1)} %choose.1.refs_16_) | copy-start | bytes 786436
  109.2 7.0 %copy-start.28 = (bf16[96,512]{1,0:T(8,128)(2,1)}, bf16[96,512]{1,0:T(8,128)(2,1)S(1)}, u32[]{:S(2)}) copy-start(bf16[96,512]{1,0:T(8,128)(2,1)S(1)} %collective-permute-done.27.refs_3_) | copy-start | bytes 294916
  109.3 7.0 %copy-start.29 = (bf16[96,512]{1,0:T(8,128)(2,1)}, bf16[96,512]{1,0:T(8,128)(2,1)S(1)}, u32[]{:S(2)}) copy-start(bf16[96,512]{1,0:T(8,128)(2,1)S(1)} %collective-permute-done.28.refs_4_) | copy-start | bytes 294916
  110.5 5.8 %copy-start.30 = (bf16[96,512]{1,0:T(8,128)(2,1)}, bf16[96,512]{1,0:T(8,128)(2,1)S(1)}, u32[]{:S(2)}) copy-start(bf16[96,512]{1,0:T(8,128)(2,1)S(1)} %collective-permute-done.29.refs_5_) | copy-start | bytes 294916
  112.8 3.5 %copy-start.31 = (bf16[96,512]{1,0:T(8,128)(2,1)}, bf16[96,512]{1,0:T(8,128)(2,1)S(1)}, u32[]{:S(2)}) copy-start(bf16[96,512]{1,0:T(8,128)(2,1)S(1)} %collective-permute-done.30.refs_6_) | copy-start | bytes 294916
  119.6 7.1 %collective-permute-start.32 = (bf16[256,512]{1,0:T(8,128)(2,1)}, bf16[256,512]{1,0:T(8,128)(2,1)S(1)}, u32[]{:S(2)}, u32[]{:S(2)}) collective-permute-start(bf16[256,512]{1,0:T(8,128)(2,1)} %combine.1.refs_5_), channel_id=1, source_target_pairs={{0,2},{1,3},{2,0},{3,1},{4,6},{5,7},{6,4},{7,5},{8,10},{9,11},{10,... | collective-permute-start | bytes 786440 | tf_op jit(solution)/shard_map/ppermute | solution.py:999
  119.9 9.9 %collective-permute-start.34 = (bf16[8,64,256]{2,1,0:T(8,128)(2,1)S(1)}, bf16[8,64,256]{2,1,0:T(8,128)(2,1)S(1)}, u32[]{:S(2)}, u32[]{:S(2)}) collective-permute-start(bf16[8,64,256]{2,1,0:T(8,128)(2,1)S(1)} %copy-done.5), channel_id=1, source_target_pairs={{0,4},{4,0},{8,12},{12,8},{16,20},{20,16},{24,28},{28,24},{1,5},{5... | collective-permute-start | bytes 786440 | tf_op jit(solution)/shard_map/ppermute | solution.py:999
  127.8 5.1 %collective-permute-start.33 = (bf16[256,512]{1,0:T(8,128)(2,1)S(1)}, bf16[256,512]{1,0:T(8,128)(2,1)S(1)}, u32[]{:S(2)}, u32[]{:S(2)}) collective-permute-start(bf16[256,512]{1,0:T(8,128)(2,1)S(1)} %add_convert_fusion), channel_id=1, source_target_pairs={{0,1},{1,0},{2,3},{3,2},{4,5},{5,4},{6,7},{7,6},{8,9},{9,8},{10,11... | collective-permute-start | bytes 786440 | tf_op jit(solution)/shard_map/ppermute | solution.py:999
  (8 other events, 5.7 us)

commit v2 on v1

--- a/solution.py
+++ b/solution.py
@@ -16,7 +16,7 @@
 TOP = 2
 MIG = 4
 EXTRA = 16
-VMEM_BYTES = 60 * 1024 * 1024
+VMEM_BYTES = 64 * 1024 * 1024
 
 
 def iota(shape, dim):
@@ -28,15 +28,15 @@
 
 
 def attention_kernel(
-    group_hbm, plen_hbm, tlen_hbm, group_row_hbm, bucket_hbm, bias_hbm, gain_hbm,
-    hidden_hbm, wq_hbm, wk_hbm, wv_hbm, prompt_hbm, tail_hbm, slots_hbm,
-    head_ref, tail_out, packet_out,
-    group_sm, plen_sm, tlen_sm, perm_sm, slots_sm, mover_sm, group_row, bucket_row, bias_rows, gain_v, perm_v,
-    hidden_v, wq_v, wk_v, wv_v, pk_v, pv_v, kbuf, vbuf,
+    group_hbm, plen_hbm, tlen_hbm, group_row_hbm, bucket_hbm, bias_hbm,
+    q_hbm, knew_hbm, vnew_hbm, prompt_hbm, tail_hbm,
+    head_ref, tail_out,
+    group_sm, plen_sm, tlen_sm, perm_sm, group_row, bucket_row, bias_rows, perm_v,
+    pk_v, pv_v, kbuf, vbuf,
     q_v, knew_v, vnew_v, table, s_p, s_t, w_p, o_v, sorted_v, qbd_v,
-    small_sem, w_sem, p_sem, in_sem, out_sem, perm_sem, packet_sem,
+    small_sem, w_sem, p_sem, in_sem, out_sem, perm_sem,
 ):
-    rows, width = hidden_v.shape
+    rows = q_v.shape[0]
     groups, prompt_rows, cols = pv_v.shape
     tail_rows = kbuf.shape[1]
     heads = cols // HD
@@ -52,15 +52,15 @@
         for i, (src, dst) in enumerate(
             (
                 (group_hbm, group_sm), (plen_hbm, plen_sm), (tlen_hbm, tlen_sm),
-                (group_row_hbm, group_row), (bucket_hbm, bucket_row),
-                (bias_hbm, bias_rows), (gain_hbm, gain_v), (slots_hbm, slots_sm),
+                (group_row_hbm, group_row), (bucket_hbm, bucket_row.at[0]),
+                (bias_hbm, bias_rows),
             )
         )
     ]
     weights = [
         pltpu.make_async_copy(src, dst, w_sem.at[i])
         for i, (src, dst) in enumerate(
-            ((hidden_hbm, hidden_v), (wq_hbm, wq_v), (wk_hbm, wk_v), (wv_hbm, wv_v))
+            ((q_hbm, q_v), (knew_hbm, knew_v), (vnew_hbm, vnew_v))
         )
     ]
     prompts = [
@@ -86,6 +86,11 @@
         copy.start()
     for copy in small:
         copy.wait()
+
+    for t in range(tiles):
+        for copy in tile_in(t):
+            copy.start()
+    prompts[1].start()
 
     eye = onehot(iota((rows, rows), 0) == iota((rows, rows), 1))
     g_row = group_row[...]
@@ -115,36 +120,8 @@
         found = jnp.where(distance >= starts[k : k + 1, 0:1], bias[:, k : k + 1], found)
     table[...] = found
 
-    base = lax.axis_index("req") * rows
-    for m in range(MIG + 1):
-        mover_sm[m] = 0
-
-    def look(i, count):
-        away = slots_sm[base + i] != base + i
-
-        @pl.when(away)
-        def _():
-            mover_sm[jnp.minimum(count, MIG)] = i
-
-        return count + away.astype(jnp.int32)
-
-    lax.fori_loop(0, rows, look, 0, unroll=16)
     for copy in weights:
         copy.wait()
-    for t in range(tiles):
-        for copy in tile_in(t):
-            copy.start()
-    prompts[1].start()
-    v = hidden_v[...].astype(F32)
-    normed = (
-        v * lax.rsqrt(jnp.mean(v * v, axis=-1, keepdims=True) + EPS) * gain_v[...]
-    ).astype(BF16)
-    query = jnp.dot(normed, wq_v[...], preferred_element_type=F32).astype(BF16)
-    q_v[...] = query * jnp.asarray(HD ** (-0.5), BF16)
-    key_new = jnp.dot(normed, wk_v[...], preferred_element_type=F32).astype(BF16)
-    value_new = jnp.dot(normed, wv_v[...], preferred_element_type=F32).astype(BF16)
-    knew_v[...] = key_new.astype(F32)
-    vnew_v[...] = value_new.astype(F32)
     perm_copy.wait()
 
     lane = iota((8, LANES), 1)
@@ -252,15 +229,6 @@
         return carry
 
     lax.fori_loop(0, tiles, scores, 0)
-    packet = [
-        pltpu.make_async_copy(
-            buf.at[mover_sm[m]], packet_out.at[2 * m + side], packet_sem.at[2 * m + side]
-        )
-        for m in range(MIG)
-        for side, buf in enumerate((kbuf, vbuf))
-    ]
-    for copy in packet:
-        copy.start()
     prompts[1].wait()
 
     def gathered(buf, first):
@@ -319,19 +287,114 @@
     lax.fori_loop(0, tiles, values, 0)
     unsort = onehot(rank_col == iota((rows, rows), 1))
     head_ref[...] = jnp.dot(unsort, sorted_v[...], preferred_element_type=F32).astype(BF16)
-    for copy in packet:
-        copy.wait()
     for t in range(tiles):
         for copy in tile_out(t):
             copy.wait()
 
 
-def attention(
-    hidden_in, prompt_kv, tail_kv, group_of, prompt_len, tail_len, bucket_of, bias_table,
-    attn_gain, w_query, w_key, w_value, new_slot,
+def project_kernel(
+    slots_hbm, tlen_hbm, hidden_hbm, gain_hbm, wq_hbm, wk_hbm, wv_hbm, tail_hbm,
+    q_ref, knew_ref, vnew_ref, packet_ref,
+    slots_sm, tlen_sm, mover_sm, hidden_v, gain_v, wq_v, wk_v, wv_v, sem, slab_sem,
 ):
+    rows = hidden_v.shape[0]
+    cols = wq_v.shape[1]
+    early = [
+        pltpu.make_async_copy(slots_hbm, slots_sm, sem.at[0]),
+        pltpu.make_async_copy(tlen_hbm, tlen_sm, sem.at[1]),
+    ]
+    late = [
+        pltpu.make_async_copy(src, dst, sem.at[2 + i])
+        for i, (src, dst) in enumerate(
+            (
+                (hidden_hbm, hidden_v), (gain_hbm, gain_v),
+                (wq_hbm, wq_v), (wk_hbm, wk_v), (wv_hbm, wv_v),
+            )
+        )
+    ]
+    for copy in early + late:
+        copy.start()
+    for copy in early:
+        copy.wait()
+    base = lax.axis_index("req") * rows
+    for m in range(MIG + 1):
+        mover_sm[m] = 0
+
+    def look(i, count):
+        mover_sm[count] = i
+        return count + (slots_sm[base + i] != base + i).astype(jnp.int32)
+
+    lax.fori_loop(0, rows, look, 0, unroll=16)
+    slabs = [
+        pltpu.make_async_copy(
+            tail_hbm.at[side, mover_sm[m]], packet_ref.at[2 * m + side], slab_sem.at[2 * m + side]
+        )
+        for m in range(MIG)
+        for side in range(2)
+    ]
+    for copy in slabs:
+        copy.start()
+    for copy in late:
+        copy.wait()
+    v = hidden_v[...].astype(F32)
+    normed = (
+        v * lax.rsqrt(jnp.mean(v * v, axis=-1, keepdims=True) + EPS) * gain_v[...]
+    ).astype(BF16)
+    query = jnp.dot(normed, wq_v[...], preferred_element_type=F32).astype(BF16)
+    q_ref[...] = query * jnp.asarray(HD ** (-0.5), BF16)
+    for new, w in ((knew_ref, wk_v), (vnew_ref, wv_v)):
+        new[...] = jnp.dot(normed, w[...], preferred_element_type=F32).astype(BF16).astype(F32)
+    for copy in slabs:
+        copy.wait()
+    at = iota((packet_ref.shape[1], cols), 0)
+    for m in range(MIG):
+        r = mover_sm[m]
+        for side, new in enumerate((knew_ref, vnew_ref)):
+            old = packet_ref[2 * m + side].astype(F32)
+            packet_ref[2 * m + side] = jnp.where(
+                at == tlen_sm[r], new[pl.ds(r, 1), :], old
+            ).astype(BF16)
+
+
+def project(new_slot, tail_len, hidden_in, gain, w_query, w_key, w_value, tail_kv):
     rows, width = hidden_in.shape
     cols = w_query.shape[1]
+    tail_rows = tail_kv.shape[2]
+    vm = pl.BlockSpec(memory_space=pltpu.VMEM)
+    hbm = pl.BlockSpec(memory_space=pl.ANY)
+    return pl.pallas_call(
+        project_kernel,
+        out_shape=(
+            jax.ShapeDtypeStruct((rows, cols), BF16),
+            jax.ShapeDtypeStruct((rows, cols), F32),
+            jax.ShapeDtypeStruct((rows, cols), F32),
+            jax.ShapeDtypeStruct((2 * MIG, tail_rows, cols), BF16),
+        ),
+        in_specs=[hbm] * 8,
+        out_specs=(vm,) * 4,
+        scratch_shapes=[
+            pltpu.SMEM(new_slot.shape, jnp.int32),
+            pltpu.SMEM(tail_len.shape, jnp.int32),
+            pltpu.SMEM((MIG + 1,), jnp.int32),
+            pltpu.VMEM((rows, width), BF16),
+            pltpu.VMEM((1, width), F32),
+            pltpu.VMEM((width, cols), BF16),
+            pltpu.VMEM((width, cols), BF16),
+            pltpu.VMEM((width, cols), BF16),
+            pltpu.SemaphoreType.DMA((7,)),
+            pltpu.SemaphoreType.DMA((2 * MIG,)),
+        ],
+        compiler_params=pltpu.CompilerParams(vmem_limit_bytes=VMEM_BYTES),
+        cost_estimate=pl.CostEstimate(flops=400_000_000, bytes_accessed=3_000_000, transcendentals=0),
+        name="project",
+    )(new_slot, tail_len, hidden_in, gain[None, :], w_query, w_key, w_value, tail_kv)
+
+
+def attention(
+    query, key_new, value_new, prompt_kv, tail_kv, group_of, prompt_len, tail_len, bucket_of,
+    bias_table,
+):
+    rows, cols = query.shape
     heads = cols // HD
     groups, prompt_rows = prompt_kv.shape[1:3]
     tail_rows = tail_kv.shape[2]
@@ -347,26 +410,18 @@
         out_shape=(
             jax.ShapeDtypeStruct((rows, cols), BF16),
             jax.ShapeDtypeStruct(tail_kv.shape, BF16),
-            jax.ShapeDtypeStruct((2 * MIG, tail_rows, cols), BF16),
         ),
-        in_specs=[hbm] * 14,
-        out_specs=(vm, hbm, hbm),
+        in_specs=[hbm] * 11,
+        out_specs=(vm, hbm),
         scratch_shapes=[
             pltpu.SMEM((rows,), jnp.int32),
             pltpu.SMEM((groups,), jnp.int32),
             pltpu.SMEM((rows,), jnp.int32),
             pltpu.SMEM((8, rows), jnp.int32),
-            pltpu.SMEM(new_slot.shape, jnp.int32),
-            pltpu.SMEM((MIG + 1,), jnp.int32),
             pltpu.VMEM((1, rows), jnp.int32),
             pltpu.VMEM((1, span), jnp.int32),
             pltpu.VMEM((heads, buckets), F32),
-            pltpu.VMEM((1, width), F32),
             pltpu.VMEM((8, rows), jnp.int32),
-            pltpu.VMEM((rows, width), BF16),
-            pltpu.VMEM((width, cols), BF16),
-            pltpu.VMEM((width, cols), BF16),
-            pltpu.VMEM((width, cols), BF16),
             pltpu.VMEM((groups, prompt_rows, cols), BF16),
             pltpu.VMEM((groups, prompt_rows, cols), BF16),
             pltpu.VMEM((rows, tail_rows, cols), BF16),
@@ -381,25 +436,29 @@
             pltpu.VMEM((cols // LANES, TILE * heads, LANES), F32),
             pltpu.VMEM((rows, cols), BF16),
             pltpu.VMEM((rows * heads, cols), BF16),
-            pltpu.SemaphoreType.DMA((8,)),
-            pltpu.SemaphoreType.DMA((4,)),
+            pltpu.SemaphoreType.DMA((6,)),
+            pltpu.SemaphoreType.DMA((3,)),
             pltpu.SemaphoreType.DMA((2,)),
             pltpu.SemaphoreType.DMA((2, tiles)),
             pltpu.SemaphoreType.DMA((2, tiles)),
             pltpu.SemaphoreType.DMA,
-            pltpu.SemaphoreType.DMA((2 * MIG,)),
         ],
         compiler_params=pltpu.CompilerParams(vmem_limit_bytes=VMEM_BYTES),
         cost_estimate=pl.CostEstimate(flops=8_000_000_000, bytes_accessed=45_000_000, transcendentals=700_000),
         name="attention",
     )(
-        group_of, prompt_len, tail_len, group_of[None, :], bucket_of[None, :], bias_table.T,
-        attn_gain[None, :], hidden_in, w_query, w_key, w_value, prompt_kv, tail_kv, new_slot,
+        group_of, prompt_len, tail_len, group_of[None, :], bucket_of, bias_table.T,
+        query, key_new, value_new, prompt_kv, tail_kv,
     )
 
 
 def block_rows(cap):
     return cap + EXTRA
+
+
+def low_part(replicas):
+    bits = (replicas.bit_length() - 1) // 2
+    return bits, 1 << bits
 
 
 def plan_kernel(cap, slots_ref, ids_ref, *refs):
@@ -446,9 +505,8 @@
     columns = lax.dot_general(
         eye, facts.astype(F32).astype(BF16), NT, preferred_element_type=F32
     )
-    wide_ref[...] = jnp.where(
-        lane == 0, columns[:, 0:1], jnp.where(lane == 1, columns[:, 1:2], 0.0)
-    ).astype(BF16)
+    wide = jnp.where(lane == 0, columns[:, 0:1], jnp.where(lane == 1, columns[:, 1:2], 0.0))
+    wide_ref[...] = wide.astype(BF16)
     dest = jnp.max(jnp.where(moved, going_to, -1), axis=1, keepdims=True)
     dest = jnp.where(dest < 0, iota((replicas, 1), 0), dest)
     hot = (dest == iota((replicas, replicas), 1)).astype(F32).astype(BF16)
@@ -464,19 +522,15 @@
     def source_of(who):
         return jnp.sum(jnp.where(dest == who, sub1, 0), axis=0, keepdims=True)
 
-    bits = replicas.bit_length() - 1
-
-    def held(diff):
-        found = jnp.zeros_like(diff)
-        for i in range(bits - 1):
-            found = found + (((diff >> (bits - 1 - i)) & 1) << i)
-        return found
-
+    low_bits, low = low_part(replicas)
     diff = source_of(me) ^ me
-    final = jnp.where((diff & 1) == 1, 1 << (bits - 1), held(diff))
-    send = held(source_of(me ^ 1) ^ (me ^ 1))
+    turn = diff & (low - 1)
+    final = jnp.where(turn == 0, diff >> low_bits, (replicas >> low_bits) + turn - 1)
     lane8 = iota((8, LANES), 1)
-    plan = jnp.where(lane8 == 0, final, jnp.where(lane8 == 1, send, -1))
+    plan = jnp.where(lane8 == 0, final, -1)
+    for j in range(1, low):
+        apart = source_of(me ^ j) ^ me
+        plan = jnp.where(lane8 == 24 + j, apart >> low_bits, plan)
     lane1 = iota((1, rows), 1)
     for m in range(MIG):
         is_m = (moved_me > 0) & (rank_me == m)
@@ -525,14 +579,20 @@
     return (v * lax.rsqrt(jnp.mean(v * v, axis=-1, keepdims=True) + EPS) * gain).astype(BF16)
 
 
+def far_part(replicas, pieces):
+    return replicas // 2, replicas // pieces
+
+
 def dispatch_kernel(pieces, replicas, *refs):
+    near, each = far_part(replicas, pieces)
+    count = near + each
     heads_hbm = refs[:pieces]
     wout_hbm = refs[pieces : 2 * pieces]
     hidden_hbm, gain_ref, place_hbm, extra_hbm, wide_hbm = refs[2 * pieces : 2 * pieces + 5]
-    refs = refs[2 * pieces + 6 :]
+    refs = refs[-11 - count :]
     resid_ref = refs[0]
-    outs = refs[1 : 1 + replicas]
-    head_v, wout_v, stack, hidden_ref, place_ref, extra_ref, wide_ref, sem, more = refs[1 + replicas :]
+    outs = refs[1 : 1 + count]
+    head_v, wout_v, stack, hidden_ref, place_ref, extra_ref, wide_ref, extra_v, sem, more = refs[1 + count :]
     tp = lax.axis_index("tp")
     core = tp & 1
     rows, width = hidden_ref.shape
@@ -568,22 +628,23 @@
     for copy in late:
         copy.wait()
     size = place_ref.shape[0] // replicas
-    extra = jnp.dot(extra_ref[:, 0:rows], stack[rows:, :], preferred_element_type=F32)
-    names = jnp.dot(extra_ref[:, rows:], wide_ref[...], preferred_element_type=F32)
-    for k in range(replicas):
+    extra_v[...] = jnp.dot(extra_ref[:, 0:rows], stack[rows:, :], preferred_element_type=F32)
+    extra_v[:, 0:LANES] += jnp.dot(extra_ref[:, rows:], wide_ref[...], preferred_element_type=F32)
+    for i in range(count):
+        k = i if i < near else near + (tp >> 1) * each + (i - near)
         block = jnp.dot(
-            place_ref[k * size : (k + 1) * size], stack[0:rows, :], preferred_element_type=F32
+            place_ref[pl.ds(k * size, size), :], stack[0:rows, :], preferred_element_type=F32
         )
-        more_k = slice(k * EXTRA, (k + 1) * EXTRA)
-        outs[k][0 : size - EXTRA, :] = block[: size - EXTRA].astype(BF16)
-        tail = block[size - EXTRA :] + extra[more_k]
-        outs[k][size - EXTRA :, 0:LANES] = (tail[:, :LANES] + names[more_k]).astype(BF16)
-        outs[k][size - EXTRA :, LANES:] = tail[:, LANES:].astype(BF16)
+        outs[i][0 : size - EXTRA, :] = block[: size - EXTRA].astype(BF16)
+        outs[i][size - EXTRA :, :] = (
+            block[size - EXTRA :] + extra_v[pl.ds(k * EXTRA, EXTRA), :]
+        ).astype(BF16)
 
 
 def dispatch(heads, wouts, hidden, gain, place, extra, wide, after, replicas):
     rows, width = hidden.shape
     pieces = len(heads)
+    count = sum(far_part(replicas, pieces))
     half = width // 2
     size = place.shape[0] // replicas
     vm = pl.BlockSpec(memory_space=pltpu.VMEM)
@@ -591,9 +652,9 @@
     return pl.pallas_call(
         functools.partial(dispatch_kernel, pieces, replicas),
         out_shape=(jax.ShapeDtypeStruct((rows, width), BF16),)
-        + tuple(jax.ShapeDtypeStruct((size, half), BF16) for _ in range(replicas)),
-        in_specs=[hbm] * (2 * pieces) + [hbm, vm, hbm, hbm, hbm, hbm],
-        out_specs=(vm,) * (1 + replicas),
+        + tuple(jax.ShapeDtypeStruct((size, half), BF16) for _ in range(count)),
+        in_specs=[hbm] * (2 * pieces) + [hbm, vm, hbm, hbm, hbm] + [hbm] * len(after),
+        out_specs=(vm,) * (1 + count),
         scratch_shapes=[
             pltpu.VMEM((rows, width), BF16),
             pltpu.VMEM((width, width), BF16),
@@ -602,64 +663,73 @@
             pltpu.VMEM(place.shape, BF16),
             pltpu.VMEM(extra.shape, BF16),
             pltpu.VMEM(wide.shape, BF16),
+            pltpu.VMEM((extra.shape[0], half), F32),
             pltpu.SemaphoreType.DMA((2, pieces)),
-            pltpu.SemaphoreType.DMA((4,)),
+            pltpu.SemaphoreType.DMA((5,)),
         ],
         compiler_params=pltpu.CompilerParams(vmem_limit_bytes=VMEM_BYTES),
         cost_estimate=pl.CostEstimate(flops=1_200_000_000, bytes_accessed=6_000_000, transcendentals=0),
         name="dispatch",
-    )(*heads, *wouts, hidden, gain[None, :], place, extra, wide, after)
-
-
-def expert_kernel(replicas, *refs):
+    )(*heads, *wouts, hidden, gain[None, :], place, extra, wide, *after)
+
+
+def pieces_of(total, step):
+    return [(at, min(step, total - at)) for at in range(0, total, step)]
+
+
+def expert_kernel(replicas, pieces, *refs):
     own = refs[:replicas]
     pair = refs[replicas : 2 * replicas]
-    wg_hbm, wu_hbm, wd_hbm, keep_ref, give_ref, x_own, x_pair, wg, wu, wd, sem, xsem = refs[2 * replicas :]
-    core = lax.axis_index("tp") & 1
+    wg_hbm, wu_hbm, wd_hbm = refs[2 * replicas : 2 * replicas + 3]
+    keep_ref, give_ref, x_own, x_pair, wg, wu, wd, act, sem, xsem = refs[-10:]
+    tp = lax.axis_index("tp")
+    core = tp & 1
     size, half = own[0].shape
-
-    def weight_copies():
-        return [
-            pltpu.make_async_copy(wg_hbm.at[0], wg, sem.at[0]),
-            pltpu.make_async_copy(wu_hbm.at[0], wu, sem.at[1]),
-            pltpu.make_async_copy(wd_hbm.at[0], wd, sem.at[2]),
+    near, each = far_part(replicas, pieces)
+    hidden = wg.shape[0]
+    chunks = pieces_of(hidden, 256)
+    blocks = []
+    for k in range(replicas):
+        there = k
+        if k >= near:
+            turn, f = divmod(k - near, each)
+            there = near + ((tp >> 1) ^ turn) * each + f
+        at = pl.ds(there * size, size)
+        blocks.append(pltpu.make_async_copy(own[k], x_own.at[at], xsem.at[0, k]))
+        blocks.append(pltpu.make_async_copy(pair[k], x_pair.at[at], xsem.at[1, k]))
+    wide = [
+        [
+            pltpu.make_async_copy(src.at[0, pl.ds(at, n)], dst.at[pl.ds(at, n)], sem.at[side, c])
+            for side, (src, dst) in enumerate(((wg_hbm, wg), (wu_hbm, wu)))
         ]
-
-    def block_copies():
-        made = []
-        for k in range(replicas):
-            at = pl.ds(k * size, size)
-            made.append(pltpu.make_async_copy(own[k], x_own.at[at], xsem.at[0, k]))
-            made.append(pltpu.make_async_copy(pair[k], x_pair.at[at], xsem.at[1, k]))
-        return made
-
-    for copy in weight_copies() + block_copies():
+        for c, (at, n) in enumerate(chunks)
+    ]
+    down = pltpu.make_async_copy(wd_hbm.at[0], wd, sem.at[2, 0])
+    for copy in wide[0] + blocks + sum(wide[1:], []) + [down]:
         copy.start()
-    for copy in block_copies() + weight_copies():
+    for copy in blocks:
         copy.wait()
     here = pl.ds(pl.multiple_of(core * half, half), half)
     there = pl.ds(pl.multiple_of((1 - core) * half, half), half)
-    total = replicas * size
-    step = 256 if total % 256 == 0 else size
-
-    def tile(i, carry):
-        at = pl.ds(pl.multiple_of(i * step, step), step)
-        a, b = x_own[at, :], x_pair[at, :]
-        gate = lax.dot_general(a, wg[:, here], NT, preferred_element_type=F32) + lax.dot_general(
-            b, wg[:, there], NT, preferred_element_type=F32
+    a, b = x_own[...], x_pair[...]
+
+    def product(w, rows):
+        return lax.dot_general(a, w[rows, here], NT, preferred_element_type=F32) + lax.dot_general(
+            b, w[rows, there], NT, preferred_element_type=F32
         )
-        up = lax.dot_general(a, wu[:, here], NT, preferred_element_type=F32) + lax.dot_general(
-            b, wu[:, there], NT, preferred_element_type=F32
-        )
-        act = (jax.nn.gelu(gate, approximate=True) * up).astype(BF16)
-        give_ref[at, :] = jnp.dot(act, wd[:, there], preferred_element_type=F32).astype(BF16)
-        keep_ref[at, :] = jnp.dot(act, wd[:, here], preferred_element_type=F32).astype(BF16)
-        return carry
-
-    lax.fori_loop(0, total // step, tile, 0)
-
-
-def expert(own, pair, w_gate, w_up, w_down):
+
+    for c, (at, n) in enumerate(chunks):
+        for copy in wide[c]:
+            copy.wait()
+        rows = pl.ds(at, n)
+        gate = product(wg, rows)
+        act[:, at : at + n] = (jax.nn.gelu(gate, approximate=True) * product(wu, rows)).astype(BF16)
+    down.wait()
+    give_ref[...] = jnp.dot(act[...], wd[:, there], preferred_element_type=F32).astype(BF16)
+    keep_ref[...] = jnp.dot(act[...], wd[:, here], preferred_element_type=F32).astype(BF16)
+
+
+def expert(own, pair, w_gate, w_up, w_down, pieces):
     replicas = len(own)
     size, half = own[0].shape
     _, width, hidden = w_gate.shape
@@ -668,7 +738,7 @@
     hbm = pl.BlockSpec(memory_space=pl.ANY)
     shape = jax.ShapeDtypeStruct((total, half), BF16)
     return pl.pallas_call(
-        functools.partial(expert_kernel, replicas),
+        functools.partial(expert_kernel, replicas, pieces),
         out_shape=(shape, shape),
         in_specs=[hbm] * (2 * replicas + 3),
         out_specs=(vm, vm),
@@ -678,7 +748,8 @@
             pltpu.VMEM((hidden, width), BF16),
             pltpu.VMEM((hidden, width), BF16),
             pltpu.VMEM((hidden, width), BF16),
-            pltpu.SemaphoreType.DMA((3,)),
+            pltpu.VMEM((total, hidden), BF16),
+            pltpu.SemaphoreType.DMA((3, len(pieces_of(hidden, 256)))),
             pltpu.SemaphoreType.DMA((2, replicas)),
         ],
         compiler_params=pltpu.CompilerParams(vmem_limit_bytes=VMEM_BYTES),
@@ -856,7 +927,7 @@
 
 def combine_kernel(replicas, *refs):
     blocks = refs[:replicas]
-    first_hbm, second_hbm, gate_hbm, out_ref, all_v, first_ref, second_ref, gate_ref, sem = refs[
+    first_hbm, second_hbm, gate_hbm, after_hbm, out_ref, all_v, first_ref, second_ref, gate_ref, sem = refs[
         replicas:
     ]
     size = blocks[0].shape[0]
@@ -873,7 +944,7 @@
     out_ref[...] = (gate * one + (1.0 - gate) * two).astype(BF16)
 
 
-def combine(blocks, first, second, gate):
+def combine(blocks, first, second, gate, after):
     replicas = len(blocks)
     size, half = blocks[0].shape
     rows = first.shape[0]
@@ -882,7 +953,7 @@
     return pl.pallas_call(
         functools.partial(combine_kernel, replicas),
         out_shape=jax.ShapeDtypeStruct((rows, half), BF16),
-        in_specs=[hbm] * (replicas + 3),
+        in_specs=[hbm] * (replicas + 4),
         out_specs=vm,
         scratch_shapes=[
             pltpu.VMEM((replicas * size, half), BF16),
@@ -894,26 +965,26 @@
         compiler_params=pltpu.CompilerParams(vmem_limit_bytes=VMEM_BYTES),
         cost_estimate=pl.CostEstimate(flops=400_000_000, bytes_accessed=2_500_000, transcendentals=0),
         name="combine",
-    )(*blocks, first, second, gate)
-
-
-def choose_kernel(plan_hbm, *refs):
-    choices = refs[:-5]
+    )(*blocks, first, second, gate, after)
+
+
+def choose_kernel(turn, plan_hbm, *refs):
+    choices = refs[:-4]
     out_ref, plan_sm, sem, plan_sem = refs[-4:]
     load(plan_sem, (plan_hbm, plan_sm))
-    index = plan_sm[0, 1]
+    index = plan_sm[0, 24 + turn]
     for i, choice in enumerate(choices):
         @pl.when(index == i)
         def _():
             load(sem, (choice, out_ref))
 
 
-def choose(plan, held, after):
+def choose(plan, held, turn):
     hbm = pl.BlockSpec(memory_space=pl.ANY)
     return pl.pallas_call(
-        choose_kernel,
+        functools.partial(choose_kernel, turn),
         out_shape=jax.ShapeDtypeStruct(held[0].shape, BF16),
-        in_specs=[hbm] * (2 + len(held)),
+        in_specs=[hbm] * (1 + len(held)),
         out_specs=pl.BlockSpec(memory_space=pltpu.VMEM),
         scratch_shapes=[
             pltpu.SMEM(plan.shape, jnp.int32),
@@ -923,19 +994,18 @@
         compiler_params=pltpu.CompilerParams(vmem_limit_bytes=VMEM_BYTES),
         cost_estimate=pl.CostEstimate(flops=0, bytes_accessed=0, transcendentals=0),
         name="choose",
-    )(plan, *held, after)
+    )(plan, *held)
 
 
 def patch_kernel(count, plan_hbm, *refs):
     choices = refs[:count]
-    after_hbm, tail_hbm, out_hbm, plan_sm, slabs, sem, slab_sem, out_sem = refs[count:]
+    tail_hbm, out_hbm, token_ref, plan_sm, slabs, sem, slab_sem, out_sem = refs[count:]
     load(sem, (plan_hbm, plan_sm))
     index = plan_sm[0, 0]
     for i, choice in enumerate(choices):
         @pl.when(index == i)
         def _():
             load(slab_sem, (choice, slabs))
-
     def moves(m):
         to = plan_sm[0, 16 + m]
         return to, [
@@ -959,16 +1029,20 @@
         def _():
             for copy in copies:
                 copy.wait()
-
-
-def patch(plan, held, after, tail_new):
+    token_ref[...] = jnp.zeros(token_ref.shape, F32)
+
+
+def patch(plan, held, tail_new):
     hbm = pl.BlockSpec(memory_space=pl.ANY)
     count = len(held)
     return pl.pallas_call(
         functools.partial(patch_kernel, count),
-        out_shape=jax.ShapeDtypeStruct(tail_new.shape, BF16),
-        in_specs=[hbm] * (3 + count),
-        out_specs=hbm,
+        out_shape=(
+            jax.ShapeDtypeStruct(tail_new.shape, BF16),
+            jax.ShapeDtypeStruct((8, LANES), F32),
+        ),
+        in_specs=[hbm] * (2 + count),
+        out_specs=(hbm, pl.BlockSpec(memory_space=pltpu.VMEM)),
         scratch_shapes=[
             pltpu.SMEM(plan.shape, jnp.int32),
             pltpu.VMEM(held[0].shape, BF16),
@@ -976,11 +1050,11 @@
             pltpu.SemaphoreType.DMA((1,)),
             pltpu.SemaphoreType.DMA((2 * MIG,)),
         ],
-        input_output_aliases={2 + count: 0},
+        input_output_aliases={1 + count: 0},
         compiler_params=pltpu.CompilerParams(vmem_limit_bytes=VMEM_BYTES),
         cost_estimate=pl.CostEstimate(flops=0, bytes_accessed=0, transcendentals=0),
         name="patch",
-    )(plan, *held, after, tail_new)
+    )(plan, *held, tail_new)
 
 
 def body(
@@ -1004,35 +1078,53 @@
     def over_tp(k):
         return across("tp", pieces, k)
 
-    wouts = [w_out] + [over_tp(k)(w_out) for k in range(1, pieces)]
-    head_out, tail_new, packet = attention(
-        hidden_in, prompt_kv, tail_kv, group_of, prompt_len, tail_len, bucket_of, bias_table,
-        attn_gain, w_query, w_key, w_value, new_slot,
+    low_bits, low = low_part(replicas)
+    query, key_new, value_new, packet = project(
+        new_slot, tail_len, hidden_in, attn_gain, w_query, w_key, w_value, tail_kv
+    )
+    held = [packet] + [
+        over_req(h << low_bits)(packet) for h in range(1, replicas >> low_bits)
+    ]
+    wouts = [w_out, over_tp(1)(w_out)]
+    for k in range(2, pieces, 2):
+        wouts += [over_tp(k)(w) for w in wouts[:2]]
+    head_out, tail_new = attention(
+        query, key_new, value_new, prompt_kv, tail_kv, group_of, prompt_len, tail_len, bucket_of,
+        bias_table,
     )
     heads = [head_out] + [over_tp(k)(head_out) for k in range(1, pieces)]
     slots = new_slot.reshape(replicas, rows)
     place, extra, wide, kron, plan = make_plan(
-        slots, expert_ids, experts, cap, [head_out] + wouts[1:]
+        slots, expert_ids, experts, cap, [head_out] + held[1:] + wouts[2:]
     )
-    bits = replicas.bit_length() - 1
-    held = [packet, over_req(1 << (bits - 1))(packet)]
+    chosen = [choose(plan, held, j) for j in range(1, low)]
     resid, *blocks = dispatch(
-        heads, wouts, hidden_in, ffn_gain, place, extra, wide, held[1], replicas
+        heads, wouts, hidden_in, ffn_gain, place, extra, wide, chosen, replicas
     )
-    own = [blocks[0]] + [over_req(k)(blocks[k]) for k in range(1, replicas)]
+    near, each = far_part(replicas, pieces)
+
+    def far(f):
+        pairs = []
+        for r in range(replicas):
+            for t in range(pieces):
+                to = r ^ (near + (t >> 1) * each + f)
+                pairs.append((r * pieces + t, to * pieces + t))
+        return lax.ppermute(blocks[near + f], ("req", "tp"), pairs)
+
+    distant = [far(f) for f in range(each)]
+    own = [blocks[0]] + [over_req(k)(blocks[k]) for k in range(1, near)] + distant
+    for turn in range(1, pieces // 2):
+        own += [over_tp(2 * turn)(b) for b in distant]
     pair = [over_tp(1)(b) for b in own]
-    keep, give = expert(own, pair, w_gate, w_up, w_down)
+    keep, give = expert(own, pair, w_gate, w_up, w_down, pieces)
+    held = held + [over_req(j + 1)(p) for j, p in enumerate(chosen)]
     back = give_back(keep, over_tp(1)(give), kron, cap, replicas)
-    for i in range(1, bits - 1):
-        held = held + [over_req(1 << (bits - 1 - i))(p) for p in held]
-    last = choose(plan, held, back[0])
-    held.append(over_req(1)(last))
     first, second, gate, resid_new = make_gates(
-        own, pair, last, resid, slots, expert_ids, ffn_gain, router_weight, cap
+        own, pair, plan, resid, slots, expert_ids, ffn_gain, router_weight, cap
     )
     result = [back[0]] + [over_req(k)(back[k]) for k in range(1, replicas)]
-    mixed = combine(result, first, second, gate)
-    new_tail_kv = patch(plan, held, mixed, tail_new)
+    new_tail_kv, token = patch(plan, held, tail_new)
+    mixed = combine(result, first, second, gate, token)
     k = 2
     while k < pieces:
         other = over_tp(k)(mixed)

time: 134 us -> 119 us (0.89); the launches traced: 134 us -> 117 us
  waiting for transfers between devices: 28.1 us -> 17.2 us
  starting transfers between devices: 44.5 us -> 39.9 us
  local copies, waits for them, and re-layouts: 6.19 us -> 1.94 us
  Pallas kernels: 52.2 us -> 55.1 us
    ppermute x35 -> x33, waiting for transfers between devices: 28.1 us -> 16.7 us  [across(): return lambda v: lax.ppermute(v, axis, [(i, i ^ k) for i in range(size)])]
    ppermute x35 -> x33, starting transfers between devices: 44.5 us -> 38.5 us  [across(): return lambda v: lax.ppermute(v, axis, [(i, i ^ k) for i in range(size)])]
    pallas_call x3 -> x4, Pallas kernels: 13.2 us -> 17.1 us  [the longest x1 8.21 us: expert(): pl.pallas_call(functools.partial(expert_kernel, replicas, pieces), out_sh...]
    unnamed x74 -> x30, local copies, waits for them, and re-layouts: 4.32 us -> 0.65 us
    ppermute x0 -> x2, starting transfers between devices: none -> 1.41 us  [far(): return lax.ppermute(blocks[near + f], ('req', 'tp'), pairs)]
  transfers between devices with their start and end apart: 35 -> 35, of which waited for: 17 -> 11; matrix products, arithmetic and copies ran while one was open for 2% -> 1% of each run, Pallas kernels for 27% -> 33%
where the time goes in v2:
time: 119 us; the launch traced here: 117 us
  Pallas kernels  55.1 us (46%)
  starting transfers between devices  39.9 us (34%)
  waiting for transfers between devices  17.2 us (14%)
  other arithmetic  2.06 us (2%)
  local copies, waits for them, and re-layouts  1.94 us (2%)
    ppermute x33, starting transfers between devices, across(): return lambda v: lax.ppermute(v, axis, [(i, i ^ k) for i in range(size)])  38.5 us
    pallas_call x1, Pallas kernels, attention(): pl.pallas_call(attention_kernel, out_shape=(jax.ShapeDtypeStruct((rows, c...  21.6 us
    ppermute x33, waiting for transfers between devices, across(): return lambda v: lax.ppermute(v, axis, [(i, i ^ k) for i in range(size)])  16.7 us
    pallas_call x1, Pallas kernels, expert(): pl.pallas_call(functools.partial(expert_kernel, replicas, pieces), out_sh...  8.21 us
    pallas_call x1, Pallas kernels, dispatch(): pl.pallas_call(functools.partial(dispatch_kernel, pieces, replicas), out_...  4.96 us
    pallas_call x1, Pallas kernels, make_gates(): pl.pallas_call(functools.partial(gates_kernel, cap, replicas), out_shape=...  4.43 us
    pallas_call x1, Pallas kernels, project(): pl.pallas_call(project_kernel, out_shape=(jax.ShapeDtypeStruct((rows, col...  3.48 us
    pallas_call x1, Pallas kernels, patch(): pl.pallas_call(functools.partial(patch_kernel, count), out_shape=(jax.Sha...  3.04 us
  transfers between devices with their start and end apart: 35, of which 11 were waited for; matrix products, arithmetic and copies ran while one was open for 1% of the time, Pallas kernels for 33%

profile of v2, /device:TPU:11, one launch (start us, length us, event | category | flops | bytes accessed | tf_op | source)
XLA Modules:
  0.0 117.1 jit_solution(11436685542959077083)
XLA Ops:
  0.6 0.7 collective-permute-start.3
  1.4 0.3 collective-permute-start.4
  1.6 3.5 %project.1 = (bf16[256,256]{1,0:T(8,128)(2,1)}, f32[256,256]{1,0:T(8,128)}, f32[256,256]{1,0:T(8,128)}, bf16[8,64,256]{2,1,0:T(8,128)(2,1)}) custom-call(s32[2048]{0:T(1024)} %slots_hbm.1, s32[256]{0:T(256)} %tlen_hbm.3, bf16[256,1024]{1,0:T(8,128)(2,1)} %refs_8_.1, f32[1,1024]{1,0:T(1,128)} %bitcast.11, bf16[1024,256]{1,0:T(8,128)(2,1)} %wq_hbm.1, ...), custom_call_target="tpu_custom_call" | custom-call | flops 400000000 | bytes 3000000 | tf_op jit(solution)/shard_map/project/pallas_call | solution.py:365
  5.1 0.1 collective-permute-start.6
  5.2 2.5 %collective-permute-start.7 = (bf16[8,64,256]{2,1,0:T(8,128)(2,1)}, bf16[8,64,256]{2,1,0:T(8,128)(2,1)}, u32[]{:S(2)}, u32[]{:S(2)}) collective-permute-start(bf16[8,64,256]{2,1,0:T(8,128)(2,1)} %get-tuple-element.40.refs_0_), channel_id=1, source_target_pairs={{0,16},{4,20},{8,24},{12,28},{16,0},{20,4},{24,8},{28,12},{1,17},{... | collective-permute-start | bytes 786440 | tf_op jit(solution)/shard_map/ppermute | solution.py:1073
  7.7 0.2 collective-permute-start.8
  7.8 1.2 %collective-permute-start.5 = (bf16[256,1024]{1,0:T(8,128)(2,1)}, bf16[256,1024]{1,0:T(8,128)(2,1)}, u32[]{:S(2)}, u32[]{:S(2)}) collective-permute-start(bf16[256,1024]{1,0:T(8,128)(2,1)} %collective-permute-done.3.refs_5_), channel_id=1, source_target_pairs={{0,2},{1,3},{2,0},{3,1},{4,6},{5,7},{6,4},{7,5},{8,10},{9,11},{10,... | collective-permute-start | bytes 1572872 | tf_op jit(solution)/shard_map/ppermute | solution.py:1073
  9.1 21.6 %attention.1 = (bf16[256,256]{1,0:T(8,128)(2,1)}, bf16[2,256,64,256]{3,2,1,0:T(8,128)(2,1)}) custom-call(s32[256]{0:T(256)} %group_hbm.1, s32[8]{0:T(128)} %plen_hbm.1, s32[256]{0:T(256)} %tlen_hbm.3, s32[1,256]{1,0:T(1,128)} %bitcast.17, s32[577]{0:T(1024)} %bucket_hbm.1, f32[4,32]{1,0:T(4,128)} %bitcast.16, bf16[256,256]{1,0:T(8,128)(2,1)} %get-tuple-element.36.q_hbm, ...), custom_call_target="tpu_custom_call" | custom-call | flops 8000000000 | bytes 45000000 | tf_op jit(solution)/shard_map/attention/pallas_call | solution.py:408
  30.7 1.5 %collective-permute-start = (bf16[256,256]{1,0:T(8,128)(2,1)}, bf16[256,256]{1,0:T(8,128)(2,1)}, u32[]{:S(2)}, u32[]{:S(2)}) collective-permute-start(bf16[256,256]{1,0:T(8,128)(2,1)} %get-tuple-element.39.refs_0_), channel_id=1, source_target_pairs={{0,1},{1,0},{2,3},{3,2},{4,5},{5,4},{6,7},{7,6},{8,9},{9,8},{10,11... | collective-permute-start | bytes 393224 | tf_op jit(solution)/shard_map/ppermute | solution.py:1073
  32.2 0.3 collective-permute-start.1
  32.5 1.4 %collective-permute-start.2 = (bf16[256,256]{1,0:T(8,128)(2,1)}, bf16[256,256]{1,0:T(8,128)(2,1)}, u32[]{:S(2)}, u32[]{:S(2)}) collective-permute-start(bf16[256,256]{1,0:T(8,128)(2,1)} %get-tuple-element.39.refs_0_), channel_id=1, source_target_pairs={{0,3},{1,2},{2,1},{3,0},{4,7},{5,6},{6,5},{7,4},{8,11},{9,10},{10,... | collective-permute-start | bytes 393224 | tf_op jit(solution)/shard_map/ppermute | solution.py:1073
  34.0 1.3 %reshape.7.slots_ref.refs_18_ = s32[8,256]{1,0:T(8,128)} reshape(s32[2048]{0:T(1024)} %slots_hbm.1) | data formatting | bytes 16384 | tf_op jit(solution)/shard_map/reshape | solution.py:1096
  35.2 1.8 %plan.1 = (bf16[768,256]{1,0:T(8,128)(2,1)}, bf16[128,512]{1,0:T(8,128)(2,1)}, bf16[256,128]{1,0:T(8,128)(2,1)}, bf16[128,128]{1,0:T(8,128)(2,1)}, s32[8,128]{1,0:T(8,128)}) custom-call(s32[8,256]{1,0:T(8,128)} %reshape.7.slots_ref.refs_18_, s32[2,256]{1,0:T(2,128)} %bitcast.9, bf16[256,256]{1,0:T(8,128)(2,1)} %get-tuple-element.39.refs_0_, ...), custom_call_target="tpu_custom_call" | custom-call | tf_op jit(solution)/shard_map/plan/pallas_call | solution.py:551
  37.1 2.4 %choose.1.refs_13_ = bf16[8,64,256]{2,1,0:T(8,128)(2,1)} custom-call(s32[8,128]{1,0:T(8,128)} %get-tuple-element.44.plan_hbm.refs_16_, bf16[8,64,256]{2,1,0:T(8,128)(2,1)} %get-tuple-element.40.refs_0_, bf16[8,64,256]{2,1,0:T(8,128)(2,1)} %collective-permute-done.6.refs_1_, bf16[8,64,256]{2,1,0:T(8,128)(2,1)} %collective-permute-done.7.refs_2_, ...), custom_call_target="tpu_custom_call" | custom-call | tf_op jit(solution)/shard_map/choose/pallas_call | solution.py:984
  39.5 1.1 collective-permute-done.2.refs_3_
  40.6 5.0 %dispatch.1 = (bf16[256,1024]{1,0:T(8,128)(2,1)}, bf16[96,512]{1,0:T(8,128)(2,1)}, bf16[96,512]{1,0:T(8,128)(2,1)}, bf16[96,512]{1,0:T(8,128)(2,1)}, bf16[96,512...) custom-call(bf16[256,256]{1,0:T(8,128)(2,1)} %get-tuple-element.39.refs_0_, ...), custom_call_target="tpu_custom_call" | custom-call | flops 1200000000 | bytes 6000000 | tf_op jit(solution)/shard_map/dispatch/pallas_call | solution.py:652
  45.6 1.3 %collective-permute-start.9 = (bf16[96,512]{1,0:T(8,128)(2,1)}, bf16[96,512]{1,0:T(8,128)(2,1)S(1)}, u32[]{:S(2)}, u32[]{:S(2)}) collective-permute-start(bf16[96,512]{1,0:T(8,128)(2,1)} %get-tuple-element.46), channel_id=1, source_target_pairs={{0,4},{4,0},{8,12},{12,8},{16,20},{20,16},{24,28},{28,24},{1,5},{5... | collective-permute-start | bytes 294920 | tf_op jit(solution)/shard_map/ppermute | solution.py:1073
  46.9 1.3 %collective-permute-start.12 = (bf16[96,512]{1,0:T(8,128)(2,1)}, bf16[96,512]{1,0:T(8,128)(2,1)S(1)}, u32[]{:S(2)}, u32[]{:S(2)}) collective-permute-start(bf16[96,512]{1,0:T(8,128)(2,1)} %get-tuple-element.49), channel_id=1, source_target_pairs={{0,16},{1,17},{2,26},{3,27},{4,20},{5,21},{6,30},{7,31},{8,24},{9,... | collective-permute-start | bytes 294920 | tf_op jit(solution)/shard_map/ppermute | solution.py:1112
  48.2 0.1 collective-permute-start.13
  48.3 3.0 %collective-permute-start.10 = (bf16[96,512]{1,0:T(8,128)(2,1)}, bf16[96,512]{1,0:T(8,128)(2,1)S(1)}, u32[]{:S(2)}, u32[]{:S(2)}) collective-permute-start(bf16[96,512]{1,0:T(8,128)(2,1)} %get-tuple-element.47), channel_id=1, source_target_pairs={{0,8},{4,12},{8,0},{12,4},{16,24},{20,28},{24,16},{28,20},{1,9},{5... | collective-permute-start | bytes 294920 | tf_op jit(solution)/shard_map/ppermute | solution.py:1073
  51.3 0.9 collective-permute-start.11
  52.2 1.1 collective-permute-start.16
  53.2 3.1 %collective-permute-start.14 = (bf16[96,512]{1,0:T(8,128)(2,1)S(1)}, bf16[96,512]{1,0:T(8,128)(2,1)S(1)}, u32[]{:S(2)}, u32[]{:S(2)}) collective-permute-start(bf16[96,512]{1,0:T(8,128)(2,1)S(1)} %collective-permute-done.12.refs_4_), channel_id=1, source_target_pairs={{0,2},{1,3},{2,0},{3,1},{4,6},{5,7},{6,4},{7,5},{8,10},{9,11},{10,... | collective-permute-start | bytes 294920 | tf_op jit(solution)/shard_map/ppermute | solution.py:1073
  56.4 0.5 collective-permute-done.13.refs_5_
  56.9 1.7 %collective-permute-start.15 = (bf16[96,512]{1,0:T(8,128)(2,1)S(1)}, bf16[96,512]{1,0:T(8,128)(2,1)S(1)}, u32[]{:S(2)}, u32[]{:S(2)}) collective-permute-start(bf16[96,512]{1,0:T(8,128)(2,1)S(1)} %collective-permute-done.13.refs_5_), channel_id=1, source_target_pairs={{0,2},{1,3},{2,0},{3,1},{4,6},{5,7},{6,4},{7,5},{8,10},{9,11},{10,... | collective-permute-start | bytes 294920 | tf_op jit(solution)/shard_map/ppermute | solution.py:1073
  58.5 1.9 %collective-permute-start.17 = (bf16[96,512]{1,0:T(8,128)(2,1)S(1)}, bf16[96,512]{1,0:T(8,128)(2,1)S(1)}, u32[]{:S(2)}, u32[]{:S(2)}) collective-permute-start(bf16[96,512]{1,0:T(8,128)(2,1)S(1)} %collective-permute-done.9.refs_1_), channel_id=1, source_target_pairs={{0,1},{1,0},{2,3},{3,2},{4,5},{5,4},{6,7},{7,6},{8,9},{9,8},{10,11... | collective-permute-start | bytes 294920 | tf_op jit(solution)/shard_map/ppermute | solution.py:1073
  60.4 1.1 collective-permute-start.18
  61.5 0.1 collective-permute-start.20
  61.6 0.4 collective-permute-start.21
  62.1 1.0 collective-permute-start.19
  63.0 0.1 collective-permute-start.22
  63.1 0.5 collective-permute-start.23
  63.6 0.4 collective-permute-done.19.refs_11_
  64.0 0.4 collective-permute-done.22.refs_14_
  64.4 0.2 collective-permute-done.23.refs_15_
  64.6 0.0 copy-done.12
  64.6 0.0 copy-done.10
  64.6 0.1 copy-done.11
  64.7 0.3 copy-done.13
  65.0 0.2 copy-done.14
  65.2 8.2 %expert.1 = (bf16[768,512]{1,0:T(8,128)(2,1)}, bf16[768,512]{1,0:T(8,128)(2,1)}) custom-call(bf16[96,512]{1,0:T(8,128)(2,1)} %get-tuple-element.45.refs_0_, bf16[96,512]{1,0:T(8,128)(2,1)} %copy-done, bf16[96,512]{1,0:T(8,128)(2,1)} %copy-done.3, bf16[96,512]{1,0:T(8,128)(2,1)} %copy-done.4, bf16[96,512]{1,0:T(8,128)(2,1)} %copy-done.1, ...), custom_call_target="tpu_custom_call" | custom-call | flops 3400000000 | bytes 8000000 | tf_op jit(solution)/shard_map/expert/pallas_call | solution.py:740
  73.4 0.4 collective-permute-start.24
  73.8 1.4 %collective-permute-start.32 = (bf16[8,64,256]{2,1,0:T(8,128)(2,1)}, bf16[8,64,256]{2,1,0:T(8,128)(2,1)}, u32[]{:S(2)}, u32[]{:S(2)}) collective-permute-start(bf16[8,64,256]{2,1,0:T(8,128)(2,1)} %choose.1.refs_13_), channel_id=1, source_target_pairs={{0,4},{4,0},{8,12},{12,8},{16,20},{20,16},{24,28},{28,24},{1,5},{5... | collective-permute-start | bytes 786440 | tf_op jit(solution)/shard_map/ppermute | solution.py:1073
  75.3 0.8 collective-permute-done.24.got_hbm
  76.1 2.4 %give_back.1 = (bf16[96,512]{1,0:T(8,128)(2,1)}, bf16[96,512]{1,0:T(8,128)(2,1)}, bf16[96,512]{1,0:T(8,128)(2,1)}, bf16[96,512]{1,0:T(8,128)(2,1)}, bf16[96,512]...) custom-call(bf16[768,512]{1,0:T(8,128)(2,1)} %get-tuple-element.53.keep_hbm, ...), custom_call_target="tpu_custom_call" | custom-call | flops 30000000 | bytes 2500000 | tf_op jit(solution)/shard_map/give_back/pallas_call | solution.py:786
  78.6 1.5 %collective-permute-start.25 = (bf16[96,512]{1,0:T(8,128)(2,1)}, bf16[96,512]{1,0:T(8,128)(2,1)}, u32[]{:S(2)}, u32[]{:S(2)}) collective-permute-start(bf16[96,512]{1,0:T(8,128)(2,1)} %get-tuple-element.57), channel_id=1, source_target_pairs={{0,4},{4,0},{8,12},{12,8},{16,20},{20,16},{24,28},{28,24},{1,5},{5... | collective-permute-start | bytes 294920 | tf_op jit(solution)/shard_map/ppermute | solution.py:1073
  80.1 1.0 collective-permute-start.26
  81.1 1.0 collective-permute-start.27
  82.1 1.5 %collective-permute-start.28 = (bf16[96,512]{1,0:T(8,128)(2,1)}, bf16[96,512]{1,0:T(8,128)(2,1)}, u32[]{:S(2)}, u32[]{:S(2)}) collective-permute-start(bf16[96,512]{1,0:T(8,128)(2,1)} %get-tuple-element.60), channel_id=1, source_target_pairs={{0,16},{4,20},{8,24},{12,28},{16,0},{20,4},{24,8},{28,12},{1,17},{... | collective-permute-start | bytes 294920 | tf_op jit(solution)/shard_map/ppermute | solution.py:1073
  83.5 1.5 %collective-permute-start.29 = (bf16[96,512]{1,0:T(8,128)(2,1)}, bf16[96,512]{1,0:T(8,128)(2,1)}, u32[]{:S(2)}, u32[]{:S(2)}) collective-permute-start(bf16[96,512]{1,0:T(8,128)(2,1)} %get-tuple-element.61), channel_id=1, source_target_pairs={{0,20},{4,16},{8,28},{12,24},{16,4},{20,0},{24,12},{28,8},{1,21},{... | collective-permute-start | bytes 294920 | tf_op jit(solution)/shard_map/ppermute | solution.py:1073
  85.1 1.2 %collective-permute-start.30 = (bf16[96,512]{1,0:T(8,128)(2,1)}, bf16[96,512]{1,0:T(8,128)(2,1)}, u32[]{:S(2)}, u32[]{:S(2)}) collective-permute-start(bf16[96,512]{1,0:T(8,128)(2,1)} %get-tuple-element.62), channel_id=1, source_target_pairs={{0,24},{4,28},{8,16},{12,20},{16,8},{20,12},{24,0},{28,4},{1,25},{... | collective-permute-start | bytes 294920 | tf_op jit(solution)/shard_map/ppermute | solution.py:1073
  86.3 0.5 collective-permute-start.31
  86.8 3.0 %patch.1 = (bf16[2,256,64,256]{3,2,1,0:T(8,128)(2,1)}, f32[8,128]{1,0:T(8,128)}) custom-call(s32[8,128]{1,0:T(8,128)} %get-tuple-element.44.plan_hbm.refs_16_, bf16[8,64,256]{2,1,0:T(8,128)(2,1)} %get-tuple-element.40.refs_0_, bf16[8,64,256]{2,1,0:T(8,128)(2,1)} %collective-permute-done.6.refs_1_, ...), custom_call_target="tpu_custom_call", output_to_operand_aliasing={{0}: (6, {})} | custom-call | tf_op jit(solution)/shard_map/patch/pallas_call | solution.py:1038
  89.9 4.4 %gates.1 = (bf16[256,768]{1,0:T(8,128)(2,1)}, bf16[256,768]{1,0:T(8,128)(2,1)}, f32[256,128]{1,0:T(8,128)}, bf16[256,512]{1,0:T(8,128)(2,1)}) custom-call(bf16[96,512]{1,0:T(8,128)(2,1)} %get-tuple-element.45.refs_0_, bf16[96,512]{1,0:T(8,128)(2,1)} %copy-done, bf16[96,512]{1,0:T(8,128)(2,1)} %copy-done.3, bf16[96,512]{1,0:T(8,128)(2,1)} %copy-done.4, ...), custom_call_target="tpu_custom_call" | custom-call | flops 200000000 | bytes 6000000 | tf_op jit(solution)/shard_map/gates/pallas_call | solution.py:906
  94.3 1.6 %collective-permute-done.29.refs_5_ = bf16[96,512]{1,0:T(8,128)(2,1)} collective-permute-done((bf16[96,512]{1,0:T(8,128)(2,1)}, bf16[96,512]{1,0:T(8,128)(2,1)}, u32[]{:S(2)}, u32[]{:S(2)}) %collective-permute-start.29) | collective-permute-done | bytes 98336 | tf_op jit(solution)/shard_map/ppermute | solution.py:1073
  95.9 4.0 %collective-permute-done.30.refs_6_ = bf16[96,512]{1,0:T(8,128)(2,1)} collective-permute-done((bf16[96,512]{1,0:T(8,128)(2,1)}, bf16[96,512]{1,0:T(8,128)(2,1)}, u32[]{:S(2)}, u32[]{:S(2)}) %collective-permute-start.30) | collective-permute-done | bytes 98336 | tf_op jit(solution)/shard_map/ppermute | solution.py:1073
  99.9 2.1 %collective-permute-done.31.refs_7_ = bf16[96,512]{1,0:T(8,128)(2,1)} collective-permute-done((bf16[96,512]{1,0:T(8,128)(2,1)}, bf16[96,512]{1,0:T(8,128)(2,1)}, u32[]{:S(2)}, u32[]{:S(2)}) %collective-permute-start.31) | collective-permute-done | bytes 98336 | tf_op jit(solution)/shard_map/ppermute | solution.py:1073
  102.0 2.7 %combine.1 = bf16[256,512]{1,0:T(8,128)(2,1)} custom-call(bf16[96,512]{1,0:T(8,128)(2,1)} %get-tuple-element.56.refs_0_, bf16[96,512]{1,0:T(8,128)(2,1)} %collective-permute-done.25.refs_1_, bf16[96,512]{1,0:T(8,128)(2,1)} %collective-permute-done.26.refs_2_, bf16[96,512]{1,0:T(8,128)(2,1)} %collective-permute-done.27.refs_3_, ...), custom_call_target="tpu_custom_call" | custom-call | flops 400000000 | bytes 2500000 | tf_op jit(solution)/shard_map/combine/pallas_call | solution.py:953
  104.8 1.4 %collective-permute-start.33 = (bf16[256,512]{1,0:T(8,128)(2,1)}, bf16[256,512]{1,0:T(8,128)(2,1)S(1)}, u32[]{:S(2)}, u32[]{:S(2)}) collective-permute-start(bf16[256,512]{1,0:T(8,128)(2,1)} %combine.1), channel_id=1, source_target_pairs={{0,2},{1,3},{2,0},{3,1},{4,6},{5,7},{6,4},{7,5},{8,10},{9,11},{10,... | collective-permute-start | bytes 786440 | tf_op jit(solution)/shard_map/ppermute | solution.py:1073
  106.2 4.9 %collective-permute-done.33 = bf16[256,512]{1,0:T(8,128)(2,1)S(1)} collective-permute-done((bf16[256,512]{1,0:T(8,128)(2,1)}, bf16[256,512]{1,0:T(8,128)(2,1)S(1)}, u32[]{:S(2)}, u32[]{:S(2)}) %collective-permute-start.33) | collective-permute-done | bytes 262176 | tf_op jit(solution)/shard_map/ppermute | solution.py:1073
  111.1 1.1 add_convert_fusion
  112.2 2.8 %collective-permute-start.34 = (bf16[256,512]{1,0:T(8,128)(2,1)S(1)}, bf16[256,512]{1,0:T(8,128)(2,1)S(1)}, u32[]{:S(2)}, u32[]{:S(2)}) collective-permute-start(bf16[256,512]{1,0:T(8,128)(2,1)S(1)} %add_convert_fusion), channel_id=1, source_target_pairs={{0,1},{1,0},{2,3},{3,2},{4,5},{5,4},{6,7},{7,6},{8,9},{9,8},{10,11... | collective-permute-start | bytes 786440 | tf_op jit(solution)/shard_map/ppermute | solution.py:1073
  115.0 1.2 collective-permute-done.34
  116.1 0.9 maximum_select_fusion
  (49 shorter events, 0.1 us)
Async XLA Ops:
  0.6 7.2 %collective-permute-start.3 = (bf16[256,1024]{1,0:T(8,128)(2,1)}, bf16[256,1024]{1,0:T(8,128)(2,1)}, u32[]{:S(2)}, u32[]{:S(2)}) collective-permute-start(bf16[256,1024]{1,0:T(8,128)(2,1)} %refs_4_.1), channel_id=1, source_target_pairs={{0,1},{1,0},{2,3},{3,2},{4,5},{5,4},{6,7},{7,6},{8,9},{9,8},{10,11... | collective-permute-start | bytes 1572872 | tf_op jit(solution)/shard_map/ppermute | solution.py:1073
  1.4 33.9 %collective-permute-start.4 = (bf16[256,1024]{1,0:T(8,128)(2,1)}, bf16[256,1024]{1,0:T(8,128)(2,1)}, u32[]{:S(2)}, u32[]{:S(2)}) collective-permute-start(bf16[256,1024]{1,0:T(8,128)(2,1)} %refs_4_.1), channel_id=1, source_target_pairs={{0,2},{1,3},{2,0},{3,1},{4,6},{5,7},{6,4},{7,5},{8,10},{9,11},{10,... | collective-permute-start | bytes 1572872 | tf_op jit(solution)/shard_map/ppermute | solution.py:1073
  5.1 25.6 %collective-permute-start.6 = (bf16[8,64,256]{2,1,0:T(8,128)(2,1)}, bf16[8,64,256]{2,1,0:T(8,128)(2,1)}, u32[]{:S(2)}, u32[]{:S(2)}) collective-permute-start(bf16[8,64,256]{2,1,0:T(8,128)(2,1)} %get-tuple-element.40.refs_0_), channel_id=1, source_target_pairs={{0,8},{4,12},{8,0},{12,4},{16,24},{20,28},{24,16},{28,20},{1,9},{5... | collective-permute-start | bytes 786440 | tf_op jit(solution)/shard_map/ppermute | solution.py:1073
  5.2 27.0 %collective-permute-start.7 = (bf16[8,64,256]{2,1,0:T(8,128)(2,1)}, bf16[8,64,256]{2,1,0:T(8,128)(2,1)}, u32[]{:S(2)}, u32[]{:S(2)}) collective-permute-start(bf16[8,64,256]{2,1,0:T(8,128)(2,1)} %get-tuple-element.40.refs_0_), channel_id=1, source_target_pairs={{0,16},{4,20},{8,24},{12,28},{16,0},{20,4},{24,8},{28,12},{1,17},{... | collective-permute-start | bytes 786440 | tf_op jit(solution)/shard_map/ppermute | solution.py:1073
  7.7 24.8 %collective-permute-start.8 = (bf16[8,64,256]{2,1,0:T(8,128)(2,1)}, bf16[8,64,256]{2,1,0:T(8,128)(2,1)}, u32[]{:S(2)}, u32[]{:S(2)}) collective-permute-start(bf16[8,64,256]{2,1,0:T(8,128)(2,1)} %get-tuple-element.40.refs_0_), channel_id=1, source_target_pairs={{0,24},{4,28},{8,16},{12,20},{16,8},{20,12},{24,0},{28,4},{1,25},{... | collective-permute-start | bytes 786440 | tf_op jit(solution)/shard_map/ppermute | solution.py:1073
  7.8 27.4 %collective-permute-start.5 = (bf16[256,1024]{1,0:T(8,128)(2,1)}, bf16[256,1024]{1,0:T(8,128)(2,1)}, u32[]{:S(2)}, u32[]{:S(2)}) collective-permute-start(bf16[256,1024]{1,0:T(8,128)(2,1)} %collective-permute-done.3.refs_5_), channel_id=1, source_target_pairs={{0,2},{1,3},{2,0},{3,1},{4,6},{5,7},{6,4},{7,5},{8,10},{9,11},{10,... | collective-permute-start | bytes 1572872 | tf_op jit(solution)/shard_map/ppermute | solution.py:1073
  30.7 8.8 %collective-permute-start = (bf16[256,256]{1,0:T(8,128)(2,1)}, bf16[256,256]{1,0:T(8,128)(2,1)}, u32[]{:S(2)}, u32[]{:S(2)}) collective-permute-start(bf16[256,256]{1,0:T(8,128)(2,1)} %get-tuple-element.39.refs_0_), channel_id=1, source_target_pairs={{0,1},{1,0},{2,3},{3,2},{4,5},{5,4},{6,7},{7,6},{8,9},{9,8},{10,11... | collective-permute-start | bytes 393224 | tf_op jit(solution)/shard_map/ppermute | solution.py:1073
  32.2 7.3 %collective-permute-start.1 = (bf16[256,256]{1,0:T(8,128)(2,1)}, bf16[256,256]{1,0:T(8,128)(2,1)}, u32[]{:S(2)}, u32[]{:S(2)}) collective-permute-start(bf16[256,256]{1,0:T(8,128)(2,1)} %get-tuple-element.39.refs_0_), channel_id=1, source_target_pairs={{0,2},{1,3},{2,0},{3,1},{4,6},{5,7},{6,4},{7,5},{8,10},{9,11},{10,... | collective-permute-start | bytes 393224 | tf_op jit(solution)/shard_map/ppermute | solution.py:1073
  32.5 8.1 %collective-permute-start.2 = (bf16[256,256]{1,0:T(8,128)(2,1)}, bf16[256,256]{1,0:T(8,128)(2,1)}, u32[]{:S(2)}, u32[]{:S(2)}) collective-permute-start(bf16[256,256]{1,0:T(8,128)(2,1)} %get-tuple-element.39.refs_0_), channel_id=1, source_target_pairs={{0,3},{1,2},{2,1},{3,0},{4,7},{5,6},{6,5},{7,4},{8,11},{9,10},{10,... | collective-permute-start | bytes 393224 | tf_op jit(solution)/shard_map/ppermute | solution.py:1073
  45.6 6.6 %collective-permute-start.9 = (bf16[96,512]{1,0:T(8,128)(2,1)}, bf16[96,512]{1,0:T(8,128)(2,1)S(1)}, u32[]{:S(2)}, u32[]{:S(2)}) collective-permute-start(bf16[96,512]{1,0:T(8,128)(2,1)} %get-tuple-element.46), channel_id=1, source_target_pairs={{0,4},{4,0},{8,12},{12,8},{16,20},{20,16},{24,28},{28,24},{1,5},{5... | collective-permute-start | bytes 294920 | tf_op jit(solution)/shard_map/ppermute | solution.py:1073
  46.9 6.4 %collective-permute-start.12 = (bf16[96,512]{1,0:T(8,128)(2,1)}, bf16[96,512]{1,0:T(8,128)(2,1)S(1)}, u32[]{:S(2)}, u32[]{:S(2)}) collective-permute-start(bf16[96,512]{1,0:T(8,128)(2,1)} %get-tuple-element.49), channel_id=1, source_target_pairs={{0,16},{1,17},{2,26},{3,27},{4,20},{5,21},{6,30},{7,31},{8,24},{9,... | collective-permute-start | bytes 294920 | tf_op jit(solution)/shard_map/ppermute | solution.py:1112
  48.2 8.7 %collective-permute-start.13 = (bf16[96,512]{1,0:T(8,128)(2,1)}, bf16[96,512]{1,0:T(8,128)(2,1)S(1)}, u32[]{:S(2)}, u32[]{:S(2)}) collective-permute-start(bf16[96,512]{1,0:T(8,128)(2,1)} %get-tuple-element.50), channel_id=1, source_target_pairs={{0,20},{1,21},{2,30},{3,31},{4,16},{5,17},{6,26},{7,27},{8,28},{9,... | collective-permute-start | bytes 294920 | tf_op jit(solution)/shard_map/ppermute | solution.py:1112
  48.3 10.3 %collective-permute-start.10 = (bf16[96,512]{1,0:T(8,128)(2,1)}, bf16[96,512]{1,0:T(8,128)(2,1)S(1)}, u32[]{:S(2)}, u32[]{:S(2)}) collective-permute-start(bf16[96,512]{1,0:T(8,128)(2,1)} %get-tuple-element.47), channel_id=1, source_target_pairs={{0,8},{4,12},{8,0},{12,4},{16,24},{20,28},{24,16},{28,20},{1,9},{5... | collective-permute-start | bytes 294920 | tf_op jit(solution)/shard_map/ppermute | solution.py:1073
  51.3 9.2 %collective-permute-start.11 = (bf16[96,512]{1,0:T(8,128)(2,1)}, bf16[96,512]{1,0:T(8,128)(2,1)S(1)}, u32[]{:S(2)}, u32[]{:S(2)}) collective-permute-start(bf16[96,512]{1,0:T(8,128)(2,1)} %get-tuple-element.48), channel_id=1, source_target_pairs={{0,12},{4,8},{8,4},{12,0},{16,28},{20,24},{24,20},{28,16},{1,13},{... | collective-permute-start | bytes 294920 | tf_op jit(solution)/shard_map/ppermute | solution.py:1073
  52.2 6.4 %copy-start = (bf16[96,512]{1,0:T(8,128)(2,1)}, bf16[96,512]{1,0:T(8,128)(2,1)S(1)}, u32[]{:S(2)}) copy-start(bf16[96,512]{1,0:T(8,128)(2,1)S(1)} %collective-permute-done.9.refs_1_) | copy-start | bytes 294916
  52.2 9.4 %collective-permute-start.16 = (bf16[96,512]{1,0:T(8,128)(2,1)}, bf16[96,512]{1,0:T(8,128)(2,1)S(1)}, u32[]{:S(2)}, u32[]{:S(2)}) collective-permute-start(bf16[96,512]{1,0:T(8,128)(2,1)} %get-tuple-element.45.refs_0_), channel_id=1, source_target_pairs={{0,1},{1,0},{2,3},{3,2},{4,5},{5,4},{6,7},{7,6},{8,9},{9,8},{10,11... | collective-permute-start | bytes 294920 | tf_op jit(solution)/shard_map/ppermute | solution.py:1073
  53.2 9.8 %copy-start.1 = (bf16[96,512]{1,0:T(8,128)(2,1)}, bf16[96,512]{1,0:T(8,128)(2,1)S(1)}, u32[]{:S(2)}) copy-start(bf16[96,512]{1,0:T(8,128)(2,1)S(1)} %collective-permute-done.12.refs_4_) | copy-start | bytes 294916
  53.2 8.4 %collective-permute-start.14 = (bf16[96,512]{1,0:T(8,128)(2,1)S(1)}, bf16[96,512]{1,0:T(8,128)(2,1)S(1)}, u32[]{:S(2)}, u32[]{:S(2)}) collective-permute-start(bf16[96,512]{1,0:T(8,128)(2,1)S(1)} %collective-permute-done.12.refs_4_), channel_id=1, source_target_pairs={{0,2},{1,3},{2,0},{3,1},{4,6},{5,7},{6,4},{7,5},{8,10},{9,11},{10,... | collective-permute-start | bytes 294920 | tf_op jit(solution)/shard_map/ppermute | solution.py:1073
  56.9 7.1 %copy-start.2 = (bf16[96,512]{1,0:T(8,128)(2,1)}, bf16[96,512]{1,0:T(8,128)(2,1)S(1)}, u32[]{:S(2)}) copy-start(bf16[96,512]{1,0:T(8,128)(2,1)S(1)} %collective-permute-done.13.refs_5_) | copy-start | bytes 294916
  56.9 5.2 %collective-permute-start.15 = (bf16[96,512]{1,0:T(8,128)(2,1)S(1)}, bf16[96,512]{1,0:T(8,128)(2,1)S(1)}, u32[]{:S(2)}, u32[]{:S(2)}) collective-permute-start(bf16[96,512]{1,0:T(8,128)(2,1)S(1)} %collective-permute-done.13.refs_5_), channel_id=1, source_target_pairs={{0,2},{1,3},{2,0},{3,1},{4,6},{5,7},{6,4},{7,5},{8,10},{9,11},{10,... | collective-permute-start | bytes 294920 | tf_op jit(solution)/shard_map/ppermute | solution.py:1073
  58.5 5.5 %copy-start.3 = (bf16[96,512]{1,0:T(8,128)(2,1)}, bf16[96,512]{1,0:T(8,128)(2,1)S(1)}, u32[]{:S(2)}) copy-start(bf16[96,512]{1,0:T(8,128)(2,1)S(1)} %collective-permute-done.10.refs_2_) | copy-start | bytes 294916
  58.5 4.5 %collective-permute-start.17 = (bf16[96,512]{1,0:T(8,128)(2,1)S(1)}, bf16[96,512]{1,0:T(8,128)(2,1)S(1)}, u32[]{:S(2)}, u32[]{:S(2)}) collective-permute-start(bf16[96,512]{1,0:T(8,128)(2,1)S(1)} %collective-permute-done.9.refs_1_), channel_id=1, source_target_pairs={{0,1},{1,0},{2,3},{3,2},{4,5},{5,4},{6,7},{7,6},{8,9},{9,8},{10,11... | collective-permute-start | bytes 294920 | tf_op jit(solution)/shard_map/ppermute | solution.py:1073
  60.4 4.0 %copy-start.4 = (bf16[96,512]{1,0:T(8,128)(2,1)}, bf16[96,512]{1,0:T(8,128)(2,1)S(1)}, u32[]{:S(2)}) copy-start(bf16[96,512]{1,0:T(8,128)(2,1)S(1)} %collective-permute-done.11.refs_3_) | copy-start | bytes 294916
  60.4 2.7 %collective-permute-start.18 = (bf16[96,512]{1,0:T(8,128)(2,1)S(1)}, bf16[96,512]{1,0:T(8,128)(2,1)S(1)}, u32[]{:S(2)}, u32[]{:S(2)}) collective-permute-start(bf16[96,512]{1,0:T(8,128)(2,1)S(1)} %collective-permute-done.10.refs_2_), channel_id=1, source_target_pairs={{0,1},{1,0},{2,3},{3,2},{4,5},{5,4},{6,7},{7,6},{8,9},{9,8},{10,11... | collective-permute-start | bytes 294920 | tf_op jit(solution)/shard_map/ppermute | solution.py:1073
  61.5 3.0 %copy-start.5 = (bf16[96,512]{1,0:T(8,128)(2,1)}, bf16[96,512]{1,0:T(8,128)(2,1)S(1)}, u32[]{:S(2)}) copy-start(bf16[96,512]{1,0:T(8,128)(2,1)S(1)} %collective-permute-done.16.refs_8_) | copy-start | bytes 294916
  61.5 2.5 %collective-permute-start.20 = (bf16[96,512]{1,0:T(8,128)(2,1)S(1)}, bf16[96,512]{1,0:T(8,128)(2,1)S(1)}, u32[]{:S(2)}, u32[]{:S(2)}) collective-permute-start(bf16[96,512]{1,0:T(8,128)(2,1)S(1)} %collective-permute-done.12.refs_4_), channel_id=1, source_target_pairs={{0,1},{1,0},{2,3},{3,2},{4,5},{5,4},{6,7},{7,6},{8,9},{9,8},{10,11... | collective-permute-start | bytes 294920 | tf_op jit(solution)/shard_map/ppermute | solution.py:1073
  61.6 3.0 %copy-start.6 = (bf16[96,512]{1,0:T(8,128)(2,1)}, bf16[96,512]{1,0:T(8,128)(2,1)S(1)}, u32[]{:S(2)}) copy-start(bf16[96,512]{1,0:T(8,128)(2,1)S(1)} %collective-permute-done.14.refs_6_) | copy-start | bytes 294916
  61.6 2.4 %collective-permute-start.21 = (bf16[96,512]{1,0:T(8,128)(2,1)S(1)}, bf16[96,512]{1,0:T(8,128)(2,1)S(1)}, u32[]{:S(2)}, u32[]{:S(2)}) collective-permute-start(bf16[96,512]{1,0:T(8,128)(2,1)S(1)} %collective-permute-done.13.refs_5_), channel_id=1, source_target_pairs={{0,1},{1,0},{2,3},{3,2},{4,5},{5,4},{6,7},{7,6},{8,9},{9,8},{10,11... | collective-permute-start | bytes 294920 | tf_op jit(solution)/shard_map/ppermute | solution.py:1073
  62.0 2.5 %copy-start.7 = (bf16[96,512]{1,0:T(8,128)(2,1)}, bf16[96,512]{1,0:T(8,128)(2,1)S(1)}, u32[]{:S(2)}) copy-start(bf16[96,512]{1,0:T(8,128)(2,1)S(1)} %collective-permute-done.15.refs_7_) | copy-start | bytes 294916
  62.1 1.9 %collective-permute-start.19 = (bf16[96,512]{1,0:T(8,128)(2,1)S(1)}, bf16[96,512]{1,0:T(8,128)(2,1)S(1)}, u32[]{:S(2)}, u32[]{:S(2)}) collective-permute-start(bf16[96,512]{1,0:T(8,128)(2,1)S(1)} %collective-permute-done.11.refs_3_), channel_id=1, source_target_pairs={{0,1},{1,0},{2,3},{3,2},{4,5},{5,4},{6,7},{7,6},{8,9},{9,8},{10,11... | collective-permute-start | bytes 294920 | tf_op jit(solution)/shard_map/ppermute | solution.py:1073
  63.0 1.5 %copy-start.8 = (bf16[96,512]{1,0:T(8,128)(2,1)}, bf16[96,512]{1,0:T(8,128)(2,1)S(1)}, u32[]{:S(2)}) copy-start(bf16[96,512]{1,0:T(8,128)(2,1)S(1)} %collective-permute-done.17.refs_9_) | copy-start | bytes 294916
  63.0 1.4 %collective-permute-start.22 = (bf16[96,512]{1,0:T(8,128)(2,1)S(1)}, bf16[96,512]{1,0:T(8,128)(2,1)S(1)}, u32[]{:S(2)}, u32[]{:S(2)}) collective-permute-start(bf16[96,512]{1,0:T(8,128)(2,1)S(1)} %collective-permute-done.14.refs_6_), channel_id=1, source_target_pairs={{0,1},{1,0},{2,3},{3,2},{4,5},{5,4},{6,7},{7,6},{8,9},{9,8},{10,11... | collective-permute-start | bytes 294920 | tf_op jit(solution)/shard_map/ppermute | solution.py:1073
  63.1 1.5 %copy-start.9 = (bf16[96,512]{1,0:T(8,128)(2,1)}, bf16[96,512]{1,0:T(8,128)(2,1)S(1)}, u32[]{:S(2)}) copy-start(bf16[96,512]{1,0:T(8,128)(2,1)S(1)} %collective-permute-done.18.refs_10_) | copy-start | bytes 294916
  63.1 1.4 %collective-permute-start.23 = (bf16[96,512]{1,0:T(8,128)(2,1)S(1)}, bf16[96,512]{1,0:T(8,128)(2,1)S(1)}, u32[]{:S(2)}, u32[]{:S(2)}) collective-permute-start(bf16[96,512]{1,0:T(8,128)(2,1)S(1)} %collective-permute-done.15.refs_7_), channel_id=1, source_target_pairs={{0,1},{1,0},{2,3},{3,2},{4,5},{5,4},{6,7},{7,6},{8,9},{9,8},{10,11... | collective-permute-start | bytes 294920 | tf_op jit(solution)/shard_map/ppermute | solution.py:1073
  64.0 0.6 copy-start.12
  64.0 0.7 copy-start.10
  64.0 0.7 copy-start.11
  64.4 0.6 copy-start.13
  64.6 0.6 copy-start.14
  73.4 2.7 %collective-permute-start.24 = (bf16[768,512]{1,0:T(8,128)(2,1)}, bf16[768,512]{1,0:T(8,128)(2,1)}, u32[]{:S(2)}, u32[]{:S(2)}) collective-permute-start(bf16[768,512]{1,0:T(8,128)(2,1)} %get-tuple-element.54), channel_id=1, source_target_pairs={{0,1},{1,0},{2,3},{3,2},{4,5},{5,4},{6,7},{7,6},{8,9},{9,8},{10,11... | collective-permute-start | bytes 2359304 | tf_op jit(solution)/shard_map/ppermute | solution.py:1073
  73.8 9.7 %collective-permute-start.32 = (bf16[8,64,256]{2,1,0:T(8,128)(2,1)}, bf16[8,64,256]{2,1,0:T(8,128)(2,1)}, u32[]{:S(2)}, u32[]{:S(2)}) collective-permute-start(bf16[8,64,256]{2,1,0:T(8,128)(2,1)} %choose.1.refs_13_), channel_id=1, source_target_pairs={{0,4},{4,0},{8,12},{12,8},{16,20},{20,16},{24,28},{28,24},{1,5},{5... | collective-permute-start | bytes 786440 | tf_op jit(solution)/shard_map/ppermute | solution.py:1073
  78.6 6.5 %collective-permute-start.25 = (bf16[96,512]{1,0:T(8,128)(2,1)}, bf16[96,512]{1,0:T(8,128)(2,1)}, u32[]{:S(2)}, u32[]{:S(2)}) collective-permute-start(bf16[96,512]{1,0:T(8,128)(2,1)} %get-tuple-element.57), channel_id=1, source_target_pairs={{0,4},{4,0},{8,12},{12,8},{16,20},{20,16},{24,28},{28,24},{1,5},{5... | collective-permute-start | bytes 294920 | tf_op jit(solution)/shard_map/ppermute | solution.py:1073
  80.1 6.2 %collective-permute-start.26 = (bf16[96,512]{1,0:T(8,128)(2,1)}, bf16[96,512]{1,0:T(8,128)(2,1)}, u32[]{:S(2)}, u32[]{:S(2)}) collective-permute-start(bf16[96,512]{1,0:T(8,128)(2,1)} %get-tuple-element.58), channel_id=1, source_target_pairs={{0,8},{4,12},{8,0},{12,4},{16,24},{20,28},{24,16},{28,20},{1,9},{5... | collective-permute-start | bytes 294920 | tf_op jit(solution)/shard_map/ppermute | solution.py:1073
  81.1 13.2 %collective-permute-start.27 = (bf16[96,512]{1,0:T(8,128)(2,1)}, bf16[96,512]{1,0:T(8,128)(2,1)}, u32[]{:S(2)}, u32[]{:S(2)}) collective-permute-start(bf16[96,512]{1,0:T(8,128)(2,1)} %get-tuple-element.59), channel_id=1, source_target_pairs={{0,12},{4,8},{8,4},{12,0},{16,28},{20,24},{24,20},{28,16},{1,13},{... | collective-permute-start | bytes 294920 | tf_op jit(solution)/shard_map/ppermute | solution.py:1073
  82.1 12.3 %collective-permute-start.28 = (bf16[96,512]{1,0:T(8,128)(2,1)}, bf16[96,512]{1,0:T(8,128)(2,1)}, u32[]{:S(2)}, u32[]{:S(2)}) collective-permute-start(bf16[96,512]{1,0:T(8,128)(2,1)} %get-tuple-element.60), channel_id=1, source_target_pairs={{0,16},{4,20},{8,24},{12,28},{16,0},{20,4},{24,8},{28,12},{1,17},{... | collective-permute-start | bytes 294920 | tf_op jit(solution)/shard_map/ppermute | solution.py:1073
  83.5 12.4 %collective-permute-start.29 = (bf16[96,512]{1,0:T(8,128)(2,1)}, bf16[96,512]{1,0:T(8,128)(2,1)}, u32[]{:S(2)}, u32[]{:S(2)}) collective-permute-start(bf16[96,512]{1,0:T(8,128)(2,1)} %get-tuple-element.61), channel_id=1, source_target_pairs={{0,20},{4,16},{8,28},{12,24},{16,4},{20,0},{24,12},{28,8},{1,21},{... | collective-permute-start | bytes 294920 | tf_op jit(solution)/shard_map/ppermute | solution.py:1073
  85.1 14.8 %collective-permute-start.30 = (bf16[96,512]{1,0:T(8,128)(2,1)}, bf16[96,512]{1,0:T(8,128)(2,1)}, u32[]{:S(2)}, u32[]{:S(2)}) collective-permute-start(bf16[96,512]{1,0:T(8,128)(2,1)} %get-tuple-element.62), channel_id=1, source_target_pairs={{0,24},{4,28},{8,16},{12,20},{16,8},{20,12},{24,0},{28,4},{1,25},{... | collective-permute-start | bytes 294920 | tf_op jit(solution)/shard_map/ppermute | solution.py:1073
  86.3 15.8 %collective-permute-start.31 = (bf16[96,512]{1,0:T(8,128)(2,1)}, bf16[96,512]{1,0:T(8,128)(2,1)}, u32[]{:S(2)}, u32[]{:S(2)}) collective-permute-start(bf16[96,512]{1,0:T(8,128)(2,1)} %get-tuple-element.63), channel_id=1, source_target_pairs={{0,28},{4,24},{8,20},{12,16},{16,12},{20,8},{24,4},{28,0},{1,29},{... | collective-permute-start | bytes 294920 | tf_op jit(solution)/shard_map/ppermute | solution.py:1073
  104.8 6.3 %collective-permute-start.33 = (bf16[256,512]{1,0:T(8,128)(2,1)}, bf16[256,512]{1,0:T(8,128)(2,1)S(1)}, u32[]{:S(2)}, u32[]{:S(2)}) collective-permute-start(bf16[256,512]{1,0:T(8,128)(2,1)} %combine.1), channel_id=1, source_target_pairs={{0,2},{1,3},{2,0},{3,1},{4,6},{5,7},{6,4},{7,5},{8,10},{9,11},{10,... | collective-permute-start | bytes 786440 | tf_op jit(solution)/shard_map/ppermute | solution.py:1073
  112.2 3.9 %collective-permute-start.34 = (bf16[256,512]{1,0:T(8,128)(2,1)S(1)}, bf16[256,512]{1,0:T(8,128)(2,1)S(1)}, u32[]{:S(2)}, u32[]{:S(2)}) collective-permute-start(bf16[256,512]{1,0:T(8,128)(2,1)S(1)} %add_convert_fusion), channel_id=1, source_target_pairs={{0,1},{1,0},{2,3},{3,2},{4,5},{5,4},{6,7},{7,6},{8,9},{9,8},{10,11... | collective-permute-start | bytes 786440 | tf_op jit(solution)/shard_map/ppermute | solution.py:1073

commit v3 on v2

--- a/solution.py
+++ b/solution.py
@@ -12,7 +12,7 @@
 BF16 = jnp.bfloat16
 NT = (((1,), (1,)), ((), ()))
 LANES = 128
-TILE = 64
+TILE = 128
 TOP = 2
 MIG = 4
 EXTRA = 16
@@ -140,11 +140,11 @@
                 length = tlen_sm[r]
                 plen = plen_sm[group_sm[r]]
                 start = span_end - plen - length
-                block = start // LANES
-                off = start - block * LANES
+                block = lax.shift_right_logical(start, 7)
+                off = start & (LANES - 1)
                 mine = (sub >= j * heads) & (sub < (j + 1) * heads)
                 window = table[:, pl.ds(pl.multiple_of(block * LANES, LANES), prompt_rows + LANES)]
-                turn = jnp.where(off == 0, 0, LANES - off)
+                turn = (LANES - off) & (LANES - 1)
                 turned = [
                     pltpu.roll(window[:, k * LANES : (k + 1) * LANES], turn, 1)
                     for k in range(pieces + 1)
@@ -156,8 +156,7 @@
                 k = place // LANES
                 place = place - k * LANES
                 own = table[:, prompt_rows : prompt_rows + LANES]
-                shift = place - (tail_rows - length)
-                shift = jnp.where(shift < 0, shift + LANES, shift)
+                shift = (place - tail_rows + length) & (LANES - 1)
                 own = pltpu.roll(own, shift, 1)
                 live = mine & (lane >= place) & (lane <= place + length)
                 out_t[k] = jnp.where(live, own, out_t[k])
@@ -168,18 +167,18 @@
                 s_t[at, k * LANES : (k + 1) * LANES] = out_t[k]
             return carry
 
-        lax.fori_loop(0, TILE // per8, step, 0, unroll=8)
+        lax.fori_loop(0, TILE // per8, step, 0, unroll=16)
 
     def insert(t):
         def step(i, carry):
             r = t * TILE + i
             length = tlen_sm[r]
-            first = pl.multiple_of(length // 16 * 16, 16)
-            hit = row16 == length - first
+            first = pl.multiple_of(length & 0x30, 16)
+            hit = row16 == (length & 15)
             for new, buf in ((knew_v, kbuf), (vnew_v, vbuf)):
-                fresh = jnp.broadcast_to(new[pl.ds(r, 1), :], (16, cols))
-                old = buf[r, pl.ds(first, 16), :].astype(F32)
-                buf[r, pl.ds(first, 16), :] = jnp.where(hit, fresh, old).astype(BF16)
+                fresh = jnp.broadcast_to(new[pl.ds(r, 1), :], (16, cols)).astype(BF16)
+                old = buf[r, pl.ds(first, 16), :]
+                buf[r, pl.ds(first, 16), :] = jnp.where(hit, fresh, old)
             return carry
 
         lax.fori_loop(0, TILE, step, 0, unroll=8)
@@ -223,12 +222,18 @@
         lax.fori_loop(low, high, one_group, 0)
         for copy in tile_in(tile):
             copy.wait()
+
+        @pl.when(tile > 0)
+        def _():
+            for copy in tile_out(tile - 1):
+                copy.start()
+
         insert(tile)
-        for copy in tile_out(tile):
-            copy.start()
         return carry
 
     lax.fori_loop(0, tiles, scores, 0)
+    for copy in tile_out(tiles - 1):
+        copy.start()
     prompts[1].wait()
 
     def gathered(buf, first):

time: 119 us -> 117 us (0.983); the launches traced: 117 us -> 116 us
  waiting for transfers between devices: 17.2 us -> 27 us
  starting transfers between devices: 39.9 us -> 32.9 us
  Pallas kernels: 55.1 us -> 51.7 us
    ppermute x33, starting transfers between devices: 38.5 us -> 31.5 us  [across(): return lambda v: lax.ppermute(v, axis, [(i, i ^ k) for i in range(size)])]
    ppermute x2, waiting for transfers between devices: 0.5 us -> 7.06 us  [far(): return lax.ppermute(blocks[near + f], ('req', 'tp'), pairs)]
    pallas_call x1, Pallas kernels: 21.6 us -> 18.2 us  [attention(): pl.pallas_call(attention_kernel, out_shape=(jax.ShapeDtypeStruct((rows, c...]
    ppermute x33, waiting for transfers between devices: 16.7 us -> 19.9 us  [across(): return lambda v: lax.ppermute(v, axis, [(i, i ^ k) for i in range(size)])]
  transfers between devices with their start and end apart: 35 -> 35, of which waited for: 11 -> 13; matrix products, arithmetic and copies ran while one was open for 1% -> 1% of each run, Pallas kernels for 33% -> 31%
where the time goes in v3:
time: 117 us; the launch traced here: 116 us
  Pallas kernels  51.7 us (44%)
  starting transfers between devices  32.9 us (28%)
  waiting for transfers between devices  27 us (23%)
  other arithmetic  2.06 us (2%)
  local copies, waits for them, and re-layouts  1.94 us (2%)
    ppermute x33, starting transfers between devices, across(): return lambda v: lax.ppermute(v, axis, [(i, i ^ k) for i in range(size)])  31.5 us
    ppermute x33, waiting for transfers between devices, across(): return lambda v: lax.ppermute(v, axis, [(i, i ^ k) for i in range(size)])  19.9 us
    pallas_call x1, Pallas kernels, attention(): pl.pallas_call(attention_kernel, out_shape=(jax.ShapeDtypeStruct((rows, c...  18.2 us
    pallas_call x1, Pallas kernels, expert(): pl.pallas_call(functools.partial(expert_kernel, replicas, pieces), out_sh...  8.2 us
    ppermute x2, waiting for transfers between devices, far(): return lax.ppermute(blocks[near + f], ('req', 'tp'), pairs)  7.06 us
    pallas_call x1, Pallas kernels, dispatch(): pl.pallas_call(functools.partial(dispatch_kernel, pieces, replicas), out_...  4.97 us
    pallas_call x1, Pallas kernels, make_gates(): pl.pallas_call(functools.partial(gates_kernel, cap, replicas), out_shape=...  4.43 us
    pallas_call x1, Pallas kernels, project(): pl.pallas_call(project_kernel, out_shape=(jax.ShapeDtypeStruct((rows, col...  3.48 us
  transfers between devices with their start and end apart: 35, of which 13 were waited for; matrix products, arithmetic and copies ran while one was open for 1% of the time, Pallas kernels for 31%

profile of v3, /device:TPU:11, one launch (start us, length us, event | category | flops | bytes accessed | tf_op | source)
XLA Modules:
  0.0 116.5 jit_solution(14961932773745886760)
XLA Ops:
  0.6 0.7 collective-permute-start.3
  1.4 0.3 collective-permute-start.4
  1.6 3.5 %project.1 = (bf16[256,256]{1,0:T(8,128)(2,1)}, f32[256,256]{1,0:T(8,128)}, f32[256,256]{1,0:T(8,128)}, bf16[8,64,256]{2,1,0:T(8,128)(2,1)}) custom-call(s32[2048]{0:T(1024)} %slots_hbm.1, s32[256]{0:T(256)} %tlen_hbm.3, bf16[256,1024]{1,0:T(8,128)(2,1)} %refs_8_.1, f32[1,1024]{1,0:T(1,128)} %bitcast.11, bf16[1024,256]{1,0:T(8,128)(2,1)} %wq_hbm.1, ...), custom_call_target="tpu_custom_call" | custom-call | flops 400000000 | bytes 3000000 | tf_op jit(solution)/shard_map/project/pallas_call | solution.py:370
  5.1 0.1 collective-permute-start.6
  5.2 2.5 %collective-permute-start.7 = (bf16[8,64,256]{2,1,0:T(8,128)(2,1)}, bf16[8,64,256]{2,1,0:T(8,128)(2,1)}, u32[]{:S(2)}, u32[]{:S(2)}) collective-permute-start(bf16[8,64,256]{2,1,0:T(8,128)(2,1)} %get-tuple-element.40.refs_0_), channel_id=1, source_target_pairs={{0,16},{4,20},{8,24},{12,28},{16,0},{20,4},{24,8},{28,12},{1,17},{... | collective-permute-start | bytes 786440 | tf_op jit(solution)/shard_map/ppermute | solution.py:1078
  7.7 0.2 collective-permute-start.8
  7.8 1.2 %collective-permute-start.5 = (bf16[256,1024]{1,0:T(8,128)(2,1)}, bf16[256,1024]{1,0:T(8,128)(2,1)}, u32[]{:S(2)}, u32[]{:S(2)}) collective-permute-start(bf16[256,1024]{1,0:T(8,128)(2,1)} %collective-permute-done.3.refs_5_), channel_id=1, source_target_pairs={{0,2},{1,3},{2,0},{3,1},{4,6},{5,7},{6,4},{7,5},{8,10},{9,11},{10,... | collective-permute-start | bytes 1572872 | tf_op jit(solution)/shard_map/ppermute | solution.py:1078
  9.1 18.2 %attention.1 = (bf16[256,256]{1,0:T(8,128)(2,1)}, bf16[2,256,64,256]{3,2,1,0:T(8,128)(2,1)}) custom-call(s32[256]{0:T(256)} %group_hbm.1, s32[8]{0:T(128)} %plen_hbm.1, s32[256]{0:T(256)} %tlen_hbm.3, s32[1,256]{1,0:T(1,128)} %bitcast.17, s32[577]{0:T(1024)} %bucket_hbm.1, f32[4,32]{1,0:T(4,128)} %bitcast.16, bf16[256,256]{1,0:T(8,128)(2,1)} %get-tuple-element.36.q_hbm, ...), custom_call_target="tpu_custom_call" | custom-call | flops 8000000000 | bytes 45000000 | tf_op jit(solution)/shard_map/attention/pallas_call | solution.py:413
  27.2 1.5 %collective-permute-start = (bf16[256,256]{1,0:T(8,128)(2,1)}, bf16[256,256]{1,0:T(8,128)(2,1)}, u32[]{:S(2)}, u32[]{:S(2)}) collective-permute-start(bf16[256,256]{1,0:T(8,128)(2,1)} %get-tuple-element.39.refs_0_), channel_id=1, source_target_pairs={{0,1},{1,0},{2,3},{3,2},{4,5},{5,4},{6,7},{7,6},{8,9},{9,8},{10,11... | collective-permute-start | bytes 393224 | tf_op jit(solution)/shard_map/ppermute | solution.py:1078
  28.8 0.0 collective-permute-done.7.refs_2_
  28.8 0.3 collective-permute-start.1
  29.0 1.9 %collective-permute-done.8.refs_3_ = bf16[8,64,256]{2,1,0:T(8,128)(2,1)} collective-permute-done((bf16[8,64,256]{2,1,0:T(8,128)(2,1)}, bf16[8,64,256]{2,1,0:T(8,128)(2,1)}, u32[]{:S(2)}, u32[]{:S(2)}) %collective-permute-start.8) | collective-permute-done | bytes 262176 | tf_op jit(solution)/shard_map/ppermute | solution.py:1078
  30.9 2.5 %collective-permute-start.2 = (bf16[256,256]{1,0:T(8,128)(2,1)}, bf16[256,256]{1,0:T(8,128)(2,1)}, u32[]{:S(2)}, u32[]{:S(2)}) collective-permute-start(bf16[256,256]{1,0:T(8,128)(2,1)} %get-tuple-element.39.refs_0_), channel_id=1, source_target_pairs={{0,3},{1,2},{2,1},{3,0},{4,7},{5,6},{6,5},{7,4},{8,11},{9,10},{10,... | collective-permute-start | bytes 393224 | tf_op jit(solution)/shard_map/ppermute | solution.py:1078
  33.4 1.3 %reshape.7.slots_ref.refs_18_ = s32[8,256]{1,0:T(8,128)} reshape(s32[2048]{0:T(1024)} %slots_hbm.1) | data formatting | bytes 16384 | tf_op jit(solution)/shard_map/reshape | solution.py:1101
  34.7 1.8 %plan.1 = (bf16[768,256]{1,0:T(8,128)(2,1)}, bf16[128,512]{1,0:T(8,128)(2,1)}, bf16[256,128]{1,0:T(8,128)(2,1)}, bf16[128,128]{1,0:T(8,128)(2,1)}, s32[8,128]{1,0:T(8,128)}) custom-call(s32[8,256]{1,0:T(8,128)} %reshape.7.slots_ref.refs_18_, s32[2,256]{1,0:T(2,128)} %bitcast.9, bf16[256,256]{1,0:T(8,128)(2,1)} %get-tuple-element.39.refs_0_, ...), custom_call_target="tpu_custom_call" | custom-call | tf_op jit(solution)/shard_map/plan/pallas_call | solution.py:556
  36.5 2.4 %choose.1.refs_13_ = bf16[8,64,256]{2,1,0:T(8,128)(2,1)} custom-call(s32[8,128]{1,0:T(8,128)} %get-tuple-element.44.plan_hbm.refs_16_, bf16[8,64,256]{2,1,0:T(8,128)(2,1)} %get-tuple-element.40.refs_0_, bf16[8,64,256]{2,1,0:T(8,128)(2,1)} %collective-permute-done.6.refs_1_, bf16[8,64,256]{2,1,0:T(8,128)(2,1)} %collective-permute-done.7.refs_2_, ...), custom_call_target="tpu_custom_call" | custom-call | tf_op jit(solution)/shard_map/choose/pallas_call | solution.py:989
  39.0 5.0 %dispatch.1 = (bf16[256,1024]{1,0:T(8,128)(2,1)}, bf16[96,512]{1,0:T(8,128)(2,1)}, bf16[96,512]{1,0:T(8,128)(2,1)}, bf16[96,512]{1,0:T(8,128)(2,1)}, bf16[96,512...) custom-call(bf16[256,256]{1,0:T(8,128)(2,1)} %get-tuple-element.39.refs_0_, ...), custom_call_target="tpu_custom_call" | custom-call | flops 1200000000 | bytes 6000000 | tf_op jit(solution)/shard_map/dispatch/pallas_call | solution.py:657
  44.0 1.3 %collective-permute-start.9 = (bf16[96,512]{1,0:T(8,128)(2,1)}, bf16[96,512]{1,0:T(8,128)(2,1)S(1)}, u32[]{:S(2)}, u32[]{:S(2)}) collective-permute-start(bf16[96,512]{1,0:T(8,128)(2,1)} %get-tuple-element.46), channel_id=1, source_target_pairs={{0,4},{4,0},{8,12},{12,8},{16,20},{20,16},{24,28},{28,24},{1,5},{5... | collective-permute-start | bytes 294920 | tf_op jit(solution)/shard_map/ppermute | solution.py:1078
  45.3 1.3 %collective-permute-start.12 = (bf16[96,512]{1,0:T(8,128)(2,1)}, bf16[96,512]{1,0:T(8,128)(2,1)S(1)}, u32[]{:S(2)}, u32[]{:S(2)}) collective-permute-start(bf16[96,512]{1,0:T(8,128)(2,1)} %get-tuple-element.49), channel_id=1, source_target_pairs={{0,16},{1,17},{2,26},{3,27},{4,20},{5,21},{6,30},{7,31},{8,24},{9,... | collective-permute-start | bytes 294920 | tf_op jit(solution)/shard_map/ppermute | solution.py:1117
  46.5 0.1 collective-permute-start.13
  46.7 1.1 collective-permute-start.10
  47.7 1.4 %collective-permute-start.11 = (bf16[96,512]{1,0:T(8,128)(2,1)}, bf16[96,512]{1,0:T(8,128)(2,1)S(1)}, u32[]{:S(2)}, u32[]{:S(2)}) collective-permute-start(bf16[96,512]{1,0:T(8,128)(2,1)} %get-tuple-element.48), channel_id=1, source_target_pairs={{0,12},{4,8},{8,4},{12,0},{16,28},{20,24},{24,20},{28,16},{1,13},{... | collective-permute-start | bytes 294920 | tf_op jit(solution)/shard_map/ppermute | solution.py:1078
  49.1 0.9 collective-permute-start.16
  50.0 4.0 %collective-permute-done.12.refs_4_ = bf16[96,512]{1,0:T(8,128)(2,1)S(1)} collective-permute-done((bf16[96,512]{1,0:T(8,128)(2,1)}, bf16[96,512]{1,0:T(8,128)(2,1)S(1)}, u32[]{:S(2)}, u32[]{:S(2)}) %collective-permute-start.12) | collective-permute-done | bytes 98336 | tf_op jit(solution)/shard_map/ppermute | solution.py:1117
  54.0 3.1 %collective-permute-done.13.refs_5_ = bf16[96,512]{1,0:T(8,128)(2,1)S(1)} collective-permute-done((bf16[96,512]{1,0:T(8,128)(2,1)}, bf16[96,512]{1,0:T(8,128)(2,1)S(1)}, u32[]{:S(2)}, u32[]{:S(2)}) %collective-permute-start.13) | collective-permute-done | bytes 98336 | tf_op jit(solution)/shard_map/ppermute | solution.py:1117
  57.1 0.8 collective-permute-start.17
  57.9 0.9 collective-permute-start.18
  58.8 0.1 collective-permute-start.20
  58.9 0.4 collective-permute-start.21
  59.3 1.2 %collective-permute-done.15.refs_7_ = bf16[96,512]{1,0:T(8,128)(2,1)S(1)} collective-permute-done((bf16[96,512]{1,0:T(8,128)(2,1)S(1)}, bf16[96,512]{1,0:T(8,128)(2,1)S(1)}, u32[]{:S(2)}, u32[]{:S(2)}) %collective-permute-start.15) | collective-permute-done | bytes 98336 | tf_op jit(solution)/shard_map/ppermute | solution.py:1078
  60.5 1.9 %collective-permute-start.19 = (bf16[96,512]{1,0:T(8,128)(2,1)S(1)}, bf16[96,512]{1,0:T(8,128)(2,1)S(1)}, u32[]{:S(2)}, u32[]{:S(2)}) collective-permute-start(bf16[96,512]{1,0:T(8,128)(2,1)S(1)} %collective-permute-done.11.refs_3_), channel_id=1, source_target_pairs={{0,1},{1,0},{2,3},{3,2},{4,5},{5,4},{6,7},{7,6},{8,9},{9,8},{10,11... | collective-permute-start | bytes 294920 | tf_op jit(solution)/shard_map/ppermute | solution.py:1078
  62.4 0.1 collective-permute-start.22
  62.5 0.5 collective-permute-start.23
  63.0 0.4 collective-permute-done.19.refs_11_
  63.4 0.4 collective-permute-done.22.refs_14_
  63.8 0.2 collective-permute-done.23.refs_15_
  64.0 0.0 copy-done.12
  64.0 0.0 copy-done.10
  64.0 0.1 copy-done.11
  64.1 0.3 copy-done.13
  64.4 0.2 copy-done.14
  64.6 8.2 %expert.1 = (bf16[768,512]{1,0:T(8,128)(2,1)}, bf16[768,512]{1,0:T(8,128)(2,1)}) custom-call(bf16[96,512]{1,0:T(8,128)(2,1)} %get-tuple-element.45.refs_0_, bf16[96,512]{1,0:T(8,128)(2,1)} %copy-done, bf16[96,512]{1,0:T(8,128)(2,1)} %copy-done.3, bf16[96,512]{1,0:T(8,128)(2,1)} %copy-done.4, bf16[96,512]{1,0:T(8,128)(2,1)} %copy-done.1, ...), custom_call_target="tpu_custom_call" | custom-call | flops 3400000000 | bytes 8000000 | tf_op jit(solution)/shard_map/expert/pallas_call | solution.py:745
  72.8 0.4 collective-permute-start.24
  73.2 1.6 %collective-permute-start.32 = (bf16[8,64,256]{2,1,0:T(8,128)(2,1)}, bf16[8,64,256]{2,1,0:T(8,128)(2,1)}, u32[]{:S(2)}, u32[]{:S(2)}) collective-permute-start(bf16[8,64,256]{2,1,0:T(8,128)(2,1)} %choose.1.refs_13_), channel_id=1, source_target_pairs={{0,4},{4,0},{8,12},{12,8},{16,20},{20,16},{24,28},{28,24},{1,5},{5... | collective-permute-start | bytes 786440 | tf_op jit(solution)/shard_map/ppermute | solution.py:1078
  74.8 0.7 collective-permute-done.24.got_hbm
  75.5 2.4 %give_back.1 = (bf16[96,512]{1,0:T(8,128)(2,1)}, bf16[96,512]{1,0:T(8,128)(2,1)}, bf16[96,512]{1,0:T(8,128)(2,1)}, bf16[96,512]{1,0:T(8,128)(2,1)}, bf16[96,512]...) custom-call(bf16[768,512]{1,0:T(8,128)(2,1)} %get-tuple-element.53.keep_hbm, ...), custom_call_target="tpu_custom_call" | custom-call | flops 30000000 | bytes 2500000 | tf_op jit(solution)/shard_map/give_back/pallas_call | solution.py:791
  77.9 1.7 %collective-permute-start.25 = (bf16[96,512]{1,0:T(8,128)(2,1)}, bf16[96,512]{1,0:T(8,128)(2,1)}, u32[]{:S(2)}, u32[]{:S(2)}) collective-permute-start(bf16[96,512]{1,0:T(8,128)(2,1)} %get-tuple-element.57), channel_id=1, source_target_pairs={{0,4},{4,0},{8,12},{12,8},{16,20},{20,16},{24,28},{28,24},{1,5},{5... | collective-permute-start | bytes 294920 | tf_op jit(solution)/shard_map/ppermute | solution.py:1078
  79.6 1.3 %collective-permute-start.27 = (bf16[96,512]{1,0:T(8,128)(2,1)}, bf16[96,512]{1,0:T(8,128)(2,1)}, u32[]{:S(2)}, u32[]{:S(2)}) collective-permute-start(bf16[96,512]{1,0:T(8,128)(2,1)} %get-tuple-element.59), channel_id=1, source_target_pairs={{0,12},{4,8},{8,4},{12,0},{16,28},{20,24},{24,20},{28,16},{1,13},{... | collective-permute-start | bytes 294920 | tf_op jit(solution)/shard_map/ppermute | solution.py:1078
  80.9 1.4 %collective-permute-start.28 = (bf16[96,512]{1,0:T(8,128)(2,1)}, bf16[96,512]{1,0:T(8,128)(2,1)}, u32[]{:S(2)}, u32[]{:S(2)}) collective-permute-start(bf16[96,512]{1,0:T(8,128)(2,1)} %get-tuple-element.60), channel_id=1, source_target_pairs={{0,16},{4,20},{8,24},{12,28},{16,0},{20,4},{24,8},{28,12},{1,17},{... | collective-permute-start | bytes 294920 | tf_op jit(solution)/shard_map/ppermute | solution.py:1078
  82.3 2.1 %collective-permute-start.29 = (bf16[96,512]{1,0:T(8,128)(2,1)}, bf16[96,512]{1,0:T(8,128)(2,1)}, u32[]{:S(2)}, u32[]{:S(2)}) collective-permute-start(bf16[96,512]{1,0:T(8,128)(2,1)} %get-tuple-element.61), channel_id=1, source_target_pairs={{0,20},{4,16},{8,28},{12,24},{16,4},{20,0},{24,12},{28,8},{1,21},{... | collective-permute-start | bytes 294920 | tf_op jit(solution)/shard_map/ppermute | solution.py:1078
  84.3 1.5 %collective-permute-start.30 = (bf16[96,512]{1,0:T(8,128)(2,1)}, bf16[96,512]{1,0:T(8,128)(2,1)}, u32[]{:S(2)}, u32[]{:S(2)}) collective-permute-start(bf16[96,512]{1,0:T(8,128)(2,1)} %get-tuple-element.62), channel_id=1, source_target_pairs={{0,24},{4,28},{8,16},{12,20},{16,8},{20,12},{24,0},{28,4},{1,25},{... | collective-permute-start | bytes 294920 | tf_op jit(solution)/shard_map/ppermute | solution.py:1078
  85.8 0.6 collective-permute-start.31
  86.4 3.0 %patch.1 = (bf16[2,256,64,256]{3,2,1,0:T(8,128)(2,1)}, f32[8,128]{1,0:T(8,128)}) custom-call(s32[8,128]{1,0:T(8,128)} %get-tuple-element.44.plan_hbm.refs_16_, bf16[8,64,256]{2,1,0:T(8,128)(2,1)} %get-tuple-element.40.refs_0_, bf16[8,64,256]{2,1,0:T(8,128)(2,1)} %collective-permute-done.6.refs_1_, ...), custom_call_target="tpu_custom_call", output_to_operand_aliasing={{0}: (6, {})} | custom-call | tf_op jit(solution)/shard_map/patch/pallas_call | solution.py:1043
  89.4 4.4 %gates.1 = (bf16[256,768]{1,0:T(8,128)(2,1)}, bf16[256,768]{1,0:T(8,128)(2,1)}, f32[256,128]{1,0:T(8,128)}, bf16[256,512]{1,0:T(8,128)(2,1)}) custom-call(bf16[96,512]{1,0:T(8,128)(2,1)} %get-tuple-element.45.refs_0_, bf16[96,512]{1,0:T(8,128)(2,1)} %copy-done, bf16[96,512]{1,0:T(8,128)(2,1)} %copy-done.3, bf16[96,512]{1,0:T(8,128)(2,1)} %copy-done.4, ...), custom_call_target="tpu_custom_call" | custom-call | flops 200000000 | bytes 6000000 | tf_op jit(solution)/shard_map/gates/pallas_call | solution.py:911
  93.9 1.5 %collective-permute-done.29.refs_5_ = bf16[96,512]{1,0:T(8,128)(2,1)} collective-permute-done((bf16[96,512]{1,0:T(8,128)(2,1)}, bf16[96,512]{1,0:T(8,128)(2,1)}, u32[]{:S(2)}, u32[]{:S(2)}) %collective-permute-start.29) | collective-permute-done | bytes 98336 | tf_op jit(solution)/shard_map/ppermute | solution.py:1078
  95.4 3.0 %collective-permute-done.30.refs_6_ = bf16[96,512]{1,0:T(8,128)(2,1)} collective-permute-done((bf16[96,512]{1,0:T(8,128)(2,1)}, bf16[96,512]{1,0:T(8,128)(2,1)}, u32[]{:S(2)}, u32[]{:S(2)}) %collective-permute-start.30) | collective-permute-done | bytes 98336 | tf_op jit(solution)/shard_map/ppermute | solution.py:1078
  98.4 3.0 %collective-permute-done.31.refs_7_ = bf16[96,512]{1,0:T(8,128)(2,1)} collective-permute-done((bf16[96,512]{1,0:T(8,128)(2,1)}, bf16[96,512]{1,0:T(8,128)(2,1)}, u32[]{:S(2)}, u32[]{:S(2)}) %collective-permute-start.31) | collective-permute-done | bytes 98336 | tf_op jit(solution)/shard_map/ppermute | solution.py:1078
  101.4 2.7 %combine.1 = bf16[256,512]{1,0:T(8,128)(2,1)} custom-call(bf16[96,512]{1,0:T(8,128)(2,1)} %get-tuple-element.56.refs_0_, bf16[96,512]{1,0:T(8,128)(2,1)} %collective-permute-done.25.refs_1_, bf16[96,512]{1,0:T(8,128)(2,1)} %collective-permute-done.26.refs_2_, bf16[96,512]{1,0:T(8,128)(2,1)} %collective-permute-done.27.refs_3_, ...), custom_call_target="tpu_custom_call" | custom-call | flops 400000000 | bytes 2500000 | tf_op jit(solution)/shard_map/combine/pallas_call | solution.py:958
  104.2 0.4 collective-permute-start.33
  104.6 6.5 %collective-permute-done.33 = bf16[256,512]{1,0:T(8,128)(2,1)S(1)} collective-permute-done((bf16[256,512]{1,0:T(8,128)(2,1)}, bf16[256,512]{1,0:T(8,128)(2,1)S(1)}, u32[]{:S(2)}, u32[]{:S(2)}) %collective-permute-start.33) | collective-permute-done | bytes 262176 | tf_op jit(solution)/shard_map/ppermute | solution.py:1078
  111.1 1.1 add_convert_fusion
  112.2 2.1 %collective-permute-start.34 = (bf16[256,512]{1,0:T(8,128)(2,1)S(1)}, bf16[256,512]{1,0:T(8,128)(2,1)S(1)}, u32[]{:S(2)}, u32[]{:S(2)}) collective-permute-start(bf16[256,512]{1,0:T(8,128)(2,1)S(1)} %add_convert_fusion), channel_id=1, source_target_pairs={{0,1},{1,0},{2,3},{3,2},{4,5},{5,4},{6,7},{7,6},{8,9},{9,8},{10,11... | collective-permute-start | bytes 786440 | tf_op jit(solution)/shard_map/ppermute | solution.py:1078
  114.4 1.2 collective-permute-done.34
  115.5 0.9 maximum_select_fusion
  (49 shorter events, 0.1 us)
Async XLA Ops:
  0.6 7.2 %collective-permute-start.3 = (bf16[256,1024]{1,0:T(8,128)(2,1)}, bf16[256,1024]{1,0:T(8,128)(2,1)}, u32[]{:S(2)}, u32[]{:S(2)}) collective-permute-start(bf16[256,1024]{1,0:T(8,128)(2,1)} %refs_4_.1), channel_id=1, source_target_pairs={{0,1},{1,0},{2,3},{3,2},{4,5},{5,4},{6,7},{7,6},{8,9},{9,8},{10,11... | collective-permute-start | bytes 1572872 | tf_op jit(solution)/shard_map/ppermute | solution.py:1078
  1.4 33.3 %collective-permute-start.4 = (bf16[256,1024]{1,0:T(8,128)(2,1)}, bf16[256,1024]{1,0:T(8,128)(2,1)}, u32[]{:S(2)}, u32[]{:S(2)}) collective-permute-start(bf16[256,1024]{1,0:T(8,128)(2,1)} %refs_4_.1), channel_id=1, source_target_pairs={{0,2},{1,3},{2,0},{3,1},{4,6},{5,7},{6,4},{7,5},{8,10},{9,11},{10,... | collective-permute-start | bytes 1572872 | tf_op jit(solution)/shard_map/ppermute | solution.py:1078
  5.1 22.1 %collective-permute-start.6 = (bf16[8,64,256]{2,1,0:T(8,128)(2,1)}, bf16[8,64,256]{2,1,0:T(8,128)(2,1)}, u32[]{:S(2)}, u32[]{:S(2)}) collective-permute-start(bf16[8,64,256]{2,1,0:T(8,128)(2,1)} %get-tuple-element.40.refs_0_), channel_id=1, source_target_pairs={{0,8},{4,12},{8,0},{12,4},{16,24},{20,28},{24,16},{28,20},{1,9},{5... | collective-permute-start | bytes 786440 | tf_op jit(solution)/shard_map/ppermute | solution.py:1078
  5.2 23.6 %collective-permute-start.7 = (bf16[8,64,256]{2,1,0:T(8,128)(2,1)}, bf16[8,64,256]{2,1,0:T(8,128)(2,1)}, u32[]{:S(2)}, u32[]{:S(2)}) collective-permute-start(bf16[8,64,256]{2,1,0:T(8,128)(2,1)} %get-tuple-element.40.refs_0_), channel_id=1, source_target_pairs={{0,16},{4,20},{8,24},{12,28},{16,0},{20,4},{24,8},{28,12},{1,17},{... | collective-permute-start | bytes 786440 | tf_op jit(solution)/shard_map/ppermute | solution.py:1078
  7.7 23.2 %collective-permute-start.8 = (bf16[8,64,256]{2,1,0:T(8,128)(2,1)}, bf16[8,64,256]{2,1,0:T(8,128)(2,1)}, u32[]{:S(2)}, u32[]{:S(2)}) collective-permute-start(bf16[8,64,256]{2,1,0:T(8,128)(2,1)} %get-tuple-element.40.refs_0_), channel_id=1, source_target_pairs={{0,24},{4,28},{8,16},{12,20},{16,8},{20,12},{24,0},{28,4},{1,25},{... | collective-permute-start | bytes 786440 | tf_op jit(solution)/shard_map/ppermute | solution.py:1078
  7.8 26.9 %collective-permute-start.5 = (bf16[256,1024]{1,0:T(8,128)(2,1)}, bf16[256,1024]{1,0:T(8,128)(2,1)}, u32[]{:S(2)}, u32[]{:S(2)}) collective-permute-start(bf16[256,1024]{1,0:T(8,128)(2,1)} %collective-permute-done.3.refs_5_), channel_id=1, source_target_pairs={{0,2},{1,3},{2,0},{3,1},{4,6},{5,7},{6,4},{7,5},{8,10},{9,11},{10,... | collective-permute-start | bytes 1572872 | tf_op jit(solution)/shard_map/ppermute | solution.py:1078
  27.2 11.7 %collective-permute-start = (bf16[256,256]{1,0:T(8,128)(2,1)}, bf16[256,256]{1,0:T(8,128)(2,1)}, u32[]{:S(2)}, u32[]{:S(2)}) collective-permute-start(bf16[256,256]{1,0:T(8,128)(2,1)} %get-tuple-element.39.refs_0_), channel_id=1, source_target_pairs={{0,1},{1,0},{2,3},{3,2},{4,5},{5,4},{6,7},{7,6},{8,9},{9,8},{10,11... | collective-permute-start | bytes 393224 | tf_op jit(solution)/shard_map/ppermute | solution.py:1078
  28.8 10.2 %collective-permute-start.1 = (bf16[256,256]{1,0:T(8,128)(2,1)}, bf16[256,256]{1,0:T(8,128)(2,1)}, u32[]{:S(2)}, u32[]{:S(2)}) collective-permute-start(bf16[256,256]{1,0:T(8,128)(2,1)} %get-tuple-element.39.refs_0_), channel_id=1, source_target_pairs={{0,2},{1,3},{2,0},{3,1},{4,6},{5,7},{6,4},{7,5},{8,10},{9,11},{10,... | collective-permute-start | bytes 393224 | tf_op jit(solution)/shard_map/ppermute | solution.py:1078
  30.9 8.1 %collective-permute-start.2 = (bf16[256,256]{1,0:T(8,128)(2,1)}, bf16[256,256]{1,0:T(8,128)(2,1)}, u32[]{:S(2)}, u32[]{:S(2)}) collective-permute-start(bf16[256,256]{1,0:T(8,128)(2,1)} %get-tuple-element.39.refs_0_), channel_id=1, source_target_pairs={{0,3},{1,2},{2,1},{3,0},{4,7},{5,6},{6,5},{7,4},{8,11},{9,10},{10,... | collective-permute-start | bytes 393224 | tf_op jit(solution)/shard_map/ppermute | solution.py:1078
  44.0 5.1 %collective-permute-start.9 = (bf16[96,512]{1,0:T(8,128)(2,1)}, bf16[96,512]{1,0:T(8,128)(2,1)S(1)}, u32[]{:S(2)}, u32[]{:S(2)}) collective-permute-start(bf16[96,512]{1,0:T(8,128)(2,1)} %get-tuple-element.46), channel_id=1, source_target_pairs={{0,4},{4,0},{8,12},{12,8},{16,20},{20,16},{24,28},{28,24},{1,5},{5... | collective-permute-start | bytes 294920 | tf_op jit(solution)/shard_map/ppermute | solution.py:1078
  45.3 8.7 %collective-permute-start.12 = (bf16[96,512]{1,0:T(8,128)(2,1)}, bf16[96,512]{1,0:T(8,128)(2,1)S(1)}, u32[]{:S(2)}, u32[]{:S(2)}) collective-permute-start(bf16[96,512]{1,0:T(8,128)(2,1)} %get-tuple-element.49), channel_id=1, source_target_pairs={{0,16},{1,17},{2,26},{3,27},{4,20},{5,21},{6,30},{7,31},{8,24},{9,... | collective-permute-start | bytes 294920 | tf_op jit(solution)/shard_map/ppermute | solution.py:1117
  46.5 10.5 %collective-permute-start.13 = (bf16[96,512]{1,0:T(8,128)(2,1)}, bf16[96,512]{1,0:T(8,128)(2,1)S(1)}, u32[]{:S(2)}, u32[]{:S(2)}) collective-permute-start(bf16[96,512]{1,0:T(8,128)(2,1)} %get-tuple-element.50), channel_id=1, source_target_pairs={{0,20},{1,21},{2,30},{3,31},{4,16},{5,17},{6,26},{7,27},{8,28},{9,... | collective-permute-start | bytes 294920 | tf_op jit(solution)/shard_map/ppermute | solution.py:1117
  46.7 10.4 %collective-permute-start.10 = (bf16[96,512]{1,0:T(8,128)(2,1)}, bf16[96,512]{1,0:T(8,128)(2,1)S(1)}, u32[]{:S(2)}, u32[]{:S(2)}) collective-permute-start(bf16[96,512]{1,0:T(8,128)(2,1)} %get-tuple-element.47), channel_id=1, source_target_pairs={{0,8},{4,12},{8,0},{12,4},{16,24},{20,28},{24,16},{28,20},{1,9},{5... | collective-permute-start | bytes 294920 | tf_op jit(solution)/shard_map/ppermute | solution.py:1078
  47.7 10.1 %collective-permute-start.11 = (bf16[96,512]{1,0:T(8,128)(2,1)}, bf16[96,512]{1,0:T(8,128)(2,1)S(1)}, u32[]{:S(2)}, u32[]{:S(2)}) collective-permute-start(bf16[96,512]{1,0:T(8,128)(2,1)} %get-tuple-element.48), channel_id=1, source_target_pairs={{0,12},{4,8},{8,4},{12,0},{16,28},{20,24},{24,20},{28,16},{1,13},{... | collective-permute-start | bytes 294920 | tf_op jit(solution)/shard_map/ppermute | solution.py:1078
  49.1 8.0 %copy-start = (bf16[96,512]{1,0:T(8,128)(2,1)}, bf16[96,512]{1,0:T(8,128)(2,1)S(1)}, u32[]{:S(2)}) copy-start(bf16[96,512]{1,0:T(8,128)(2,1)S(1)} %collective-permute-done.9.refs_1_) | copy-start | bytes 294916
  49.1 9.7 %collective-permute-start.16 = (bf16[96,512]{1,0:T(8,128)(2,1)}, bf16[96,512]{1,0:T(8,128)(2,1)S(1)}, u32[]{:S(2)}, u32[]{:S(2)}) collective-permute-start(bf16[96,512]{1,0:T(8,128)(2,1)} %get-tuple-element.45.refs_0_), channel_id=1, source_target_pairs={{0,1},{1,0},{2,3},{3,2},{4,5},{5,4},{6,7},{7,6},{8,9},{9,8},{10,11... | collective-permute-start | bytes 294920 | tf_op jit(solution)/shard_map/ppermute | solution.py:1078
  54.0 8.4 %copy-start.1 = (bf16[96,512]{1,0:T(8,128)(2,1)}, bf16[96,512]{1,0:T(8,128)(2,1)S(1)}, u32[]{:S(2)}) copy-start(bf16[96,512]{1,0:T(8,128)(2,1)S(1)} %collective-permute-done.12.refs_4_) | copy-start | bytes 294916
  54.0 4.9 %collective-permute-start.14 = (bf16[96,512]{1,0:T(8,128)(2,1)S(1)}, bf16[96,512]{1,0:T(8,128)(2,1)S(1)}, u32[]{:S(2)}, u32[]{:S(2)}) collective-permute-start(bf16[96,512]{1,0:T(8,128)(2,1)S(1)} %collective-permute-done.12.refs_4_), channel_id=1, source_target_pairs={{0,2},{1,3},{2,0},{3,1},{4,6},{5,7},{6,4},{7,5},{8,10},{9,11},{10,... | collective-permute-start | bytes 294920 | tf_op jit(solution)/shard_map/ppermute | solution.py:1078
  57.1 6.3 %copy-start.2 = (bf16[96,512]{1,0:T(8,128)(2,1)}, bf16[96,512]{1,0:T(8,128)(2,1)S(1)}, u32[]{:S(2)}) copy-start(bf16[96,512]{1,0:T(8,128)(2,1)S(1)} %collective-permute-done.13.refs_5_) | copy-start | bytes 294916
  57.1 3.5 %collective-permute-start.15 = (bf16[96,512]{1,0:T(8,128)(2,1)S(1)}, bf16[96,512]{1,0:T(8,128)(2,1)S(1)}, u32[]{:S(2)}, u32[]{:S(2)}) collective-permute-start(bf16[96,512]{1,0:T(8,128)(2,1)S(1)} %collective-permute-done.13.refs_5_), channel_id=1, source_target_pairs={{0,2},{1,3},{2,0},{3,1},{4,6},{5,7},{6,4},{7,5},{8,10},{9,11},{10,... | collective-permute-start | bytes 294920 | tf_op jit(solution)/shard_map/ppermute | solution.py:1078
  57.1 6.3 %copy-start.3 = (bf16[96,512]{1,0:T(8,128)(2,1)}, bf16[96,512]{1,0:T(8,128)(2,1)S(1)}, u32[]{:S(2)}) copy-start(bf16[96,512]{1,0:T(8,128)(2,1)S(1)} %collective-permute-done.10.refs_2_) | copy-start | bytes 294916
  57.1 5.3 %collective-permute-start.17 = (bf16[96,512]{1,0:T(8,128)(2,1)S(1)}, bf16[96,512]{1,0:T(8,128)(2,1)S(1)}, u32[]{:S(2)}, u32[]{:S(2)}) collective-permute-start(bf16[96,512]{1,0:T(8,128)(2,1)S(1)} %collective-permute-done.9.refs_1_), channel_id=1, source_target_pairs={{0,1},{1,0},{2,3},{3,2},{4,5},{5,4},{6,7},{7,6},{8,9},{9,8},{10,11... | collective-permute-start | bytes 294920 | tf_op jit(solution)/shard_map/ppermute | solution.py:1078
  57.9 5.9 %copy-start.4 = (bf16[96,512]{1,0:T(8,128)(2,1)}, bf16[96,512]{1,0:T(8,128)(2,1)S(1)}, u32[]{:S(2)}) copy-start(bf16[96,512]{1,0:T(8,128)(2,1)S(1)} %collective-permute-done.11.refs_3_) | copy-start | bytes 294916
  57.9 4.6 %collective-permute-start.18 = (bf16[96,512]{1,0:T(8,128)(2,1)S(1)}, bf16[96,512]{1,0:T(8,128)(2,1)S(1)}, u32[]{:S(2)}, u32[]{:S(2)}) collective-permute-start(bf16[96,512]{1,0:T(8,128)(2,1)S(1)} %collective-permute-done.10.refs_2_), channel_id=1, source_target_pairs={{0,1},{1,0},{2,3},{3,2},{4,5},{5,4},{6,7},{7,6},{8,9},{9,8},{10,11... | collective-permute-start | bytes 294920 | tf_op jit(solution)/shard_map/ppermute | solution.py:1078
  58.8 5.1 %copy-start.5 = (bf16[96,512]{1,0:T(8,128)(2,1)}, bf16[96,512]{1,0:T(8,128)(2,1)S(1)}, u32[]{:S(2)}) copy-start(bf16[96,512]{1,0:T(8,128)(2,1)S(1)} %collective-permute-done.16.refs_8_) | copy-start | bytes 294916
  58.8 4.6 %collective-permute-start.20 = (bf16[96,512]{1,0:T(8,128)(2,1)S(1)}, bf16[96,512]{1,0:T(8,128)(2,1)S(1)}, u32[]{:S(2)}, u32[]{:S(2)}) collective-permute-start(bf16[96,512]{1,0:T(8,128)(2,1)S(1)} %collective-permute-done.12.refs_4_), channel_id=1, source_target_pairs={{0,1},{1,0},{2,3},{3,2},{4,5},{5,4},{6,7},{7,6},{8,9},{9,8},{10,11... | collective-permute-start | bytes 294920 | tf_op jit(solution)/shard_map/ppermute | solution.py:1078
  58.9 5.1 %copy-start.6 = (bf16[96,512]{1,0:T(8,128)(2,1)}, bf16[96,512]{1,0:T(8,128)(2,1)S(1)}, u32[]{:S(2)}) copy-start(bf16[96,512]{1,0:T(8,128)(2,1)S(1)} %collective-permute-done.14.refs_6_) | copy-start | bytes 294916
  58.9 4.5 %collective-permute-start.21 = (bf16[96,512]{1,0:T(8,128)(2,1)S(1)}, bf16[96,512]{1,0:T(8,128)(2,1)S(1)}, u32[]{:S(2)}, u32[]{:S(2)}) collective-permute-start(bf16[96,512]{1,0:T(8,128)(2,1)S(1)} %collective-permute-done.13.refs_5_), channel_id=1, source_target_pairs={{0,1},{1,0},{2,3},{3,2},{4,5},{5,4},{6,7},{7,6},{8,9},{9,8},{10,11... | collective-permute-start | bytes 294920 | tf_op jit(solution)/shard_map/ppermute | solution.py:1078
  60.5 3.4 %copy-start.7 = (bf16[96,512]{1,0:T(8,128)(2,1)}, bf16[96,512]{1,0:T(8,128)(2,1)S(1)}, u32[]{:S(2)}) copy-start(bf16[96,512]{1,0:T(8,128)(2,1)S(1)} %collective-permute-done.15.refs_7_) | copy-start | bytes 294916
  60.5 2.8 %collective-permute-start.19 = (bf16[96,512]{1,0:T(8,128)(2,1)S(1)}, bf16[96,512]{1,0:T(8,128)(2,1)S(1)}, u32[]{:S(2)}, u32[]{:S(2)}) collective-permute-start(bf16[96,512]{1,0:T(8,128)(2,1)S(1)} %collective-permute-done.11.refs_3_), channel_id=1, source_target_pairs={{0,1},{1,0},{2,3},{3,2},{4,5},{5,4},{6,7},{7,6},{8,9},{9,8},{10,11... | collective-permute-start | bytes 294920 | tf_op jit(solution)/shard_map/ppermute | solution.py:1078
  62.4 1.5 %copy-start.8 = (bf16[96,512]{1,0:T(8,128)(2,1)}, bf16[96,512]{1,0:T(8,128)(2,1)S(1)}, u32[]{:S(2)}) copy-start(bf16[96,512]{1,0:T(8,128)(2,1)S(1)} %collective-permute-done.17.refs_9_) | copy-start | bytes 294916
  62.4 1.4 %collective-permute-start.22 = (bf16[96,512]{1,0:T(8,128)(2,1)S(1)}, bf16[96,512]{1,0:T(8,128)(2,1)S(1)}, u32[]{:S(2)}, u32[]{:S(2)}) collective-permute-start(bf16[96,512]{1,0:T(8,128)(2,1)S(1)} %collective-permute-done.14.refs_6_), channel_id=1, source_target_pairs={{0,1},{1,0},{2,3},{3,2},{4,5},{5,4},{6,7},{7,6},{8,9},{9,8},{10,11... | collective-permute-start | bytes 294920 | tf_op jit(solution)/shard_map/ppermute | solution.py:1078
  62.5 1.5 %copy-start.9 = (bf16[96,512]{1,0:T(8,128)(2,1)}, bf16[96,512]{1,0:T(8,128)(2,1)S(1)}, u32[]{:S(2)}) copy-start(bf16[96,512]{1,0:T(8,128)(2,1)S(1)} %collective-permute-done.18.refs_10_) | copy-start | bytes 294916
  62.5 1.4 %collective-permute-start.23 = (bf16[96,512]{1,0:T(8,128)(2,1)S(1)}, bf16[96,512]{1,0:T(8,128)(2,1)S(1)}, u32[]{:S(2)}, u32[]{:S(2)}) collective-permute-start(bf16[96,512]{1,0:T(8,128)(2,1)S(1)} %collective-permute-done.15.refs_7_), channel_id=1, source_target_pairs={{0,1},{1,0},{2,3},{3,2},{4,5},{5,4},{6,7},{7,6},{8,9},{9,8},{10,11... | collective-permute-start | bytes 294920 | tf_op jit(solution)/shard_map/ppermute | solution.py:1078
  63.4 0.6 copy-start.12
  63.4 0.7 copy-start.10
  63.4 0.7 copy-start.11
  63.8 0.6 copy-start.13
  63.9 0.6 copy-start.14
  72.8 2.7 %collective-permute-start.24 = (bf16[768,512]{1,0:T(8,128)(2,1)}, bf16[768,512]{1,0:T(8,128)(2,1)}, u32[]{:S(2)}, u32[]{:S(2)}) collective-permute-start(bf16[768,512]{1,0:T(8,128)(2,1)} %get-tuple-element.54), channel_id=1, source_target_pairs={{0,1},{1,0},{2,3},{3,2},{4,5},{5,4},{6,7},{7,6},{8,9},{9,8},{10,11... | collective-permute-start | bytes 2359304 | tf_op jit(solution)/shard_map/ppermute | solution.py:1078
  73.2 9.1 %collective-permute-start.32 = (bf16[8,64,256]{2,1,0:T(8,128)(2,1)}, bf16[8,64,256]{2,1,0:T(8,128)(2,1)}, u32[]{:S(2)}, u32[]{:S(2)}) collective-permute-start(bf16[8,64,256]{2,1,0:T(8,128)(2,1)} %choose.1.refs_13_), channel_id=1, source_target_pairs={{0,4},{4,0},{8,12},{12,8},{16,20},{20,16},{24,28},{28,24},{1,5},{5... | collective-permute-start | bytes 786440 | tf_op jit(solution)/shard_map/ppermute | solution.py:1078
  77.9 6.4 %collective-permute-start.25 = (bf16[96,512]{1,0:T(8,128)(2,1)}, bf16[96,512]{1,0:T(8,128)(2,1)}, u32[]{:S(2)}, u32[]{:S(2)}) collective-permute-start(bf16[96,512]{1,0:T(8,128)(2,1)} %get-tuple-element.57), channel_id=1, source_target_pairs={{0,4},{4,0},{8,12},{12,8},{16,20},{20,16},{24,28},{28,24},{1,5},{5... | collective-permute-start | bytes 294920 | tf_op jit(solution)/shard_map/ppermute | solution.py:1078
  79.6 6.2 %collective-permute-start.26 = (bf16[96,512]{1,0:T(8,128)(2,1)}, bf16[96,512]{1,0:T(8,128)(2,1)}, u32[]{:S(2)}, u32[]{:S(2)}) collective-permute-start(bf16[96,512]{1,0:T(8,128)(2,1)} %get-tuple-element.58), channel_id=1, source_target_pairs={{0,8},{4,12},{8,0},{12,4},{16,24},{20,28},{24,16},{28,20},{1,9},{5... | collective-permute-start | bytes 294920 | tf_op jit(solution)/shard_map/ppermute | solution.py:1078
  79.6 14.3 %collective-permute-start.27 = (bf16[96,512]{1,0:T(8,128)(2,1)}, bf16[96,512]{1,0:T(8,128)(2,1)}, u32[]{:S(2)}, u32[]{:S(2)}) collective-permute-start(bf16[96,512]{1,0:T(8,128)(2,1)} %get-tuple-element.59), channel_id=1, source_target_pairs={{0,12},{4,8},{8,4},{12,0},{16,28},{20,24},{24,20},{28,16},{1,13},{... | collective-permute-start | bytes 294920 | tf_op jit(solution)/shard_map/ppermute | solution.py:1078
  80.9 13.0 %collective-permute-start.28 = (bf16[96,512]{1,0:T(8,128)(2,1)}, bf16[96,512]{1,0:T(8,128)(2,1)}, u32[]{:S(2)}, u32[]{:S(2)}) collective-permute-start(bf16[96,512]{1,0:T(8,128)(2,1)} %get-tuple-element.60), channel_id=1, source_target_pairs={{0,16},{4,20},{8,24},{12,28},{16,0},{20,4},{24,8},{28,12},{1,17},{... | collective-permute-start | bytes 294920 | tf_op jit(solution)/shard_map/ppermute | solution.py:1078
  82.3 13.2 %collective-permute-start.29 = (bf16[96,512]{1,0:T(8,128)(2,1)}, bf16[96,512]{1,0:T(8,128)(2,1)}, u32[]{:S(2)}, u32[]{:S(2)}) collective-permute-start(bf16[96,512]{1,0:T(8,128)(2,1)} %get-tuple-element.61), channel_id=1, source_target_pairs={{0,20},{4,16},{8,28},{12,24},{16,4},{20,0},{24,12},{28,8},{1,21},{... | collective-permute-start | bytes 294920 | tf_op jit(solution)/shard_map/ppermute | solution.py:1078
  84.3 14.1 %collective-permute-start.30 = (bf16[96,512]{1,0:T(8,128)(2,1)}, bf16[96,512]{1,0:T(8,128)(2,1)}, u32[]{:S(2)}, u32[]{:S(2)}) collective-permute-start(bf16[96,512]{1,0:T(8,128)(2,1)} %get-tuple-element.62), channel_id=1, source_target_pairs={{0,24},{4,28},{8,16},{12,20},{16,8},{20,12},{24,0},{28,4},{1,25},{... | collective-permute-start | bytes 294920 | tf_op jit(solution)/shard_map/ppermute | solution.py:1078
  85.8 15.6 %collective-permute-start.31 = (bf16[96,512]{1,0:T(8,128)(2,1)}, bf16[96,512]{1,0:T(8,128)(2,1)}, u32[]{:S(2)}, u32[]{:S(2)}) collective-permute-start(bf16[96,512]{1,0:T(8,128)(2,1)} %get-tuple-element.63), channel_id=1, source_target_pairs={{0,28},{4,24},{8,20},{12,16},{16,12},{20,8},{24,4},{28,0},{1,29},{... | collective-permute-start | bytes 294920 | tf_op jit(solution)/shard_map/ppermute | solution.py:1078
  104.2 6.9 %collective-permute-start.33 = (bf16[256,512]{1,0:T(8,128)(2,1)}, bf16[256,512]{1,0:T(8,128)(2,1)S(1)}, u32[]{:S(2)}, u32[]{:S(2)}) collective-permute-start(bf16[256,512]{1,0:T(8,128)(2,1)} %combine.1), channel_id=1, source_target_pairs={{0,2},{1,3},{2,0},{3,1},{4,6},{5,7},{6,4},{7,5},{8,10},{9,11},{10,... | collective-permute-start | bytes 786440 | tf_op jit(solution)/shard_map/ppermute | solution.py:1078
  112.2 3.3 %collective-permute-start.34 = (bf16[256,512]{1,0:T(8,128)(2,1)S(1)}, bf16[256,512]{1,0:T(8,128)(2,1)S(1)}, u32[]{:S(2)}, u32[]{:S(2)}) collective-permute-start(bf16[256,512]{1,0:T(8,128)(2,1)S(1)} %add_convert_fusion), channel_id=1, source_target_pairs={{0,1},{1,0},{2,3},{3,2},{4,5},{5,4},{6,7},{7,6},{8,9},{9,8},{10,11... | collective-permute-start | bytes 786440 | tf_op jit(solution)/shard_map/ppermute | solution.py:1078

commit v4 on v3

--- a/solution.py
+++ b/solution.py
@@ -277,7 +277,7 @@
             w = jnp.where(member == g, w_p[...].astype(F32), 0.0).astype(BF16)
             o_p = jnp.dot(w, pv_v[g], preferred_element_type=F32)
             for b in range(cols // LANES):
-                o_v[b] += o_p[:, b * LANES : (b + 1) * LANES]
+                o_v[b, 0:tile_rows, :] += o_p[:, b * LANES : (b + 1) * LANES]
             return carry
 
         low, high = group_range(tile)
@@ -438,7 +438,7 @@
             pltpu.VMEM((rows * heads, prompt_rows), F32),
             pltpu.VMEM((rows * heads, width_t), F32),
             pltpu.VMEM((TILE * heads, prompt_rows), BF16),
-            pltpu.VMEM((cols // LANES, TILE * heads, LANES), F32),
+            pltpu.VMEM((cols // LANES, TILE * heads + 8, LANES), F32),
             pltpu.VMEM((rows, cols), BF16),
             pltpu.VMEM((rows * heads, cols), BF16),
             pltpu.SemaphoreType.DMA((6,)),
@@ -686,7 +686,7 @@
     own = refs[:replicas]
     pair = refs[replicas : 2 * replicas]
     wg_hbm, wu_hbm, wd_hbm = refs[2 * replicas : 2 * replicas + 3]
-    keep_ref, give_ref, x_own, x_pair, wg, wu, wd, act, sem, xsem = refs[-10:]
+    keep_hbm, give_hbm, keep_ref, give_ref, x_own, x_pair, wg, wu, wd, act, sem, xsem, osem = refs[-13:]
     tp = lax.axis_index("tp")
     core = tp & 1
     size, half = own[0].shape
@@ -730,8 +730,16 @@
         gate = product(wg, rows)
         act[:, at : at + n] = (jax.nn.gelu(gate, approximate=True) * product(wu, rows)).astype(BF16)
     down.wait()
+    leave = [
+        pltpu.make_async_copy(give_ref, give_hbm, osem.at[0]),
+        pltpu.make_async_copy(keep_ref, keep_hbm, osem.at[1]),
+    ]
     give_ref[...] = jnp.dot(act[...], wd[:, there], preferred_element_type=F32).astype(BF16)
+    leave[0].start()
     keep_ref[...] = jnp.dot(act[...], wd[:, here], preferred_element_type=F32).astype(BF16)
+    leave[1].start()
+    for copy in leave:
+        copy.wait()
 
 
 def expert(own, pair, w_gate, w_up, w_down, pieces):
@@ -739,15 +747,16 @@
     size, half = own[0].shape
     _, width, hidden = w_gate.shape
     total = replicas * size
-    vm = pl.BlockSpec(memory_space=pltpu.VMEM)
     hbm = pl.BlockSpec(memory_space=pl.ANY)
     shape = jax.ShapeDtypeStruct((total, half), BF16)
     return pl.pallas_call(
         functools.partial(expert_kernel, replicas, pieces),
         out_shape=(shape, shape),
         in_specs=[hbm] * (2 * replicas + 3),
-        out_specs=(vm, vm),
+        out_specs=(hbm, hbm),
         scratch_shapes=[
+            pltpu.VMEM((total, half), BF16),
+            pltpu.VMEM((total, half), BF16),
             pltpu.VMEM((total, half), BF16),
             pltpu.VMEM((total, half), BF16),
             pltpu.VMEM((hidden, width), BF16),
@@ -756,6 +765,7 @@
             pltpu.VMEM((total, hidden), BF16),
             pltpu.SemaphoreType.DMA((3, len(pieces_of(hidden, 256)))),
             pltpu.SemaphoreType.DMA((2, replicas)),
+            pltpu.SemaphoreType.DMA((2,)),
         ],
         compiler_params=pltpu.CompilerParams(vmem_limit_bytes=VMEM_BYTES),
         cost_estimate=pl.CostEstimate(flops=3_400_000_000, bytes_accessed=8_000_000, transcendentals=600_000),
@@ -1015,7 +1025,9 @@
         to = plan_sm[0, 16 + m]
         return to, [
             pltpu.make_async_copy(
-                slabs.at[2 * m + side], out_hbm.at[side, to], out_sem.at[2 * m + side]
+                slabs.at[2 * m + side],
+                out_hbm.at[side, jnp.maximum(to, 0)],
+                out_sem.at[2 * m + side],
             )
             for side in range(2)
         ]

time: 117 us -> 117 us (level)
  no operation moved by 1% of the time
where the time goes in v4:
time: 117 us
  Pallas kernels  51.7 us (44%)
  starting transfers between devices  34 us (29%)
  waiting for transfers between devices  25.9 us (22%)
  other arithmetic  2.06 us (2%)
  local copies, waits for them, and re-layouts  1.94 us (2%)
    ppermute x33, starting transfers between devices, across(): return lambda v: lax.ppermute(v, axis, [(i, i ^ k) for i in range(size)])  32.6 us
    ppermute x33, waiting for transfers between devices, across(): return lambda v: lax.ppermute(v, axis, [(i, i ^ k) for i in range(size)])  19.4 us
    pallas_call x1, Pallas kernels, attention(): pl.pallas_call(attention_kernel, out_shape=(jax.ShapeDtypeStruct((rows, c...  18.2 us
    pallas_call x1, Pallas kernels, expert(): pl.pallas_call(functools.partial(expert_kernel, replicas, pieces), out_sh...  8.22 us
    ppermute x2, waiting for transfers between devices, far(): return lax.ppermute(blocks[near + f], ('req', 'tp'), pairs)  6.54 us
    pallas_call x1, Pallas kernels, dispatch(): pl.pallas_call(functools.partial(dispatch_kernel, pieces, replicas), out_...  4.97 us
    pallas_call x1, Pallas kernels, make_gates(): pl.pallas_call(functools.partial(gates_kernel, cap, replicas), out_shape=...  4.43 us
    pallas_call x1, Pallas kernels, project(): pl.pallas_call(project_kernel, out_shape=(jax.ShapeDtypeStruct((rows, col...  3.48 us
  transfers between devices with their start and end apart: 35, of which 13 were waited for; matrix products, arithmetic and copies ran while one was open for 1% of the time, Pallas kernels for 31%

profile of v4, /device:TPU:11, one launch (start us, length us, event | category | flops | bytes accessed | tf_op | source)
XLA Modules:
  0.0 116.6 jit_solution(14975300791589280779)
XLA Ops:
  0.6 0.7 collective-permute-start.3
  1.4 0.3 collective-permute-start.4
  1.6 3.5 %project.1 = (bf16[256,256]{1,0:T(8,128)(2,1)}, f32[256,256]{1,0:T(8,128)}, f32[256,256]{1,0:T(8,128)}, bf16[8,64,256]{2,1,0:T(8,128)(2,1)}) custom-call(s32[2048]{0:T(1024)} %slots_hbm.1, s32[256]{0:T(256)} %tlen_hbm.3, bf16[256,1024]{1,0:T(8,128)(2,1)} %refs_8_.1, f32[1,1024]{1,0:T(1,128)} %bitcast.11, bf16[1024,256]{1,0:T(8,128)(2,1)} %wq_hbm.1, ...), custom_call_target="tpu_custom_call" | custom-call | flops 400000000 | bytes 3000000 | tf_op jit(solution)/shard_map/project/pallas_call | solution.py:370
  5.1 0.1 collective-permute-start.6
  5.2 2.5 %collective-permute-start.7 = (bf16[8,64,256]{2,1,0:T(8,128)(2,1)}, bf16[8,64,256]{2,1,0:T(8,128)(2,1)}, u32[]{:S(2)}, u32[]{:S(2)}) collective-permute-start(bf16[8,64,256]{2,1,0:T(8,128)(2,1)} %get-tuple-element.40.refs_0_), channel_id=1, source_target_pairs={{0,16},{4,20},{8,24},{12,28},{16,0},{20,4},{24,8},{28,12},{1,17},{... | collective-permute-start | bytes 786440 | tf_op jit(solution)/shard_map/ppermute | solution.py:1090
  7.7 0.2 collective-permute-start.8
  7.8 0.0 collective-permute-done.3.refs_5_
  7.8 1.2 %collective-permute-start.5 = (bf16[256,1024]{1,0:T(8,128)(2,1)}, bf16[256,1024]{1,0:T(8,128)(2,1)}, u32[]{:S(2)}, u32[]{:S(2)}) collective-permute-start(bf16[256,1024]{1,0:T(8,128)(2,1)} %collective-permute-done.3.refs_5_), channel_id=1, source_target_pairs={{0,2},{1,3},{2,0},{3,1},{4,6},{5,7},{6,4},{7,5},{8,10},{9,11},{10,... | collective-permute-start | bytes 1572872 | tf_op jit(solution)/shard_map/ppermute | solution.py:1090
  9.1 18.2 %attention.1 = (bf16[256,256]{1,0:T(8,128)(2,1)}, bf16[2,256,64,256]{3,2,1,0:T(8,128)(2,1)}) custom-call(s32[256]{0:T(256)} %group_hbm.1, s32[8]{0:T(128)} %plen_hbm.1, s32[256]{0:T(256)} %tlen_hbm.3, s32[1,256]{1,0:T(1,128)} %bitcast.17, s32[577]{0:T(1024)} %bucket_hbm.1, f32[4,32]{1,0:T(4,128)} %bitcast.16, bf16[256,256]{1,0:T(8,128)(2,1)} %get-tuple-element.36.q_hbm, ...), custom_call_target="tpu_custom_call" | custom-call | flops 8000000000 | bytes 45000000 | tf_op jit(solution)/shard_map/attention/pallas_call | solution.py:413
  27.3 1.5 %collective-permute-start = (bf16[256,256]{1,0:T(8,128)(2,1)}, bf16[256,256]{1,0:T(8,128)(2,1)}, u32[]{:S(2)}, u32[]{:S(2)}) collective-permute-start(bf16[256,256]{1,0:T(8,128)(2,1)} %get-tuple-element.39.refs_0_), channel_id=1, source_target_pairs={{0,1},{1,0},{2,3},{3,2},{4,5},{5,4},{6,7},{7,6},{8,9},{9,8},{10,11... | collective-permute-start | bytes 393224 | tf_op jit(solution)/shard_map/ppermute | solution.py:1090
  28.8 0.3 collective-permute-start.1
  29.1 1.8 %collective-permute-done.8.refs_3_ = bf16[8,64,256]{2,1,0:T(8,128)(2,1)} collective-permute-done((bf16[8,64,256]{2,1,0:T(8,128)(2,1)}, bf16[8,64,256]{2,1,0:T(8,128)(2,1)}, u32[]{:S(2)}, u32[]{:S(2)}) %collective-permute-start.8) | collective-permute-done | bytes 262176 | tf_op jit(solution)/shard_map/ppermute | solution.py:1090
  30.9 2.5 %collective-permute-start.2 = (bf16[256,256]{1,0:T(8,128)(2,1)}, bf16[256,256]{1,0:T(8,128)(2,1)}, u32[]{:S(2)}, u32[]{:S(2)}) collective-permute-start(bf16[256,256]{1,0:T(8,128)(2,1)} %get-tuple-element.39.refs_0_), channel_id=1, source_target_pairs={{0,3},{1,2},{2,1},{3,0},{4,7},{5,6},{6,5},{7,4},{8,11},{9,10},{10,... | collective-permute-start | bytes 393224 | tf_op jit(solution)/shard_map/ppermute | solution.py:1090
  33.4 1.3 %reshape.7.slots_ref.refs_18_ = s32[8,256]{1,0:T(8,128)} reshape(s32[2048]{0:T(1024)} %slots_hbm.1) | data formatting | bytes 16384 | tf_op jit(solution)/shard_map/reshape | solution.py:1113
  34.7 1.8 %plan.1 = (bf16[768,256]{1,0:T(8,128)(2,1)}, bf16[128,512]{1,0:T(8,128)(2,1)}, bf16[256,128]{1,0:T(8,128)(2,1)}, bf16[128,128]{1,0:T(8,128)(2,1)}, s32[8,128]{1,0:T(8,128)}) custom-call(s32[8,256]{1,0:T(8,128)} %reshape.7.slots_ref.refs_18_, s32[2,256]{1,0:T(2,128)} %bitcast.9, bf16[256,256]{1,0:T(8,128)(2,1)} %get-tuple-element.39.refs_0_, ...), custom_call_target="tpu_custom_call" | custom-call | tf_op jit(solution)/shard_map/plan/pallas_call | solution.py:556
  36.5 2.4 %choose.1.refs_13_ = bf16[8,64,256]{2,1,0:T(8,128)(2,1)} custom-call(s32[8,128]{1,0:T(8,128)} %get-tuple-element.44.plan_hbm.refs_16_, bf16[8,64,256]{2,1,0:T(8,128)(2,1)} %get-tuple-element.40.refs_0_, bf16[8,64,256]{2,1,0:T(8,128)(2,1)} %collective-permute-done.6.refs_1_, bf16[8,64,256]{2,1,0:T(8,128)(2,1)} %collective-permute-done.7.refs_2_, ...), custom_call_target="tpu_custom_call" | custom-call | tf_op jit(solution)/shard_map/choose/pallas_call | solution.py:999
  39.0 5.0 %dispatch.1 = (bf16[256,1024]{1,0:T(8,128)(2,1)}, bf16[96,512]{1,0:T(8,128)(2,1)}, bf16[96,512]{1,0:T(8,128)(2,1)}, bf16[96,512]{1,0:T(8,128)(2,1)}, bf16[96,512...) custom-call(bf16[256,256]{1,0:T(8,128)(2,1)} %get-tuple-element.39.refs_0_, ...), custom_call_target="tpu_custom_call" | custom-call | flops 1200000000 | bytes 6000000 | tf_op jit(solution)/shard_map/dispatch/pallas_call | solution.py:657
  44.0 1.3 %collective-permute-start.9 = (bf16[96,512]{1,0:T(8,128)(2,1)}, bf16[96,512]{1,0:T(8,128)(2,1)S(1)}, u32[]{:S(2)}, u32[]{:S(2)}) collective-permute-start(bf16[96,512]{1,0:T(8,128)(2,1)} %get-tuple-element.46), channel_id=1, source_target_pairs={{0,4},{4,0},{8,12},{12,8},{16,20},{20,16},{24,28},{28,24},{1,5},{5... | collective-permute-start | bytes 294920 | tf_op jit(solution)/shard_map/ppermute | solution.py:1090
  45.3 1.3 %collective-permute-start.12 = (bf16[96,512]{1,0:T(8,128)(2,1)}, bf16[96,512]{1,0:T(8,128)(2,1)S(1)}, u32[]{:S(2)}, u32[]{:S(2)}) collective-permute-start(bf16[96,512]{1,0:T(8,128)(2,1)} %get-tuple-element.49), channel_id=1, source_target_pairs={{0,16},{1,17},{2,26},{3,27},{4,20},{5,21},{6,30},{7,31},{8,24},{9,... | collective-permute-start | bytes 294920 | tf_op jit(solution)/shard_map/ppermute | solution.py:1129
  46.5 0.1 collective-permute-start.13
  46.7 1.2 %collective-permute-start.10 = (bf16[96,512]{1,0:T(8,128)(2,1)}, bf16[96,512]{1,0:T(8,128)(2,1)S(1)}, u32[]{:S(2)}, u32[]{:S(2)}) collective-permute-start(bf16[96,512]{1,0:T(8,128)(2,1)} %get-tuple-element.47), channel_id=1, source_target_pairs={{0,8},{4,12},{8,0},{12,4},{16,24},{20,28},{24,16},{28,20},{1,9},{5... | collective-permute-start | bytes 294920 | tf_op jit(solution)/shard_map/ppermute | solution.py:1090
  47.8 1.3 %collective-permute-start.11 = (bf16[96,512]{1,0:T(8,128)(2,1)}, bf16[96,512]{1,0:T(8,128)(2,1)S(1)}, u32[]{:S(2)}, u32[]{:S(2)}) collective-permute-start(bf16[96,512]{1,0:T(8,128)(2,1)} %get-tuple-element.48), channel_id=1, source_target_pairs={{0,12},{4,8},{8,4},{12,0},{16,28},{20,24},{24,20},{28,16},{1,13},{... | collective-permute-start | bytes 294920 | tf_op jit(solution)/shard_map/ppermute | solution.py:1090
  49.1 0.9 collective-permute-start.16
  50.0 4.1 %collective-permute-done.12.refs_4_ = bf16[96,512]{1,0:T(8,128)(2,1)S(1)} collective-permute-done((bf16[96,512]{1,0:T(8,128)(2,1)}, bf16[96,512]{1,0:T(8,128)(2,1)S(1)}, u32[]{:S(2)}, u32[]{:S(2)}) %collective-permute-start.12) | collective-permute-done | bytes 98336 | tf_op jit(solution)/shard_map/ppermute | solution.py:1129
  54.2 2.4 %collective-permute-done.13.refs_5_ = bf16[96,512]{1,0:T(8,128)(2,1)S(1)} collective-permute-done((bf16[96,512]{1,0:T(8,128)(2,1)}, bf16[96,512]{1,0:T(8,128)(2,1)S(1)}, u32[]{:S(2)}, u32[]{:S(2)}) %collective-permute-start.13) | collective-permute-done | bytes 98336 | tf_op jit(solution)/shard_map/ppermute | solution.py:1129
  56.6 0.8 collective-permute-start.17
  57.4 1.1 collective-permute-start.18
  58.5 0.1 collective-permute-start.20
  58.6 0.8 collective-permute-start.21
  59.4 0.7 collective-permute-done.15.refs_7_
  60.0 1.9 %collective-permute-start.19 = (bf16[96,512]{1,0:T(8,128)(2,1)S(1)}, bf16[96,512]{1,0:T(8,128)(2,1)S(1)}, u32[]{:S(2)}, u32[]{:S(2)}) collective-permute-start(bf16[96,512]{1,0:T(8,128)(2,1)S(1)} %collective-permute-done.11.refs_3_), channel_id=1, source_target_pairs={{0,1},{1,0},{2,3},{3,2},{4,5},{5,4},{6,7},{7,6},{8,9},{9,8},{10,11... | collective-permute-start | bytes 294920 | tf_op jit(solution)/shard_map/ppermute | solution.py:1090
  61.9 0.1 collective-permute-start.22
  62.0 0.5 collective-permute-start.23
  62.5 0.4 collective-permute-done.19.refs_11_
  62.9 0.4 collective-permute-done.22.refs_14_
  63.3 0.2 collective-permute-done.23.refs_15_
  63.5 0.0 copy-done.12
  63.5 0.0 copy-done.10
  63.5 0.1 copy-done.11
  63.6 0.3 copy-done.13
  63.9 0.2 copy-done.14
  64.1 8.2 %expert.1 = (bf16[768,512]{1,0:T(8,128)(2,1)}, bf16[768,512]{1,0:T(8,128)(2,1)}) custom-call(bf16[96,512]{1,0:T(8,128)(2,1)} %get-tuple-element.45.refs_0_, bf16[96,512]{1,0:T(8,128)(2,1)} %copy-done, bf16[96,512]{1,0:T(8,128)(2,1)} %copy-done.3, bf16[96,512]{1,0:T(8,128)(2,1)} %copy-done.4, bf16[96,512]{1,0:T(8,128)(2,1)} %copy-done.1, ...), custom_call_target="tpu_custom_call" | custom-call | flops 3400000000 | bytes 8000000 | tf_op jit(solution)/shard_map/expert/pallas_call | solution.py:752
  72.3 0.4 collective-permute-start.24
  72.7 2.1 %collective-permute-start.32 = (bf16[8,64,256]{2,1,0:T(8,128)(2,1)}, bf16[8,64,256]{2,1,0:T(8,128)(2,1)}, u32[]{:S(2)}, u32[]{:S(2)}) collective-permute-start(bf16[8,64,256]{2,1,0:T(8,128)(2,1)} %choose.1.refs_13_), channel_id=1, source_target_pairs={{0,4},{4,0},{8,12},{12,8},{16,20},{20,16},{24,28},{28,24},{1,5},{5... | collective-permute-start | bytes 786440 | tf_op jit(solution)/shard_map/ppermute | solution.py:1090
  74.8 0.2 collective-permute-done.24.got_hbm
  75.0 2.4 %give_back.1 = (bf16[96,512]{1,0:T(8,128)(2,1)}, bf16[96,512]{1,0:T(8,128)(2,1)}, bf16[96,512]{1,0:T(8,128)(2,1)}, bf16[96,512]{1,0:T(8,128)(2,1)}, bf16[96,512]...) custom-call(bf16[768,512]{1,0:T(8,128)(2,1)} %get-tuple-element.53.keep_hbm, ...), custom_call_target="tpu_custom_call" | custom-call | flops 30000000 | bytes 2500000 | tf_op jit(solution)/shard_map/give_back/pallas_call | solution.py:801
  77.4 2.2 %collective-permute-start.25 = (bf16[96,512]{1,0:T(8,128)(2,1)}, bf16[96,512]{1,0:T(8,128)(2,1)}, u32[]{:S(2)}, u32[]{:S(2)}) collective-permute-start(bf16[96,512]{1,0:T(8,128)(2,1)} %get-tuple-element.57), channel_id=1, source_target_pairs={{0,4},{4,0},{8,12},{12,8},{16,20},{20,16},{24,28},{28,24},{1,5},{5... | collective-permute-start | bytes 294920 | tf_op jit(solution)/shard_map/ppermute | solution.py:1090
  79.6 1.3 %collective-permute-start.27 = (bf16[96,512]{1,0:T(8,128)(2,1)}, bf16[96,512]{1,0:T(8,128)(2,1)}, u32[]{:S(2)}, u32[]{:S(2)}) collective-permute-start(bf16[96,512]{1,0:T(8,128)(2,1)} %get-tuple-element.59), channel_id=1, source_target_pairs={{0,12},{4,8},{8,4},{12,0},{16,28},{20,24},{24,20},{28,16},{1,13},{... | collective-permute-start | bytes 294920 | tf_op jit(solution)/shard_map/ppermute | solution.py:1090
  80.9 1.4 %collective-permute-start.28 = (bf16[96,512]{1,0:T(8,128)(2,1)}, bf16[96,512]{1,0:T(8,128)(2,1)}, u32[]{:S(2)}, u32[]{:S(2)}) collective-permute-start(bf16[96,512]{1,0:T(8,128)(2,1)} %get-tuple-element.60), channel_id=1, source_target_pairs={{0,16},{4,20},{8,24},{12,28},{16,0},{20,4},{24,8},{28,12},{1,17},{... | collective-permute-start | bytes 294920 | tf_op jit(solution)/shard_map/ppermute | solution.py:1090
  82.3 2.1 %collective-permute-start.29 = (bf16[96,512]{1,0:T(8,128)(2,1)}, bf16[96,512]{1,0:T(8,128)(2,1)}, u32[]{:S(2)}, u32[]{:S(2)}) collective-permute-start(bf16[96,512]{1,0:T(8,128)(2,1)} %get-tuple-element.61), channel_id=1, source_target_pairs={{0,20},{4,16},{8,28},{12,24},{16,4},{20,0},{24,12},{28,8},{1,21},{... | collective-permute-start | bytes 294920 | tf_op jit(solution)/shard_map/ppermute | solution.py:1090
  84.3 1.5 %collective-permute-start.30 = (bf16[96,512]{1,0:T(8,128)(2,1)}, bf16[96,512]{1,0:T(8,128)(2,1)}, u32[]{:S(2)}, u32[]{:S(2)}) collective-permute-start(bf16[96,512]{1,0:T(8,128)(2,1)} %get-tuple-element.62), channel_id=1, source_target_pairs={{0,24},{4,28},{8,16},{12,20},{16,8},{20,12},{24,0},{28,4},{1,25},{... | collective-permute-start | bytes 294920 | tf_op jit(solution)/shard_map/ppermute | solution.py:1090
  85.8 0.6 collective-permute-start.31
  86.4 3.0 %patch.1 = (bf16[2,256,64,256]{3,2,1,0:T(8,128)(2,1)}, f32[8,128]{1,0:T(8,128)}) custom-call(s32[8,128]{1,0:T(8,128)} %get-tuple-element.44.plan_hbm.refs_16_, bf16[8,64,256]{2,1,0:T(8,128)(2,1)} %get-tuple-element.40.refs_0_, bf16[8,64,256]{2,1,0:T(8,128)(2,1)} %collective-permute-done.6.refs_1_, ...), custom_call_target="tpu_custom_call", output_to_operand_aliasing={{0}: (6, {})} | custom-call | tf_op jit(solution)/shard_map/patch/pallas_call | solution.py:1055
  89.4 4.4 %gates.1 = (bf16[256,768]{1,0:T(8,128)(2,1)}, bf16[256,768]{1,0:T(8,128)(2,1)}, f32[256,128]{1,0:T(8,128)}, bf16[256,512]{1,0:T(8,128)(2,1)}) custom-call(bf16[96,512]{1,0:T(8,128)(2,1)} %get-tuple-element.45.refs_0_, bf16[96,512]{1,0:T(8,128)(2,1)} %copy-done, bf16[96,512]{1,0:T(8,128)(2,1)} %copy-done.3, bf16[96,512]{1,0:T(8,128)(2,1)} %copy-done.4, ...), custom_call_target="tpu_custom_call" | custom-call | flops 200000000 | bytes 6000000 | tf_op jit(solution)/shard_map/gates/pallas_call | solution.py:921
  93.9 1.5 %collective-permute-done.29.refs_5_ = bf16[96,512]{1,0:T(8,128)(2,1)} collective-permute-done((bf16[96,512]{1,0:T(8,128)(2,1)}, bf16[96,512]{1,0:T(8,128)(2,1)}, u32[]{:S(2)}, u32[]{:S(2)}) %collective-permute-start.29) | collective-permute-done | bytes 98336 | tf_op jit(solution)/shard_map/ppermute | solution.py:1090
  95.4 3.3 %collective-permute-done.30.refs_6_ = bf16[96,512]{1,0:T(8,128)(2,1)} collective-permute-done((bf16[96,512]{1,0:T(8,128)(2,1)}, bf16[96,512]{1,0:T(8,128)(2,1)}, u32[]{:S(2)}, u32[]{:S(2)}) %collective-permute-start.30) | collective-permute-done | bytes 98336 | tf_op jit(solution)/shard_map/ppermute | solution.py:1090
  98.7 2.8 %collective-permute-done.31.refs_7_ = bf16[96,512]{1,0:T(8,128)(2,1)} collective-permute-done((bf16[96,512]{1,0:T(8,128)(2,1)}, bf16[96,512]{1,0:T(8,128)(2,1)}, u32[]{:S(2)}, u32[]{:S(2)}) %collective-permute-start.31) | collective-permute-done | bytes 98336 | tf_op jit(solution)/shard_map/ppermute | solution.py:1090
  101.5 2.7 %combine.1 = bf16[256,512]{1,0:T(8,128)(2,1)} custom-call(bf16[96,512]{1,0:T(8,128)(2,1)} %get-tuple-element.56.refs_0_, bf16[96,512]{1,0:T(8,128)(2,1)} %collective-permute-done.25.refs_1_, bf16[96,512]{1,0:T(8,128)(2,1)} %collective-permute-done.26.refs_2_, bf16[96,512]{1,0:T(8,128)(2,1)} %collective-permute-done.27.refs_3_, ...), custom_call_target="tpu_custom_call" | custom-call | flops 400000000 | bytes 2500000 | tf_op jit(solution)/shard_map/combine/pallas_call | solution.py:968
  104.3 0.1 collective-permute-start.33
  104.4 7.0 %collective-permute-done.33 = bf16[256,512]{1,0:T(8,128)(2,1)S(1)} collective-permute-done((bf16[256,512]{1,0:T(8,128)(2,1)}, bf16[256,512]{1,0:T(8,128)(2,1)S(1)}, u32[]{:S(2)}, u32[]{:S(2)}) %collective-permute-start.33) | collective-permute-done | bytes 262176 | tf_op jit(solution)/shard_map/ppermute | solution.py:1090
  111.3 1.1 add_convert_fusion
  112.5 2.0 %collective-permute-start.34 = (bf16[256,512]{1,0:T(8,128)(2,1)S(1)}, bf16[256,512]{1,0:T(8,128)(2,1)S(1)}, u32[]{:S(2)}, u32[]{:S(2)}) collective-permute-start(bf16[256,512]{1,0:T(8,128)(2,1)S(1)} %add_convert_fusion), channel_id=1, source_target_pairs={{0,1},{1,0},{2,3},{3,2},{4,5},{5,4},{6,7},{7,6},{8,9},{9,8},{10,11... | collective-permute-start | bytes 786440 | tf_op jit(solution)/shard_map/ppermute | solution.py:1090
  114.5 1.2 collective-permute-done.34
  115.7 0.9 maximum_select_fusion
  (49 shorter events, 0.1 us)
Async XLA Ops:
  0.6 7.2 %collective-permute-start.3 = (bf16[256,1024]{1,0:T(8,128)(2,1)}, bf16[256,1024]{1,0:T(8,128)(2,1)}, u32[]{:S(2)}, u32[]{:S(2)}) collective-permute-start(bf16[256,1024]{1,0:T(8,128)(2,1)} %refs_4_.1), channel_id=1, source_target_pairs={{0,1},{1,0},{2,3},{3,2},{4,5},{5,4},{6,7},{7,6},{8,9},{9,8},{10,11... | collective-permute-start | bytes 1572872 | tf_op jit(solution)/shard_map/ppermute | solution.py:1090
  1.4 33.3 %collective-permute-start.4 = (bf16[256,1024]{1,0:T(8,128)(2,1)}, bf16[256,1024]{1,0:T(8,128)(2,1)}, u32[]{:S(2)}, u32[]{:S(2)}) collective-permute-start(bf16[256,1024]{1,0:T(8,128)(2,1)} %refs_4_.1), channel_id=1, source_target_pairs={{0,2},{1,3},{2,0},{3,1},{4,6},{5,7},{6,4},{7,5},{8,10},{9,11},{10,... | collective-permute-start | bytes 1572872 | tf_op jit(solution)/shard_map/ppermute | solution.py:1090
  5.1 22.1 %collective-permute-start.6 = (bf16[8,64,256]{2,1,0:T(8,128)(2,1)}, bf16[8,64,256]{2,1,0:T(8,128)(2,1)}, u32[]{:S(2)}, u32[]{:S(2)}) collective-permute-start(bf16[8,64,256]{2,1,0:T(8,128)(2,1)} %get-tuple-element.40.refs_0_), channel_id=1, source_target_pairs={{0,8},{4,12},{8,0},{12,4},{16,24},{20,28},{24,16},{28,20},{1,9},{5... | collective-permute-start | bytes 786440 | tf_op jit(solution)/shard_map/ppermute | solution.py:1090
  5.2 23.6 %collective-permute-start.7 = (bf16[8,64,256]{2,1,0:T(8,128)(2,1)}, bf16[8,64,256]{2,1,0:T(8,128)(2,1)}, u32[]{:S(2)}, u32[]{:S(2)}) collective-permute-start(bf16[8,64,256]{2,1,0:T(8,128)(2,1)} %get-tuple-element.40.refs_0_), channel_id=1, source_target_pairs={{0,16},{4,20},{8,24},{12,28},{16,0},{20,4},{24,8},{28,12},{1,17},{... | collective-permute-start | bytes 786440 | tf_op jit(solution)/shard_map/ppermute | solution.py:1090
  7.7 23.2 %collective-permute-start.8 = (bf16[8,64,256]{2,1,0:T(8,128)(2,1)}, bf16[8,64,256]{2,1,0:T(8,128)(2,1)}, u32[]{:S(2)}, u32[]{:S(2)}) collective-permute-start(bf16[8,64,256]{2,1,0:T(8,128)(2,1)} %get-tuple-element.40.refs_0_), channel_id=1, source_target_pairs={{0,24},{4,28},{8,16},{12,20},{16,8},{20,12},{24,0},{28,4},{1,25},{... | collective-permute-start | bytes 786440 | tf_op jit(solution)/shard_map/ppermute | solution.py:1090
  7.8 26.9 %collective-permute-start.5 = (bf16[256,1024]{1,0:T(8,128)(2,1)}, bf16[256,1024]{1,0:T(8,128)(2,1)}, u32[]{:S(2)}, u32[]{:S(2)}) collective-permute-start(bf16[256,1024]{1,0:T(8,128)(2,1)} %collective-permute-done.3.refs_5_), channel_id=1, source_target_pairs={{0,2},{1,3},{2,0},{3,1},{4,6},{5,7},{6,4},{7,5},{8,10},{9,11},{10,... | collective-permute-start | bytes 1572872 | tf_op jit(solution)/shard_map/ppermute | solution.py:1090
  27.3 11.7 %collective-permute-start = (bf16[256,256]{1,0:T(8,128)(2,1)}, bf16[256,256]{1,0:T(8,128)(2,1)}, u32[]{:S(2)}, u32[]{:S(2)}) collective-permute-start(bf16[256,256]{1,0:T(8,128)(2,1)} %get-tuple-element.39.refs_0_), channel_id=1, source_target_pairs={{0,1},{1,0},{2,3},{3,2},{4,5},{5,4},{6,7},{7,6},{8,9},{9,8},{10,11... | collective-permute-start | bytes 393224 | tf_op jit(solution)/shard_map/ppermute | solution.py:1090
  28.8 10.1 %collective-permute-start.1 = (bf16[256,256]{1,0:T(8,128)(2,1)}, bf16[256,256]{1,0:T(8,128)(2,1)}, u32[]{:S(2)}, u32[]{:S(2)}) collective-permute-start(bf16[256,256]{1,0:T(8,128)(2,1)} %get-tuple-element.39.refs_0_), channel_id=1, source_target_pairs={{0,2},{1,3},{2,0},{3,1},{4,6},{5,7},{6,4},{7,5},{8,10},{9,11},{10,... | collective-permute-start | bytes 393224 | tf_op jit(solution)/shard_map/ppermute | solution.py:1090
  30.9 8.1 %collective-permute-start.2 = (bf16[256,256]{1,0:T(8,128)(2,1)}, bf16[256,256]{1,0:T(8,128)(2,1)}, u32[]{:S(2)}, u32[]{:S(2)}) collective-permute-start(bf16[256,256]{1,0:T(8,128)(2,1)} %get-tuple-element.39.refs_0_), channel_id=1, source_target_pairs={{0,3},{1,2},{2,1},{3,0},{4,7},{5,6},{6,5},{7,4},{8,11},{9,10},{10,... | collective-permute-start | bytes 393224 | tf_op jit(solution)/shard_map/ppermute | solution.py:1090
  44.0 5.1 %collective-permute-start.9 = (bf16[96,512]{1,0:T(8,128)(2,1)}, bf16[96,512]{1,0:T(8,128)(2,1)S(1)}, u32[]{:S(2)}, u32[]{:S(2)}) collective-permute-start(bf16[96,512]{1,0:T(8,128)(2,1)} %get-tuple-element.46), channel_id=1, source_target_pairs={{0,4},{4,0},{8,12},{12,8},{16,20},{20,16},{24,28},{28,24},{1,5},{5... | collective-permute-start | bytes 294920 | tf_op jit(solution)/shard_map/ppermute | solution.py:1090
  45.3 8.9 %collective-permute-start.12 = (bf16[96,512]{1,0:T(8,128)(2,1)}, bf16[96,512]{1,0:T(8,128)(2,1)S(1)}, u32[]{:S(2)}, u32[]{:S(2)}) collective-permute-start(bf16[96,512]{1,0:T(8,128)(2,1)} %get-tuple-element.49), channel_id=1, source_target_pairs={{0,16},{1,17},{2,26},{3,27},{4,20},{5,21},{6,30},{7,31},{8,24},{9,... | collective-permute-start | bytes 294920 | tf_op jit(solution)/shard_map/ppermute | solution.py:1129
  46.5 10.0 %collective-permute-start.13 = (bf16[96,512]{1,0:T(8,128)(2,1)}, bf16[96,512]{1,0:T(8,128)(2,1)S(1)}, u32[]{:S(2)}, u32[]{:S(2)}) collective-permute-start(bf16[96,512]{1,0:T(8,128)(2,1)} %get-tuple-element.50), channel_id=1, source_target_pairs={{0,20},{1,21},{2,30},{3,31},{4,16},{5,17},{6,26},{7,27},{8,28},{9,... | collective-permute-start | bytes 294920 | tf_op jit(solution)/shard_map/ppermute | solution.py:1129
  46.7 9.9 %collective-permute-start.10 = (bf16[96,512]{1,0:T(8,128)(2,1)}, bf16[96,512]{1,0:T(8,128)(2,1)S(1)}, u32[]{:S(2)}, u32[]{:S(2)}) collective-permute-start(bf16[96,512]{1,0:T(8,128)(2,1)} %get-tuple-element.47), channel_id=1, source_target_pairs={{0,8},{4,12},{8,0},{12,4},{16,24},{20,28},{24,16},{28,20},{1,9},{5... | collective-permute-start | bytes 294920 | tf_op jit(solution)/shard_map/ppermute | solution.py:1090
  47.8 9.5 %collective-permute-start.11 = (bf16[96,512]{1,0:T(8,128)(2,1)}, bf16[96,512]{1,0:T(8,128)(2,1)S(1)}, u32[]{:S(2)}, u32[]{:S(2)}) collective-permute-start(bf16[96,512]{1,0:T(8,128)(2,1)} %get-tuple-element.48), channel_id=1, source_target_pairs={{0,12},{4,8},{8,4},{12,0},{16,28},{20,24},{24,20},{28,16},{1,13},{... | collective-permute-start | bytes 294920 | tf_op jit(solution)/shard_map/ppermute | solution.py:1090
  49.1 7.5 %copy-start = (bf16[96,512]{1,0:T(8,128)(2,1)}, bf16[96,512]{1,0:T(8,128)(2,1)S(1)}, u32[]{:S(2)}) copy-start(bf16[96,512]{1,0:T(8,128)(2,1)S(1)} %collective-permute-done.9.refs_1_) | copy-start | bytes 294916
  49.1 9.4 %collective-permute-start.16 = (bf16[96,512]{1,0:T(8,128)(2,1)}, bf16[96,512]{1,0:T(8,128)(2,1)S(1)}, u32[]{:S(2)}, u32[]{:S(2)}) collective-permute-start(bf16[96,512]{1,0:T(8,128)(2,1)} %get-tuple-element.45.refs_0_), channel_id=1, source_target_pairs={{0,1},{1,0},{2,3},{3,2},{4,5},{5,4},{6,7},{7,6},{8,9},{9,8},{10,11... | collective-permute-start | bytes 294920 | tf_op jit(solution)/shard_map/ppermute | solution.py:1090
  54.1 7.8 %copy-start.1 = (bf16[96,512]{1,0:T(8,128)(2,1)}, bf16[96,512]{1,0:T(8,128)(2,1)S(1)}, u32[]{:S(2)}) copy-start(bf16[96,512]{1,0:T(8,128)(2,1)S(1)} %collective-permute-done.12.refs_4_) | copy-start | bytes 294916
  54.2 4.4 %collective-permute-start.14 = (bf16[96,512]{1,0:T(8,128)(2,1)S(1)}, bf16[96,512]{1,0:T(8,128)(2,1)S(1)}, u32[]{:S(2)}, u32[]{:S(2)}) collective-permute-start(bf16[96,512]{1,0:T(8,128)(2,1)S(1)} %collective-permute-done.12.refs_4_), channel_id=1, source_target_pairs={{0,2},{1,3},{2,0},{3,1},{4,6},{5,7},{6,4},{7,5},{8,10},{9,11},{10,... | collective-permute-start | bytes 294920 | tf_op jit(solution)/shard_map/ppermute | solution.py:1090
  56.6 6.3 %copy-start.2 = (bf16[96,512]{1,0:T(8,128)(2,1)}, bf16[96,512]{1,0:T(8,128)(2,1)S(1)}, u32[]{:S(2)}) copy-start(bf16[96,512]{1,0:T(8,128)(2,1)S(1)} %collective-permute-done.13.refs_5_) | copy-start | bytes 294916
  56.6 3.5 %collective-permute-start.15 = (bf16[96,512]{1,0:T(8,128)(2,1)S(1)}, bf16[96,512]{1,0:T(8,128)(2,1)S(1)}, u32[]{:S(2)}, u32[]{:S(2)}) collective-permute-start(bf16[96,512]{1,0:T(8,128)(2,1)S(1)} %collective-permute-done.13.refs_5_), channel_id=1, source_target_pairs={{0,2},{1,3},{2,0},{3,1},{4,6},{5,7},{6,4},{7,5},{8,10},{9,11},{10,... | collective-permute-start | bytes 294920 | tf_op jit(solution)/shard_map/ppermute | solution.py:1090
  56.6 6.3 %copy-start.3 = (bf16[96,512]{1,0:T(8,128)(2,1)}, bf16[96,512]{1,0:T(8,128)(2,1)S(1)}, u32[]{:S(2)}) copy-start(bf16[96,512]{1,0:T(8,128)(2,1)S(1)} %collective-permute-done.10.refs_2_) | copy-start | bytes 294916
  56.6 5.3 %collective-permute-start.17 = (bf16[96,512]{1,0:T(8,128)(2,1)S(1)}, bf16[96,512]{1,0:T(8,128)(2,1)S(1)}, u32[]{:S(2)}, u32[]{:S(2)}) collective-permute-start(bf16[96,512]{1,0:T(8,128)(2,1)S(1)} %collective-permute-done.9.refs_1_), channel_id=1, source_target_pairs={{0,1},{1,0},{2,3},{3,2},{4,5},{5,4},{6,7},{7,6},{8,9},{9,8},{10,11... | collective-permute-start | bytes 294920 | tf_op jit(solution)/shard_map/ppermute | solution.py:1090
  57.4 5.9 %copy-start.4 = (bf16[96,512]{1,0:T(8,128)(2,1)}, bf16[96,512]{1,0:T(8,128)(2,1)S(1)}, u32[]{:S(2)}) copy-start(bf16[96,512]{1,0:T(8,128)(2,1)S(1)} %collective-permute-done.11.refs_3_) | copy-start | bytes 294916
  57.4 4.6 %collective-permute-start.18 = (bf16[96,512]{1,0:T(8,128)(2,1)S(1)}, bf16[96,512]{1,0:T(8,128)(2,1)S(1)}, u32[]{:S(2)}, u32[]{:S(2)}) collective-permute-start(bf16[96,512]{1,0:T(8,128)(2,1)S(1)} %collective-permute-done.10.refs_2_), channel_id=1, source_target_pairs={{0,1},{1,0},{2,3},{3,2},{4,5},{5,4},{6,7},{7,6},{8,9},{9,8},{10,11... | collective-permute-start | bytes 294920 | tf_op jit(solution)/shard_map/ppermute | solution.py:1090
  58.5 5.0 %copy-start.5 = (bf16[96,512]{1,0:T(8,128)(2,1)}, bf16[96,512]{1,0:T(8,128)(2,1)S(1)}, u32[]{:S(2)}) copy-start(bf16[96,512]{1,0:T(8,128)(2,1)S(1)} %collective-permute-done.16.refs_8_) | copy-start | bytes 294916
  58.5 4.4 %collective-permute-start.20 = (bf16[96,512]{1,0:T(8,128)(2,1)S(1)}, bf16[96,512]{1,0:T(8,128)(2,1)S(1)}, u32[]{:S(2)}, u32[]{:S(2)}) collective-permute-start(bf16[96,512]{1,0:T(8,128)(2,1)S(1)} %collective-permute-done.12.refs_4_), channel_id=1, source_target_pairs={{0,1},{1,0},{2,3},{3,2},{4,5},{5,4},{6,7},{7,6},{8,9},{9,8},{10,11... | collective-permute-start | bytes 294920 | tf_op jit(solution)/shard_map/ppermute | solution.py:1090
  58.6 4.9 %copy-start.6 = (bf16[96,512]{1,0:T(8,128)(2,1)}, bf16[96,512]{1,0:T(8,128)(2,1)S(1)}, u32[]{:S(2)}) copy-start(bf16[96,512]{1,0:T(8,128)(2,1)S(1)} %collective-permute-done.14.refs_6_) | copy-start | bytes 294916
  58.6 4.3 %collective-permute-start.21 = (bf16[96,512]{1,0:T(8,128)(2,1)S(1)}, bf16[96,512]{1,0:T(8,128)(2,1)S(1)}, u32[]{:S(2)}, u32[]{:S(2)}) collective-permute-start(bf16[96,512]{1,0:T(8,128)(2,1)S(1)} %collective-permute-done.13.refs_5_), channel_id=1, source_target_pairs={{0,1},{1,0},{2,3},{3,2},{4,5},{5,4},{6,7},{7,6},{8,9},{9,8},{10,11... | collective-permute-start | bytes 294920 | tf_op jit(solution)/shard_map/ppermute | solution.py:1090
  60.0 3.4 %copy-start.7 = (bf16[96,512]{1,0:T(8,128)(2,1)}, bf16[96,512]{1,0:T(8,128)(2,1)S(1)}, u32[]{:S(2)}) copy-start(bf16[96,512]{1,0:T(8,128)(2,1)S(1)} %collective-permute-done.15.refs_7_) | copy-start | bytes 294916
  60.0 2.8 %collective-permute-start.19 = (bf16[96,512]{1,0:T(8,128)(2,1)S(1)}, bf16[96,512]{1,0:T(8,128)(2,1)S(1)}, u32[]{:S(2)}, u32[]{:S(2)}) collective-permute-start(bf16[96,512]{1,0:T(8,128)(2,1)S(1)} %collective-permute-done.11.refs_3_), channel_id=1, source_target_pairs={{0,1},{1,0},{2,3},{3,2},{4,5},{5,4},{6,7},{7,6},{8,9},{9,8},{10,11... | collective-permute-start | bytes 294920 | tf_op jit(solution)/shard_map/ppermute | solution.py:1090
  61.9 1.5 %copy-start.8 = (bf16[96,512]{1,0:T(8,128)(2,1)}, bf16[96,512]{1,0:T(8,128)(2,1)S(1)}, u32[]{:S(2)}) copy-start(bf16[96,512]{1,0:T(8,128)(2,1)S(1)} %collective-permute-done.17.refs_9_) | copy-start | bytes 294916
  61.9 1.4 %collective-permute-start.22 = (bf16[96,512]{1,0:T(8,128)(2,1)S(1)}, bf16[96,512]{1,0:T(8,128)(2,1)S(1)}, u32[]{:S(2)}, u32[]{:S(2)}) collective-permute-start(bf16[96,512]{1,0:T(8,128)(2,1)S(1)} %collective-permute-done.14.refs_6_), channel_id=1, source_target_pairs={{0,1},{1,0},{2,3},{3,2},{4,5},{5,4},{6,7},{7,6},{8,9},{9,8},{10,11... | collective-permute-start | bytes 294920 | tf_op jit(solution)/shard_map/ppermute | solution.py:1090
  62.0 1.5 %copy-start.9 = (bf16[96,512]{1,0:T(8,128)(2,1)}, bf16[96,512]{1,0:T(8,128)(2,1)S(1)}, u32[]{:S(2)}) copy-start(bf16[96,512]{1,0:T(8,128)(2,1)S(1)} %collective-permute-done.18.refs_10_) | copy-start | bytes 294916
  62.0 1.4 %collective-permute-start.23 = (bf16[96,512]{1,0:T(8,128)(2,1)S(1)}, bf16[96,512]{1,0:T(8,128)(2,1)S(1)}, u32[]{:S(2)}, u32[]{:S(2)}) collective-permute-start(bf16[96,512]{1,0:T(8,128)(2,1)S(1)} %collective-permute-done.15.refs_7_), channel_id=1, source_target_pairs={{0,1},{1,0},{2,3},{3,2},{4,5},{5,4},{6,7},{7,6},{8,9},{9,8},{10,11... | collective-permute-start | bytes 294920 | tf_op jit(solution)/shard_map/ppermute | solution.py:1090
  62.8 0.6 copy-start.12
  62.9 0.7 copy-start.10
  62.9 0.7 copy-start.11
  63.3 0.6 copy-start.13
  63.4 0.6 copy-start.14
  72.3 2.7 %collective-permute-start.24 = (bf16[768,512]{1,0:T(8,128)(2,1)}, bf16[768,512]{1,0:T(8,128)(2,1)}, u32[]{:S(2)}, u32[]{:S(2)}) collective-permute-start(bf16[768,512]{1,0:T(8,128)(2,1)} %get-tuple-element.54), channel_id=1, source_target_pairs={{0,1},{1,0},{2,3},{3,2},{4,5},{5,4},{6,7},{7,6},{8,9},{9,8},{10,11... | collective-permute-start | bytes 2359304 | tf_op jit(solution)/shard_map/ppermute | solution.py:1090
  72.7 9.5 %collective-permute-start.32 = (bf16[8,64,256]{2,1,0:T(8,128)(2,1)}, bf16[8,64,256]{2,1,0:T(8,128)(2,1)}, u32[]{:S(2)}, u32[]{:S(2)}) collective-permute-start(bf16[8,64,256]{2,1,0:T(8,128)(2,1)} %choose.1.refs_13_), channel_id=1, source_target_pairs={{0,4},{4,0},{8,12},{12,8},{16,20},{20,16},{24,28},{28,24},{1,5},{5... | collective-permute-start | bytes 786440 | tf_op jit(solution)/shard_map/ppermute | solution.py:1090
  77.4 6.9 %collective-permute-start.25 = (bf16[96,512]{1,0:T(8,128)(2,1)}, bf16[96,512]{1,0:T(8,128)(2,1)}, u32[]{:S(2)}, u32[]{:S(2)}) collective-permute-start(bf16[96,512]{1,0:T(8,128)(2,1)} %get-tuple-element.57), channel_id=1, source_target_pairs={{0,4},{4,0},{8,12},{12,8},{16,20},{20,16},{24,28},{28,24},{1,5},{5... | collective-permute-start | bytes 294920 | tf_op jit(solution)/shard_map/ppermute | solution.py:1090
  79.6 6.2 %collective-permute-start.26 = (bf16[96,512]{1,0:T(8,128)(2,1)}, bf16[96,512]{1,0:T(8,128)(2,1)}, u32[]{:S(2)}, u32[]{:S(2)}) collective-permute-start(bf16[96,512]{1,0:T(8,128)(2,1)} %get-tuple-element.58), channel_id=1, source_target_pairs={{0,8},{4,12},{8,0},{12,4},{16,24},{20,28},{24,16},{28,20},{1,9},{5... | collective-permute-start | bytes 294920 | tf_op jit(solution)/shard_map/ppermute | solution.py:1090
  79.6 14.3 %collective-permute-start.27 = (bf16[96,512]{1,0:T(8,128)(2,1)}, bf16[96,512]{1,0:T(8,128)(2,1)}, u32[]{:S(2)}, u32[]{:S(2)}) collective-permute-start(bf16[96,512]{1,0:T(8,128)(2,1)} %get-tuple-element.59), channel_id=1, source_target_pairs={{0,12},{4,8},{8,4},{12,0},{16,28},{20,24},{24,20},{28,16},{1,13},{... | collective-permute-start | bytes 294920 | tf_op jit(solution)/shard_map/ppermute | solution.py:1090
  80.9 13.0 %collective-permute-start.28 = (bf16[96,512]{1,0:T(8,128)(2,1)}, bf16[96,512]{1,0:T(8,128)(2,1)}, u32[]{:S(2)}, u32[]{:S(2)}) collective-permute-start(bf16[96,512]{1,0:T(8,128)(2,1)} %get-tuple-element.60), channel_id=1, source_target_pairs={{0,16},{4,20},{8,24},{12,28},{16,0},{20,4},{24,8},{28,12},{1,17},{... | collective-permute-start | bytes 294920 | tf_op jit(solution)/shard_map/ppermute | solution.py:1090
  82.3 13.2 %collective-permute-start.29 = (bf16[96,512]{1,0:T(8,128)(2,1)}, bf16[96,512]{1,0:T(8,128)(2,1)}, u32[]{:S(2)}, u32[]{:S(2)}) collective-permute-start(bf16[96,512]{1,0:T(8,128)(2,1)} %get-tuple-element.61), channel_id=1, source_target_pairs={{0,20},{4,16},{8,28},{12,24},{16,4},{20,0},{24,12},{28,8},{1,21},{... | collective-permute-start | bytes 294920 | tf_op jit(solution)/shard_map/ppermute | solution.py:1090
  84.3 14.4 %collective-permute-start.30 = (bf16[96,512]{1,0:T(8,128)(2,1)}, bf16[96,512]{1,0:T(8,128)(2,1)}, u32[]{:S(2)}, u32[]{:S(2)}) collective-permute-start(bf16[96,512]{1,0:T(8,128)(2,1)} %get-tuple-element.62), channel_id=1, source_target_pairs={{0,24},{4,28},{8,16},{12,20},{16,8},{20,12},{24,0},{28,4},{1,25},{... | collective-permute-start | bytes 294920 | tf_op jit(solution)/shard_map/ppermute | solution.py:1090
  85.8 15.7 %collective-permute-start.31 = (bf16[96,512]{1,0:T(8,128)(2,1)}, bf16[96,512]{1,0:T(8,128)(2,1)}, u32[]{:S(2)}, u32[]{:S(2)}) collective-permute-start(bf16[96,512]{1,0:T(8,128)(2,1)} %get-tuple-element.63), channel_id=1, source_target_pairs={{0,28},{4,24},{8,20},{12,16},{16,12},{20,8},{24,4},{28,0},{1,29},{... | collective-permute-start | bytes 294920 | tf_op jit(solution)/shard_map/ppermute | solution.py:1090
  104.3 7.0 %collective-permute-start.33 = (bf16[256,512]{1,0:T(8,128)(2,1)}, bf16[256,512]{1,0:T(8,128)(2,1)S(1)}, u32[]{:S(2)}, u32[]{:S(2)}) collective-permute-start(bf16[256,512]{1,0:T(8,128)(2,1)} %combine.1), channel_id=1, source_target_pairs={{0,2},{1,3},{2,0},{3,1},{4,6},{5,7},{6,4},{7,5},{8,10},{9,11},{10,... | collective-permute-start | bytes 786440 | tf_op jit(solution)/shard_map/ppermute | solution.py:1090
  112.5 3.2 %collective-permute-start.34 = (bf16[256,512]{1,0:T(8,128)(2,1)S(1)}, bf16[256,512]{1,0:T(8,128)(2,1)S(1)}, u32[]{:S(2)}, u32[]{:S(2)}) collective-permute-start(bf16[256,512]{1,0:T(8,128)(2,1)S(1)} %add_convert_fusion), channel_id=1, source_target_pairs={{0,1},{1,0},{2,3},{3,2},{4,5},{5,4},{6,7},{7,6},{8,9},{9,8},{10,11... | collective-permute-start | bytes 786440 | tf_op jit(solution)/shard_map/ppermute | solution.py:1090

commit v5 on v4

--- a/solution.py
+++ b/solution.py
@@ -604,26 +604,33 @@
     cols = width // pieces
     half = width // 2
 
-    def copies():
-        made = []
-        for k in range(pieces):
-            at = pl.ds(pl.multiple_of((tp ^ k) * cols, cols), cols)
-            made.append(pltpu.make_async_copy(wout_hbm[k], wout_v.at[at], sem.at[0, k]))
-            made.append(pltpu.make_async_copy(heads_hbm[k], head_v.at[:, at], sem.at[1, k]))
-        made.append(pltpu.make_async_copy(hidden_hbm, hidden_ref, more.at[0]))
-        return made
-
+    def place_of(at):
+        return pl.ds(pl.multiple_of(at * cols, cols), cols)
+
+    made = [pltpu.make_async_copy(hidden_hbm, hidden_ref, more.at[0])]
+    for k in range(pieces):
+        at = tp ^ k
+        made.append(
+            pltpu.make_async_copy(heads_hbm[k], head_v.at[:, place_of(at)], sem.at[1, at])
+        )
+    for k in range(pieces):
+        at = tp ^ k
+        made.append(pltpu.make_async_copy(wout_hbm[k], wout_v.at[place_of(at)], sem.at[0, at]))
     late = [
         pltpu.make_async_copy(place_hbm, place_ref, more.at[1]),
         pltpu.make_async_copy(extra_hbm, extra_ref, more.at[2]),
         pltpu.make_async_copy(wide_hbm, wide_ref, more.at[3]),
     ]
 
-    for copy in copies() + late:
+    for copy in made + late:
         copy.start()
-    for copy in copies():
-        copy.wait()
-    attn = jnp.dot(head_v[...], wout_v[...], preferred_element_type=F32)
+    made[0].wait()
+    attn = jnp.zeros((rows, width), F32)
+    for at in range(pieces):
+        here = slice(at * cols, (at + 1) * cols)
+        pltpu.make_async_copy(heads_hbm[0], head_v.at[:, here], sem.at[1, at]).wait()
+        pltpu.make_async_copy(wout_hbm[0], wout_v.at[here], sem.at[0, at]).wait()
+        attn = attn + jnp.dot(head_v[:, here], wout_v[here, :], preferred_element_type=F32)
     resid = (hidden_ref[...].astype(F32) + attn).astype(BF16)
     resid_ref[...] = resid
     normed = norm(resid, gain_ref[...])

time: 117 us -> 117 us (level)
  no operation moved by 1% of the time
where the time goes in v5:
time: 117 us
  Pallas kernels  51.7 us (44%)
  starting transfers between devices  34 us (29%)
  waiting for transfers between devices  26 us (22%)
  other arithmetic  2.06 us (2%)
  local copies, waits for them, and re-layouts  1.94 us (2%)
    ppermute x33, starting transfers between devices, across(): return lambda v: lax.ppermute(v, axis, [(i, i ^ k) for i in range(size)])  32.6 us
    ppermute x33, waiting for transfers between devices, across(): return lambda v: lax.ppermute(v, axis, [(i, i ^ k) for i in range(size)])  19.4 us
    pallas_call x1, Pallas kernels, attention(): pl.pallas_call(attention_kernel, out_shape=(jax.ShapeDtypeStruct((rows, c...  18.2 us
    pallas_call x1, Pallas kernels, expert(): pl.pallas_call(functools.partial(expert_kernel, replicas, pieces), out_sh...  8.22 us
    ppermute x2, waiting for transfers between devices, far(): return lax.ppermute(blocks[near + f], ('req', 'tp'), pairs)  6.6 us
    pallas_call x1, Pallas kernels, dispatch(): pl.pallas_call(functools.partial(dispatch_kernel, pieces, replicas), out_...  4.98 us
    pallas_call x1, Pallas kernels, make_gates(): pl.pallas_call(functools.partial(gates_kernel, cap, replicas), out_shape=...  4.43 us
    pallas_call x1, Pallas kernels, project(): pl.pallas_call(project_kernel, out_shape=(jax.ShapeDtypeStruct((rows, col...  3.48 us
  transfers between devices with their start and end apart: 35, of which 13 were waited for; matrix products, arithmetic and copies ran while one was open for 1% of the time, Pallas kernels for 31%

profile of v5, /device:TPU:11, one launch (start us, length us, event | category | flops | bytes accessed | tf_op | source)
XLA Modules:
  0.0 116.6 jit_solution(8490144262551790925)
XLA Ops:
  0.6 0.7 collective-permute-start.3
  1.4 0.3 collective-permute-start.4
  1.6 3.5 %project.1 = (bf16[256,256]{1,0:T(8,128)(2,1)}, f32[256,256]{1,0:T(8,128)}, f32[256,256]{1,0:T(8,128)}, bf16[8,64,256]{2,1,0:T(8,128)(2,1)}) custom-call(s32[2048]{0:T(1024)} %slots_hbm.1, s32[256]{0:T(256)} %tlen_hbm.3, bf16[256,1024]{1,0:T(8,128)(2,1)} %refs_8_.1, f32[1,1024]{1,0:T(1,128)} %bitcast.11, bf16[1024,256]{1,0:T(8,128)(2,1)} %wq_hbm.1, ...), custom_call_target="tpu_custom_call" | custom-call | flops 400000000 | bytes 3000000 | tf_op jit(solution)/shard_map/project/pallas_call | solution.py:370
  5.1 0.1 collective-permute-start.6
  5.2 2.5 %collective-permute-start.7 = (bf16[8,64,256]{2,1,0:T(8,128)(2,1)}, bf16[8,64,256]{2,1,0:T(8,128)(2,1)}, u32[]{:S(2)}, u32[]{:S(2)}) collective-permute-start(bf16[8,64,256]{2,1,0:T(8,128)(2,1)} %get-tuple-element.40.refs_0_), channel_id=1, source_target_pairs={{0,16},{4,20},{8,24},{12,28},{16,0},{20,4},{24,8},{28,12},{1,17},{... | collective-permute-start | bytes 786440 | tf_op jit(solution)/shard_map/ppermute | solution.py:1097
  7.7 0.2 collective-permute-start.8
  7.8 1.2 %collective-permute-start.5 = (bf16[256,1024]{1,0:T(8,128)(2,1)}, bf16[256,1024]{1,0:T(8,128)(2,1)}, u32[]{:S(2)}, u32[]{:S(2)}) collective-permute-start(bf16[256,1024]{1,0:T(8,128)(2,1)} %collective-permute-done.3.refs_5_), channel_id=1, source_target_pairs={{0,2},{1,3},{2,0},{3,1},{4,6},{5,7},{6,4},{7,5},{8,10},{9,11},{10,... | collective-permute-start | bytes 1572872 | tf_op jit(solution)/shard_map/ppermute | solution.py:1097
  9.1 18.2 %attention.1 = (bf16[256,256]{1,0:T(8,128)(2,1)}, bf16[2,256,64,256]{3,2,1,0:T(8,128)(2,1)}) custom-call(s32[256]{0:T(256)} %group_hbm.1, s32[8]{0:T(128)} %plen_hbm.1, s32[256]{0:T(256)} %tlen_hbm.3, s32[1,256]{1,0:T(1,128)} %bitcast.17, s32[577]{0:T(1024)} %bucket_hbm.1, f32[4,32]{1,0:T(4,128)} %bitcast.16, bf16[256,256]{1,0:T(8,128)(2,1)} %get-tuple-element.36.q_hbm, ...), custom_call_target="tpu_custom_call" | custom-call | flops 8000000000 | bytes 45000000 | tf_op jit(solution)/shard_map/attention/pallas_call | solution.py:413
  27.3 0.0 collective-permute-done.6.refs_1_
  27.3 1.5 %collective-permute-start = (bf16[256,256]{1,0:T(8,128)(2,1)}, bf16[256,256]{1,0:T(8,128)(2,1)}, u32[]{:S(2)}, u32[]{:S(2)}) collective-permute-start(bf16[256,256]{1,0:T(8,128)(2,1)} %get-tuple-element.39.refs_0_), channel_id=1, source_target_pairs={{0,1},{1,0},{2,3},{3,2},{4,5},{5,4},{6,7},{7,6},{8,9},{9,8},{10,11... | collective-permute-start | bytes 393224 | tf_op jit(solution)/shard_map/ppermute | solution.py:1097
  28.8 0.3 collective-permute-start.1
  29.1 1.8 %collective-permute-done.8.refs_3_ = bf16[8,64,256]{2,1,0:T(8,128)(2,1)} collective-permute-done((bf16[8,64,256]{2,1,0:T(8,128)(2,1)}, bf16[8,64,256]{2,1,0:T(8,128)(2,1)}, u32[]{:S(2)}, u32[]{:S(2)}) %collective-permute-start.8) | collective-permute-done | bytes 262176 | tf_op jit(solution)/shard_map/ppermute | solution.py:1097
  30.9 2.5 %collective-permute-start.2 = (bf16[256,256]{1,0:T(8,128)(2,1)}, bf16[256,256]{1,0:T(8,128)(2,1)}, u32[]{:S(2)}, u32[]{:S(2)}) collective-permute-start(bf16[256,256]{1,0:T(8,128)(2,1)} %get-tuple-element.39.refs_0_), channel_id=1, source_target_pairs={{0,3},{1,2},{2,1},{3,0},{4,7},{5,6},{6,5},{7,4},{8,11},{9,10},{10,... | collective-permute-start | bytes 393224 | tf_op jit(solution)/shard_map/ppermute | solution.py:1097
  33.4 1.3 %reshape.7.slots_ref.refs_18_ = s32[8,256]{1,0:T(8,128)} reshape(s32[2048]{0:T(1024)} %slots_hbm.1) | data formatting | bytes 16384 | tf_op jit(solution)/shard_map/reshape | solution.py:1120
  34.7 1.8 %plan.1 = (bf16[768,256]{1,0:T(8,128)(2,1)}, bf16[128,512]{1,0:T(8,128)(2,1)}, bf16[256,128]{1,0:T(8,128)(2,1)}, bf16[128,128]{1,0:T(8,128)(2,1)}, s32[8,128]{1,0:T(8,128)}) custom-call(s32[8,256]{1,0:T(8,128)} %reshape.7.slots_ref.refs_18_, s32[2,256]{1,0:T(2,128)} %bitcast.9, bf16[256,256]{1,0:T(8,128)(2,1)} %get-tuple-element.39.refs_0_, ...), custom_call_target="tpu_custom_call" | custom-call | tf_op jit(solution)/shard_map/plan/pallas_call | solution.py:556
  36.5 2.4 %choose.1.refs_13_ = bf16[8,64,256]{2,1,0:T(8,128)(2,1)} custom-call(s32[8,128]{1,0:T(8,128)} %get-tuple-element.44.plan_hbm.refs_16_, bf16[8,64,256]{2,1,0:T(8,128)(2,1)} %get-tuple-element.40.refs_0_, bf16[8,64,256]{2,1,0:T(8,128)(2,1)} %collective-permute-done.6.refs_1_, bf16[8,64,256]{2,1,0:T(8,128)(2,1)} %collective-permute-done.7.refs_2_, ...), custom_call_target="tpu_custom_call" | custom-call | tf_op jit(solution)/shard_map/choose/pallas_call | solution.py:1006
  39.0 5.0 %dispatch.1 = (bf16[256,1024]{1,0:T(8,128)(2,1)}, bf16[96,512]{1,0:T(8,128)(2,1)}, bf16[96,512]{1,0:T(8,128)(2,1)}, bf16[96,512]{1,0:T(8,128)(2,1)}, bf16[96,512...) custom-call(bf16[256,256]{1,0:T(8,128)(2,1)} %get-tuple-element.39.refs_0_, ...), custom_call_target="tpu_custom_call" | custom-call | flops 1200000000 | bytes 6000000 | tf_op jit(solution)/shard_map/dispatch/pallas_call | solution.py:664
  44.0 1.3 %collective-permute-start.9 = (bf16[96,512]{1,0:T(8,128)(2,1)}, bf16[96,512]{1,0:T(8,128)(2,1)S(1)}, u32[]{:S(2)}, u32[]{:S(2)}) collective-permute-start(bf16[96,512]{1,0:T(8,128)(2,1)} %get-tuple-element.46), channel_id=1, source_target_pairs={{0,4},{4,0},{8,12},{12,8},{16,20},{20,16},{24,28},{28,24},{1,5},{5... | collective-permute-start | bytes 294920 | tf_op jit(solution)/shard_map/ppermute | solution.py:1097
  45.3 1.3 %collective-permute-start.12 = (bf16[96,512]{1,0:T(8,128)(2,1)}, bf16[96,512]{1,0:T(8,128)(2,1)S(1)}, u32[]{:S(2)}, u32[]{:S(2)}) collective-permute-start(bf16[96,512]{1,0:T(8,128)(2,1)} %get-tuple-element.49), channel_id=1, source_target_pairs={{0,16},{1,17},{2,26},{3,27},{4,20},{5,21},{6,30},{7,31},{8,24},{9,... | collective-permute-start | bytes 294920 | tf_op jit(solution)/shard_map/ppermute | solution.py:1136
  46.6 0.1 collective-permute-start.13
  46.7 1.2 %collective-permute-start.10 = (bf16[96,512]{1,0:T(8,128)(2,1)}, bf16[96,512]{1,0:T(8,128)(2,1)S(1)}, u32[]{:S(2)}, u32[]{:S(2)}) collective-permute-start(bf16[96,512]{1,0:T(8,128)(2,1)} %get-tuple-element.47), channel_id=1, source_target_pairs={{0,8},{4,12},{8,0},{12,4},{16,24},{20,28},{24,16},{28,20},{1,9},{5... | collective-permute-start | bytes 294920 | tf_op jit(solution)/shard_map/ppermute | solution.py:1097
  47.9 1.3 %collective-permute-start.11 = (bf16[96,512]{1,0:T(8,128)(2,1)}, bf16[96,512]{1,0:T(8,128)(2,1)S(1)}, u32[]{:S(2)}, u32[]{:S(2)}) collective-permute-start(bf16[96,512]{1,0:T(8,128)(2,1)} %get-tuple-element.48), channel_id=1, source_target_pairs={{0,12},{4,8},{8,4},{12,0},{16,28},{20,24},{24,20},{28,16},{1,13},{... | collective-permute-start | bytes 294920 | tf_op jit(solution)/shard_map/ppermute | solution.py:1097
  49.1 0.9 collective-permute-start.16
  50.0 4.2 %collective-permute-done.12.refs_4_ = bf16[96,512]{1,0:T(8,128)(2,1)S(1)} collective-permute-done((bf16[96,512]{1,0:T(8,128)(2,1)}, bf16[96,512]{1,0:T(8,128)(2,1)S(1)}, u32[]{:S(2)}, u32[]{:S(2)}) %collective-permute-start.12) | collective-permute-done | bytes 98336 | tf_op jit(solution)/shard_map/ppermute | solution.py:1136
  54.2 2.4 %collective-permute-done.13.refs_5_ = bf16[96,512]{1,0:T(8,128)(2,1)S(1)} collective-permute-done((bf16[96,512]{1,0:T(8,128)(2,1)}, bf16[96,512]{1,0:T(8,128)(2,1)S(1)}, u32[]{:S(2)}, u32[]{:S(2)}) %collective-permute-start.13) | collective-permute-done | bytes 98336 | tf_op jit(solution)/shard_map/ppermute | solution.py:1136
  56.6 0.8 collective-permute-start.17
  57.4 1.1 collective-permute-start.18
  58.5 0.1 collective-permute-start.20
  58.6 0.8 collective-permute-start.21
  59.4 0.6 collective-permute-done.15.refs_7_
  60.1 1.9 %collective-permute-start.19 = (bf16[96,512]{1,0:T(8,128)(2,1)S(1)}, bf16[96,512]{1,0:T(8,128)(2,1)S(1)}, u32[]{:S(2)}, u32[]{:S(2)}) collective-permute-start(bf16[96,512]{1,0:T(8,128)(2,1)S(1)} %collective-permute-done.11.refs_3_), channel_id=1, source_target_pairs={{0,1},{1,0},{2,3},{3,2},{4,5},{5,4},{6,7},{7,6},{8,9},{9,8},{10,11... | collective-permute-start | bytes 294920 | tf_op jit(solution)/shard_map/ppermute | solution.py:1097
  61.9 0.1 collective-permute-start.22
  62.0 0.5 collective-permute-start.23
  62.5 0.4 collective-permute-done.19.refs_11_
  62.9 0.4 collective-permute-done.22.refs_14_
  63.3 0.2 collective-permute-done.23.refs_15_
  63.5 0.0 copy-done.12
  63.5 0.0 copy-done.10
  63.6 0.1 copy-done.11
  63.6 0.3 copy-done.13
  63.9 0.2 copy-done.14
  64.1 8.2 %expert.1 = (bf16[768,512]{1,0:T(8,128)(2,1)}, bf16[768,512]{1,0:T(8,128)(2,1)}) custom-call(bf16[96,512]{1,0:T(8,128)(2,1)} %get-tuple-element.45.refs_0_, bf16[96,512]{1,0:T(8,128)(2,1)} %copy-done, bf16[96,512]{1,0:T(8,128)(2,1)} %copy-done.3, bf16[96,512]{1,0:T(8,128)(2,1)} %copy-done.4, bf16[96,512]{1,0:T(8,128)(2,1)} %copy-done.1, ...), custom_call_target="tpu_custom_call" | custom-call | flops 3400000000 | bytes 8000000 | tf_op jit(solution)/shard_map/expert/pallas_call | solution.py:759
  72.3 0.4 collective-permute-start.24
  72.8 2.1 %collective-permute-start.32 = (bf16[8,64,256]{2,1,0:T(8,128)(2,1)}, bf16[8,64,256]{2,1,0:T(8,128)(2,1)}, u32[]{:S(2)}, u32[]{:S(2)}) collective-permute-start(bf16[8,64,256]{2,1,0:T(8,128)(2,1)} %choose.1.refs_13_), channel_id=1, source_target_pairs={{0,4},{4,0},{8,12},{12,8},{16,20},{20,16},{24,28},{28,24},{1,5},{5... | collective-permute-start | bytes 786440 | tf_op jit(solution)/shard_map/ppermute | solution.py:1097
  74.8 0.2 collective-permute-done.24.got_hbm
  75.0 2.4 %give_back.1 = (bf16[96,512]{1,0:T(8,128)(2,1)}, bf16[96,512]{1,0:T(8,128)(2,1)}, bf16[96,512]{1,0:T(8,128)(2,1)}, bf16[96,512]{1,0:T(8,128)(2,1)}, bf16[96,512]...) custom-call(bf16[768,512]{1,0:T(8,128)(2,1)} %get-tuple-element.53.keep_hbm, ...), custom_call_target="tpu_custom_call" | custom-call | flops 30000000 | bytes 2500000 | tf_op jit(solution)/shard_map/give_back/pallas_call | solution.py:808
  77.5 2.1 %collective-permute-start.25 = (bf16[96,512]{1,0:T(8,128)(2,1)}, bf16[96,512]{1,0:T(8,128)(2,1)}, u32[]{:S(2)}, u32[]{:S(2)}) collective-permute-start(bf16[96,512]{1,0:T(8,128)(2,1)} %get-tuple-element.57), channel_id=1, source_target_pairs={{0,4},{4,0},{8,12},{12,8},{16,20},{20,16},{24,28},{28,24},{1,5},{5... | collective-permute-start | bytes 294920 | tf_op jit(solution)/shard_map/ppermute | solution.py:1097
  79.6 1.3 %collective-permute-start.27 = (bf16[96,512]{1,0:T(8,128)(2,1)}, bf16[96,512]{1,0:T(8,128)(2,1)}, u32[]{:S(2)}, u32[]{:S(2)}) collective-permute-start(bf16[96,512]{1,0:T(8,128)(2,1)} %get-tuple-element.59), channel_id=1, source_target_pairs={{0,12},{4,8},{8,4},{12,0},{16,28},{20,24},{24,20},{28,16},{1,13},{... | collective-permute-start | bytes 294920 | tf_op jit(solution)/shard_map/ppermute | solution.py:1097
  80.9 1.5 %collective-permute-start.28 = (bf16[96,512]{1,0:T(8,128)(2,1)}, bf16[96,512]{1,0:T(8,128)(2,1)}, u32[]{:S(2)}, u32[]{:S(2)}) collective-permute-start(bf16[96,512]{1,0:T(8,128)(2,1)} %get-tuple-element.60), channel_id=1, source_target_pairs={{0,16},{4,20},{8,24},{12,28},{16,0},{20,4},{24,8},{28,12},{1,17},{... | collective-permute-start | bytes 294920 | tf_op jit(solution)/shard_map/ppermute | solution.py:1097
  82.3 2.0 %collective-permute-start.29 = (bf16[96,512]{1,0:T(8,128)(2,1)}, bf16[96,512]{1,0:T(8,128)(2,1)}, u32[]{:S(2)}, u32[]{:S(2)}) collective-permute-start(bf16[96,512]{1,0:T(8,128)(2,1)} %get-tuple-element.61), channel_id=1, source_target_pairs={{0,20},{4,16},{8,28},{12,24},{16,4},{20,0},{24,12},{28,8},{1,21},{... | collective-permute-start | bytes 294920 | tf_op jit(solution)/shard_map/ppermute | solution.py:1097
  84.3 1.5 %collective-permute-start.30 = (bf16[96,512]{1,0:T(8,128)(2,1)}, bf16[96,512]{1,0:T(8,128)(2,1)}, u32[]{:S(2)}, u32[]{:S(2)}) collective-permute-start(bf16[96,512]{1,0:T(8,128)(2,1)} %get-tuple-element.62), channel_id=1, source_target_pairs={{0,24},{4,28},{8,16},{12,20},{16,8},{20,12},{24,0},{28,4},{1,25},{... | collective-permute-start | bytes 294920 | tf_op jit(solution)/shard_map/ppermute | solution.py:1097
  85.9 0.6 collective-permute-start.31
  86.4 3.0 %patch.1 = (bf16[2,256,64,256]{3,2,1,0:T(8,128)(2,1)}, f32[8,128]{1,0:T(8,128)}) custom-call(s32[8,128]{1,0:T(8,128)} %get-tuple-element.44.plan_hbm.refs_16_, bf16[8,64,256]{2,1,0:T(8,128)(2,1)} %get-tuple-element.40.refs_0_, bf16[8,64,256]{2,1,0:T(8,128)(2,1)} %collective-permute-done.6.refs_1_, ...), custom_call_target="tpu_custom_call", output_to_operand_aliasing={{0}: (6, {})} | custom-call | tf_op jit(solution)/shard_map/patch/pallas_call | solution.py:1062
  89.5 4.4 %gates.1 = (bf16[256,768]{1,0:T(8,128)(2,1)}, bf16[256,768]{1,0:T(8,128)(2,1)}, f32[256,128]{1,0:T(8,128)}, bf16[256,512]{1,0:T(8,128)(2,1)}) custom-call(bf16[96,512]{1,0:T(8,128)(2,1)} %get-tuple-element.45.refs_0_, bf16[96,512]{1,0:T(8,128)(2,1)} %copy-done, bf16[96,512]{1,0:T(8,128)(2,1)} %copy-done.3, bf16[96,512]{1,0:T(8,128)(2,1)} %copy-done.4, ...), custom_call_target="tpu_custom_call" | custom-call | flops 200000000 | bytes 6000000 | tf_op jit(solution)/shard_map/gates/pallas_call | solution.py:928
  93.9 1.5 %collective-permute-done.29.refs_5_ = bf16[96,512]{1,0:T(8,128)(2,1)} collective-permute-done((bf16[96,512]{1,0:T(8,128)(2,1)}, bf16[96,512]{1,0:T(8,128)(2,1)}, u32[]{:S(2)}, u32[]{:S(2)}) %collective-permute-start.29) | collective-permute-done | bytes 98336 | tf_op jit(solution)/shard_map/ppermute | solution.py:1097
  95.4 3.1 %collective-permute-done.30.refs_6_ = bf16[96,512]{1,0:T(8,128)(2,1)} collective-permute-done((bf16[96,512]{1,0:T(8,128)(2,1)}, bf16[96,512]{1,0:T(8,128)(2,1)}, u32[]{:S(2)}, u32[]{:S(2)}) %collective-permute-start.30) | collective-permute-done | bytes 98336 | tf_op jit(solution)/shard_map/ppermute | solution.py:1097
  98.5 3.1 %collective-permute-done.31.refs_7_ = bf16[96,512]{1,0:T(8,128)(2,1)} collective-permute-done((bf16[96,512]{1,0:T(8,128)(2,1)}, bf16[96,512]{1,0:T(8,128)(2,1)}, u32[]{:S(2)}, u32[]{:S(2)}) %collective-permute-start.31) | collective-permute-done | bytes 98336 | tf_op jit(solution)/shard_map/ppermute | solution.py:1097
  101.6 2.7 %combine.1 = bf16[256,512]{1,0:T(8,128)(2,1)} custom-call(bf16[96,512]{1,0:T(8,128)(2,1)} %get-tuple-element.56.refs_0_, bf16[96,512]{1,0:T(8,128)(2,1)} %collective-permute-done.25.refs_1_, bf16[96,512]{1,0:T(8,128)(2,1)} %collective-permute-done.26.refs_2_, bf16[96,512]{1,0:T(8,128)(2,1)} %collective-permute-done.27.refs_3_, ...), custom_call_target="tpu_custom_call" | custom-call | flops 400000000 | bytes 2500000 | tf_op jit(solution)/shard_map/combine/pallas_call | solution.py:975
  104.3 0.1 collective-permute-start.33
  104.4 6.9 %collective-permute-done.33 = bf16[256,512]{1,0:T(8,128)(2,1)S(1)} collective-permute-done((bf16[256,512]{1,0:T(8,128)(2,1)}, bf16[256,512]{1,0:T(8,128)(2,1)S(1)}, u32[]{:S(2)}, u32[]{:S(2)}) %collective-permute-start.33) | collective-permute-done | bytes 262176 | tf_op jit(solution)/shard_map/ppermute | solution.py:1097
  111.4 1.1 add_convert_fusion
  112.5 2.0 %collective-permute-start.34 = (bf16[256,512]{1,0:T(8,128)(2,1)S(1)}, bf16[256,512]{1,0:T(8,128)(2,1)S(1)}, u32[]{:S(2)}, u32[]{:S(2)}) collective-permute-start(bf16[256,512]{1,0:T(8,128)(2,1)S(1)} %add_convert_fusion), channel_id=1, source_target_pairs={{0,1},{1,0},{2,3},{3,2},{4,5},{5,4},{6,7},{7,6},{8,9},{9,8},{10,11... | collective-permute-start | bytes 786440 | tf_op jit(solution)/shard_map/ppermute | solution.py:1097
  114.5 1.2 collective-permute-done.34
  115.7 0.9 maximum_select_fusion
  (49 shorter events, 0.1 us)
Async XLA Ops:
  0.6 7.2 %collective-permute-start.3 = (bf16[256,1024]{1,0:T(8,128)(2,1)}, bf16[256,1024]{1,0:T(8,128)(2,1)}, u32[]{:S(2)}, u32[]{:S(2)}) collective-permute-start(bf16[256,1024]{1,0:T(8,128)(2,1)} %refs_4_.1), channel_id=1, source_target_pairs={{0,1},{1,0},{2,3},{3,2},{4,5},{5,4},{6,7},{7,6},{8,9},{9,8},{10,11... | collective-permute-start | bytes 1572872 | tf_op jit(solution)/shard_map/ppermute | solution.py:1097
  1.4 33.3 %collective-permute-start.4 = (bf16[256,1024]{1,0:T(8,128)(2,1)}, bf16[256,1024]{1,0:T(8,128)(2,1)}, u32[]{:S(2)}, u32[]{:S(2)}) collective-permute-start(bf16[256,1024]{1,0:T(8,128)(2,1)} %refs_4_.1), channel_id=1, source_target_pairs={{0,2},{1,3},{2,0},{3,1},{4,6},{5,7},{6,4},{7,5},{8,10},{9,11},{10,... | collective-permute-start | bytes 1572872 | tf_op jit(solution)/shard_map/ppermute | solution.py:1097
  5.1 22.1 %collective-permute-start.6 = (bf16[8,64,256]{2,1,0:T(8,128)(2,1)}, bf16[8,64,256]{2,1,0:T(8,128)(2,1)}, u32[]{:S(2)}, u32[]{:S(2)}) collective-permute-start(bf16[8,64,256]{2,1,0:T(8,128)(2,1)} %get-tuple-element.40.refs_0_), channel_id=1, source_target_pairs={{0,8},{4,12},{8,0},{12,4},{16,24},{20,28},{24,16},{28,20},{1,9},{5... | collective-permute-start | bytes 786440 | tf_op jit(solution)/shard_map/ppermute | solution.py:1097
  5.2 23.6 %collective-permute-start.7 = (bf16[8,64,256]{2,1,0:T(8,128)(2,1)}, bf16[8,64,256]{2,1,0:T(8,128)(2,1)}, u32[]{:S(2)}, u32[]{:S(2)}) collective-permute-start(bf16[8,64,256]{2,1,0:T(8,128)(2,1)} %get-tuple-element.40.refs_0_), channel_id=1, source_target_pairs={{0,16},{4,20},{8,24},{12,28},{16,0},{20,4},{24,8},{28,12},{1,17},{... | collective-permute-start | bytes 786440 | tf_op jit(solution)/shard_map/ppermute | solution.py:1097
  7.7 23.2 %collective-permute-start.8 = (bf16[8,64,256]{2,1,0:T(8,128)(2,1)}, bf16[8,64,256]{2,1,0:T(8,128)(2,1)}, u32[]{:S(2)}, u32[]{:S(2)}) collective-permute-start(bf16[8,64,256]{2,1,0:T(8,128)(2,1)} %get-tuple-element.40.refs_0_), channel_id=1, source_target_pairs={{0,24},{4,28},{8,16},{12,20},{16,8},{20,12},{24,0},{28,4},{1,25},{... | collective-permute-start | bytes 786440 | tf_op jit(solution)/shard_map/ppermute | solution.py:1097
  7.8 26.9 %collective-permute-start.5 = (bf16[256,1024]{1,0:T(8,128)(2,1)}, bf16[256,1024]{1,0:T(8,128)(2,1)}, u32[]{:S(2)}, u32[]{:S(2)}) collective-permute-start(bf16[256,1024]{1,0:T(8,128)(2,1)} %collective-permute-done.3.refs_5_), channel_id=1, source_target_pairs={{0,2},{1,3},{2,0},{3,1},{4,6},{5,7},{6,4},{7,5},{8,10},{9,11},{10,... | collective-permute-start | bytes 1572872 | tf_op jit(solution)/shard_map/ppermute | solution.py:1097
  27.3 11.7 %collective-permute-start = (bf16[256,256]{1,0:T(8,128)(2,1)}, bf16[256,256]{1,0:T(8,128)(2,1)}, u32[]{:S(2)}, u32[]{:S(2)}) collective-permute-start(bf16[256,256]{1,0:T(8,128)(2,1)} %get-tuple-element.39.refs_0_), channel_id=1, source_target_pairs={{0,1},{1,0},{2,3},{3,2},{4,5},{5,4},{6,7},{7,6},{8,9},{9,8},{10,11... | collective-permute-start | bytes 393224 | tf_op jit(solution)/shard_map/ppermute | solution.py:1097
  28.8 10.1 %collective-permute-start.1 = (bf16[256,256]{1,0:T(8,128)(2,1)}, bf16[256,256]{1,0:T(8,128)(2,1)}, u32[]{:S(2)}, u32[]{:S(2)}) collective-permute-start(bf16[256,256]{1,0:T(8,128)(2,1)} %get-tuple-element.39.refs_0_), channel_id=1, source_target_pairs={{0,2},{1,3},{2,0},{3,1},{4,6},{5,7},{6,4},{7,5},{8,10},{9,11},{10,... | collective-permute-start | bytes 393224 | tf_op jit(solution)/shard_map/ppermute | solution.py:1097
  30.9 8.1 %collective-permute-start.2 = (bf16[256,256]{1,0:T(8,128)(2,1)}, bf16[256,256]{1,0:T(8,128)(2,1)}, u32[]{:S(2)}, u32[]{:S(2)}) collective-permute-start(bf16[256,256]{1,0:T(8,128)(2,1)} %get-tuple-element.39.refs_0_), channel_id=1, source_target_pairs={{0,3},{1,2},{2,1},{3,0},{4,7},{5,6},{6,5},{7,4},{8,11},{9,10},{10,... | collective-permute-start | bytes 393224 | tf_op jit(solution)/shard_map/ppermute | solution.py:1097
  44.0 5.2 %collective-permute-start.9 = (bf16[96,512]{1,0:T(8,128)(2,1)}, bf16[96,512]{1,0:T(8,128)(2,1)S(1)}, u32[]{:S(2)}, u32[]{:S(2)}) collective-permute-start(bf16[96,512]{1,0:T(8,128)(2,1)} %get-tuple-element.46), channel_id=1, source_target_pairs={{0,4},{4,0},{8,12},{12,8},{16,20},{20,16},{24,28},{28,24},{1,5},{5... | collective-permute-start | bytes 294920 | tf_op jit(solution)/shard_map/ppermute | solution.py:1097
  45.3 8.9 %collective-permute-start.12 = (bf16[96,512]{1,0:T(8,128)(2,1)}, bf16[96,512]{1,0:T(8,128)(2,1)S(1)}, u32[]{:S(2)}, u32[]{:S(2)}) collective-permute-start(bf16[96,512]{1,0:T(8,128)(2,1)} %get-tuple-element.49), channel_id=1, source_target_pairs={{0,16},{1,17},{2,26},{3,27},{4,20},{5,21},{6,30},{7,31},{8,24},{9,... | collective-permute-start | bytes 294920 | tf_op jit(solution)/shard_map/ppermute | solution.py:1136
  46.6 10.1 %collective-permute-start.13 = (bf16[96,512]{1,0:T(8,128)(2,1)}, bf16[96,512]{1,0:T(8,128)(2,1)S(1)}, u32[]{:S(2)}, u32[]{:S(2)}) collective-permute-start(bf16[96,512]{1,0:T(8,128)(2,1)} %get-tuple-element.50), channel_id=1, source_target_pairs={{0,20},{1,21},{2,30},{3,31},{4,16},{5,17},{6,26},{7,27},{8,28},{9,... | collective-permute-start | bytes 294920 | tf_op jit(solution)/shard_map/ppermute | solution.py:1136
  46.7 9.9 %collective-permute-start.10 = (bf16[96,512]{1,0:T(8,128)(2,1)}, bf16[96,512]{1,0:T(8,128)(2,1)S(1)}, u32[]{:S(2)}, u32[]{:S(2)}) collective-permute-start(bf16[96,512]{1,0:T(8,128)(2,1)} %get-tuple-element.47), channel_id=1, source_target_pairs={{0,8},{4,12},{8,0},{12,4},{16,24},{20,28},{24,16},{28,20},{1,9},{5... | collective-permute-start | bytes 294920 | tf_op jit(solution)/shard_map/ppermute | solution.py:1097
  47.9 9.6 %collective-permute-start.11 = (bf16[96,512]{1,0:T(8,128)(2,1)}, bf16[96,512]{1,0:T(8,128)(2,1)S(1)}, u32[]{:S(2)}, u32[]{:S(2)}) collective-permute-start(bf16[96,512]{1,0:T(8,128)(2,1)} %get-tuple-element.48), channel_id=1, source_target_pairs={{0,12},{4,8},{8,4},{12,0},{16,28},{20,24},{24,20},{28,16},{1,13},{... | collective-permute-start | bytes 294920 | tf_op jit(solution)/shard_map/ppermute | solution.py:1097
  49.1 7.5 %copy-start = (bf16[96,512]{1,0:T(8,128)(2,1)}, bf16[96,512]{1,0:T(8,128)(2,1)S(1)}, u32[]{:S(2)}) copy-start(bf16[96,512]{1,0:T(8,128)(2,1)S(1)} %collective-permute-done.9.refs_1_) | copy-start | bytes 294916
  49.1 9.4 %collective-permute-start.16 = (bf16[96,512]{1,0:T(8,128)(2,1)}, bf16[96,512]{1,0:T(8,128)(2,1)S(1)}, u32[]{:S(2)}, u32[]{:S(2)}) collective-permute-start(bf16[96,512]{1,0:T(8,128)(2,1)} %get-tuple-element.45.refs_0_), channel_id=1, source_target_pairs={{0,1},{1,0},{2,3},{3,2},{4,5},{5,4},{6,7},{7,6},{8,9},{9,8},{10,11... | collective-permute-start | bytes 294920 | tf_op jit(solution)/shard_map/ppermute | solution.py:1097
  54.2 7.7 %copy-start.1 = (bf16[96,512]{1,0:T(8,128)(2,1)}, bf16[96,512]{1,0:T(8,128)(2,1)S(1)}, u32[]{:S(2)}) copy-start(bf16[96,512]{1,0:T(8,128)(2,1)S(1)} %collective-permute-done.12.refs_4_) | copy-start | bytes 294916
  54.2 4.4 %collective-permute-start.14 = (bf16[96,512]{1,0:T(8,128)(2,1)S(1)}, bf16[96,512]{1,0:T(8,128)(2,1)S(1)}, u32[]{:S(2)}, u32[]{:S(2)}) collective-permute-start(bf16[96,512]{1,0:T(8,128)(2,1)S(1)} %collective-permute-done.12.refs_4_), channel_id=1, source_target_pairs={{0,2},{1,3},{2,0},{3,1},{4,6},{5,7},{6,4},{7,5},{8,10},{9,11},{10,... | collective-permute-start | bytes 294920 | tf_op jit(solution)/shard_map/ppermute | solution.py:1097
  56.6 6.3 %copy-start.2 = (bf16[96,512]{1,0:T(8,128)(2,1)}, bf16[96,512]{1,0:T(8,128)(2,1)S(1)}, u32[]{:S(2)}) copy-start(bf16[96,512]{1,0:T(8,128)(2,1)S(1)} %collective-permute-done.13.refs_5_) | copy-start | bytes 294916
  56.6 3.5 %collective-permute-start.15 = (bf16[96,512]{1,0:T(8,128)(2,1)S(1)}, bf16[96,512]{1,0:T(8,128)(2,1)S(1)}, u32[]{:S(2)}, u32[]{:S(2)}) collective-permute-start(bf16[96,512]{1,0:T(8,128)(2,1)S(1)} %collective-permute-done.13.refs_5_), channel_id=1, source_target_pairs={{0,2},{1,3},{2,0},{3,1},{4,6},{5,7},{6,4},{7,5},{8,10},{9,11},{10,... | collective-permute-start | bytes 294920 | tf_op jit(solution)/shard_map/ppermute | solution.py:1097
  56.6 6.3 %copy-start.3 = (bf16[96,512]{1,0:T(8,128)(2,1)}, bf16[96,512]{1,0:T(8,128)(2,1)S(1)}, u32[]{:S(2)}) copy-start(bf16[96,512]{1,0:T(8,128)(2,1)S(1)} %collective-permute-done.10.refs_2_) | copy-start | bytes 294916
  56.6 5.3 %collective-permute-start.17 = (bf16[96,512]{1,0:T(8,128)(2,1)S(1)}, bf16[96,512]{1,0:T(8,128)(2,1)S(1)}, u32[]{:S(2)}, u32[]{:S(2)}) collective-permute-start(bf16[96,512]{1,0:T(8,128)(2,1)S(1)} %collective-permute-done.9.refs_1_), channel_id=1, source_target_pairs={{0,1},{1,0},{2,3},{3,2},{4,5},{5,4},{6,7},{7,6},{8,9},{9,8},{10,11... | collective-permute-start | bytes 294920 | tf_op jit(solution)/shard_map/ppermute | solution.py:1097
  57.4 5.9 %copy-start.4 = (bf16[96,512]{1,0:T(8,128)(2,1)}, bf16[96,512]{1,0:T(8,128)(2,1)S(1)}, u32[]{:S(2)}) copy-start(bf16[96,512]{1,0:T(8,128)(2,1)S(1)} %collective-permute-done.11.refs_3_) | copy-start | bytes 294916
  57.4 4.6 %collective-permute-start.18 = (bf16[96,512]{1,0:T(8,128)(2,1)S(1)}, bf16[96,512]{1,0:T(8,128)(2,1)S(1)}, u32[]{:S(2)}, u32[]{:S(2)}) collective-permute-start(bf16[96,512]{1,0:T(8,128)(2,1)S(1)} %collective-permute-done.10.refs_2_), channel_id=1, source_target_pairs={{0,1},{1,0},{2,3},{3,2},{4,5},{5,4},{6,7},{7,6},{8,9},{9,8},{10,11... | collective-permute-start | bytes 294920 | tf_op jit(solution)/shard_map/ppermute | solution.py:1097
  58.5 4.9 %copy-start.5 = (bf16[96,512]{1,0:T(8,128)(2,1)}, bf16[96,512]{1,0:T(8,128)(2,1)S(1)}, u32[]{:S(2)}) copy-start(bf16[96,512]{1,0:T(8,128)(2,1)S(1)} %collective-permute-done.16.refs_8_) | copy-start | bytes 294916
  58.5 4.3 %collective-permute-start.20 = (bf16[96,512]{1,0:T(8,128)(2,1)S(1)}, bf16[96,512]{1,0:T(8,128)(2,1)S(1)}, u32[]{:S(2)}, u32[]{:S(2)}) collective-permute-start(bf16[96,512]{1,0:T(8,128)(2,1)S(1)} %collective-permute-done.12.refs_4_), channel_id=1, source_target_pairs={{0,1},{1,0},{2,3},{3,2},{4,5},{5,4},{6,7},{7,6},{8,9},{9,8},{10,11... | collective-permute-start | bytes 294920 | tf_op jit(solution)/shard_map/ppermute | solution.py:1097
  58.6 4.9 %copy-start.6 = (bf16[96,512]{1,0:T(8,128)(2,1)}, bf16[96,512]{1,0:T(8,128)(2,1)S(1)}, u32[]{:S(2)}) copy-start(bf16[96,512]{1,0:T(8,128)(2,1)S(1)} %collective-permute-done.14.refs_6_) | copy-start | bytes 294916
  58.6 4.3 %collective-permute-start.21 = (bf16[96,512]{1,0:T(8,128)(2,1)S(1)}, bf16[96,512]{1,0:T(8,128)(2,1)S(1)}, u32[]{:S(2)}, u32[]{:S(2)}) collective-permute-start(bf16[96,512]{1,0:T(8,128)(2,1)S(1)} %collective-permute-done.13.refs_5_), channel_id=1, source_target_pairs={{0,1},{1,0},{2,3},{3,2},{4,5},{5,4},{6,7},{7,6},{8,9},{9,8},{10,11... | collective-permute-start | bytes 294920 | tf_op jit(solution)/shard_map/ppermute | solution.py:1097
  60.1 3.4 %copy-start.7 = (bf16[96,512]{1,0:T(8,128)(2,1)}, bf16[96,512]{1,0:T(8,128)(2,1)S(1)}, u32[]{:S(2)}) copy-start(bf16[96,512]{1,0:T(8,128)(2,1)S(1)} %collective-permute-done.15.refs_7_) | copy-start | bytes 294916
  60.1 2.8 %collective-permute-start.19 = (bf16[96,512]{1,0:T(8,128)(2,1)S(1)}, bf16[96,512]{1,0:T(8,128)(2,1)S(1)}, u32[]{:S(2)}, u32[]{:S(2)}) collective-permute-start(bf16[96,512]{1,0:T(8,128)(2,1)S(1)} %collective-permute-done.11.refs_3_), channel_id=1, source_target_pairs={{0,1},{1,0},{2,3},{3,2},{4,5},{5,4},{6,7},{7,6},{8,9},{9,8},{10,11... | collective-permute-start | bytes 294920 | tf_op jit(solution)/shard_map/ppermute | solution.py:1097
  61.9 1.5 %copy-start.8 = (bf16[96,512]{1,0:T(8,128)(2,1)}, bf16[96,512]{1,0:T(8,128)(2,1)S(1)}, u32[]{:S(2)}) copy-start(bf16[96,512]{1,0:T(8,128)(2,1)S(1)} %collective-permute-done.17.refs_9_) | copy-start | bytes 294916
  61.9 1.4 %collective-permute-start.22 = (bf16[96,512]{1,0:T(8,128)(2,1)S(1)}, bf16[96,512]{1,0:T(8,128)(2,1)S(1)}, u32[]{:S(2)}, u32[]{:S(2)}) collective-permute-start(bf16[96,512]{1,0:T(8,128)(2,1)S(1)} %collective-permute-done.14.refs_6_), channel_id=1, source_target_pairs={{0,1},{1,0},{2,3},{3,2},{4,5},{5,4},{6,7},{7,6},{8,9},{9,8},{10,11... | collective-permute-start | bytes 294920 | tf_op jit(solution)/shard_map/ppermute | solution.py:1097
  62.0 1.5 %copy-start.9 = (bf16[96,512]{1,0:T(8,128)(2,1)}, bf16[96,512]{1,0:T(8,128)(2,1)S(1)}, u32[]{:S(2)}) copy-start(bf16[96,512]{1,0:T(8,128)(2,1)S(1)} %collective-permute-done.18.refs_10_) | copy-start | bytes 294916
  62.0 1.4 %collective-permute-start.23 = (bf16[96,512]{1,0:T(8,128)(2,1)S(1)}, bf16[96,512]{1,0:T(8,128)(2,1)S(1)}, u32[]{:S(2)}, u32[]{:S(2)}) collective-permute-start(bf16[96,512]{1,0:T(8,128)(2,1)S(1)} %collective-permute-done.15.refs_7_), channel_id=1, source_target_pairs={{0,1},{1,0},{2,3},{3,2},{4,5},{5,4},{6,7},{7,6},{8,9},{9,8},{10,11... | collective-permute-start | bytes 294920 | tf_op jit(solution)/shard_map/ppermute | solution.py:1097
  62.9 0.6 copy-start.12
  62.9 0.7 copy-start.10
  62.9 0.7 copy-start.11
  63.3 0.6 copy-start.13
  63.5 0.6 copy-start.14
  72.3 2.7 %collective-permute-start.24 = (bf16[768,512]{1,0:T(8,128)(2,1)}, bf16[768,512]{1,0:T(8,128)(2,1)}, u32[]{:S(2)}, u32[]{:S(2)}) collective-permute-start(bf16[768,512]{1,0:T(8,128)(2,1)} %get-tuple-element.54), channel_id=1, source_target_pairs={{0,1},{1,0},{2,3},{3,2},{4,5},{5,4},{6,7},{7,6},{8,9},{9,8},{10,11... | collective-permute-start | bytes 2359304 | tf_op jit(solution)/shard_map/ppermute | solution.py:1097
  72.8 9.6 %collective-permute-start.32 = (bf16[8,64,256]{2,1,0:T(8,128)(2,1)}, bf16[8,64,256]{2,1,0:T(8,128)(2,1)}, u32[]{:S(2)}, u32[]{:S(2)}) collective-permute-start(bf16[8,64,256]{2,1,0:T(8,128)(2,1)} %choose.1.refs_13_), channel_id=1, source_target_pairs={{0,4},{4,0},{8,12},{12,8},{16,20},{20,16},{24,28},{28,24},{1,5},{5... | collective-permute-start | bytes 786440 | tf_op jit(solution)/shard_map/ppermute | solution.py:1097
  77.5 6.9 %collective-permute-start.25 = (bf16[96,512]{1,0:T(8,128)(2,1)}, bf16[96,512]{1,0:T(8,128)(2,1)}, u32[]{:S(2)}, u32[]{:S(2)}) collective-permute-start(bf16[96,512]{1,0:T(8,128)(2,1)} %get-tuple-element.57), channel_id=1, source_target_pairs={{0,4},{4,0},{8,12},{12,8},{16,20},{20,16},{24,28},{28,24},{1,5},{5... | collective-permute-start | bytes 294920 | tf_op jit(solution)/shard_map/ppermute | solution.py:1097
  79.6 6.3 %collective-permute-start.26 = (bf16[96,512]{1,0:T(8,128)(2,1)}, bf16[96,512]{1,0:T(8,128)(2,1)}, u32[]{:S(2)}, u32[]{:S(2)}) collective-permute-start(bf16[96,512]{1,0:T(8,128)(2,1)} %get-tuple-element.58), channel_id=1, source_target_pairs={{0,8},{4,12},{8,0},{12,4},{16,24},{20,28},{24,16},{28,20},{1,9},{5... | collective-permute-start | bytes 294920 | tf_op jit(solution)/shard_map/ppermute | solution.py:1097
  79.6 14.3 %collective-permute-start.27 = (bf16[96,512]{1,0:T(8,128)(2,1)}, bf16[96,512]{1,0:T(8,128)(2,1)}, u32[]{:S(2)}, u32[]{:S(2)}) collective-permute-start(bf16[96,512]{1,0:T(8,128)(2,1)} %get-tuple-element.59), channel_id=1, source_target_pairs={{0,12},{4,8},{8,4},{12,0},{16,28},{20,24},{24,20},{28,16},{1,13},{... | collective-permute-start | bytes 294920 | tf_op jit(solution)/shard_map/ppermute | solution.py:1097
  80.9 13.1 %collective-permute-start.28 = (bf16[96,512]{1,0:T(8,128)(2,1)}, bf16[96,512]{1,0:T(8,128)(2,1)}, u32[]{:S(2)}, u32[]{:S(2)}) collective-permute-start(bf16[96,512]{1,0:T(8,128)(2,1)} %get-tuple-element.60), channel_id=1, source_target_pairs={{0,16},{4,20},{8,24},{12,28},{16,0},{20,4},{24,8},{28,12},{1,17},{... | collective-permute-start | bytes 294920 | tf_op jit(solution)/shard_map/ppermute | solution.py:1097
  82.3 13.1 %collective-permute-start.29 = (bf16[96,512]{1,0:T(8,128)(2,1)}, bf16[96,512]{1,0:T(8,128)(2,1)}, u32[]{:S(2)}, u32[]{:S(2)}) collective-permute-start(bf16[96,512]{1,0:T(8,128)(2,1)} %get-tuple-element.61), channel_id=1, source_target_pairs={{0,20},{4,16},{8,28},{12,24},{16,4},{20,0},{24,12},{28,8},{1,21},{... | collective-permute-start | bytes 294920 | tf_op jit(solution)/shard_map/ppermute | solution.py:1097
  84.3 14.2 %collective-permute-start.30 = (bf16[96,512]{1,0:T(8,128)(2,1)}, bf16[96,512]{1,0:T(8,128)(2,1)}, u32[]{:S(2)}, u32[]{:S(2)}) collective-permute-start(bf16[96,512]{1,0:T(8,128)(2,1)} %get-tuple-element.62), channel_id=1, source_target_pairs={{0,24},{4,28},{8,16},{12,20},{16,8},{20,12},{24,0},{28,4},{1,25},{... | collective-permute-start | bytes 294920 | tf_op jit(solution)/shard_map/ppermute | solution.py:1097
  85.9 15.7 %collective-permute-start.31 = (bf16[96,512]{1,0:T(8,128)(2,1)}, bf16[96,512]{1,0:T(8,128)(2,1)}, u32[]{:S(2)}, u32[]{:S(2)}) collective-permute-start(bf16[96,512]{1,0:T(8,128)(2,1)} %get-tuple-element.63), channel_id=1, source_target_pairs={{0,28},{4,24},{8,20},{12,16},{16,12},{20,8},{24,4},{28,0},{1,29},{... | collective-permute-start | bytes 294920 | tf_op jit(solution)/shard_map/ppermute | solution.py:1097
  104.3 7.0 %collective-permute-start.33 = (bf16[256,512]{1,0:T(8,128)(2,1)}, bf16[256,512]{1,0:T(8,128)(2,1)S(1)}, u32[]{:S(2)}, u32[]{:S(2)}) collective-permute-start(bf16[256,512]{1,0:T(8,128)(2,1)} %combine.1), channel_id=1, source_target_pairs={{0,2},{1,3},{2,0},{3,1},{4,6},{5,7},{6,4},{7,5},{8,10},{9,11},{10,... | collective-permute-start | bytes 786440 | tf_op jit(solution)/shard_map/ppermute | solution.py:1097
  112.5 3.2 %collective-permute-start.34 = (bf16[256,512]{1,0:T(8,128)(2,1)S(1)}, bf16[256,512]{1,0:T(8,128)(2,1)S(1)}, u32[]{:S(2)}, u32[]{:S(2)}) collective-permute-start(bf16[256,512]{1,0:T(8,128)(2,1)S(1)} %add_convert_fusion), channel_id=1, source_target_pairs={{0,1},{1,0},{2,3},{3,2},{4,5},{5,4},{6,7},{7,6},{8,9},{9,8},{10,11... | collective-permute-start | bytes 786440 | tf_op jit(solution)/shard_map/ppermute | solution.py:1097
